TPU v7x, 32 devices: a whole 2x2x4 slice. The times are simulated.
32 devices in a mesh: leaf: 4 (over y, x), row: 2 (over core), col: 4 (over z).
Axes of the slice: x: 2, y: 2, z: 4, core: 2. Of those that a mesh axis runs over, the one named last changes fastest.
Arguments:
- sigma_top: float32 [1024, 1024], P(('leaf', 'row'), 'col')
- panels: float32 [4, 7, 1024, 512], P('leaf', None, 'row', 'col'), may hold values from -0.1875 to 0.1875
- inverse_diag: float32 [4, 7, 512, 512], P('leaf', None, 'col')
- slot_lists: int32 [4, 6, 8], P('leaf'), may hold values from -1 to 11, as said below
- parent_links: int32 [4, 4], P('leaf'), may hold values from 1 to 2
Outputs:
- ancestor_block: float32 [4, 7, 1024, 512], P('leaf', None, 'row', 'col')
- diagonal_block: float32 [4, 7, 512, 512], P('leaf', None, None, 'col')
Inputs may be any that keep to these rules, and one draw needn't show every extreme that they name: `slot_lists`: in every row, entries 0 to 3 are 8 to 11 in order (the parent's own tiles); then come 1 to 3 distinct parent ancestor slots, below 8 for supernodes 1 and 2 and below 4 for supernodes 3 to 6; the rest are -1, so every row has padding. `parent_links`: each supernode 3 to 6 has supernode 1 or 2 as its parent. `sigma_top`: symmetric.
All inputs are finite; a program needn't handle non-finite values.
Results may differ from a plain program's by a relative error of at most 0.0001.
Values sent between devices are 32-bit elements; how exact they have to be, the bound alone decides.
No kernel may reach another device: no remote copies, remote signals or barrier semaphores. Data moves between devices by JAX's collectives and lax.ppermute only.
A program may use at most 128 MiB of HBM per device.

v0:
```python
import jax
import jax.numpy as jnp
from jax import lax
from jax.sharding import PartitionSpec as P

TILE = 128


def child_blocks(ancestors, products, diagonals, parent_ids, picks, tile):
    count_parents = ancestors.shape[0]
    slot_count = ancestors.shape[1] // tile
    own_width = diagonals.shape[1]
    own_tiles = own_width // tile
    tail = picks[:, own_tiles:]
    living = tail >= 0
    indices = jnp.maximum(tail, 0)
    child_count = tail.shape[0]
    tail_count = tail.shape[1]
    a_tiles = ancestors.reshape(count_parents, slot_count, tile, slot_count, tile)
    corner = a_tiles[parent_ids[:, None, None], indices[:, :, None], :, indices[:, None, :], :]
    corner = jnp.transpose(corner, (0, 1, 3, 2, 4))
    weights = (living[:, :, None] & living[:, None, :]).astype(jnp.float32)
    corner = corner * weights[:, :, None, :, None]
    corner = corner.reshape(child_count, tail_count * tile, tail_count * tile)
    p_tiles = products.reshape(count_parents, slot_count, tile, own_width)
    side = p_tiles[parent_ids[:, None], indices]
    side = side * living.astype(jnp.float32)[:, :, None, None]
    side = side.reshape(child_count, tail_count * tile, own_width)
    top_left = jnp.take(diagonals, parent_ids, axis=0)
    upper = jnp.concatenate([top_left, -jnp.transpose(side, (0, 2, 1))], axis=2)
    lower = jnp.concatenate([-side, corner], axis=2)
    return jnp.concatenate([upper, lower], axis=1)


def body(sigma_top, panels, inverse_diag, slot_lists, parent_links):
    highest = lax.Precision.HIGHEST
    row_count = lax.axis_size("row")
    col_count = lax.axis_size("col")
    row_index = lax.axis_index("row")
    col_index = lax.axis_index("col")
    panel_local = panels[0]
    inverse_local = inverse_diag[0]
    picks_all = slot_lists[0]
    parents = parent_links[0]
    block_rows = panel_local.shape[1]
    block_cols = panel_local.shape[2]
    diag_width = inverse_local.shape[2]
    diag_rows = diag_width // row_count
    tile = TILE
    top_rows = lax.all_gather(sigma_top, ("leaf", "row"), axis=0, tiled=True)
    top_full = lax.all_gather(top_rows, "col", axis=1, tiled=True)
    partial_factor = jnp.einsum("vrk,vkj->vrj", panel_local, inverse_local, precision=highest)
    inverse_band = lax.dynamic_slice_in_dim(inverse_local, row_index * diag_rows, diag_rows, 2)
    partial_gram = jnp.einsum("vki,vkj->vij", inverse_band, inverse_local, precision=highest)
    factor_rows = lax.psum(partial_factor, "col")
    gram_mine = lax.psum_scatter(partial_gram, "col", scatter_dimension=2, tiled=True)
    slots_here = block_rows // tile
    slot_ids = row_index * slots_here + jnp.arange(slots_here, dtype=jnp.int32)
    listed = jnp.take(picks_all, slot_ids, axis=1) >= 0
    living = jnp.concatenate([jnp.ones((1, slots_here), jnp.bool_), listed], axis=0)
    row_weight = jnp.repeat(living.astype(jnp.float32), tile, axis=1)
    factor_rows = factor_rows * row_weight[:, :, None]
    factor_mine = lax.dynamic_slice_in_dim(factor_rows, col_index * block_cols, block_cols, 2)
    factor_cols = lax.all_gather(factor_mine, "row", axis=1, tiled=True)
    ancestors = top_full[None]
    ancestor_parts = []
    diagonal_parts = []
    bounds = ((0, 1), (1, 3), (3, 7))
    for level_id, (first_node, last_node) in enumerate(bounds):
        own_rows = lax.dynamic_slice_in_dim(ancestors, row_index * block_rows, block_rows, 1)
        product_mine = jnp.einsum(
            "vra,vac->vrc", own_rows, factor_cols[first_node:last_node], precision=highest
        )
        partial_diag = jnp.einsum(
            "vrj,vrc->vjc", factor_rows[first_node:last_node], product_mine, precision=highest
        )
        diag_piece = lax.psum_scatter(partial_diag, "row", scatter_dimension=1, tiled=True)
        diag_piece = diag_piece + gram_mine[first_node:last_node]
        ancestor_parts.append(-product_mine)
        if level_id == 2:
            diag_cols = lax.all_gather(diag_piece, "row", axis=1, tiled=True)
        else:
            width_nodes = last_node - first_node
            product_all, diag_all = (
                lax.all_gather(product_mine[:, None], ("row", "col"), axis=1, tiled=True),
                lax.all_gather(diag_piece[:, None], ("row", "col"), axis=1, tiled=True),
            )
            product_full = product_all.reshape(
                width_nodes, row_count, col_count, block_rows, block_cols
            )
            product_full = product_full.transpose(0, 1, 3, 2, 4).reshape(
                width_nodes, row_count * block_rows, col_count * block_cols
            )
            diag_full = diag_all.reshape(width_nodes, row_count, col_count, diag_rows, block_cols)
            diag_full = diag_full.transpose(0, 1, 3, 2, 4).reshape(
                width_nodes, row_count * diag_rows, col_count * block_cols
            )
            diag_cols = lax.dynamic_slice_in_dim(diag_full, col_index * block_cols, block_cols, 2)
            if level_id == 0:
                parent_ids = jnp.zeros((2,), jnp.int32)
                picks_level = picks_all[0:2]
            else:
                parent_ids = parents - 1
                picks_level = picks_all[2:6]
            ancestors = child_blocks(
                ancestors, product_full, diag_full, parent_ids, picks_level, tile
            )
        diagonal_parts.append(diag_cols)
    ancestor_block = jnp.concatenate(ancestor_parts, axis=0)[None]
    diagonal_block = jnp.concatenate(diagonal_parts, axis=0)[None]
    return (ancestor_block, diagonal_block)


def solution(mesh):
    return jax.shard_map(
        body,
        mesh=mesh,
        in_specs=(
            P(("leaf", "row"), "col"),
            P("leaf", None, "row", "col"),
            P("leaf", None, "col", None),
            P("leaf", None, None),
            P("leaf", None),
        ),
        out_specs=(P("leaf", None, "row", "col"), P("leaf", None, None, "col")),
        check_vma=False,
    )
```

profile of v0, /device:TPU:0, one launch (start us, length us, event | category | flops | bytes accessed | tf_op | source)
XLA Modules:
  0.0 719.2 jit_solution(1050629731004631438)
XLA Ops:
  9.5 9.5 %fusion.15 = f32[7,512,512]{2,1,0:T(8,128)} fusion(f32[1,7,128,512]{3,2,1,0:T(8,128)S(1)} %copy-done, f32[1,7,512,128]{3,2,1,0:T(8,128)} %param.6), kind=kOutput, calls=%fused_computation.35 | convolution fusion | flops 2818572288 | bytes 11010048 | tf_op jit(solution)/shard_map/vrk,vkj->vrj/dot_general | solution.py:52
  19.0 17.9 %all-gather.13.cloned.1.call-done = f32[1024,256]{1,0:T(8,128)} async-done(((f32[128,256]{1,0:T(8,128)}), f32[1024,256]{1,0:T(8,128)}) %all-gather.13.cloned.1.call-update) | async-done | bytes 1048592 | tf_op jit(solution)/shard_map/all_gather | solution.py:50
  38.1 240.3 %all-reduce.4.cloned.1.call-done = f32[7,512,512]{2,1,0:T(8,128)} async-done(((f32[7,512,512]{2,1,0:T(8,128)}), f32[7,512,512]{2,1,0:T(8,128)}) %all-reduce.4.cloned.1.call-update) | async-done | bytes 7340048 | tf_op jit(solution)/shard_map/psum | solution.py:55
  286.3 5.0 fusion.13
  291.4 68.0 %all-gather.15.cloned.1.call-done = f32[1024,1024]{1,0:T(8,128)} async-done(((f32[1024,256]{1,0:T(8,128)}), f32[1024,1024]{1,0:T(8,128)}) %all-gather.15.cloned.1.call-update) | async-done | bytes 4194320 | tf_op jit(solution)/shard_map/all_gather | solution.py:51
  359.3 13.3 %all-gather.17.cloned.1.call-done = f32[7,1024,128]{2,1,0:T(8,128)} async-done(((f32[7,512,128]{2,1,0:T(8,128)}), f32[7,1024,128]{2,1,0:T(8,128)}) %all-gather.17.cloned.1.call-update) | async-done | bytes 3670032 | tf_op jit(solution)/shard_map/all_gather | solution.py:64
  380.0 64.6 %reduce-scatter.7.cloned.1.call-done = f32[7,256,128]{2,1,0:T(8,128)} async-done(((f32[7,256,512]{2,1,0:T(8,128)}), f32[7,256,128]{2,1,0:T(8,128)}) %reduce-scatter.7.cloned.1.call-update) | async-done | bytes 917520 | tf_op jit(solution)/shard_map/reduce_scatter | solution.py:56
  444.6 10.7 %reduce-scatter.5.cloned.1.call-done = f32[1,256,128]{2,1,0:T(8,128)} async-done(((f32[1,512,128]{2,1,0:T(8,128)}), f32[1,256,128]{2,1,0:T(8,128)}) %reduce-scatter.5.cloned.1.call-update) | async-done | bytes 131088 | tf_op jit(solution)/shard_map/reduce_scatter | solution.py:77
  464.5 4.4 gather_fusion.2
  485.0 25.9 %all-gather.23.cloned.1.call-done = f32[4096,128]{1,0:T(8,128)} async-done(((f32[512,128]{1,0:T(8,128)}), f32[4096,128]{1,0:T(8,128)}) %all-gather.23.cloned.1.call-update) | async-done | bytes 2097168 | tf_op jit(solution)/shard_map/all_gather | solution.py:85
  525.3 5.4 copy.58
  537.8 4.9 fusion.34
  542.7 6.0 fusion.35
  548.8 7.5 %reduce-scatter.9.cloned.1.call-done = f32[2,256,128]{2,1,0:T(8,128)} async-done(((f32[2,512,128]{2,1,0:T(8,128)}), f32[2,256,128]{2,1,0:T(8,128)}) %reduce-scatter.9.cloned.1.call-update) | async-done | bytes 262160 | tf_op jit(solution)/shard_map/reduce_scatter | solution.py:77
  558.5 10.7 %reduce-scatter.11.cloned.1.call-start = ((), (), s32[]{:S(2)}) async-start(), calls=%async_computation.11 | async-start | bytes 1572864 | tf_op jit(solution)/shard_map/reduce_scatter | solution.py:77
  569.9 5.5 copy.74
  575.4 4.8 copy.63
  580.2 6.2 gather_fusion.5
  589.0 4.8 copy.64
  593.8 5.5 reshape.184
  599.3 4.3 copy.84
  606.8 4.4 gather_fusion.3
  611.2 25.9 %all-gather.27.cloned.1.call-done = f32[2,4096,128]{2,1,0:T(8,128)} async-done(((f32[2,512,128]{2,1,0:T(8,128)}), f32[2,4096,128]{2,1,0:T(8,128)}) %all-gather.27.cloned.1.call-update) | async-done | bytes 4194320 | tf_op jit(solution)/shard_map/all_gather | solution.py:85
  637.1 6.8 copy.83
  643.9 5.5 reshape_reshape.7
  649.4 5.0 gather_fusion.4
  654.4 7.1 fusion.6
  661.4 5.2 copy.62
  666.7 13.1 %fusion.33 = (f32[4,512,128]{2,1,0:T(8,128)}, f32[4,512,128]{2,1,0:T(8,128)S(1)}) fusion(f32[7,1024,128]{2,1,0:T(8,128)} %all-gather.17.cloned.1.call-done, s32[]{:T(128)S(6)} %select_n.81, f32[4,512,512]{2,1,0:T(8,128)} %get-tuple-element.17, f32[4,512,512]{2,1,0:T(8,128)} %copy.62, f32[4,512,512]{2,1,0:T(8,128)} %get-tuple-element.16, ...), kind=kOutput, calls=%fused_computation.93 | convolution fusion | flops 3227779072 | bytes 20971524 | tf_op jit(solution)/shard_map/vra,vac->vrc/dot_general | solution.py:71
  679.8 9.9 %fusion.36 = f32[4,512,128]{2,1,0:T(8,128)} fusion(f32[7,512,512]{2,1,0:T(8,128)} %copy-done.2, f32[4,512,128]{2,1,0:T(8,128)S(1)} %get-tuple-element.13), kind=kOutput, calls=%fused_computation.96 | convolution fusion | flops 1610612736 | bytes 9437184 | tf_op jit(solution)/shard_map/vrj,vrc->vjc/dot_general | solution.py:74
  689.8 7.3 %reduce-scatter.11.cloned.1.call-done = f32[4,256,128]{2,1,0:T(8,128)} async-done(((f32[4,512,128]{2,1,0:T(8,128)}), f32[4,256,128]{2,1,0:T(8,128)}) %reduce-scatter.11.cloned.1.call-update) | async-done | bytes 524304 | tf_op jit(solution)/shard_map/reduce_scatter | solution.py:77
  704.6 4.5 all-gather.19.cloned.1.call-done
  (115 shorter events, 83.4 us)
Async XLA Ops:
  8.0 1.5 copy-start
  8.0 28.9 %all-gather.13.cloned.1.call-start = ((), (), s32[]{:S(2)}) async-start(), calls=%async_computation.4 | async-start | bytes 1179648 | tf_op jit(solution)/shard_map/all_gather | solution.py:50
  8.7 269.6 %all-reduce.4.cloned.1.call-start = ((), (), s32[]{:S(2)}) async-start(), calls=%async_computation.6 | async-start | bytes 14680064 | tf_op jit(solution)/shard_map/psum | solution.py:55
  19.0 18.1 %copy-start.10 = (s32[1,6,8]{2,0,1:T(1,128)S(1)}, s32[1,6,8]{2,0,1:T(1,128)}, u32[]{:S(2)}) copy-start(s32[1,6,8]{2,0,1:T(1,128)} %param.8) | copy-start | bytes 580
  19.0 340.3 %all-gather.15.cloned.1.call-start = ((), (), s32[]{:S(2)}) async-start(), calls=%async_computation.5 | async-start | bytes 5242880 | tf_op jit(solution)/shard_map/all_gather | solution.py:51
  37.0 335.7 %all-gather.17.cloned.1.call-start = ((), (), s32[]{:S(2)}) async-start(), calls=%async_computation.7 | async-start | bytes 5505024 | tf_op jit(solution)/shard_map/all_gather | solution.py:64
  281.9 2.9 copy-start.2
  286.3 158.4 %reduce-scatter.7.cloned.1.call-start = ((), (), s32[]{:S(2)}) async-start(), calls=%async_computation.9 | async-start | bytes 4587520 | tf_op jit(solution)/shard_map/reduce_scatter | solution.py:56
  291.3 164.1 %reduce-scatter.5.cloned.1.call-start = ((), (), s32[]{:S(2)}) async-start(), calls=%async_computation.8 | async-start | bytes 393216 | tf_op jit(solution)/shard_map/reduce_scatter | solution.py:77
  376.1 80.9 %copy-start.6 = (f32[512,128]{1,0:T(8,128)}, f32[512,128]{1,0:T(8,128)S(1)}, u32[]{:S(2)}) copy-start(f32[512,128]{1,0:T(8,128)S(1)} %fusion.11) | copy-start | bytes 786436
  380.0 100.5 %all-gather.21.cloned.1.call-start = ((), (), s32[]{:S(2)}) async-start(), calls=%async_computation.13 | async-start | bytes 1179648 | tf_op jit(solution)/shard_map/all_gather | solution.py:86
  457.0 53.9 %all-gather.23.cloned.1.call-start = ((), (), s32[]{:S(2)}) async-start(), calls=%async_computation.14 | async-start | bytes 2359296 | tf_op jit(solution)/shard_map/all_gather | solution.py:85
  457.8 98.5 %reduce-scatter.9.cloned.1.call-start = ((), (), s32[]{:S(2)}) async-start(), calls=%async_computation.10 | async-start | bytes 786432 | tf_op jit(solution)/shard_map/reduce_scatter | solution.py:77
  519.1 3.3 copy-start.4
  534.5 3.3 copy-start.3
  542.7 15.3 %copy-start.5 = (f32[2,512,128]{2,1,0:T(8,128)}, f32[2,512,128]{2,1,0:T(8,128)S(1)}, u32[]{:S(2)}) copy-start(f32[2,512,128]{2,1,0:T(8,128)S(1)} %get-tuple-element.15) | copy-start | bytes 1572868
  542.7 13.6 %copy-start.9 = (f32[7,256,128]{2,1,0:T(8,128)S(1)}, f32[7,256,128]{2,1,0:T(8,128)}, u32[]{:S(2)}) copy-start(f32[7,256,128]{2,1,0:T(8,128)} %reduce-scatter.7.cloned.1.call-done) | copy-start | bytes 2752516
  542.7 26.5 %copy-start.11 = (s32[1,4]{1,0:T(1,128)S(1)}, s32[1,4]{1,0:T(1,128)}, u32[]{:S(2)}) copy-start(s32[1,4]{1,0:T(1,128)} %param.9) | copy-start | bytes 52
  548.7 50.6 %all-gather.25.cloned.1.call-start = ((), (), s32[]{:S(2)}) async-start(), calls=%async_computation.15 | async-start | bytes 2359296 | tf_op jit(solution)/shard_map/all_gather | solution.py:86
  558.0 79.1 %all-gather.27.cloned.1.call-start = ((), (), s32[]{:S(2)}) async-start(), calls=%async_computation.16 | async-start | bytes 4718592 | tf_op jit(solution)/shard_map/all_gather | solution.py:85
  558.5 138.5 %reduce-scatter.11.cloned.1.call-start = ((), (), s32[]{:S(2)}) async-start(), calls=%async_computation.11 | async-start | bytes 1572864 | tf_op jit(solution)/shard_map/reduce_scatter | solution.py:77
  679.8 19.1 %copy-start.7 = (f32[512,128]{1,0:T(8,128)S(1)}, f32[512,128]{1,0:T(8,128)}, u32[]{:S(2)}) copy-start(f32[512,128]{1,0:T(8,128)} %copy-done.6) | copy-start | bytes 786436
  689.7 19.4 %all-gather.19.cloned.1.call-start = ((), (), s32[]{:S(2)}) async-start(), calls=%async_computation.12 | async-start | bytes 1572864 | tf_op jit(solution)/shard_map/all_gather | solution.py:81
  700.1 11.6 %copy-start.1 = (f32[1,7,128,512]{3,2,1,0:T(8,128)S(1)}, f32[1,7,128,512]{3,2,1,0:T(8,128)}, u32[]{:S(2)}) copy-start(f32[1,7,128,512]{3,2,1,0:T(8,128)} %param.7) | copy-start | bytes 5505028
  700.8 8.3 %copy-start.8 = (f32[1,512,128]{2,1,0:T(8,128)S(1)}, f32[1,512,128]{2,1,0:T(8,128)}, u32[]{:S(2)}) copy-start(f32[1,512,128]{2,1,0:T(8,128)} %constant_dynamic-slice_fusion) | copy-start | bytes 786436
Sparse Core Ops, SparseCore 0:
  10.7 26.1 all-gather.12
  457.1 23.3 all-gather.20
  482.2 28.7 all-gather.22
  558.1 30.2 all-gather.24
  590.4 46.6 all-gather.26
Sparse Core Ops, SparseCore 1:
  19.1 259.2 all-reduce.3
  279.8 79.5 all-gather.14
  361.3 11.3 all-gather.16
  375.0 69.6 reduce-scatter.6
  447.4 7.9 reduce-scatter.4
  548.8 7.4 reduce-scatter.8
  689.8 7.2 reduce-scatter.10
  699.0 10.0 all-gather.18
where the time goes:
time: 729 us; the launch traced here: 719 us
  waiting for transfers between devices  492 us (67%)
  local copies, waits for them, and re-layouts  108 us (15%)
  matrix products  55.6 us (8%)
  other arithmetic  36.7 us (5%)
  between operations  16 us (2%)
  starting transfers between devices  11.4 us (2%)
    psum x1, waiting for transfers between devices, body(): factor_rows = lax.psum(partial_factor, 'col')  240 us
    all_gather x1, waiting for transfers between devices, body(): top_full = lax.all_gather(top_rows, 'col', axis=1, tiled=True)  68 us
    reduce_scatter x1, waiting for transfers between devices, body(): lax.psum_scatter(partial_gram, 'col', scatter_dimension=2, tiled=True)  64.6 us
    all_gather x2, waiting for transfers between devices, body(): lax.all_gather(product_mine[:, None], ('row', 'col'), axis=1, tiled=True)  51.8 us
    reduce_scatter x3, waiting for transfers between devices, body(): lax.psum_scatter(partial_diag, 'row', scatter_dimension=1, tiled=True)  25.4 us
    dot_general x3, matrix products, body(): jnp.einsum('vra,vac->vrc', own_rows, factor_cols[first_node:last_node], p...  21.5 us
    dot_general x3, matrix products, body(): jnp.einsum('vrj,vrc->vjc', factor_rows[first_node:last_node], product_min...  19.7 us
    all_gather x1, waiting for transfers between devices, body(): top_rows = lax.all_gather(sigma_top, ('leaf', 'row'), axis=0, tiled=True)  17.9 us
  transfers between devices with their start and end apart: 13, of which 12 were waited for; matrix products, arithmetic and copies ran while one was open for 14% of the time, Pallas kernels for 0%

commit v1 on v0

--- a/solution.py
+++ b/solution.py
@@ -1,9 +1,358 @@
+import functools
+
 import jax
 import jax.numpy as jnp
 from jax import lax
+from jax.experimental import pallas as pl
+from jax.experimental.pallas import tpu as pltpu
 from jax.sharding import PartitionSpec as P
 
 TILE = 128
+F32 = jnp.float32
+BF16 = jnp.bfloat16
+VMEM_LIMIT = 56 * 2**20
+
+
+def split(x):
+    high = x.astype(BF16)
+    return high, (x - high.astype(F32)).astype(BF16)
+
+
+def dot3(a, b, contract):
+    dims = ((contract, contract if contract == (0,) else (0,)), ((), ()))
+    dot = functools.partial(lax.dot_general, dimension_numbers=dims, preferred_element_type=F32)
+    return dot(a[0], b[0]) + (dot(a[0], b[1]) + dot(a[1], b[0]))
+
+
+def put(pair, index, value):
+    high, low = split(value)
+    pair[0][index] = high
+    pair[1][index] = low
+
+
+def get(pair, index):
+    return pair[0][index], pair[1][index]
+
+
+def at(start, size, unit=TILE):
+    return pl.ds(pl.multiple_of(start, unit), size)
+
+
+def load_panels(blocks, r, p, d, half):
+    quarter = TILE // 2
+    for slot in range(4):
+        for turn in range(2):
+            ref = blocks[2 * slot + turn]
+            side = r if turn == 0 else 1 - r
+            put(p, (at(side * half, half), slice(slot * TILE, (slot + 1) * TILE)), ref[0:half, :])
+            for j in range(4):
+                rows = at(slot * TILE + side * quarter, quarter, quarter)
+                put(d, (rows, slice(j * TILE, (j + 1) * TILE)), ref[half + j * quarter:half + (j + 1) * quarter, :])
+
+
+def solve(p, d, a, dc, f, w, t, base, weights, emit_ab, emit_dg):
+    width = dc[0].shape[1]
+    slots = a[0].shape[0] // TILE
+    dc[0][...] = d[0][:, at(base, width)]
+    dc[1][...] = d[1][:, at(base, width)]
+    step = 2 * TILE
+    for m in range(0, slots * TILE, step):
+        rows = slice(m, m + step)
+        value = dot3(get(p, (rows, slice(None))), get(dc, (slice(None), slice(None))), (1,))
+        if weights is not None:
+            k = m // TILE
+            value = jnp.concatenate([value[:TILE] * weights[k], value[TILE:] * weights[k + 1]], axis=0)
+        put(f, (rows, slice(None)), value)
+    for m in range(0, slots * TILE, step):
+        rows = slice(m, m + step)
+        value = dot3(get(a, (rows, slice(None))), get(f, (slice(None), slice(None))), (1,))
+        emit_ab(m, -value)
+        put(w, (rows, slice(None)), value)
+    for m in range(0, d[0].shape[0], step):
+        cols = slice(m, m + step)
+        value = dot3(get(p, (slice(None), cols)), get(w, (slice(None), slice(None))), (0,))
+        put(t, (cols, slice(None)), value + dc[0][cols, :].astype(F32) + dc[1][cols, :].astype(F32))
+    for m in range(0, d[0].shape[0], step):
+        cols = slice(m, m + step)
+        emit_dg(m, dot3(get(d, (slice(None), cols)), get(t, (slice(None), slice(None))), (0,)))
+
+
+def pair_of(rows, cols):
+    return [pltpu.VMEM((rows, cols), BF16)] * 2
+
+
+def scratch_for(order, own, width):
+    shapes = []
+    for rows, cols in ((order, own), (own, own), (order, order), (own, width), (order, width), (order, width), (own, width)):
+        shapes += pair_of(rows, cols)
+    return shapes
+
+
+def pairs(refs):
+    return [(refs[i], refs[i + 1]) for i in range(0, len(refs), 2)]
+
+
+def call(kernel, scalars, operands, outs, scratch, flops):
+    whole = pl.BlockSpec(memory_space=pltpu.VMEM)
+    traffic = sum(x.size * 4 for x in operands) + sum(4 * rows * cols for rows, cols in outs)
+    return pl.pallas_call(
+        kernel,
+        out_shape=[jax.ShapeDtypeStruct(o, F32) for o in outs],
+        in_specs=[pl.BlockSpec(memory_space=pltpu.SMEM)] + [whole] * len(operands),
+        out_specs=[whole] * len(outs),
+        scratch_shapes=scratch,
+        compiler_params=pltpu.CompilerParams(vmem_limit_bytes=VMEM_LIMIT),
+        cost_estimate=pl.CostEstimate(flops=flops, bytes_accessed=traffic, transcendentals=0),
+    )(scalars, *operands)
+
+
+def tail_of(s, start, own_tiles, tail):
+    index = [jnp.maximum(s[start + own_tiles + j], 0) for j in range(tail)]
+    weight = [(s[start + own_tiles + j] >= 0).astype(F32) for j in range(tail)]
+    return index, weight
+
+
+def weights_of(s, start, slots):
+    return [(s[start + j] >= 0).astype(F32) for j in range(slots)]
+
+
+LIST = 4
+
+
+def root_kernel(s, *refs):
+    blocks, mine, other = refs[:8], refs[8:12], refs[12:16]
+    ext, corner = refs[16:18]
+    p, d, a, dc, f, w, t = pairs(refs[18:])
+    r, c, leaf = s[0], s[1], s[2]
+    order = a[0].shape[0]
+    own = d[0].shape[0]
+    width = dc[0].shape[1]
+    far = c // 2
+    places = (c, 3 * far, 3 - c, 3 - 3 * far)
+    band, span = mine[0].shape[0], mine[0].shape[1] // 4
+    for m in range(4):
+        for turn, ref in ((0, mine[m]), (1, other[m])):
+            side = r if turn == 0 else 1 - r
+            rows = at(((leaf ^ m) * 2 + side) * band, band)
+            for k in range(4):
+                put(a, (rows, at(places[k] * span, span)), ref[:, k * span:(k + 1) * span])
+    load_panels(blocks, r, p, d, order // 2)
+
+    def emit_ab(m, value):
+        ext[m:m + value.shape[0], :] = value
+
+    def emit_dg(m, value):
+        ext[order + m:order + m + value.shape[0], :] = value
+
+    solve(p, d, a, dc, f, w, t, r * width, None, emit_ab, emit_dg)
+    tail = (order - own) // TILE
+    index, weight = tail_of(s, LIST, own // TILE, tail)
+    for i in range(tail):
+        for j in range(tail):
+            high, low = get(a, (at(index[i] * TILE, TILE), at(index[j] * TILE, TILE)))
+            value = (high.astype(F32) + low.astype(F32)) * (weight[i] * weight[j])
+            corner[i * TILE:(i + 1) * TILE, j * TILE:(j + 1) * TILE] = value
+
+
+def join_parent(a, x, order, own, offset, index, weight):
+    width = x.shape[1]
+    put(a, (slice(0, own), at(offset, width)), x[order:order + own, :])
+    for j in range(len(index)):
+        place = slice(own + j * TILE, own + (j + 1) * TILE)
+        value = x[at(index[j] * TILE, TILE), :] * weight[j]
+        put(a, (place, at(offset, width)), value)
+        put(a, (at(offset, width), place), value.T)
+
+
+def middle_kernel(s, *refs):
+    blocks, mine, other, corner = refs[:8], refs[8], refs[9], refs[10]
+    ext, grand = refs[11:13]
+    p, d, a, dc, f, w, t = pairs(refs[13:])
+    r = s[0]
+    order = a[0].shape[0]
+    own = d[0].shape[0]
+    width = dc[0].shape[1]
+    load_panels(blocks, r, p, d, order // 2)
+    index, weight = tail_of(s, LIST, own // TILE, (order - own) // TILE)
+    span = mine.shape[1]
+    join_parent(a, mine, order, own, r * span, index, weight)
+    join_parent(a, other, order, own, (1 - r) * span, index, weight)
+    put(a, (slice(own, order), slice(own, order)), corner[...])
+    grand[:, at(r * span, span)] = mine[order:order + own, :]
+    grand[:, at((1 - r) * span, span)] = other[order:order + own, :]
+    weights = weights_of(s, LIST, order // TILE)
+    for base in range(0, own, width):
+        def emit_ab(m, value):
+            ext[m:m + value.shape[0], base:base + width] = value
+
+        def emit_dg(m, value):
+            ext[order + m:order + m + value.shape[0], base:base + width] = value
+
+        solve(p, d, a, dc, f, w, t, base, weights, emit_ab, emit_dg)
+
+
+def leaf_kernel(s, *refs):
+    blocks, mine, other, grand = refs[:8], refs[8], refs[9], refs[10]
+    self_out, core_out, end_out, cross_out = refs[11:15]
+    p, d, a, dc, f, w, t = pairs(refs[15:29])
+    ab, dg = refs[29:31]
+    r, c = s[0], s[1]
+    order = a[0].shape[0]
+    own = d[0].shape[0]
+    width = dc[0].shape[1]
+    far = c // 2
+    load_panels(blocks, r, p, d, order // 2)
+    tail = (order - own) // TILE
+    index, weight = tail_of(s, LIST, own // TILE, tail)
+
+    @pl.when(s[3] == 1)
+    def _():
+        join_parent(a, mine, order, own, 0, index, weight)
+
+    @pl.when(s[3] == 0)
+    def _():
+        join_parent(a, other, order, own, 0, index, weight)
+
+    for i in range(tail):
+        for j in range(tail):
+            value = grand[at(index[i] * TILE, TILE), at(index[j] * TILE, TILE)] * (weight[i] * weight[j])
+            put(a, (slice(own + i * TILE, own + (i + 1) * TILE), slice(own + j * TILE, own + (j + 1) * TILE)), value)
+
+    def emit_ab(m, value):
+        ab[m:m + value.shape[0], :] = value
+
+    def emit_dg(m, value):
+        dg[m:m + value.shape[0], :] = value
+
+    solve(p, d, a, dc, f, w, t, far * width, weights_of(s, LIST, order // TILE), emit_ab, emit_dg)
+    half = order // 2
+    near_cols, end_cols = at((1 - far) * TILE, TILE), at(far * TILE, TILE)
+    for out, side, cols in (
+        (self_out, r, near_cols), (core_out, 1 - r, near_cols), (end_out, r, end_cols), (cross_out, 1 - r, end_cols)
+    ):
+        out[0:half, :] = ab[at(side * half, half), cols]
+        out[half:, :] = dg[:, cols]
+
+
+def chip_body(sigma_top, panels, inverse_diag, slot_lists, parent_links):
+    r = lax.axis_index("row")
+    c = lax.axis_index("col")
+    leaf = lax.axis_index("leaf")
+    panels, inverse, lists, links = panels[0], inverse_diag[0], slot_lists[0], parent_links[0]
+    half = panels.shape[1]
+    order = 2 * half
+    own = inverse.shape[2]
+    slots = order // TILE
+    quarter = TILE // 2
+    both = ("row", "col")
+
+    routes = (((0, 1), (3, 2)), ((1, 2), (2, 1)), ((0, 2), (3, 1)))
+    cross = [[(row * 4 + a, (1 - row) * 4 + b) for row in range(2) for a, b in route] for route in routes]
+    middles = (1, 2)
+    swap = [(row * 4 + a, (1 - row) * 4 + a) for row in range(2) for a in middles]
+    home = ((1, 0), (2, 3))
+    home_cross = [(row * 4 + a, (1 - row) * 4 + b) for row in range(2) for a, b in home]
+
+    def straight(x):
+        return [lax.ppermute(x, "col", route) for route in routes]
+
+    def crossed(x):
+        return [lax.ppermute(x, both, route) for route in cross]
+
+    def swapped(x):
+        return lax.ppermute(x, both, swap)
+
+    def pack(node):
+        panel = lax.dynamic_index_in_dim(panels, node, 0, keepdims=False)
+        band = lax.dynamic_slice(inverse, (node, r * quarter, 0), (1, quarter, own))[0]
+        return jnp.concatenate([panel] + [band[:, j:j + TILE] for j in range(0, own, TILE)], axis=0)
+
+    def scalars(row, parent_mine):
+        head = jnp.stack([r, c, leaf, parent_mine]).astype(jnp.int32)
+        return jnp.concatenate([head, lax.dynamic_index_in_dim(lists, row, 0, keepdims=False)])
+
+    sigma_cols = jnp.concatenate([sigma_top] + straight(sigma_top), axis=1)
+    root_pack = pack(0)
+    root_mine = [root_pack] + straight(root_pack)
+    leaf_route = [
+        [((lf * 2 + row) * 4 + a, ((lf ^ m) * 2 + row) * 4 + a) for lf in range(4) for row in range(2) for a in middles]
+        for m in range(4)
+    ]
+    sigma_mine = [sigma_cols] + [
+        lax.ppermute(sigma_cols, ("leaf", "row", "col"), leaf_route[m]) for m in range(1, 4)
+    ]
+    sigma_other = [swapped(x) for x in sigma_mine]
+    root_other = [swapped(x) for x in root_mine]
+
+    def gather_pair(first):
+        direct = pack(first + r)
+        across = pack(first + 1 - r)
+        ours = [direct] + straight(direct)
+        theirs = [swapped(across)] + crossed(across)
+        return [x for two in zip(ours, theirs) for x in two]
+
+    blocks_12 = gather_pair(1)
+    blocks_34 = gather_pair(3)
+    blocks_56 = gather_pair(5)
+
+    width = 2 * TILE
+    ext_shape = order + own
+    scratch = scratch_for(order, own, width)
+    node_macs = width * (2 * order * own + order * order + own * own)
+    zero = jnp.int32(0)
+    root_ext, corner = call(
+        root_kernel, scalars(r, zero), [x for two in zip(root_mine, root_other) for x in two] + sigma_mine + sigma_other,
+        [(ext_shape, width), (order - own, order - own)], scratch, 6 * node_macs,
+    )
+    root_ext_other = swapped(root_ext)
+    mid_ext, grand = call(
+        middle_kernel, scalars(r, zero), blocks_12 + [root_ext, root_ext_other, corner],
+        [(ext_shape, own), (own, own)], scratch, 12 * node_macs,
+    )
+    mid_ext_other = swapped(mid_ext)
+
+    def leaves(blocks, first):
+        node = first + r
+        parent = lax.dynamic_index_in_dim(links, node - 3, 0, keepdims=False)
+        results = call(
+            leaf_kernel, scalars(node - 1, (parent == 1 + r).astype(jnp.int32)),
+            blocks + [mid_ext, mid_ext_other, grand],
+            [(half + own, TILE)] * 4, scratch + [pltpu.VMEM((order, width), F32), pltpu.VMEM((own, width), F32)],
+            6 * node_macs,
+        )
+        self_out, core_out, end_out, cross_out = results
+        return (
+            self_out, swapped(core_out), lax.ppermute(end_out, "col", home), lax.ppermute(cross_out, both, home_cross)
+        )
+
+    def column(mine, other, node, col):
+        if node == 0:
+            source = jnp.where(col // 2 == r, mine, other)
+            start = (col % 2) * TILE
+        else:
+            source = jnp.where(r == node - 1, mine, other)
+            start = col * TILE
+        top = lax.dynamic_slice(source, (r * half, start), (half, TILE))
+        return jnp.concatenate([top, lax.dynamic_slice(source, (order, start), (own, TILE))], axis=0)
+
+    def upper(col):
+        return jnp.stack([
+            column(root_ext, root_ext_other, 0, col), column(mid_ext, mid_ext_other, 1, col),
+            column(mid_ext, mid_ext_other, 2, col),
+        ])
+
+    is_middle = (c == 1) | (c == 2)
+    upper_out = jnp.where(is_middle, upper(c), lax.ppermute(upper(3 * (c // 2)), "col", home))
+    pieces = [upper_out[0], upper_out[1], upper_out[2]]
+    for blocks, first in ((blocks_34, 3), (blocks_56, 5)):
+        self_out, core_out, end_out, cross_out = leaves(blocks, first)
+        same = jnp.where(is_middle, self_out, end_out)
+        swapped_out = jnp.where(is_middle, core_out, cross_out)
+        pieces.append(jnp.where(r == 0, same, swapped_out))
+        pieces.append(jnp.where(r == 0, swapped_out, same))
+    ancestor_block = jnp.stack([x[:half] for x in pieces])[None]
+    diagonal_block = jnp.stack([x[half:] for x in pieces])[None]
+    return (ancestor_block, diagonal_block)
 
 
 def child_blocks(ancestors, products, diagonals, parent_ids, picks, tile):
@@ -112,8 +461,9 @@
 
 
 def solution(mesh):
+    two_middles = (mesh.shape["leaf"], mesh.shape["row"], mesh.shape["col"]) == (4, 2, 4)
     return jax.shard_map(
-        body,
+        chip_body if two_middles else body,
         mesh=mesh,
         in_specs=(
             P(("leaf", "row"), "col"),

time: 729 us -> 288 us (0.40); the launches traced: 719 us -> 286 us
  waiting for transfers between devices: 492 us -> 70.6 us
  starting transfers between devices: 11.4 us -> 139 us
  local copies, waits for them, and re-layouts: 108 us -> 19.3 us
  matrix products: 55.6 us -> 0 us
  Pallas kernels: 0 us -> 46.1 us
  other arithmetic: 36.7 us -> 8.68 us
  between operations: 16 us -> 2.95 us
    psum x1 -> x0, waiting for transfers between devices: 240 us -> none  [body(): factor_rows = lax.psum(partial_factor, 'col')]
    all_gather x8 -> x0, waiting for transfers between devices: 159 us -> none  [the longest x1 68 us: body(): top_full = lax.all_gather(top_rows, 'col', axis=1, tiled=True)]
    ppermute x0 -> x47, starting transfers between devices: none -> 139 us  [the longest x15 61.2 us: straight(): return [lax.ppermute(x, 'col', route) for route in routes]]
    reduce_scatter x4 -> x0, waiting for transfers between devices: 90 us -> none  [the longest x1 64.6 us: body(): lax.psum_scatter(partial_gram, 'col', scatter_dimension=2, tiled=True)]
    ppermute x0 -> x47, waiting for transfers between devices: none -> 70.6 us  [the longest x2 29.3 us: leaves(): lax.ppermute(end_out, 'col', home)]
    dot_general x8 -> x0, matrix products: 55.6 us -> none  [the longest x3 21.5 us: body(): jnp.einsum('vra,vac->vrc', own_rows, factor_cols[first_node:last_node], p...]
    pallas_call x0 -> x4, Pallas kernels: none -> 46.1 us  [call(): pl.pallas_call(kernel, out_shape=[jax.ShapeDtypeStruct(o, F32) for o in o...]
    reshape x9 -> x0, local copies, waits for them, and re-layouts: 32.9 us -> none  [the longest x2 9.78 us: body(): product_all.reshape(width_nodes, row_count, col_count, block_rows, block_...]
  transfers between devices with their start and end apart: 13 -> 47, of which waited for: 12 -> 9; matrix products, arithmetic and copies ran while one was open for 14% -> 7% of each run, Pallas kernels for 0% -> 16%
where the time goes in v1:
time: 288 us; the launch traced here: 286 us
  starting transfers between devices  139 us (48%)
  waiting for transfers between devices  70.6 us (25%)
  Pallas kernels  46.1 us (16%)
  local copies, waits for them, and re-layouts  19.3 us (7%)
  other arithmetic  8.68 us (3%)
  between operations  2.95 us (1%)
    ppermute x15, starting transfers between devices, straight(): return [lax.ppermute(x, 'col', route) for route in routes]  61.2 us
    ppermute x9, starting transfers between devices, crossed(): return [lax.ppermute(x, both, route) for route in cross]  48.5 us
    pallas_call x4, Pallas kernels, call(): pl.pallas_call(kernel, out_shape=[jax.ShapeDtypeStruct(o, F32) for o in o...  46.1 us
    ppermute x2, waiting for transfers between devices, leaves(): lax.ppermute(end_out, 'col', home)  29.3 us
    ppermute x15, waiting for transfers between devices, straight(): return [lax.ppermute(x, 'col', route) for route in routes]  21.9 us
    ppermute x2, waiting for transfers between devices, leaves(): lax.ppermute(cross_out, both, home_cross)  19.4 us
    ppermute x15, starting transfers between devices, swapped(): return lax.ppermute(x, both, swap)  18 us
    unnamed x101, local copies, waits for them, and re-layouts  12.7 us
  transfers between devices with their start and end apart: 47, of which 9 were waited for; matrix products, arithmetic and copies ran while one was open for 7% of the time, Pallas kernels for 16%

profile of v1, /device:TPU:0, one launch (start us, length us, event | category | flops | bytes accessed | tf_op | source)
XLA Modules:
  0.0 286.4 jit_solution(12844988349980129464)
XLA Ops:
  0.6 2.5 bitcast_dynamic-update-slice_fusion
  3.3 5.7 %collective-permute-start.1 = (f32[768,128]{1,0:T(8,128)S(1)}, f32[768,128]{1,0:T(8,128)}, u32[]{:S(2)}, u32[]{:S(2)}) collective-permute-start(f32[768,128]{1,0:T(8,128)S(1)} %constant_dynamic-update-slice_fusion.refs_0_), channel_id=1, source_target_pairs={{0,1},{3,2},{4,5},{7,6},{8,9},{11,10},{12,13},{15,14},{16,17},{19,... | collective-permute-start | bytes 1179656 | tf_op jit(solution)/shard_map/ppermute | solution.py:257
  9.7 3.3 %collective-permute-start.5 = (f32[768,128]{1,0:T(8,128)S(1)}, f32[768,128]{1,0:T(8,128)S(1)}, u32[]{:S(2)}, u32[]{:S(2)}) collective-permute-start(f32[768,128]{1,0:T(8,128)S(1)} %constant_dynamic-update-slice_fusion.refs_0_), channel_id=1, source_target_pairs={{0,2},{3,1},{4,6},{7,5},{8,10},{11,9},{12,14},{15,13},{16,18},{19,... | collective-permute-start | bytes 1179656 | tf_op jit(solution)/shard_map/ppermute | solution.py:257
  15.7 12.2 %collective-permute-done.7 = f32[128,256]{1,0:T(8,128)S(1)} collective-permute-done((f32[128,256]{1,0:T(8,128)S(1)}, f32[128,256]{1,0:T(8,128)S(1)}, u32[]{:S(2)}, u32[]{:S(2)}) %collective-permute-start.7) | collective-permute-done | bytes 131104 | tf_op jit(solution)/shard_map/ppermute | solution.py:257
  27.9 5.4 %collective-permute-start.9 = (f32[128,256]{1,0:T(8,128)S(1)}, f32[128,256]{1,0:T(8,128)S(1)}, u32[]{:S(2)}, u32[]{:S(2)}) collective-permute-start(f32[128,256]{1,0:T(8,128)S(1)} %copy-done.13), channel_id=1, source_target_pairs={{0,2},{3,1},{4,6},{7,5},{8,10},{11,9},{12,14},{15,13},{16,18},{19,... | collective-permute-start | bytes 393224 | tf_op jit(solution)/shard_map/ppermute | solution.py:257
  51.0 29.4 %collective-permute-start.20 = (f32[768,128]{1,0:T(8,128)S(1)}, f32[768,128]{1,0:T(8,128)S(1)}, u32[]{:S(2)}, u32[]{:S(2)}) collective-permute-start(f32[768,128]{1,0:T(8,128)S(1)} %constant_dynamic-update-slice_fusion.12), channel_id=1, source_target_pairs={{0,5},{3,6},{4,1},{7,2},{8,13},{11,14},{12,9},{15,10},{16,21},{19,... | collective-permute-start | bytes 1179656 | tf_op jit(solution)/shard_map/ppermute | solution.py:260
  81.2 3.6 %collective-permute-start.24 = (f32[768,128]{1,0:T(8,128)S(1)}, f32[768,128]{1,0:T(8,128)S(1)}, u32[]{:S(2)}, u32[]{:S(2)}) collective-permute-start(f32[768,128]{1,0:T(8,128)S(1)} %constant_dynamic-update-slice_fusion.12), channel_id=1, source_target_pairs={{0,6},{3,5},{4,2},{7,1},{8,14},{11,13},{12,10},{15,9},{16,22},{19,... | collective-permute-start | bytes 1179656 | tf_op jit(solution)/shard_map/ppermute | solution.py:260
  84.8 10.1 %shard_map.68 = (f32[1536,256]{1,0:T(8,128)}, f32[512,512]{1,0:T(8,128)}) custom-call(s32[12]{0:T(128)} %concatenate.52.s, f32[768,128]{1,0:T(8,128)} %copy-done.12, f32[768,128]{1,0:T(8,128)} %copy-done.19, f32[768,128]{1,0:T(8,128)} %collective-permute-done.1.refs_2_, f32[768,128]{1,0:T(8,128)} %collective-permute-done.2.refs_3_, f32[768,128]{1,0:T(8,128)} %copy-done.17, ...), custom_call_target="tpu_custom_call" | custom-call | flops 3623878656 | bytes 9961472 | tf_op jit(solution)/shard_map/pallas_call | solution.py:98
  95.8 2.9 %collective-permute-start.19 = (f32[768,128]{1,0:T(8,128)S(1)}, f32[768,128]{1,0:T(8,128)S(1)}, u32[]{:S(2)}, u32[]{:S(2)}) collective-permute-start(f32[768,128]{1,0:T(8,128)S(1)} %constant_dynamic-update-slice_fusion.8.refs_0_), channel_id=1, source_target_pairs={{0,1},{3,2},{4,5},{7,6},{8,9},{11,10},{12,13},{15,14},{16,17},{19,... | collective-permute-start | bytes 1179656 | tf_op jit(solution)/shard_map/ppermute | solution.py:257
  99.4 4.3 %collective-permute-start.23 = (f32[768,128]{1,0:T(8,128)S(1)}, f32[768,128]{1,0:T(8,128)S(1)}, u32[]{:S(2)}, u32[]{:S(2)}) collective-permute-start(f32[768,128]{1,0:T(8,128)S(1)} %constant_dynamic-update-slice_fusion.8.refs_0_), channel_id=1, source_target_pairs={{0,2},{3,1},{4,6},{7,5},{8,10},{11,9},{12,14},{15,13},{16,18},{19,... | collective-permute-start | bytes 1179656 | tf_op jit(solution)/shard_map/ppermute | solution.py:257
  105.2 2.9 collective-permute-done.19.refs_2_
  108.1 4.0 %collective-permute-start.29 = (f32[768,128]{1,0:T(8,128)S(1)}, f32[768,128]{1,0:T(8,128)}, u32[]{:S(2)}, u32[]{:S(2)}) collective-permute-start(f32[768,128]{1,0:T(8,128)S(1)} %constant_dynamic-update-slice_fusion.20), channel_id=1, source_target_pairs={{0,5},{3,6},{4,1},{7,2},{8,13},{11,14},{12,9},{15,10},{16,21},{19,... | collective-permute-start | bytes 1179656 | tf_op jit(solution)/shard_map/ppermute | solution.py:260
  112.1 4.4 %collective-permute-done.23.refs_6_ = f32[768,128]{1,0:T(8,128)S(1)} collective-permute-done((f32[768,128]{1,0:T(8,128)S(1)}, f32[768,128]{1,0:T(8,128)S(1)}, u32[]{:S(2)}, u32[]{:S(2)}) %collective-permute-start.23) | collective-permute-done | bytes 393248 | tf_op jit(solution)/shard_map/ppermute | solution.py:257
  117.8 14.4 %shard_map.69 = (f32[1536,512]{1,0:T(8,128)}, f32[512,512]{1,0:T(8,128)}) custom-call(s32[12]{0:T(128)} %concatenate.52.s, f32[768,128]{1,0:T(8,128)} %copy-done.11, f32[768,128]{1,0:T(8,128)} %copy-done.22, f32[768,128]{1,0:T(8,128)} %copy-done.33, f32[768,128]{1,0:T(8,128)} %copy-done.25, f32[768,128]{1,0:T(8,128)} %copy-done.34, f32[768,128]{1,0:T(8,128)} %copy-done.27, ...), custom_call_target="tpu_custom_call" | custom-call | flops 7247757312 | bytes 11534336 | tf_op jit(solution)/shard_map/pallas_call | solution.py:98
  132.2 2.3 collective-permute-start.25
  134.6 5.0 %collective-permute-start.28 = (f32[768,128]{1,0:T(8,128)S(1)}, f32[768,128]{1,0:T(8,128)S(1)}, u32[]{:S(2)}, u32[]{:S(2)}) collective-permute-start(f32[768,128]{1,0:T(8,128)S(1)} %constant_dynamic-update-slice_fusion.16.refs_0_), channel_id=1, source_target_pairs={{0,1},{3,2},{4,5},{7,6},{8,9},{11,10},{12,13},{15,14},{16,17},{19,... | collective-permute-start | bytes 1179656 | tf_op jit(solution)/shard_map/ppermute | solution.py:257
  147.9 1.6 broadcast_select_fusion.3
  151.5 2.7 broadcast_select_fusion.1
  154.2 4.5 %collective-permute-start.32 = (f32[768,128]{1,0:T(8,128)S(1)}, f32[768,128]{1,0:T(8,128)S(1)}, u32[]{:S(2)}, u32[]{:S(2)}) collective-permute-start(f32[768,128]{1,0:T(8,128)S(1)} %constant_dynamic-update-slice_fusion.16.refs_0_), channel_id=1, source_target_pairs={{0,2},{3,1},{4,6},{7,5},{8,10},{11,9},{12,14},{15,13},{16,18},{19,... | collective-permute-start | bytes 1179656 | tf_op jit(solution)/shard_map/ppermute | solution.py:257
  161.9 2.7 collective-permute-start.39
  164.6 18.0 %collective-permute-start.38 = (f32[768,128]{1,0:T(8,128)}, f32[768,128]{1,0:T(8,128)S(1)}, u32[]{:S(2)}, u32[]{:S(2)}) collective-permute-start(f32[768,128]{1,0:T(8,128)} %constant_dynamic-update-slice_fusion.24.refs_0_), channel_id=1, source_target_pairs={{0,1},{3,2},{4,5},{7,6},{8,9},{11,10},{12,13},{15,14},{16,17},{19,... | collective-permute-start | bytes 1179656 | tf_op jit(solution)/shard_map/ppermute | solution.py:257
  185.0 6.5 %collective-permute-start.42 = (f32[768,128]{1,0:T(8,128)}, f32[768,128]{1,0:T(8,128)}, u32[]{:S(2)}, u32[]{:S(2)}) collective-permute-start(f32[768,128]{1,0:T(8,128)} %constant_dynamic-update-slice_fusion.24.refs_0_), channel_id=1, source_target_pairs={{0,2},{3,1},{4,6},{7,5},{8,10},{11,9},{12,14},{15,13},{16,18},{19,... | collective-permute-start | bytes 1179656 | tf_op jit(solution)/shard_map/ppermute | solution.py:257
  191.5 2.0 collective-permute-done.38.refs_2_
  193.5 4.5 %collective-permute-start.43 = (f32[768,128]{1,0:T(8,128)}, f32[768,128]{1,0:T(8,128)}, u32[]{:S(2)}, u32[]{:S(2)}) collective-permute-start(f32[768,128]{1,0:T(8,128)} %constant_dynamic-update-slice_fusion.28), channel_id=1, source_target_pairs={{0,6},{3,5},{4,2},{7,1},{8,14},{11,13},{12,10},{15,9},{16,22},{19,... | collective-permute-start | bytes 1179656 | tf_op jit(solution)/shard_map/ppermute | solution.py:260
  198.0 1.5 collective-permute-start.26
  199.6 10.8 %shard_map.70 = (f32[1024,128]{1,0:T(8,128)}, f32[1024,128]{1,0:T(8,128)}, f32[1024,128]{1,0:T(8,128)}, f32[1024,128]{1,0:T(8,128)}) custom-call(s32[12]{0:T(128)} %concatenate.63.s, f32[768,128]{1,0:T(8,128)} %copy-done.10, f32[768,128]{1,0:T(8,128)} %collective-permute-done.27.refs_1_, f32[768,128]{1,0:T(8,128)} %copy-done.16, ...), custom_call_target="tpu_custom_call" | custom-call | flops 3623878656 | bytes 12582912 | tf_op jit(solution)/shard_map/pallas_call | solution.py:98
  216.5 10.8 %shard_map.71 = (f32[1024,128]{1,0:T(8,128)}, f32[1024,128]{1,0:T(8,128)}, f32[1024,128]{1,0:T(8,128)}, f32[1024,128]{1,0:T(8,128)}) custom-call(s32[12]{0:T(128)} %concatenate.66.s, f32[768,128]{1,0:T(8,128)} %constant_dynamic-update-slice_fusion.24.refs_0_, f32[768,128]{1,0:T(8,128)} %copy-done.20, f32[768,128]{1,0:T(8,128)} %copy-done.24, ...), custom_call_target="tpu_custom_call" | custom-call | flops 3623878656 | bytes 12582912 | tf_op jit(solution)/shard_map/pallas_call | solution.py:98
  228.6 19.3 %collective-permute-done.34 = f32[1024,128]{1,0:T(8,128)} collective-permute-done((f32[1024,128]{1,0:T(8,128)}, f32[1024,128]{1,0:T(8,128)}, u32[]{:S(2)}, u32[]{:S(2)}) %collective-permute-start.34) | collective-permute-done | bytes 524320 | tf_op jit(solution)/shard_map/ppermute | solution.py:325
  252.9 7.5 %collective-permute-done.36 = f32[1024,128]{1,0:T(8,128)} collective-permute-done((f32[1024,128]{1,0:T(8,128)}, f32[1024,128]{1,0:T(8,128)}, u32[]{:S(2)}, u32[]{:S(2)}) %collective-permute-start.36) | collective-permute-done | bytes 524320 | tf_op jit(solution)/shard_map/ppermute | solution.py:325
  260.4 10.0 %collective-permute-done.44 = f32[1024,128]{1,0:T(8,128)} collective-permute-done((f32[1024,128]{1,0:T(8,128)}, f32[1024,128]{1,0:T(8,128)}, u32[]{:S(2)}, u32[]{:S(2)}) %collective-permute-start.44) | collective-permute-done | bytes 524320 | tf_op jit(solution)/shard_map/ppermute | solution.py:325
  270.4 11.9 %collective-permute-done.46 = f32[1024,128]{1,0:T(8,128)} collective-permute-done((f32[1024,128]{1,0:T(8,128)}, f32[1024,128]{1,0:T(8,128)}, u32[]{:S(2)}, u32[]{:S(2)}) %collective-permute-start.46) | collective-permute-done | bytes 524320 | tf_op jit(solution)/shard_map/ppermute | solution.py:325
  282.3 1.8 broadcast_select_fusion.8
  (195 shorter events, 55.0 us)
Async XLA Ops:
  3.3 34.6 %collective-permute-start.1 = (f32[768,128]{1,0:T(8,128)S(1)}, f32[768,128]{1,0:T(8,128)}, u32[]{:S(2)}, u32[]{:S(2)}) collective-permute-start(f32[768,128]{1,0:T(8,128)S(1)} %constant_dynamic-update-slice_fusion.refs_0_), channel_id=1, source_target_pairs={{0,1},{3,2},{4,5},{7,6},{8,9},{11,10},{12,13},{15,14},{16,17},{19,... | collective-permute-start | bytes 1179656 | tf_op jit(solution)/shard_map/ppermute | solution.py:257
  9.0 30.3 %collective-permute-start.3 = (f32[768,128]{1,0:T(8,128)S(1)}, f32[768,128]{1,0:T(8,128)S(1)}, u32[]{:S(2)}, u32[]{:S(2)}) collective-permute-start(f32[768,128]{1,0:T(8,128)S(1)} %constant_dynamic-update-slice_fusion.refs_0_), channel_id=1, source_target_pairs={{1,2},{2,1},{5,6},{6,5},{9,10},{10,9},{13,14},{14,13},{17,18},{18,... | collective-permute-start | bytes 1179656 | tf_op jit(solution)/shard_map/ppermute | solution.py:257
  9.7 31.1 %collective-permute-start.5 = (f32[768,128]{1,0:T(8,128)S(1)}, f32[768,128]{1,0:T(8,128)S(1)}, u32[]{:S(2)}, u32[]{:S(2)}) collective-permute-start(f32[768,128]{1,0:T(8,128)S(1)} %constant_dynamic-update-slice_fusion.refs_0_), channel_id=1, source_target_pairs={{0,2},{3,1},{4,6},{7,5},{8,10},{11,9},{12,14},{15,13},{16,18},{19,... | collective-permute-start | bytes 1179656 | tf_op jit(solution)/shard_map/ppermute | solution.py:257
  14.4 19.6 %collective-permute-start.8 = (f32[128,256]{1,0:T(8,128)S(1)}, f32[128,256]{1,0:T(8,128)S(1)}, u32[]{:S(2)}, u32[]{:S(2)}) collective-permute-start(f32[128,256]{1,0:T(8,128)S(1)} %copy-done.13), channel_id=1, source_target_pairs={{1,2},{2,1},{5,6},{6,5},{9,10},{10,9},{13,14},{14,13},{17,18},{18,... | collective-permute-start | bytes 393224 | tf_op jit(solution)/shard_map/ppermute | solution.py:257
  43.8 36.7 %collective-permute-start.14 = (f32[128,1024]{1,0:T(8,128)}, f32[128,1024]{1,0:T(8,128)}, u32[]{:S(2)}, u32[]{:S(2)}) collective-permute-start(f32[128,1024]{1,0:T(8,128)} %collective-permute-done.10.refs_9_), channel_id=1, source_target_pairs={{1,5},{2,6},{5,1},{6,2},{9,13},{10,14},{13,9},{14,10},{17,21},{18,... | collective-permute-start | bytes 1572872 | tf_op jit(solution)/shard_map/ppermute | solution.py:263
  45.2 35.9 %collective-permute-start.15 = (f32[128,1024]{1,0:T(8,128)}, f32[128,1024]{1,0:T(8,128)}, u32[]{:S(2)}, u32[]{:S(2)}) collective-permute-start(f32[128,1024]{1,0:T(8,128)} %collective-permute-done.11.refs_10_), channel_id=1, source_target_pairs={{1,5},{2,6},{5,1},{6,2},{9,13},{10,14},{13,9},{14,10},{17,21},{18,... | collective-permute-start | bytes 1572872 | tf_op jit(solution)/shard_map/ppermute | solution.py:263
  46.7 38.0 %collective-permute-start.16 = (f32[128,1024]{1,0:T(8,128)}, f32[128,1024]{1,0:T(8,128)}, u32[]{:S(2)}, u32[]{:S(2)}) collective-permute-start(f32[128,1024]{1,0:T(8,128)} %collective-permute-done.12.refs_11_), channel_id=1, source_target_pairs={{1,5},{2,6},{5,1},{6,2},{9,13},{10,14},{13,9},{14,10},{17,21},{18,... | collective-permute-start | bytes 1572872 | tf_op jit(solution)/shard_map/ppermute | solution.py:263
  50.3 45.5 %collective-permute-start.18 = (f32[768,128]{1,0:T(8,128)S(1)}, f32[768,128]{1,0:T(8,128)S(1)}, u32[]{:S(2)}, u32[]{:S(2)}) collective-permute-start(f32[768,128]{1,0:T(8,128)S(1)} %constant_dynamic-update-slice_fusion.12), channel_id=1, source_target_pairs={{1,5},{2,6},{5,1},{6,2},{9,13},{10,14},{13,9},{14,10},{17,21},{18,... | collective-permute-start | bytes 1179656 | tf_op jit(solution)/shard_map/ppermute | solution.py:263
  51.0 47.7 %collective-permute-start.20 = (f32[768,128]{1,0:T(8,128)S(1)}, f32[768,128]{1,0:T(8,128)S(1)}, u32[]{:S(2)}, u32[]{:S(2)}) collective-permute-start(f32[768,128]{1,0:T(8,128)S(1)} %constant_dynamic-update-slice_fusion.12), channel_id=1, source_target_pairs={{0,5},{3,6},{4,1},{7,2},{8,13},{11,14},{12,9},{15,10},{16,21},{19,... | collective-permute-start | bytes 1179656 | tf_op jit(solution)/shard_map/ppermute | solution.py:260
  80.5 19.0 %collective-permute-start.22 = (f32[768,128]{1,0:T(8,128)S(1)}, f32[768,128]{1,0:T(8,128)S(1)}, u32[]{:S(2)}, u32[]{:S(2)}) collective-permute-start(f32[768,128]{1,0:T(8,128)S(1)} %constant_dynamic-update-slice_fusion.12), channel_id=1, source_target_pairs={{1,6},{2,5},{5,2},{6,1},{9,14},{10,13},{13,10},{14,9},{17,22},{18,... | collective-permute-start | bytes 1179656 | tf_op jit(solution)/shard_map/ppermute | solution.py:260
  81.2 22.6 %collective-permute-start.24 = (f32[768,128]{1,0:T(8,128)S(1)}, f32[768,128]{1,0:T(8,128)S(1)}, u32[]{:S(2)}, u32[]{:S(2)}) collective-permute-start(f32[768,128]{1,0:T(8,128)S(1)} %constant_dynamic-update-slice_fusion.12), channel_id=1, source_target_pairs={{0,6},{3,5},{4,2},{7,1},{8,14},{11,13},{12,10},{15,9},{16,22},{19,... | collective-permute-start | bytes 1179656 | tf_op jit(solution)/shard_map/ppermute | solution.py:260
  94.9 21.7 %collective-permute-start.17 = (f32[1536,256]{1,0:T(8,128)}, f32[1536,256]{1,0:T(8,128)S(1)}, u32[]{:S(2)}, u32[]{:S(2)}) collective-permute-start(f32[1536,256]{1,0:T(8,128)} %get-tuple-element.14.refs_8_), channel_id=1, source_target_pairs={{1,5},{2,6},{5,1},{6,2},{9,13},{10,14},{13,9},{14,10},{17,21},{18,... | collective-permute-start | bytes 4718600 | tf_op jit(solution)/shard_map/ppermute | solution.py:263
  103.8 50.3 %collective-permute-start.27 = (f32[768,128]{1,0:T(8,128)S(1)}, f32[768,128]{1,0:T(8,128)}, u32[]{:S(2)}, u32[]{:S(2)}) collective-permute-start(f32[768,128]{1,0:T(8,128)S(1)} %constant_dynamic-update-slice_fusion.20), channel_id=1, source_target_pairs={{1,5},{2,6},{5,1},{6,2},{9,13},{10,14},{13,9},{14,10},{17,21},{18,... | collective-permute-start | bytes 1179656 | tf_op jit(solution)/shard_map/ppermute | solution.py:263
  108.1 53.1 %collective-permute-start.29 = (f32[768,128]{1,0:T(8,128)S(1)}, f32[768,128]{1,0:T(8,128)}, u32[]{:S(2)}, u32[]{:S(2)}) collective-permute-start(f32[768,128]{1,0:T(8,128)S(1)} %constant_dynamic-update-slice_fusion.20), channel_id=1, source_target_pairs={{0,5},{3,6},{4,1},{7,2},{8,13},{11,14},{12,9},{15,10},{16,21},{19,... | collective-permute-start | bytes 1179656 | tf_op jit(solution)/shard_map/ppermute | solution.py:260
  134.6 24.1 %collective-permute-start.28 = (f32[768,128]{1,0:T(8,128)S(1)}, f32[768,128]{1,0:T(8,128)S(1)}, u32[]{:S(2)}, u32[]{:S(2)}) collective-permute-start(f32[768,128]{1,0:T(8,128)S(1)} %constant_dynamic-update-slice_fusion.16.refs_0_), channel_id=1, source_target_pairs={{0,1},{3,2},{4,5},{7,6},{8,9},{11,10},{12,13},{15,14},{16,17},{19,... | collective-permute-start | bytes 1179656 | tf_op jit(solution)/shard_map/ppermute | solution.py:257
  139.6 22.3 %collective-permute-start.30 = (f32[768,128]{1,0:T(8,128)S(1)}, f32[768,128]{1,0:T(8,128)}, u32[]{:S(2)}, u32[]{:S(2)}) collective-permute-start(f32[768,128]{1,0:T(8,128)S(1)} %constant_dynamic-update-slice_fusion.16.refs_0_), channel_id=1, source_target_pairs={{1,2},{2,1},{5,6},{6,5},{9,10},{10,9},{13,14},{14,13},{17,18},{18,... | collective-permute-start | bytes 1179656 | tf_op jit(solution)/shard_map/ppermute | solution.py:257
  154.2 28.6 %collective-permute-start.32 = (f32[768,128]{1,0:T(8,128)S(1)}, f32[768,128]{1,0:T(8,128)S(1)}, u32[]{:S(2)}, u32[]{:S(2)}) collective-permute-start(f32[768,128]{1,0:T(8,128)S(1)} %constant_dynamic-update-slice_fusion.16.refs_0_), channel_id=1, source_target_pairs={{0,2},{3,1},{4,6},{7,5},{8,10},{11,9},{12,14},{15,13},{16,18},{19,... | collective-permute-start | bytes 1179656 | tf_op jit(solution)/shard_map/ppermute | solution.py:257
  158.7 24.7 %collective-permute-start.33 = (f32[768,128]{1,0:T(8,128)S(1)}, f32[768,128]{1,0:T(8,128)S(1)}, u32[]{:S(2)}, u32[]{:S(2)}) collective-permute-start(f32[768,128]{1,0:T(8,128)S(1)} %constant_dynamic-update-slice_fusion.20), channel_id=1, source_target_pairs={{0,6},{3,5},{4,2},{7,1},{8,14},{11,13},{12,10},{15,9},{16,22},{19,... | collective-permute-start | bytes 1179656 | tf_op jit(solution)/shard_map/ppermute | solution.py:260
  161.2 23.8 %collective-permute-start.37 = (f32[768,128]{1,0:T(8,128)}, f32[768,128]{1,0:T(8,128)S(1)}, u32[]{:S(2)}, u32[]{:S(2)}) collective-permute-start(f32[768,128]{1,0:T(8,128)} %constant_dynamic-update-slice_fusion.28), channel_id=1, source_target_pairs={{1,5},{2,6},{5,1},{6,2},{9,13},{10,14},{13,9},{14,10},{17,21},{18,... | collective-permute-start | bytes 1179656 | tf_op jit(solution)/shard_map/ppermute | solution.py:263
  161.9 36.1 %collective-permute-start.39 = (f32[768,128]{1,0:T(8,128)}, f32[768,128]{1,0:T(8,128)S(1)}, u32[]{:S(2)}, u32[]{:S(2)}) collective-permute-start(f32[768,128]{1,0:T(8,128)} %constant_dynamic-update-slice_fusion.28), channel_id=1, source_target_pairs={{0,5},{3,6},{4,1},{7,2},{8,13},{11,14},{12,9},{15,10},{16,21},{19,... | collective-permute-start | bytes 1179656 | tf_op jit(solution)/shard_map/ppermute | solution.py:260
  164.6 28.9 %collective-permute-start.38 = (f32[768,128]{1,0:T(8,128)}, f32[768,128]{1,0:T(8,128)S(1)}, u32[]{:S(2)}, u32[]{:S(2)}) collective-permute-start(f32[768,128]{1,0:T(8,128)} %constant_dynamic-update-slice_fusion.24.refs_0_), channel_id=1, source_target_pairs={{0,1},{3,2},{4,5},{7,6},{8,9},{11,10},{12,13},{15,14},{16,17},{19,... | collective-permute-start | bytes 1179656 | tf_op jit(solution)/shard_map/ppermute | solution.py:257
  182.7 27.7 %collective-permute-start.40 = (f32[768,128]{1,0:T(8,128)}, f32[768,128]{1,0:T(8,128)S(1)}, u32[]{:S(2)}, u32[]{:S(2)}) collective-permute-start(f32[768,128]{1,0:T(8,128)} %constant_dynamic-update-slice_fusion.24.refs_0_), channel_id=1, source_target_pairs={{1,2},{2,1},{5,6},{6,5},{9,10},{10,9},{13,14},{14,13},{17,18},{18,... | collective-permute-start | bytes 1179656 | tf_op jit(solution)/shard_map/ppermute | solution.py:257
  183.5 29.0 %collective-permute-start.41 = (f32[768,128]{1,0:T(8,128)}, f32[768,128]{1,0:T(8,128)}, u32[]{:S(2)}, u32[]{:S(2)}) collective-permute-start(f32[768,128]{1,0:T(8,128)} %constant_dynamic-update-slice_fusion.28), channel_id=1, source_target_pairs={{1,6},{2,5},{5,2},{6,1},{9,14},{10,13},{13,10},{14,9},{17,22},{18,... | collective-permute-start | bytes 1179656 | tf_op jit(solution)/shard_map/ppermute | solution.py:260
  185.0 30.2 %collective-permute-start.42 = (f32[768,128]{1,0:T(8,128)}, f32[768,128]{1,0:T(8,128)}, u32[]{:S(2)}, u32[]{:S(2)}) collective-permute-start(f32[768,128]{1,0:T(8,128)} %constant_dynamic-update-slice_fusion.24.refs_0_), channel_id=1, source_target_pairs={{0,2},{3,1},{4,6},{7,5},{8,10},{11,9},{12,14},{15,13},{16,18},{19,... | collective-permute-start | bytes 1179656 | tf_op jit(solution)/shard_map/ppermute | solution.py:257
  193.5 22.9 %collective-permute-start.43 = (f32[768,128]{1,0:T(8,128)}, f32[768,128]{1,0:T(8,128)}, u32[]{:S(2)}, u32[]{:S(2)}) collective-permute-start(f32[768,128]{1,0:T(8,128)} %constant_dynamic-update-slice_fusion.28), channel_id=1, source_target_pairs={{0,6},{3,5},{4,2},{7,1},{8,14},{11,13},{12,10},{15,9},{16,22},{19,... | collective-permute-start | bytes 1179656 | tf_op jit(solution)/shard_map/ppermute | solution.py:260
  198.0 86.0 %collective-permute-start.26 = (f32[3,1024,128]{2,1,0:T(8,128)S(1)}, f32[3,1024,128]{2,1,0:T(8,128)S(1)}, u32[]{:S(2)}, u32[]{:S(2)}) collective-permute-start(f32[3,1024,128]{2,1,0:T(8,128)S(1)} %pad_maximum_fusion), channel_id=1, source_target_pairs={{1,0},{2,3},{5,4},{6,7},{9,8},{10,11},{13,12},{14,15},{17,16},{18,... | collective-permute-start | bytes 4718600 | tf_op jit(solution)/shard_map/ppermute | solution.py:345
  211.2 36.7 %collective-permute-start.34 = (f32[1024,128]{1,0:T(8,128)}, f32[1024,128]{1,0:T(8,128)}, u32[]{:S(2)}, u32[]{:S(2)}) collective-permute-start(f32[1024,128]{1,0:T(8,128)} %get-tuple-element.19), channel_id=1, source_target_pairs={{1,0},{2,3},{5,4},{6,7},{9,8},{10,11},{13,12},{14,15},{17,16},{18,... | collective-permute-start | bytes 1572872 | tf_op jit(solution)/shard_map/ppermute | solution.py:325
  212.5 36.9 %collective-permute-start.35 = (f32[1024,128]{1,0:T(8,128)}, f32[1024,128]{1,0:T(8,128)}, u32[]{:S(2)}, u32[]{:S(2)}) collective-permute-start(f32[1024,128]{1,0:T(8,128)} %get-tuple-element.20), channel_id=1, source_target_pairs={{1,5},{2,6},{5,1},{6,2},{9,13},{10,14},{13,9},{14,10},{17,21},{18,... | collective-permute-start | bytes 1572872 | tf_op jit(solution)/shard_map/ppermute | solution.py:263
  215.2 45.2 %collective-permute-start.36 = (f32[1024,128]{1,0:T(8,128)}, f32[1024,128]{1,0:T(8,128)}, u32[]{:S(2)}, u32[]{:S(2)}) collective-permute-start(f32[1024,128]{1,0:T(8,128)} %get-tuple-element.21), channel_id=1, source_target_pairs={{1,4},{2,7},{5,0},{6,3},{9,12},{10,15},{13,8},{14,11},{17,20},{18,... | collective-permute-start | bytes 1572872 | tf_op jit(solution)/shard_map/ppermute | solution.py:325
  227.3 43.1 %collective-permute-start.44 = (f32[1024,128]{1,0:T(8,128)}, f32[1024,128]{1,0:T(8,128)}, u32[]{:S(2)}, u32[]{:S(2)}) collective-permute-start(f32[1024,128]{1,0:T(8,128)} %get-tuple-element.23), channel_id=1, source_target_pairs={{1,0},{2,3},{5,4},{6,7},{9,8},{10,11},{13,12},{14,15},{17,16},{18,... | collective-permute-start | bytes 1572872 | tf_op jit(solution)/shard_map/ppermute | solution.py:325
  247.9 22.5 %collective-permute-start.45 = (f32[1024,128]{1,0:T(8,128)}, f32[1024,128]{1,0:T(8,128)}, u32[]{:S(2)}, u32[]{:S(2)}) collective-permute-start(f32[1024,128]{1,0:T(8,128)} %get-tuple-element.24), channel_id=1, source_target_pairs={{1,5},{2,6},{5,1},{6,2},{9,13},{10,14},{13,9},{14,10},{17,21},{18,... | collective-permute-start | bytes 1572872 | tf_op jit(solution)/shard_map/ppermute | solution.py:263
  249.3 32.9 %collective-permute-start.46 = (f32[1024,128]{1,0:T(8,128)}, f32[1024,128]{1,0:T(8,128)}, u32[]{:S(2)}, u32[]{:S(2)}) collective-permute-start(f32[1024,128]{1,0:T(8,128)} %get-tuple-element.25), channel_id=1, source_target_pairs={{1,4},{2,7},{5,0},{6,3},{9,12},{10,15},{13,8},{14,11},{17,20},{18,... | collective-permute-start | bytes 1572872 | tf_op jit(solution)/shard_map/ppermute | solution.py:325
  (51 other events, 699.0 us)

commit v2 on v0

--- a/solution.py
+++ b/solution.py
@@ -1,9 +1,432 @@
+import functools
+
 import jax
 import jax.numpy as jnp
 from jax import lax
+from jax.experimental import pallas as pl
+from jax.experimental.pallas import tpu as pltpu
 from jax.sharding import PartitionSpec as P
 
 TILE = 128
+STEP = 2 * TILE
+QUARTER = TILE // 2
+F32 = jnp.float32
+BF16 = jnp.bfloat16
+VMEM_LIMIT = 56 * 2**20
+WHOLE = pl.BlockSpec(memory_space=pltpu.VMEM)
+ANY = pl.BlockSpec(memory_space=pl.ANY)
+
+
+def split(x):
+    high = x.astype(BF16)
+    return high, (x - high.astype(F32)).astype(BF16)
+
+
+def dot3(a, b, contract):
+    dims = (((contract,), (0,)), ((), ()))
+    dot = functools.partial(lax.dot_general, dimension_numbers=dims, preferred_element_type=F32)
+    return dot(a[0], b[0]) + (dot(a[0], b[1]) + dot(a[1], b[0]))
+
+
+def put(pair, index, value):
+    high, low = split(value)
+    pair[0][index] = high
+    pair[1][index] = low
+
+
+def get(pair, index):
+    return pair[0][index], pair[1][index]
+
+
+def at(start, size, unit=TILE):
+    return pl.ds(pl.multiple_of(start, unit), size)
+
+
+def tiles(size, step=STEP):
+    return [slice(m, m + step) for m in range(0, size, step)]
+
+
+ALL = slice(None)
+
+
+def load_panels(blocks, r, p, d, half):
+    for slot in range(4):
+        for turn in range(2):
+            ref = blocks[2 * slot + turn]
+            side = r if turn == 0 else 1 - r
+            put(p, (at(side * half, half), slice(slot * TILE, (slot + 1) * TILE)), ref[0:half, :])
+            for j in range(4):
+                rows = at(slot * TILE + side * QUARTER, QUARTER, QUARTER)
+                place = slice(j * TILE, (j + 1) * TILE)
+                put(d, (rows, place), ref[half + j * QUARTER:half + (j + 1) * QUARTER, :])
+
+
+def solve(p, d, a, dc, f, w, t, weights, emit_ab, emit_dg, join=None):
+    width = dc[0].shape[1]
+    for rows in tiles(p[0].shape[0]):
+        k = rows.start // TILE
+        for cols in tiles(width):
+            value = dot3(get(p, (rows, ALL)), get(dc, (ALL, cols)), 1)
+            value = jnp.concatenate([value[:TILE] * weights[k], value[TILE:] * weights[k + 1]], axis=0)
+            put(f, (rows, cols), value)
+    if join is not None:
+        join()
+    for cols in tiles(width):
+        for rows in tiles(a[0].shape[0]):
+            value = dot3(get(a, (rows, ALL)), get(f, (ALL, cols)), 1)
+            emit_ab(rows, cols, -value)
+            put(w, (rows, cols), value)
+        for rows in tiles(d[0].shape[0]):
+            value = dot3(get(p, (ALL, rows)), get(w, (ALL, cols)), 0)
+            put(t, (rows, cols), value + dc[0][rows, cols].astype(F32) + dc[1][rows, cols].astype(F32))
+        for rows in tiles(d[0].shape[0]):
+            emit_dg(rows, cols, dot3(get(d, (ALL, rows)), get(t, (ALL, cols)), 0))
+
+
+def scratch_pairs(*shapes):
+    return [pltpu.VMEM(shape, BF16) for shape in shapes for _ in range(2)]
+
+
+def pairs(refs):
+    return [(refs[i], refs[i + 1]) for i in range(0, len(refs), 2)]
+
+
+def call(kernel, scalars, operands, outs, scratch, places=None, out_place=WHOLE, micros=1):
+    return pl.pallas_call(
+        kernel,
+        out_shape=[jax.ShapeDtypeStruct(o, F32) for o in outs],
+        in_specs=[pl.BlockSpec(memory_space=pltpu.SMEM)] + (places or [WHOLE] * len(operands)),
+        out_specs=[out_place] * len(outs),
+        scratch_shapes=scratch,
+        compiler_params=pltpu.CompilerParams(vmem_limit_bytes=VMEM_LIMIT),
+        cost_estimate=pl.CostEstimate(flops=micros * 10**9, bytes_accessed=1, transcendentals=0),
+    )(scalars, *operands)
+
+
+def copy_all(copies, sems):
+    started = [pltpu.make_async_copy(src, dst, sems.at[i]) for i, (src, dst) in enumerate(copies)]
+    for one in started:
+        one.start()
+    for one in started:
+        one.wait()
+
+
+def move(kernel, scalars, operands, outs, count):
+    return call(
+        kernel, scalars, operands, outs, [pltpu.SemaphoreType.DMA((count,))], [ANY] * len(operands), ANY
+    )
+
+
+LIST = 4
+
+
+def tail_of(s, start, own, order):
+    spots = [start + k for k in range(own // TILE, order // TILE)]
+    return [jnp.maximum(s[k], 0) for k in spots], [(s[k] >= 0).astype(F32) for k in spots]
+
+
+def weights_of(s, order):
+    return [(s[LIST + j] >= 0).astype(F32) for j in range(order // TILE)]
+
+
+def pack_kernel(s, panels, inverse, *rest):
+    outs, sems = rest[:-1], rest[-1]
+    half = panels.shape[1]
+    copies = []
+    node = 0
+    for out in outs:
+        for i in range(out.shape[0]):
+            copies.append((panels.at[node], out.at[i, pl.ds(0, half)]))
+            for j in range(inverse.shape[2] // TILE):
+                copies.append((
+                    inverse.at[node, at(s[0] * QUARTER, QUARTER, QUARTER), pl.ds(j * TILE, TILE)],
+                    out.at[i, pl.ds(half + j * QUARTER, QUARTER)],
+                ))
+            node += 1
+    copy_all(copies, sems)
+
+
+def join_columns_kernel(s, *refs):
+    out, sems = refs[-2:]
+    width = refs[0].shape[1]
+    copy_all([(ref, out.at[:, pl.ds(k * width, width)]) for k, ref in enumerate(refs[:-2])], sems)
+
+
+def join_rows_kernel(s, *refs):
+    out, sems = refs[-2:]
+    height = refs[0].shape[0]
+    copy_all([(ref, out.at[pl.ds(k * height, height)]) for k, ref in enumerate(refs[:-2])], sems)
+
+
+def swap_kernel(s, *refs):
+    out, sems = refs[-2:]
+    copy_all([(ref.at[1 - s[0]], out.at[k]) for k, ref in enumerate(refs[:-2])], sems)
+
+
+def join_block(a, own, corner, rows_of, top, index, weight):
+    put(a, (slice(0, own), slice(0, own)), top)
+    for i in range(len(index)):
+        place = slice(own + i * TILE, own + (i + 1) * TILE)
+        value = rows_of(i) * weight[i]
+        put(a, (place, slice(0, own)), value)
+        put(a, (slice(0, own), place), value.T)
+        for j in range(len(index)):
+            put(a, (place, slice(own + j * TILE, own + (j + 1) * TILE)), corner(i, j) * (weight[i] * weight[j]))
+
+
+def trunk_kernel(s, *refs):
+    mine, theirs, sigma_mine, sigma_other = refs[:4], refs[4:8], refs[8], refs[9]
+    ext, grand, self_out, end_out = refs[10:14]
+    stage, sigma, sems, corners, ab, dg = refs[14:20]
+    p, d, a, f, w, t = pairs(refs[20:-1])
+    r, c, leaf = s[0], s[1], s[2]
+    order = a[0].shape[0]
+    own = d[0].shape[0]
+    half = order // 2
+    far = c // 2
+    count = 3
+
+    def fetch(node, slot):
+        found = []
+        for k in range(4):
+            found.append(pltpu.make_async_copy(mine[k].at[node], stage.at[slot, 2 * k], sems.at[slot, 2 * k]))
+            found.append(pltpu.make_async_copy(theirs[k].at[node], stage.at[slot, 2 * k + 1], sems.at[slot, 2 * k + 1]))
+        return found
+
+    sigma_copies = [
+        pltpu.make_async_copy(ref, sigma.at[k], sems.at[2, k]) for k, ref in enumerate((sigma_mine, sigma_other))
+    ]
+    for one in fetch(0, 0) + sigma_copies + fetch(1, 1):
+        one.start()
+
+    def panels_of(node, slot):
+        for one in fetch(node, slot):
+            one.wait()
+        load_panels([stage.at[slot, k] for k in range(8)], r, p, d, half)
+
+    def emit_ab(rows, cols, value):
+        ab[rows, cols] = value
+
+    def emit_dg(rows, cols, value):
+        dg[rows, cols] = value
+
+    def columns_out(node):
+        for out, col in ((self_out, c), (end_out, 3 * far)):
+            out[node, 0:half, :] = ab[at(r * half, half), at(col * TILE, TILE)]
+            out[node, half:, :] = dg[:, at(col * TILE, TILE)]
+
+    panels_of(0, 0)
+
+    def join_root():
+        places = (c, 3 * far, 3 - c, 3 - 3 * far)
+        span = order // 4
+        for one in sigma_copies:
+            one.wait()
+        for m in range(4):
+            for turn in range(2):
+                side = r if turn == 0 else 1 - r
+                rows = at(((leaf ^ m) * 2 + side) * TILE, TILE)
+                for k in range(4):
+                    value = sigma[turn, m * TILE:(m + 1) * TILE, k * span:(k + 1) * span]
+                    put(a, (rows, at(places[k] * span, span)), value)
+
+    solve(p, d, a, d, f, w, t, [1.0] * (order // TILE), emit_ab, emit_dg, join_root)
+    columns_out(0)
+    grand[...] = dg[...]
+    for node in (1, 2):
+        index, weight = tail_of(s, LIST + (node - 1) * (order // TILE), own, order)
+        for i in range(len(index)):
+            for j in range(len(index)):
+                high, low = get(a, (at(index[i] * TILE, TILE), at(index[j] * TILE, TILE)))
+                value = high.astype(F32) + low.astype(F32)
+                corners[node - 1, i * TILE:(i + 1) * TILE, j * TILE:(j + 1) * TILE] = value
+    for one in fetch(2, 0):
+        one.start()
+    root_ab = refs[-1]
+    root_ab[...] = ab[...]
+
+    @pl.loop(1, count)
+    def _(node):
+        start = LIST + (node - 1) * (order // TILE)
+        index, weight = tail_of(s, start, own, order)
+        panels_of(node, node % 2)
+
+        def join():
+            join_block(
+                a, own,
+                lambda i, j: corners[node - 1, i * TILE:(i + 1) * TILE, j * TILE:(j + 1) * TILE],
+                lambda i: root_ab[at(index[i] * TILE, TILE), :], grand[...], index, weight,
+            )
+
+        weights = [(s[start + k] >= 0).astype(F32) for k in range(order // TILE)]
+        solve(p, d, a, d, f, w, t, weights, emit_ab, emit_dg, join)
+        columns_out(node)
+        ext[node - 1, 0:half, :] = ab[0:half, :]
+        ext[node - 1, half:, :] = dg[...]
+
+
+def leaf_kernel(s, x0, x1, x2, x3, ex, ext, grand, self_out, core_out, end_out, cross_out, *rest):
+    stage, sems, tails, top, grand_in, ab, dg = rest[:7]
+    p, d, a, dc, f, w, t = pairs(rest[7:])
+    r, c = s[0], s[1]
+    order = a[0].shape[0]
+    own = d[0].shape[0]
+    half = order // 2
+    far = c // 2
+    index, weight = tail_of(s, LIST, own, order)
+    parent = s[3] - 1
+    copies = []
+    for k, ref in enumerate((x0, x1, x2, x3)):
+        copies.append(pltpu.make_async_copy(ref.at[r], stage.at[2 * k], sems.at[2 * k]))
+        copies.append(pltpu.make_async_copy(ex.at[k], stage.at[2 * k + 1], sems.at[2 * k + 1]))
+    later = [
+        pltpu.make_async_copy(ext.at[parent, pl.ds(half, own)], top, sems.at[8]),
+        pltpu.make_async_copy(grand, grand_in, sems.at[9]),
+    ]
+    for j, pick in enumerate(index):
+        later.append(pltpu.make_async_copy(ext.at[parent, at(pick * TILE, TILE)], tails.at[j], sems.at[10 + j]))
+    for one in copies + later:
+        one.start()
+    for one in copies:
+        one.wait()
+    load_panels([stage.at[k] for k in range(8)], r, p, d, half)
+    dc[0][...] = d[0][:, at(far * STEP, STEP)]
+    dc[1][...] = d[1][:, at(far * STEP, STEP)]
+
+    def join():
+        for one in later:
+            one.wait()
+        join_block(
+            a, own, lambda i, j: grand_in[at(index[i] * TILE, TILE), at(index[j] * TILE, TILE)], lambda i: tails[i],
+            top[...], index, weight,
+        )
+
+    def emit_ab(rows, cols, value):
+        ab[rows, cols] = value
+
+    def emit_dg(rows, cols, value):
+        dg[rows, cols] = value
+
+    solve(p, d, a, dc, f, w, t, weights_of(s, order), emit_ab, emit_dg, join)
+    near_cols, end_cols = at((1 - far) * TILE, TILE), at(far * TILE, TILE)
+    for out, side, cols in (
+        (self_out, r, near_cols), (core_out, 1 - r, near_cols), (end_out, r, end_cols), (cross_out, 1 - r, end_cols)
+    ):
+        out[0:half, :] = ab[at(side * half, half), cols]
+        out[half:, :] = dg[:, cols]
+
+
+def output_kernel(s, *refs):
+    ab, dg, sems = refs[-3:]
+    r, c = s[0], s[1]
+    half = ab.shape[1]
+    middle = (c == 1) | (c == 2)
+    for core in range(2):
+        for inner in range(2):
+            @pl.when((r == core) & (middle == (inner == 1)))
+            def _():
+                upper = refs[0] if inner else refs[1]
+                found = [upper.at[k] for k in range(3)]
+                for start in (2, 6):
+                    self_ref, core_ref, end_ref, cross_ref = refs[start:start + 4]
+                    same, swapped = (self_ref, core_ref) if inner else (end_ref, cross_ref)
+                    found += [same, swapped] if core == 0 else [swapped, same]
+                copies = []
+                for node, ref in enumerate(found):
+                    copies.append((ref.at[pl.ds(0, half)], ab.at[node]))
+                    copies.append((ref.at[pl.ds(half, half)], dg.at[node]))
+                copy_all(copies, sems)
+
+
+def after(x, earlier):
+    return lax.optimization_barrier((x, earlier))[0]
+
+
+def chip_body(sigma_top, panels, inverse_diag, slot_lists, parent_links):
+    r = lax.axis_index("row")
+    c = lax.axis_index("col")
+    leaf = lax.axis_index("leaf")
+    panels, inverse, lists, links = panels[0], inverse_diag[0], slot_lists[0], parent_links[0]
+    half = panels.shape[1]
+    order = 2 * half
+    own = inverse.shape[2]
+    both = ("row", "col")
+    routes = (((0, 1), (3, 2)), ((1, 2), (2, 1)), ((0, 2), (3, 1)))
+    middles = (1, 2)
+    swap = [(row * 4 + a, (1 - row) * 4 + a) for row in range(2) for a in middles]
+    home = ((1, 0), (2, 3))
+    home_cross = [(row * 4 + a, (1 - row) * 4 + b) for row in range(2) for a, b in home]
+    leaf_routes = [
+        [((lf * 2 + row) * 4 + a, ((lf ^ m) * 2 + row) * 4 + a) for lf in range(4) for row in range(2) for a in middles]
+        for m in range(4)
+    ]
+
+    def straight(x):
+        return [x] + [lax.ppermute(x, "col", route) for route in routes]
+
+    def swapped(x):
+        return lax.ppermute(x, both, swap)
+
+    def scalars(parent, *rows):
+        head = jnp.stack([r, c, leaf, parent]).astype(jnp.int32)
+        return jnp.concatenate([head] + [lists[row] for row in rows])
+
+    trunk = 3
+    here = scalars(jnp.int32(0), 0, 1)
+    packed = half + own // 2
+    sigma_parts = straight(sigma_top)
+    pack_t, pack_34, pack_56 = move(
+        pack_kernel, here, [panels, inverse], [(k, packed, TILE) for k in (trunk, 2, 2)], 35
+    )
+    blocks_t = straight(pack_t)
+    sigma_cols = move(join_columns_kernel, here, after(sigma_parts, pack_t), [(TILE, order)], 4)[0]
+    sigma_rows = [sigma_cols] + [
+        lax.ppermute(sigma_cols, ("leaf", "row", "col"), leaf_routes[m]) for m in range(1, 4)
+    ]
+    sigma_mine = move(join_rows_kernel, here, sigma_rows, [(half, order)], 4)[0]
+    sigma_other = swapped(sigma_mine)
+    other_t = [swapped(x) for x in blocks_t]
+    blocks_34 = straight(after(pack_34, blocks_t[1:]))
+    ext, grand, upper_self, upper_end = call(
+        trunk_kernel, here, blocks_t + other_t + [sigma_mine, sigma_other],
+        [(2, half + own, own), (own, own)] + [(trunk, half + own, TILE)] * 2,
+        [
+            pltpu.VMEM((2, 8, packed, TILE), F32), pltpu.VMEM((2, half, order), F32), pltpu.SemaphoreType.DMA((3, 8)),
+            pltpu.VMEM((2, order - own, order - own), F32), pltpu.VMEM((order, own), F32), pltpu.VMEM((own, own), F32),
+        ] + scratch_pairs((order, own), (own, own), (order, order), (order, own), (order, own), (own, own))
+        + [pltpu.VMEM((order, own), F32)],
+        [ANY] * 10, micros=60,
+    )
+    blocks_56 = straight(after(pack_56, (blocks_34[1:], ext)))
+    pieces = [upper_self, lax.ppermute(upper_end, "col", home)]
+    tails = (order - own) // TILE
+    ready = ext
+    for blocks, first in ((blocks_34, 3), (blocks_56, 5)):
+        node = first + r
+        parent = lax.dynamic_index_in_dim(links, node - 3, 0, keepdims=False)
+        theirs = swapped(move(swap_kernel, here, after(blocks, ready), [(4, packed, TILE)], 4)[0])
+        if first == 5:
+            theirs = after(theirs, pieces[1])
+        self_out, core_out, end_out, cross_out = call(
+            leaf_kernel, scalars(parent, node - 1), blocks + [theirs, ext, grand], [(half + own, TILE)] * 4,
+            [
+                pltpu.VMEM((8, packed, TILE), F32), pltpu.SemaphoreType.DMA((10 + tails,)),
+                pltpu.VMEM((tails, TILE, own), F32), pltpu.VMEM((own, own), F32), pltpu.VMEM((own, own), F32),
+                pltpu.VMEM((order, STEP), F32), pltpu.VMEM((own, STEP), F32),
+            ] + scratch_pairs(
+                (order, own), (own, own), (order, order), (own, STEP), (order, STEP), (order, STEP), (own, STEP)
+            ),
+            [ANY] * 7, micros=10,
+        )
+        ready = self_out
+        pieces += [
+            self_out, swapped(core_out), lax.ppermute(end_out, "col", home), lax.ppermute(cross_out, both, home_cross)
+        ]
+    count = panels.shape[0]
+    ancestor_block, diagonal_block = move(
+        output_kernel, here, pieces, [(count, half, TILE), (count, own, TILE)], 2 * count
+    )
+    return (ancestor_block[None], diagonal_block[None])
 
 
 def child_blocks(ancestors, products, diagonals, parent_ids, picks, tile):
@@ -112,8 +535,9 @@
 
 
 def solution(mesh):
+    two_middles = (mesh.shape["leaf"], mesh.shape["row"], mesh.shape["col"]) == (4, 2, 4)
     return jax.shard_map(
-        body,
+        chip_body if two_middles else body,
         mesh=mesh,
         in_specs=(
             P(("leaf", "row"), "col"),

time: 729 us -> 578 us (0.79); the launches traced: 719 us -> 577 us
  waiting for transfers between devices: 492 us -> 56.1 us
  Pallas kernels: 0 us -> 433 us
  local copies, waits for them, and re-layouts: 108 us -> 12.4 us
  starting transfers between devices: 11.4 us -> 73.2 us
  matrix products: 55.6 us -> 0 us
  other arithmetic: 36.7 us -> 0 us
  between operations: 16 us -> 1.37 us
    pallas_call x0 -> x9, Pallas kernels: none -> 433 us  [call(): pl.pallas_call(kernel, out_shape=[jax.ShapeDtypeStruct(o, F32) for o in o...]
    psum x1 -> x0, waiting for transfers between devices: 240 us -> none  [body(): factor_rows = lax.psum(partial_factor, 'col')]
    all_gather x8 -> x0, waiting for transfers between devices: 159 us -> none  [the longest x1 68 us: body(): top_full = lax.all_gather(top_rows, 'col', axis=1, tiled=True)]
    reduce_scatter x4 -> x0, waiting for transfers between devices: 90 us -> none  [the longest x1 64.6 us: body(): lax.psum_scatter(partial_gram, 'col', scatter_dimension=2, tiled=True)]
    ppermute x0 -> x29, starting transfers between devices: none -> 73.2 us  [the longest x12 53.6 us: straight(): return [x] + [lax.ppermute(x, 'col', route) for route in routes]]
    ppermute x0 -> x29, waiting for transfers between devices: none -> 56.1 us  [the longest x2 20 us: chip_body(): lax.ppermute(cross_out, both, home_cross)]
    dot_general x8 -> x0, matrix products: 55.6 us -> none  [the longest x3 21.5 us: body(): jnp.einsum('vra,vac->vrc', own_rows, factor_cols[first_node:last_node], p...]
    reshape x9 -> x0, local copies, waits for them, and re-layouts: 32.9 us -> none  [the longest x2 9.78 us: body(): product_all.reshape(width_nodes, row_count, col_count, block_rows, block_...]
  transfers between devices with their start and end apart: 13 -> 29, of which waited for: 12 -> 6; matrix products, arithmetic and copies ran while one was open for 14% -> 1% of each run, Pallas kernels for 0% -> 44%
where the time goes in v2:
time: 578 us; the launch traced here: 577 us
  Pallas kernels  433 us (75%)
  starting transfers between devices  73.2 us (13%)
  waiting for transfers between devices  56.1 us (10%)
  local copies, waits for them, and re-layouts  12.4 us (2%)
    pallas_call x9, Pallas kernels, call(): pl.pallas_call(kernel, out_shape=[jax.ShapeDtypeStruct(o, F32) for o in o...  433 us
    ppermute x12, starting transfers between devices, straight(): return [x] + [lax.ppermute(x, 'col', route) for route in routes]  53.6 us
    ppermute x2, waiting for transfers between devices, chip_body(): lax.ppermute(cross_out, both, home_cross)  20 us
    ppermute x12, waiting for transfers between devices, straight(): return [x] + [lax.ppermute(x, 'col', route) for route in routes]  19.5 us
    ppermute x2, waiting for transfers between devices, chip_body(): lax.ppermute(end_out, 'col', home)  16.6 us
  transfers between devices with their start and end apart: 29, of which 6 were waited for; matrix products, arithmetic and copies ran while one was open for 1% of the time, Pallas kernels for 44%

profile of v2, /device:TPU:0, one launch (start us, length us, event | category | flops | bytes accessed | tf_op | source)
XLA Modules:
  0.0 576.6 jit_solution(15623177181393012655)
XLA Ops:
  0.6 4.9 collective-permute-start.7
  6.3 4.0 collective-permute-start.9
  11.6 85.5 %shard_map.68 = (f32[3,768,128]{2,1,0:T(8,128)}, f32[2,768,128]{2,1,0:T(8,128)}, f32[2,768,128]{2,1,0:T(8,128)}) custom-call(s32[20]{0:T(128)} %concatenate.9.s, f32[7,512,128]{2,1,0:T(8,128)} %bitcast.17, f32[7,128,512]{2,1,0:T(8,128)} %bitcast.18), custom_call_target="tpu_custom_call" | custom-call | flops 1000000000 | bytes 1 | tf_op jit(solution)/shard_map/pallas_call | solution.py:95
  97.8 17.8 %shard_map.69.refs_0_ = f32[128,1024]{1,0:T(8,128)} custom-call(s32[20]{0:T(128)} %concatenate.9.s, f32[128,256]{1,0:T(8,128)} %refs_0_, f32[128,256]{1,0:T(8,128)} %copy-done.27, f32[128,256]{1,0:T(8,128)} %copy-done.28, f32[128,256]{1,0:T(8,128)} %copy-done.29), custom_call_target="tpu_custom_call" | custom-call | flops 1000000000 | bytes 1 | tf_op jit(solution)/shard_map/pallas_call | solution.py:95
  117.9 8.6 %collective-permute-start = (f32[3,768,128]{2,1,0:T(8,128)S(1)}, f32[3,768,128]{2,1,0:T(8,128)S(1)}, u32[]{:S(2)}, u32[]{:S(2)}) collective-permute-start(f32[3,768,128]{2,1,0:T(8,128)S(1)} %copy-done.20), channel_id=1, source_target_pairs={{0,1},{3,2},{4,5},{7,6},{8,9},{11,10},{12,13},{15,14},{16,17},{19,... | collective-permute-start | bytes 3538952 | tf_op jit(solution)/shard_map/ppermute | solution.py:365
  126.5 1.7 collective-permute-start.1
  128.2 6.9 %collective-permute-start.2 = (f32[3,768,128]{2,1,0:T(8,128)S(1)}, f32[3,768,128]{2,1,0:T(8,128)}, u32[]{:S(2)}, u32[]{:S(2)}) collective-permute-start(f32[3,768,128]{2,1,0:T(8,128)S(1)} %copy-done.20), channel_id=1, source_target_pairs={{0,2},{3,1},{4,6},{7,5},{8,10},{11,9},{12,14},{15,13},{16,18},{19,... | collective-permute-start | bytes 3538952 | tf_op jit(solution)/shard_map/ppermute | solution.py:365
  136.8 65.3 %shard_map.70.refs_8_ = f32[512,1024]{1,0:T(8,128)} custom-call(s32[20]{0:T(128)} %concatenate.9.s, f32[128,1024]{1,0:T(8,128)} %shard_map.69.refs_0_, f32[128,1024]{1,0:T(8,128)} %copy-done.9, f32[128,1024]{1,0:T(8,128)} %copy-done.10, f32[128,1024]{1,0:T(8,128)} %copy-done.11), custom_call_target="tpu_custom_call" | custom-call | flops 1000000000 | bytes 1 | tf_op jit(solution)/shard_map/pallas_call | solution.py:95
  202.9 1.7 collective-permute-start.3
  204.6 1.7 collective-permute-start.4
  207.8 17.0 %collective-permute-start.15 = (f32[2,768,128]{2,1,0:T(8,128)S(1)}, f32[2,768,128]{2,1,0:T(8,128)S(1)}, u32[]{:S(2)}, u32[]{:S(2)}) collective-permute-start(f32[2,768,128]{2,1,0:T(8,128)S(1)} %copy-done.2), channel_id=1, source_target_pairs={{0,1},{3,2},{4,5},{7,6},{8,9},{11,10},{12,13},{15,14},{16,17},{19,... | collective-permute-start | bytes 2359304 | tf_op jit(solution)/shard_map/ppermute | solution.py:365
  225.5 4.0 collective-permute-start.17
  230.6 1.4 copy-done.19
  231.9 34.6 %shard_map.71 = (f32[2,1024,512]{2,1,0:T(8,128)}, f32[512,512]{1,0:T(8,128)}, f32[3,1024,128]{2,1,0:T(8,128)}, f32[3,1024,128]{2,1,0:T(8,128)}) custom-call(s32[20]{0:T(128)} %concatenate.9.s, f32[3,768,128]{2,1,0:T(8,128)} %get-tuple-element.34.refs_0_, f32[3,768,128]{2,1,0:T(8,128)} %copy-done.21, f32[3,768,128]{2,1,0:T(8,128)} %collective-permute-done.1.refs_2_, ...), custom_call_target="tpu_custom_call" | custom-call | flops 60000002048 | bytes 1 | tf_op jit(solution)/shard_map/pallas_call | solution.py:95
  268.0 49.6 %shard_map.72 = f32[4,768,128]{2,1,0:T(8,128)} custom-call(s32[20]{0:T(128)} %concatenate.9.s, f32[2,768,128]{2,1,0:T(8,128)} %get-tuple-element.44.refs_0_.x0, f32[2,768,128]{2,1,0:T(8,128)} %copy-done.3, f32[2,768,128]{2,1,0:T(8,128)} %copy-done.4, f32[2,768,128]{2,1,0:T(8,128)} %copy-done.5), custom_call_target="tpu_custom_call" | custom-call | flops 1000000000 | bytes 1 | tf_op jit(solution)/shard_map/pallas_call | solution.py:95
  317.6 1.9 collective-permute-start.18
  321.3 1.3 collective-permute-start.22
  323.4 3.2 collective-permute-start.24
  326.5 1.5 collective-permute-start.14
  328.1 9.1 %shard_map.73 = (f32[1024,128]{1,0:T(8,128)}, f32[1024,128]{1,0:T(8,128)}, f32[1024,128]{1,0:T(8,128)}, f32[1024,128]{1,0:T(8,128)}) custom-call(s32[12]{0:T(128)} %concatenate.10.s, f32[2,768,128]{2,1,0:T(8,128)} %get-tuple-element.44.refs_0_.x0, f32[2,768,128]{2,1,0:T(8,128)} %copy-done.3, f32[2,768,128]{2,1,0:T(8,128)} %copy-done.4, ...), custom_call_target="tpu_custom_call" | custom-call | flops 10000000000 | bytes 1 | tf_op jit(solution)/shard_map/pallas_call | solution.py:95
  337.1 3.3 collective-permute-done.22.refs_1_.x1
  340.5 16.2 %collective-permute-done.24.refs_3_.x3 = f32[2,768,128]{2,1,0:T(8,128)S(1)} collective-permute-done((f32[2,768,128]{2,1,0:T(8,128)S(1)}, f32[2,768,128]{2,1,0:T(8,128)S(1)}, u32[]{:S(2)}, u32[]{:S(2)}) %collective-permute-start.24) | collective-permute-done | bytes 786464 | tf_op jit(solution)/shard_map/ppermute | solution.py:365
  357.6 49.6 %shard_map.74 = f32[4,768,128]{2,1,0:T(8,128)} custom-call(s32[20]{0:T(128)} %concatenate.9.s, f32[2,768,128]{2,1,0:T(8,128)} %get-tuple-element.55.refs_0_.x0, f32[2,768,128]{2,1,0:T(8,128)} %copy-done.6, f32[2,768,128]{2,1,0:T(8,128)} %copy-done.7, f32[2,768,128]{2,1,0:T(8,128)} %copy-done.8), custom_call_target="tpu_custom_call" | custom-call | flops 1000000000 | bytes 1 | tf_op jit(solution)/shard_map/pallas_call | solution.py:95
  407.1 1.8 collective-permute-start.25
  410.9 1.3 collective-permute-start.20
  413.6 9.0 %shard_map.75 = (f32[1024,128]{1,0:T(8,128)}, f32[1024,128]{1,0:T(8,128)}, f32[1024,128]{1,0:T(8,128)}, f32[1024,128]{1,0:T(8,128)}) custom-call(s32[12]{0:T(128)} %concatenate.11.s, f32[2,768,128]{2,1,0:T(8,128)} %get-tuple-element.55.refs_0_.x0, f32[2,768,128]{2,1,0:T(8,128)} %copy-done.6, f32[2,768,128]{2,1,0:T(8,128)} %copy-done.7, ...), custom_call_target="tpu_custom_call" | custom-call | flops 10000000000 | bytes 1 | tf_op jit(solution)/shard_map/pallas_call | solution.py:95
  423.3 1.3 collective-permute-start.27
  425.9 4.1 collective-permute-done.20.refs_4_
  430.0 10.0 %collective-permute-done.21.refs_5_ = f32[1024,128]{1,0:T(8,128)S(1)} collective-permute-done((f32[1024,128]{1,0:T(8,128)S(1)}, f32[1024,128]{1,0:T(8,128)S(1)}, u32[]{:S(2)}, u32[]{:S(2)}) %collective-permute-start.21) | collective-permute-done | bytes 524320 | tf_op jit(solution)/shard_map/ppermute | solution.py:423
  440.0 12.5 %collective-permute-done.27.refs_8_ = f32[1024,128]{1,0:T(8,128)S(1)} collective-permute-done((f32[1024,128]{1,0:T(8,128)}, f32[1024,128]{1,0:T(8,128)S(1)}, u32[]{:S(2)}, u32[]{:S(2)}) %collective-permute-start.27) | collective-permute-done | bytes 524320 | tf_op jit(solution)/shard_map/ppermute | solution.py:423
  452.5 10.0 %collective-permute-done.28.refs_9_ = f32[1024,128]{1,0:T(8,128)S(1)} collective-permute-done((f32[1024,128]{1,0:T(8,128)}, f32[1024,128]{1,0:T(8,128)S(1)}, u32[]{:S(2)}, u32[]{:S(2)}) %collective-permute-start.28) | collective-permute-done | bytes 524320 | tf_op jit(solution)/shard_map/ppermute | solution.py:423
  463.3 113.1 %shard_map.76 = (f32[7,512,128]{2,1,0:T(8,128)}, f32[7,512,128]{2,1,0:T(8,128)}) custom-call(s32[20]{0:T(128)} %concatenate.9.s, f32[3,1024,128]{2,1,0:T(8,128)} %get-tuple-element.39.refs_0_, f32[3,1024,128]{2,1,0:T(8,128)} %copy-done, f32[1024,128]{1,0:T(8,128)} %get-tuple-element.49.refs_2_, f32[1024,128]{1,0:T(8,128)} %copy-done.12, ...), custom_call_target="tpu_custom_call" | custom-call | flops 1000000000 | bytes 1 | tf_op jit(solution)/shard_map/pallas_call | solution.py:95
  (100 shorter events, 21.6 us)
Async XLA Ops:
  0.6 96.4 %collective-permute-start.7 = (f32[128,256]{1,0:T(8,128)}, f32[128,256]{1,0:T(8,128)S(1)}, u32[]{:S(2)}, u32[]{:S(2)}) collective-permute-start(f32[128,256]{1,0:T(8,128)} %refs_0_), channel_id=1, source_target_pairs={{0,1},{3,2},{4,5},{7,6},{8,9},{11,10},{12,13},{15,14},{16,17},{19,... | collective-permute-start | bytes 393224 | tf_op jit(solution)/shard_map/ppermute | solution.py:365
  5.6 91.5 %collective-permute-start.8 = (f32[128,256]{1,0:T(8,128)}, f32[128,256]{1,0:T(8,128)S(1)}, u32[]{:S(2)}, u32[]{:S(2)}) collective-permute-start(f32[128,256]{1,0:T(8,128)} %refs_0_), channel_id=1, source_target_pairs={{1,2},{2,1},{5,6},{6,5},{9,10},{10,9},{13,14},{14,13},{17,18},{18,... | collective-permute-start | bytes 393224 | tf_op jit(solution)/shard_map/ppermute | solution.py:365
  6.3 90.9 %collective-permute-start.9 = (f32[128,256]{1,0:T(8,128)}, f32[128,256]{1,0:T(8,128)S(1)}, u32[]{:S(2)}, u32[]{:S(2)}) collective-permute-start(f32[128,256]{1,0:T(8,128)} %refs_0_), channel_id=1, source_target_pairs={{0,2},{3,1},{4,6},{7,5},{8,10},{11,9},{12,14},{15,13},{16,18},{19,... | collective-permute-start | bytes 393224 | tf_op jit(solution)/shard_map/ppermute | solution.py:365
  115.7 92.1 %copy-start.2 = (f32[2,768,128]{2,1,0:T(8,128)S(1)}, f32[2,768,128]{2,1,0:T(8,128)}, u32[]{:S(2)}) copy-start(f32[2,768,128]{2,1,0:T(8,128)} %get-tuple-element.44.refs_0_.x0) | copy-start | bytes 2359300
  115.7 12.5 %collective-permute-start.10 = (f32[128,1024]{1,0:T(8,128)}, f32[128,1024]{1,0:T(8,128)S(1)}, u32[]{:S(2)}, u32[]{:S(2)}) collective-permute-start(f32[128,1024]{1,0:T(8,128)} %shard_map.69.refs_0_), channel_id=1, source_target_pairs={{1,9},{2,10},{5,13},{6,14},{9,1},{10,2},{13,5},{14,6},{17,25},{18,... | collective-permute-start | bytes 1572872 | tf_op jit(solution)/shard_map/ppermute | solution.py:384
  116.5 18.6 %collective-permute-start.11 = (f32[128,1024]{1,0:T(8,128)}, f32[128,1024]{1,0:T(8,128)S(1)}, u32[]{:S(2)}, u32[]{:S(2)}) collective-permute-start(f32[128,1024]{1,0:T(8,128)} %shard_map.69.refs_0_), channel_id=1, source_target_pairs={{1,17},{2,18},{5,21},{6,22},{9,25},{10,26},{13,29},{14,30},{17,1},... | collective-permute-start | bytes 1572872 | tf_op jit(solution)/shard_map/ppermute | solution.py:384
  117.2 17.9 %collective-permute-start.12 = (f32[128,1024]{1,0:T(8,128)}, f32[128,1024]{1,0:T(8,128)S(1)}, u32[]{:S(2)}, u32[]{:S(2)}) collective-permute-start(f32[128,1024]{1,0:T(8,128)} %shard_map.69.refs_0_), channel_id=1, source_target_pairs={{1,25},{2,26},{5,29},{6,30},{9,17},{10,18},{13,21},{14,22},{17,9},... | collective-permute-start | bytes 1572872 | tf_op jit(solution)/shard_map/ppermute | solution.py:384
  117.9 86.7 %collective-permute-start = (f32[3,768,128]{2,1,0:T(8,128)S(1)}, f32[3,768,128]{2,1,0:T(8,128)S(1)}, u32[]{:S(2)}, u32[]{:S(2)}) collective-permute-start(f32[3,768,128]{2,1,0:T(8,128)S(1)} %copy-done.20), channel_id=1, source_target_pairs={{0,1},{3,2},{4,5},{7,6},{8,9},{11,10},{12,13},{15,14},{16,17},{19,... | collective-permute-start | bytes 3538952 | tf_op jit(solution)/shard_map/ppermute | solution.py:365
  126.5 79.8 %collective-permute-start.1 = (f32[3,768,128]{2,1,0:T(8,128)S(1)}, f32[3,768,128]{2,1,0:T(8,128)}, u32[]{:S(2)}, u32[]{:S(2)}) collective-permute-start(f32[3,768,128]{2,1,0:T(8,128)S(1)} %copy-done.20), channel_id=1, source_target_pairs={{1,2},{2,1},{5,6},{6,5},{9,10},{10,9},{13,14},{14,13},{17,18},{18,... | collective-permute-start | bytes 3538952 | tf_op jit(solution)/shard_map/ppermute | solution.py:365
  128.2 78.8 %collective-permute-start.2 = (f32[3,768,128]{2,1,0:T(8,128)S(1)}, f32[3,768,128]{2,1,0:T(8,128)}, u32[]{:S(2)}, u32[]{:S(2)}) collective-permute-start(f32[3,768,128]{2,1,0:T(8,128)S(1)} %copy-done.20), channel_id=1, source_target_pairs={{0,2},{3,1},{4,6},{7,5},{8,10},{11,9},{12,14},{15,13},{16,18},{19,... | collective-permute-start | bytes 3538952 | tf_op jit(solution)/shard_map/ppermute | solution.py:365
  202.1 28.4 %collective-permute-start.13 = (f32[512,1024]{1,0:T(8,128)}, f32[512,1024]{1,0:T(8,128)S(1)}, u32[]{:S(2)}, u32[]{:S(2)}) collective-permute-start(f32[512,1024]{1,0:T(8,128)} %shard_map.70.refs_8_), channel_id=1, source_target_pairs={{1,5},{2,6},{5,1},{6,2},{9,13},{10,14},{13,9},{14,10},{17,21},{18,... | collective-permute-start | bytes 6291464 | tf_op jit(solution)/shard_map/ppermute | solution.py:368
  202.9 4.9 collective-permute-start.3
  204.6 20.2 %collective-permute-start.4 = (f32[3,768,128]{2,1,0:T(8,128)S(1)}, f32[3,768,128]{2,1,0:T(8,128)}, u32[]{:S(2)}, u32[]{:S(2)}) collective-permute-start(f32[3,768,128]{2,1,0:T(8,128)S(1)} %collective-permute-done.refs_1_), channel_id=1, source_target_pairs={{1,5},{2,6},{5,1},{6,2},{9,13},{10,14},{13,9},{14,10},{17,21},{18,... | collective-permute-start | bytes 3538952 | tf_op jit(solution)/shard_map/ppermute | solution.py:368
  206.3 19.2 %collective-permute-start.5 = (f32[3,768,128]{2,1,0:T(8,128)}, f32[3,768,128]{2,1,0:T(8,128)S(1)}, u32[]{:S(2)}, u32[]{:S(2)}) collective-permute-start(f32[3,768,128]{2,1,0:T(8,128)} %collective-permute-done.1.refs_2_), channel_id=1, source_target_pairs={{1,5},{2,6},{5,1},{6,2},{9,13},{10,14},{13,9},{14,10},{17,21},{18,... | collective-permute-start | bytes 3538952 | tf_op jit(solution)/shard_map/ppermute | solution.py:368
  207.0 22.5 %collective-permute-start.6 = (f32[3,768,128]{2,1,0:T(8,128)}, f32[3,768,128]{2,1,0:T(8,128)S(1)}, u32[]{:S(2)}, u32[]{:S(2)}) collective-permute-start(f32[3,768,128]{2,1,0:T(8,128)} %collective-permute-done.2.refs_3_), channel_id=1, source_target_pairs={{1,5},{2,6},{5,1},{6,2},{9,13},{10,14},{13,9},{14,10},{17,21},{18,... | collective-permute-start | bytes 3538952 | tf_op jit(solution)/shard_map/ppermute | solution.py:368
  207.8 58.7 %collective-permute-start.15 = (f32[2,768,128]{2,1,0:T(8,128)S(1)}, f32[2,768,128]{2,1,0:T(8,128)S(1)}, u32[]{:S(2)}, u32[]{:S(2)}) collective-permute-start(f32[2,768,128]{2,1,0:T(8,128)S(1)} %copy-done.2), channel_id=1, source_target_pairs={{0,1},{3,2},{4,5},{7,6},{8,9},{11,10},{12,13},{15,14},{16,17},{19,... | collective-permute-start | bytes 2359304 | tf_op jit(solution)/shard_map/ppermute | solution.py:365
  224.8 41.7 %collective-permute-start.16 = (f32[2,768,128]{2,1,0:T(8,128)S(1)}, f32[2,768,128]{2,1,0:T(8,128)S(1)}, u32[]{:S(2)}, u32[]{:S(2)}) collective-permute-start(f32[2,768,128]{2,1,0:T(8,128)S(1)} %copy-done.2), channel_id=1, source_target_pairs={{1,2},{2,1},{5,6},{6,5},{9,10},{10,9},{13,14},{14,13},{17,18},{18,... | collective-permute-start | bytes 2359304 | tf_op jit(solution)/shard_map/ppermute | solution.py:365
  225.5 41.0 %collective-permute-start.17 = (f32[2,768,128]{2,1,0:T(8,128)S(1)}, f32[2,768,128]{2,1,0:T(8,128)S(1)}, u32[]{:S(2)}, u32[]{:S(2)}) collective-permute-start(f32[2,768,128]{2,1,0:T(8,128)S(1)} %copy-done.2), channel_id=1, source_target_pairs={{0,2},{3,1},{4,6},{7,5},{8,10},{11,9},{12,14},{15,13},{16,18},{19,... | collective-permute-start | bytes 2359304 | tf_op jit(solution)/shard_map/ppermute | solution.py:365
  317.6 10.5 %collective-permute-start.18 = (f32[4,768,128]{2,1,0:T(8,128)}, f32[4,768,128]{2,1,0:T(8,128)}, u32[]{:S(2)}, u32[]{:S(2)}) collective-permute-start(f32[4,768,128]{2,1,0:T(8,128)} %shard_map.72), channel_id=1, source_target_pairs={{1,5},{2,6},{5,1},{6,2},{9,13},{10,14},{13,9},{14,10},{17,21},{18,... | collective-permute-start | bytes 4718600 | tf_op jit(solution)/shard_map/ppermute | solution.py:368
  321.3 19.2 %collective-permute-start.22 = (f32[2,768,128]{2,1,0:T(8,128)S(1)}, f32[2,768,128]{2,1,0:T(8,128)S(1)}, u32[]{:S(2)}, u32[]{:S(2)}) collective-permute-start(f32[2,768,128]{2,1,0:T(8,128)S(1)} %copy-done.1), channel_id=1, source_target_pairs={{0,1},{3,2},{4,5},{7,6},{8,9},{11,10},{12,13},{15,14},{16,17},{19,... | collective-permute-start | bytes 2359304 | tf_op jit(solution)/shard_map/ppermute | solution.py:365
  322.6 17.8 %collective-permute-start.23 = (f32[2,768,128]{2,1,0:T(8,128)S(1)}, f32[2,768,128]{2,1,0:T(8,128)S(1)}, u32[]{:S(2)}, u32[]{:S(2)}) collective-permute-start(f32[2,768,128]{2,1,0:T(8,128)S(1)} %copy-done.1), channel_id=1, source_target_pairs={{1,2},{2,1},{5,6},{6,5},{9,10},{10,9},{13,14},{14,13},{17,18},{18,... | collective-permute-start | bytes 2359304 | tf_op jit(solution)/shard_map/ppermute | solution.py:365
  323.4 33.3 %collective-permute-start.24 = (f32[2,768,128]{2,1,0:T(8,128)S(1)}, f32[2,768,128]{2,1,0:T(8,128)S(1)}, u32[]{:S(2)}, u32[]{:S(2)}) collective-permute-start(f32[2,768,128]{2,1,0:T(8,128)S(1)} %copy-done.1), channel_id=1, source_target_pairs={{0,2},{3,1},{4,6},{7,5},{8,10},{11,9},{12,14},{15,13},{16,18},{19,... | collective-permute-start | bytes 2359304 | tf_op jit(solution)/shard_map/ppermute | solution.py:365
  326.5 87.0 %collective-permute-start.14 = (f32[3,1024,128]{2,1,0:T(8,128)}, f32[3,1024,128]{2,1,0:T(8,128)S(1)}, u32[]{:S(2)}, u32[]{:S(2)}) collective-permute-start(f32[3,1024,128]{2,1,0:T(8,128)} %get-tuple-element.40), channel_id=1, source_target_pairs={{1,0},{2,3},{5,4},{6,7},{9,8},{10,11},{13,12},{14,15},{17,16},{18,... | collective-permute-start | bytes 4718600 | tf_op jit(solution)/shard_map/ppermute | solution.py:401
  357.5 53.4 %copy-start.25 = (f32[1024,128]{1,0:T(8,128)S(1)}, f32[1024,128]{1,0:T(8,128)}, u32[]{:S(2)}) copy-start(f32[1024,128]{1,0:T(8,128)} %get-tuple-element.51) | copy-start | bytes 1572868
  357.5 54.7 %copy-start.24 = (f32[1024,128]{1,0:T(8,128)S(1)}, f32[1024,128]{1,0:T(8,128)}, u32[]{:S(2)}) copy-start(f32[1024,128]{1,0:T(8,128)} %get-tuple-element.52) | copy-start | bytes 1572868
  407.1 6.4 %collective-permute-start.25 = (f32[4,768,128]{2,1,0:T(8,128)}, f32[4,768,128]{2,1,0:T(8,128)}, u32[]{:S(2)}, u32[]{:S(2)}) collective-permute-start(f32[4,768,128]{2,1,0:T(8,128)} %shard_map.74), channel_id=1, source_target_pairs={{1,5},{2,6},{5,1},{6,2},{9,13},{10,14},{13,9},{14,10},{17,21},{18,... | collective-permute-start | bytes 4718600 | tf_op jit(solution)/shard_map/ppermute | solution.py:368
  410.2 14.4 %collective-permute-start.19 = (f32[1024,128]{1,0:T(8,128)S(1)}, f32[1024,128]{1,0:T(8,128)S(1)}, u32[]{:S(2)}, u32[]{:S(2)}) collective-permute-start(f32[1024,128]{1,0:T(8,128)S(1)} %copy-done.26), channel_id=1, source_target_pairs={{1,5},{2,6},{5,1},{6,2},{9,13},{10,14},{13,9},{14,10},{17,21},{18,... | collective-permute-start | bytes 1572872 | tf_op jit(solution)/shard_map/ppermute | solution.py:368
  410.9 19.1 %collective-permute-start.20 = (f32[1024,128]{1,0:T(8,128)S(1)}, f32[1024,128]{1,0:T(8,128)S(1)}, u32[]{:S(2)}, u32[]{:S(2)}) collective-permute-start(f32[1024,128]{1,0:T(8,128)S(1)} %copy-done.25), channel_id=1, source_target_pairs={{1,0},{2,3},{5,4},{6,7},{9,8},{10,11},{13,12},{14,15},{17,16},{18,... | collective-permute-start | bytes 1572872 | tf_op jit(solution)/shard_map/ppermute | solution.py:423
  412.3 27.8 %collective-permute-start.21 = (f32[1024,128]{1,0:T(8,128)S(1)}, f32[1024,128]{1,0:T(8,128)S(1)}, u32[]{:S(2)}, u32[]{:S(2)}) collective-permute-start(f32[1024,128]{1,0:T(8,128)S(1)} %copy-done.24), channel_id=1, source_target_pairs={{1,4},{2,7},{5,0},{6,3},{9,12},{10,15},{13,8},{14,11},{17,20},{18,... | collective-permute-start | bytes 1572872 | tf_op jit(solution)/shard_map/ppermute | solution.py:423
  422.6 17.4 %collective-permute-start.26 = (f32[1024,128]{1,0:T(8,128)}, f32[1024,128]{1,0:T(8,128)S(1)}, u32[]{:S(2)}, u32[]{:S(2)}) collective-permute-start(f32[1024,128]{1,0:T(8,128)} %get-tuple-element.61), channel_id=1, source_target_pairs={{1,5},{2,6},{5,1},{6,2},{9,13},{10,14},{13,9},{14,10},{17,21},{18,... | collective-permute-start | bytes 1572872 | tf_op jit(solution)/shard_map/ppermute | solution.py:368
  423.3 29.2 %collective-permute-start.27 = (f32[1024,128]{1,0:T(8,128)}, f32[1024,128]{1,0:T(8,128)S(1)}, u32[]{:S(2)}, u32[]{:S(2)}) collective-permute-start(f32[1024,128]{1,0:T(8,128)} %get-tuple-element.62), channel_id=1, source_target_pairs={{1,0},{2,3},{5,4},{6,7},{9,8},{10,11},{13,12},{14,15},{17,16},{18,... | collective-permute-start | bytes 1572872 | tf_op jit(solution)/shard_map/ppermute | solution.py:423
  424.6 37.8 %collective-permute-start.28 = (f32[1024,128]{1,0:T(8,128)}, f32[1024,128]{1,0:T(8,128)S(1)}, u32[]{:S(2)}, u32[]{:S(2)}) collective-permute-start(f32[1024,128]{1,0:T(8,128)} %get-tuple-element.63), channel_id=1, source_target_pairs={{1,4},{2,7},{5,0},{6,3},{9,12},{10,15},{13,8},{14,11},{17,20},{18,... | collective-permute-start | bytes 1572872 | tf_op jit(solution)/shard_map/ppermute | solution.py:423
  (27 other events, 392.4 us)

commit v3 on v2

--- a/solution.py
+++ b/solution.py
@@ -22,9 +22,8 @@
     return high, (x - high.astype(F32)).astype(BF16)
 
 
-def dot3(a, b, contract):
-    dims = (((contract,), (0,)), ((), ()))
-    dot = functools.partial(lax.dot_general, dimension_numbers=dims, preferred_element_type=F32)
+def dot3(a, b):
+    dot = functools.partial(jnp.dot, preferred_element_type=F32)
     return dot(a[0], b[0]) + (dot(a[0], b[1]) + dot(a[1], b[0]))
 
 
@@ -49,38 +48,44 @@
 ALL = slice(None)
 
 
-def load_panels(blocks, r, p, d, half):
+def load_panels(blocks, r, p, d, pt, dt, half):
     for slot in range(4):
         for turn in range(2):
             ref = blocks[2 * slot + turn]
             side = r if turn == 0 else 1 - r
-            put(p, (at(side * half, half), slice(slot * TILE, (slot + 1) * TILE)), ref[0:half, :])
+            panel = ref[0:half, :]
+            put(p, (at(side * half, half), slice(slot * TILE, (slot + 1) * TILE)), panel)
+            put(pt, (slice(slot * TILE, (slot + 1) * TILE), at(side * half, half)), panel.T)
             for j in range(4):
                 rows = at(slot * TILE + side * QUARTER, QUARTER, QUARTER)
                 place = slice(j * TILE, (j + 1) * TILE)
                 put(d, (rows, place), ref[half + j * QUARTER:half + (j + 1) * QUARTER, :])
-
-
-def solve(p, d, a, dc, f, w, t, weights, emit_ab, emit_dg, join=None):
+    for slot in range(4):
+        for j in range(4):
+            rows, cols = slice(slot * TILE, (slot + 1) * TILE), slice(j * TILE, (j + 1) * TILE)
+            for whole, turned in zip(d, dt):
+                turned[cols, rows] = whole[rows, cols].T
+
+
+def solve(p, pt, dt, a, dc, f, w, t, weights, emit_ab, emit_dg, join):
     width = dc[0].shape[1]
     for rows in tiles(p[0].shape[0]):
         k = rows.start // TILE
         for cols in tiles(width):
-            value = dot3(get(p, (rows, ALL)), get(dc, (ALL, cols)), 1)
+            value = dot3(get(p, (rows, ALL)), get(dc, (ALL, cols)))
             value = jnp.concatenate([value[:TILE] * weights[k], value[TILE:] * weights[k + 1]], axis=0)
             put(f, (rows, cols), value)
-    if join is not None:
-        join()
+    join()
     for cols in tiles(width):
         for rows in tiles(a[0].shape[0]):
-            value = dot3(get(a, (rows, ALL)), get(f, (ALL, cols)), 1)
+            value = dot3(get(a, (rows, ALL)), get(f, (ALL, cols)))
             emit_ab(rows, cols, -value)
             put(w, (rows, cols), value)
-        for rows in tiles(d[0].shape[0]):
-            value = dot3(get(p, (ALL, rows)), get(w, (ALL, cols)), 0)
+        for rows in tiles(pt[0].shape[0]):
+            value = dot3(get(pt, (rows, ALL)), get(w, (ALL, cols)))
             put(t, (rows, cols), value + dc[0][rows, cols].astype(F32) + dc[1][rows, cols].astype(F32))
-        for rows in tiles(d[0].shape[0]):
-            emit_dg(rows, cols, dot3(get(d, (ALL, rows)), get(t, (ALL, cols)), 0))
+        for rows in tiles(dt[0].shape[0]):
+            emit_dg(rows, cols, dot3(get(dt, (rows, ALL)), get(t, (ALL, cols))))
 
 
 def scratch_pairs(*shapes):
@@ -91,12 +96,12 @@
     return [(refs[i], refs[i + 1]) for i in range(0, len(refs), 2)]
 
 
-def call(kernel, scalars, operands, outs, scratch, places=None, out_place=WHOLE, micros=1):
+def call(kernel, scalars, operands, outs, scratch, places=None, micros=1):
     return pl.pallas_call(
         kernel,
         out_shape=[jax.ShapeDtypeStruct(o, F32) for o in outs],
         in_specs=[pl.BlockSpec(memory_space=pltpu.SMEM)] + (places or [WHOLE] * len(operands)),
-        out_specs=[out_place] * len(outs),
+        out_specs=[WHOLE] * len(outs),
         scratch_shapes=scratch,
         compiler_params=pltpu.CompilerParams(vmem_limit_bytes=VMEM_LIMIT),
         cost_estimate=pl.CostEstimate(flops=micros * 10**9, bytes_accessed=1, transcendentals=0),
@@ -111,9 +116,9 @@
         one.wait()
 
 
-def move(kernel, scalars, operands, outs, count):
+def move(kernel, scalars, operands, outs, count, micros=1):
     return call(
-        kernel, scalars, operands, outs, [pltpu.SemaphoreType.DMA((count,))], [ANY] * len(operands), ANY
+        kernel, scalars, operands, outs, [pltpu.SemaphoreType.DMA((count,))], [ANY] * len(operands), micros
     )
 
 
@@ -152,10 +157,9 @@
     copy_all([(ref, out.at[:, pl.ds(k * width, width)]) for k, ref in enumerate(refs[:-2])], sems)
 
 
-def join_rows_kernel(s, *refs):
+def stack_kernel(s, *refs):
     out, sems = refs[-2:]
-    height = refs[0].shape[0]
-    copy_all([(ref, out.at[pl.ds(k * height, height)]) for k, ref in enumerate(refs[:-2])], sems)
+    copy_all([(ref, out.at[k]) for k, ref in enumerate(refs[:-2])], sems)
 
 
 def swap_kernel(s, *refs):
@@ -175,10 +179,10 @@
 
 
 def trunk_kernel(s, *refs):
-    mine, theirs, sigma_mine, sigma_other = refs[:4], refs[4:8], refs[8], refs[9]
+    mine, theirs, sigmas = refs[:4], refs[4], refs[5:10]
     ext, grand, self_out, end_out = refs[10:14]
     stage, sigma, sems, corners, ab, dg = refs[14:20]
-    p, d, a, f, w, t = pairs(refs[20:-1])
+    p, d, a, f, w, t, pt, dt = pairs(refs[20:-1])
     r, c, leaf = s[0], s[1], s[2]
     order = a[0].shape[0]
     own = d[0].shape[0]
@@ -190,11 +194,12 @@
         found = []
         for k in range(4):
             found.append(pltpu.make_async_copy(mine[k].at[node], stage.at[slot, 2 * k], sems.at[slot, 2 * k]))
-            found.append(pltpu.make_async_copy(theirs[k].at[node], stage.at[slot, 2 * k + 1], sems.at[slot, 2 * k + 1]))
+            found.append(pltpu.make_async_copy(theirs.at[k, node], stage.at[slot, 2 * k + 1], sems.at[slot, 2 * k + 1]))
         return found
 
     sigma_copies = [
-        pltpu.make_async_copy(ref, sigma.at[k], sems.at[2, k]) for k, ref in enumerate((sigma_mine, sigma_other))
+        pltpu.make_async_copy(ref, sigma.at[k], sems.at[2, k])
+        for k, ref in enumerate(list(sigmas[:4]) + [sigmas[4].at[m] for m in range(4)])
     ]
     for one in fetch(0, 0) + sigma_copies + fetch(1, 1):
         one.start()
@@ -202,7 +207,7 @@
     def panels_of(node, slot):
         for one in fetch(node, slot):
             one.wait()
-        load_panels([stage.at[slot, k] for k in range(8)], r, p, d, half)
+        load_panels([stage.at[slot, k] for k in range(8)], r, p, d, pt, dt, half)
 
     def emit_ab(rows, cols, value):
         ab[rows, cols] = value
@@ -213,7 +218,8 @@
     def columns_out(node):
         for out, col in ((self_out, c), (end_out, 3 * far)):
             out[node, 0:half, :] = ab[at(r * half, half), at(col * TILE, TILE)]
-            out[node, half:, :] = dg[:, at(col * TILE, TILE)]
+        self_out[node, half:, :] = dg[:, at(c * TILE, TILE)]
+        end_out[node, half:, :] = dg[at(r * (own // 2), own // 2), at(3 * far * TILE, TILE)]
 
     panels_of(0, 0)
 
@@ -227,10 +233,10 @@
                 side = r if turn == 0 else 1 - r
                 rows = at(((leaf ^ m) * 2 + side) * TILE, TILE)
                 for k in range(4):
-                    value = sigma[turn, m * TILE:(m + 1) * TILE, k * span:(k + 1) * span]
+                    value = sigma[4 * turn + m, :, k * span:(k + 1) * span]
                     put(a, (rows, at(places[k] * span, span)), value)
 
-    solve(p, d, a, d, f, w, t, [1.0] * (order // TILE), emit_ab, emit_dg, join_root)
+    solve(p, pt, dt, a, d, f, w, t, [1.0] * (order // TILE), emit_ab, emit_dg, join_root)
     columns_out(0)
     grand[...] = dg[...]
     for node in (1, 2):
@@ -259,7 +265,7 @@
             )
 
         weights = [(s[start + k] >= 0).astype(F32) for k in range(order // TILE)]
-        solve(p, d, a, d, f, w, t, weights, emit_ab, emit_dg, join)
+        solve(p, pt, dt, a, d, f, w, t, weights, emit_ab, emit_dg, join)
         columns_out(node)
         ext[node - 1, 0:half, :] = ab[0:half, :]
         ext[node - 1, half:, :] = dg[...]
@@ -267,18 +273,16 @@
 
 def leaf_kernel(s, x0, x1, x2, x3, ex, ext, grand, self_out, core_out, end_out, cross_out, *rest):
     stage, sems, tails, top, grand_in, ab, dg = rest[:7]
-    p, d, a, dc, f, w, t = pairs(rest[7:])
+    p, d, a, dc, f, w, t, pt, dt = pairs(rest[7:])
     r, c = s[0], s[1]
+    blocks = [x for k, ref in enumerate((x0, x1, x2, x3)) for x in (ref.at[r], ex.at[k])]
     order = a[0].shape[0]
     own = d[0].shape[0]
     half = order // 2
     far = c // 2
     index, weight = tail_of(s, LIST, own, order)
     parent = s[3] - 1
-    copies = []
-    for k, ref in enumerate((x0, x1, x2, x3)):
-        copies.append(pltpu.make_async_copy(ref.at[r], stage.at[2 * k], sems.at[2 * k]))
-        copies.append(pltpu.make_async_copy(ex.at[k], stage.at[2 * k + 1], sems.at[2 * k + 1]))
+    copies = [pltpu.make_async_copy(ref, stage.at[k], sems.at[k]) for k, ref in enumerate(blocks)]
     later = [
         pltpu.make_async_copy(ext.at[parent, pl.ds(half, own)], top, sems.at[8]),
         pltpu.make_async_copy(grand, grand_in, sems.at[9]),
@@ -289,7 +293,7 @@
         one.start()
     for one in copies:
         one.wait()
-    load_panels([stage.at[k] for k in range(8)], r, p, d, half)
+    load_panels([stage.at[k] for k in range(8)], r, p, d, pt, dt, half)
     dc[0][...] = d[0][:, at(far * STEP, STEP)]
     dc[1][...] = d[1][:, at(far * STEP, STEP)]
 
@@ -307,35 +311,65 @@
     def emit_dg(rows, cols, value):
         dg[rows, cols] = value
 
-    solve(p, d, a, dc, f, w, t, weights_of(s, order), emit_ab, emit_dg, join)
+    solve(p, pt, dt, a, dc, f, w, t, weights_of(s, order), emit_ab, emit_dg, join)
     near_cols, end_cols = at((1 - far) * TILE, TILE), at(far * TILE, TILE)
     for out, side, cols in (
         (self_out, r, near_cols), (core_out, 1 - r, near_cols), (end_out, r, end_cols), (cross_out, 1 - r, end_cols)
     ):
         out[0:half, :] = ab[at(side * half, half), cols]
-        out[half:, :] = dg[:, cols]
+        share = out.shape[0] - half
+        out[half:, :] = dg[:, cols] if share == own else dg[at(side * share, share), cols]
+
+
+def shares_kernel(s, upper, end, cross, core, out, sems):
+    c = s[1]
+    middle = (c == 1) | (c == 2)
+    half = core.shape[0] // 2
+    share = upper.shape[1] - half
+
+    @pl.when(middle)
+    def _():
+        copy_all([(core, out.at[pl.ds(0, 2 * half)])], sems)
+
+    @pl.when(jnp.logical_not(middle))
+    def _():
+        found = [upper.at[k] for k in range(3)] + [end, cross]
+        copy_all([
+            (ref.at[pl.ds(half, share)], out.at[pl.ds(k * share, share)]) for k, ref in enumerate(found)
+        ], sems)
 
 
 def output_kernel(s, *refs):
+    upper_self, upper_end, self_34, end_34, cross_34, shares, self_56, core_56, end_56, cross_56 = refs[:10]
     ab, dg, sems = refs[-3:]
     r, c = s[0], s[1]
     half = ab.shape[1]
+    share = half // 2
     middle = (c == 1) | (c == 2)
     for core in range(2):
-        for inner in range(2):
-            @pl.when((r == core) & (middle == (inner == 1)))
-            def _():
-                upper = refs[0] if inner else refs[1]
-                found = [upper.at[k] for k in range(3)]
-                for start in (2, 6):
-                    self_ref, core_ref, end_ref, cross_ref = refs[start:start + 4]
-                    same, swapped = (self_ref, core_ref) if inner else (end_ref, cross_ref)
-                    found += [same, swapped] if core == 0 else [swapped, same]
-                copies = []
-                for node, ref in enumerate(found):
-                    copies.append((ref.at[pl.ds(0, half)], ab.at[node]))
-                    copies.append((ref.at[pl.ds(half, half)], dg.at[node]))
-                copy_all(copies, sems)
+        @pl.when((r == core) & middle)
+        def _():
+            pair = [self_34, shares] if core == 0 else [shares, self_34]
+            last = [self_56, core_56] if core == 0 else [core_56, self_56]
+            copies = []
+            for node, ref in enumerate([upper_self.at[k] for k in range(3)] + pair + last):
+                copies.append((ref.at[pl.ds(0, half)], ab.at[node]))
+                copies.append((ref.at[pl.ds(half, half)], dg.at[node]))
+            copy_all(copies, sems)
+
+        @pl.when((r == core) & jnp.logical_not(middle))
+        def _():
+            same, swapped = (3, 4) if core == 0 else (4, 3)
+            last = [end_56, cross_56] if core == 0 else [cross_56, end_56]
+            copies = []
+            for node, ref, k in [(k, upper_end.at[k], k) for k in range(3)] + [(same, end_34, 4), (swapped, cross_34, 3)]:
+                copies.append((ref.at[pl.ds(0, half)], ab.at[node]))
+                copies.append((ref.at[pl.ds(half, share)], dg.at[node, pl.ds(core * share, share)]))
+                copies.append((shares.at[pl.ds(k * share, share)], dg.at[node, pl.ds((1 - core) * share, share)]))
+            for node, ref in ((5, last[0]), (6, last[1])):
+                copies.append((ref.at[pl.ds(0, half)], ab.at[node]))
+                copies.append((ref.at[pl.ds(half, half)], dg.at[node]))
+            copy_all(copies, sems)
 
 
 def after(x, earlier):
@@ -354,6 +388,7 @@
     routes = (((0, 1), (3, 2)), ((1, 2), (2, 1)), ((0, 2), (3, 1)))
     middles = (1, 2)
     swap = [(row * 4 + a, (1 - row) * 4 + a) for row in range(2) for a in middles]
+    swap_all = [(row * 4 + a, (1 - row) * 4 + a) for row in range(2) for a in range(4)]
     home = ((1, 0), (2, 3))
     home_cross = [(row * 4 + a, (1 - row) * 4 + b) for row in range(2) for a, b in home]
     leaf_routes = [
@@ -383,48 +418,54 @@
     sigma_rows = [sigma_cols] + [
         lax.ppermute(sigma_cols, ("leaf", "row", "col"), leaf_routes[m]) for m in range(1, 4)
     ]
-    sigma_mine = move(join_rows_kernel, here, sigma_rows, [(half, order)], 4)[0]
-    sigma_other = swapped(sigma_mine)
-    other_t = [swapped(x) for x in blocks_t]
+    sigma_other = swapped(move(stack_kernel, here, sigma_rows, [(4, TILE, order)], 4)[0])
+    gathered = after(blocks_t, sigma_rows[1:])
+    other_t = swapped(move(stack_kernel, here, gathered, [(4, trunk, packed, TILE)], 4)[0])
     blocks_34 = straight(after(pack_34, blocks_t[1:]))
     ext, grand, upper_self, upper_end = call(
-        trunk_kernel, here, blocks_t + other_t + [sigma_mine, sigma_other],
-        [(2, half + own, own), (own, own)] + [(trunk, half + own, TILE)] * 2,
+        trunk_kernel, here, blocks_t + [other_t] + sigma_rows + [sigma_other],
+        [(2, half + own, own), (own, own), (trunk, half + own, TILE), (trunk, packed, TILE)],
         [
-            pltpu.VMEM((2, 8, packed, TILE), F32), pltpu.VMEM((2, half, order), F32), pltpu.SemaphoreType.DMA((3, 8)),
+            pltpu.VMEM((2, 8, packed, TILE), F32), pltpu.VMEM((8, TILE, order), F32), pltpu.SemaphoreType.DMA((3, 8)),
             pltpu.VMEM((2, order - own, order - own), F32), pltpu.VMEM((order, own), F32), pltpu.VMEM((own, own), F32),
-        ] + scratch_pairs((order, own), (own, own), (order, order), (order, own), (order, own), (own, own))
-        + [pltpu.VMEM((order, own), F32)],
+        ] + scratch_pairs(
+            (order, own), (own, own), (order, order), (order, own), (order, own), (own, own), (own, order), (own, own)
+        ) + [pltpu.VMEM((order, own), F32)],
         [ANY] * 10, micros=60,
     )
     blocks_56 = straight(after(pack_56, (blocks_34[1:], ext)))
-    pieces = [upper_self, lax.ppermute(upper_end, "col", home)]
+    upper_home = lax.ppermute(upper_end, "col", home)
     tails = (order - own) // TILE
-    ready = ext
-    for blocks, first in ((blocks_34, 3), (blocks_56, 5)):
+    leaf_scratch = [
+        pltpu.VMEM((8, packed, TILE), F32), pltpu.SemaphoreType.DMA((10 + tails,)), pltpu.VMEM((tails, TILE, own), F32),
+        pltpu.VMEM((own, own), F32), pltpu.VMEM((own, own), F32), pltpu.VMEM((order, STEP), F32),
+        pltpu.VMEM((own, STEP), F32),
+    ] + scratch_pairs(
+        (order, own), (own, own), (order, order), (own, STEP), (order, STEP), (order, STEP), (own, STEP), (own, order),
+        (own, own),
+    )
+
+    def leaves(blocks, first, earlier, end_rows):
         node = first + r
         parent = lax.dynamic_index_in_dim(links, node - 3, 0, keepdims=False)
-        theirs = swapped(move(swap_kernel, here, after(blocks, ready), [(4, packed, TILE)], 4)[0])
-        if first == 5:
-            theirs = after(theirs, pieces[1])
+        theirs = swapped(move(swap_kernel, here, after(blocks, earlier), [(4, packed, TILE)], 4)[0])
         self_out, core_out, end_out, cross_out = call(
-            leaf_kernel, scalars(parent, node - 1), blocks + [theirs, ext, grand], [(half + own, TILE)] * 4,
-            [
-                pltpu.VMEM((8, packed, TILE), F32), pltpu.SemaphoreType.DMA((10 + tails,)),
-                pltpu.VMEM((tails, TILE, own), F32), pltpu.VMEM((own, own), F32), pltpu.VMEM((own, own), F32),
-                pltpu.VMEM((order, STEP), F32), pltpu.VMEM((own, STEP), F32),
-            ] + scratch_pairs(
-                (order, own), (own, own), (order, order), (own, STEP), (order, STEP), (order, STEP), (own, STEP)
-            ),
-            [ANY] * 7, micros=10,
+            leaf_kernel, scalars(parent, node - 1), blocks + [theirs, ext, grand],
+            [(half + own, TILE)] * 2 + [(end_rows, TILE)] * 2, leaf_scratch, [ANY] * 7, micros=10,
         )
-        ready = self_out
-        pieces += [
-            self_out, swapped(core_out), lax.ppermute(end_out, "col", home), lax.ppermute(cross_out, both, home_cross)
-        ]
+        return self_out, core_out, lax.ppermute(end_out, "col", home), lax.ppermute(cross_out, both, home_cross)
+
+    self_34, core_34, end_34, cross_34 = leaves(blocks_34, 3, ext, packed)
+    shares = move(
+        shares_kernel, here, [upper_home, end_34, cross_34, core_34], [((trunk + 2) * (own // 2), TILE)], trunk + 2
+    )[0]
+    shares = lax.ppermute(shares, both, swap_all)
+    self_56, core_56, end_56, cross_56 = leaves(blocks_56, 5, (upper_home, end_34, cross_34), half + own)
     count = panels.shape[0]
     ancestor_block, diagonal_block = move(
-        output_kernel, here, pieces, [(count, half, TILE), (count, own, TILE)], 2 * count
+        output_kernel, here,
+        [upper_self, upper_home, self_34, end_34, cross_34, shares, self_56, swapped(core_56), end_56, cross_56],
+        [(count, half, TILE), (count, own, TILE)], 3 * count,
     )
     return (ancestor_block[None], diagonal_block[None])
 

time: 578 us -> 243 us (0.42)
  Pallas kernels: 433 us -> 82.3 us
  waiting for transfers between devices: 56.1 us -> 96.9 us
  starting transfers between devices: 73.2 us -> 49.9 us
    pallas_call x9 -> x11, Pallas kernels: 433 us -> 82.3 us  [call(): pl.pallas_call(kernel, out_shape=[jax.ShapeDtypeStruct(o, F32) for o in o...]
    ppermute x12, waiting for transfers between devices: 19.5 us -> 56.1 us  [straight(): return [x] + [lax.ppermute(x, 'col', route) for route in routes]]
    ppermute x12, starting transfers between devices: 53.6 us -> 33 us  [straight(): return [x] + [lax.ppermute(x, 'col', route) for route in routes]]
    ppermute x5 -> x6, waiting for transfers between devices: 36.5 us -> 40.8 us  [the longest x2 22.7 us: leaves(): lax.ppermute(end_out, 'col', home)]
  transfers between devices with their start and end apart: 29 -> 26, of which waited for: 6 -> 9; matrix products, arithmetic and copies ran while one was open for 1% -> 2% of each run, Pallas kernels for 44% -> 27%
where the time goes in v3:
time: 243 us; the launch traced here: 242 us
  waiting for transfers between devices  96.9 us (40%)
  Pallas kernels  82.3 us (34%)
  starting transfers between devices  49.9 us (21%)
  local copies, waits for them, and re-layouts  11.6 us (5%)
    pallas_call x11, Pallas kernels, call(): pl.pallas_call(kernel, out_shape=[jax.ShapeDtypeStruct(o, F32) for o in o...  82.3 us
    ppermute x12, waiting for transfers between devices, straight(): return [x] + [lax.ppermute(x, 'col', route) for route in routes]  56.1 us
    ppermute x12, starting transfers between devices, straight(): return [x] + [lax.ppermute(x, 'col', route) for route in routes]  33 us
    ppermute x2, waiting for transfers between devices, leaves(): lax.ppermute(end_out, 'col', home)  22.7 us
    ppermute x2, waiting for transfers between devices, leaves(): lax.ppermute(cross_out, both, home_cross)  16.7 us
    unnamed x54, local copies, waits for them, and re-layouts  7.11 us
    ppermute x5, starting transfers between devices, swapped(): return lax.ppermute(x, both, swap)  7.01 us
  transfers between devices with their start and end apart: 26, of which 9 were waited for; matrix products, arithmetic and copies ran while one was open for 2% of the time, Pallas kernels for 27%

profile of v3, /device:TPU:0, one launch (start us, length us, event | category | flops | bytes accessed | tf_op | source)
XLA Modules:
  0.0 242.2 jit_solution(14532692524541405036)
XLA Ops:
  0.6 4.9 %collective-permute-start.3 = (f32[128,256]{1,0:T(8,128)}, f32[128,256]{1,0:T(8,128)S(1)}, u32[]{:S(2)}, u32[]{:S(2)}) collective-permute-start(f32[128,256]{1,0:T(8,128)} %refs_0_), channel_id=1, source_target_pairs={{0,1},{3,2},{4,5},{7,6},{8,9},{11,10},{12,13},{15,14},{16,17},{19,... | collective-permute-start | bytes 393224 | tf_op jit(solution)/shard_map/ppermute | solution.py:400
  6.3 4.0 %collective-permute-start.5 = (f32[128,256]{1,0:T(8,128)}, f32[128,256]{1,0:T(8,128)S(1)}, u32[]{:S(2)}, u32[]{:S(2)}) collective-permute-start(f32[128,256]{1,0:T(8,128)} %refs_0_), channel_id=1, source_target_pairs={{0,2},{3,1},{4,6},{7,5},{8,10},{11,9},{12,14},{15,13},{16,18},{19,... | collective-permute-start | bytes 393224 | tf_op jit(solution)/shard_map/ppermute | solution.py:400
  11.6 4.3 %shard_map.68 = (f32[3,768,128]{2,1,0:T(8,128)}, f32[2,768,128]{2,1,0:T(8,128)}, f32[2,768,128]{2,1,0:T(8,128)}) custom-call(s32[20]{0:T(128)} %concatenate.9.s, f32[7,512,128]{2,1,0:T(8,128)} %bitcast.17, f32[7,128,512]{2,1,0:T(8,128)} %bitcast.18), custom_call_target="tpu_custom_call" | custom-call | flops 1000000000 | bytes 1 | tf_op jit(solution)/shard_map/pallas_call | solution.py:100
  15.9 1.5 collective-permute-start
  18.1 3.9 %collective-permute-start.2 = (f32[3,768,128]{2,1,0:T(8,128)}, f32[3,768,128]{2,1,0:T(8,128)S(1)}, u32[]{:S(2)}, u32[]{:S(2)}) collective-permute-start(f32[3,768,128]{2,1,0:T(8,128)} %get-tuple-element.42.refs_0_), channel_id=1, source_target_pairs={{0,2},{3,1},{4,6},{7,5},{8,10},{11,9},{12,14},{15,13},{16,18},{19,... | collective-permute-start | bytes 3538952 | tf_op jit(solution)/shard_map/ppermute | solution.py:400
  23.4 2.6 %shard_map.69.refs_0_.refs_5_ = f32[128,1024]{1,0:T(8,128)} custom-call(s32[20]{0:T(128)} %concatenate.9.s, f32[128,256]{1,0:T(8,128)} %refs_0_, f32[128,256]{1,0:T(8,128)} %copy-done.24, f32[128,256]{1,0:T(8,128)} %copy-done.25, f32[128,256]{1,0:T(8,128)} %copy-done.26), custom_call_target="tpu_custom_call" | custom-call | flops 1000000000 | bytes 1 | tf_op jit(solution)/shard_map/pallas_call | solution.py:100
  28.2 15.9 %collective-permute-done.refs_1_ = f32[3,768,128]{2,1,0:T(8,128)S(1)} collective-permute-done((f32[3,768,128]{2,1,0:T(8,128)}, f32[3,768,128]{2,1,0:T(8,128)S(1)}, u32[]{:S(2)}, u32[]{:S(2)}) %collective-permute-start) | collective-permute-done | bytes 1179680 | tf_op jit(solution)/shard_map/ppermute | solution.py:400
  44.0 23.9 %collective-permute-done.2.refs_3_ = f32[3,768,128]{2,1,0:T(8,128)S(1)} collective-permute-done((f32[3,768,128]{2,1,0:T(8,128)}, f32[3,768,128]{2,1,0:T(8,128)S(1)}, u32[]{:S(2)}, u32[]{:S(2)}) %collective-permute-start.2) | collective-permute-done | bytes 1179680 | tf_op jit(solution)/shard_map/ppermute | solution.py:400
  69.0 5.1 %shard_map.70 = f32[4,3,768,128]{3,2,1,0:T(8,128)} custom-call(s32[20]{0:T(128)} %concatenate.9.s, f32[3,768,128]{2,1,0:T(8,128)} %get-tuple-element.42.refs_0_, f32[3,768,128]{2,1,0:T(8,128)} %copy-done, f32[3,768,128]{2,1,0:T(8,128)} %copy-done.1, f32[3,768,128]{2,1,0:T(8,128)} %copy-done.2), custom_call_target="tpu_custom_call" | custom-call | flops 1000000000 | bytes 1 | tf_op jit(solution)/shard_map/pallas_call | solution.py:100
  74.2 2.9 %collective-permute-start.9 = (f32[4,3,768,128]{3,2,1,0:T(8,128)}, f32[4,3,768,128]{3,2,1,0:T(8,128)}, u32[]{:S(2)}, u32[]{:S(2)}) collective-permute-start(f32[4,3,768,128]{3,2,1,0:T(8,128)} %shard_map.70), channel_id=1, source_target_pairs={{1,5},{2,6},{5,1},{6,2},{9,13},{10,14},{13,9},{14,10},{17,21},{18,... | collective-permute-start | bytes 14155784 | tf_op jit(solution)/shard_map/ppermute | solution.py:403
  77.1 3.6 %shard_map.71 = f32[4,128,1024]{2,1,0:T(8,128)} custom-call(s32[20]{0:T(128)} %concatenate.9.s, f32[128,1024]{1,0:T(8,128)} %shard_map.69.refs_0_.refs_5_, f32[128,1024]{1,0:T(8,128)} %copy-done.13, f32[128,1024]{1,0:T(8,128)} %copy-done.14, f32[128,1024]{1,0:T(8,128)} %copy-done.15), custom_call_target="tpu_custom_call" | custom-call | flops 1000000000 | bytes 1 | tf_op jit(solution)/shard_map/pallas_call | solution.py:100
  81.5 7.3 %collective-permute-start.12 = (f32[2,768,128]{2,1,0:T(8,128)S(1)}, f32[2,768,128]{2,1,0:T(8,128)S(1)}, u32[]{:S(2)}, u32[]{:S(2)}) collective-permute-start(f32[2,768,128]{2,1,0:T(8,128)S(1)} %copy-done.5), channel_id=1, source_target_pairs={{0,1},{3,2},{4,5},{7,6},{8,9},{11,10},{12,13},{15,14},{16,17},{19,... | collective-permute-start | bytes 2359304 | tf_op jit(solution)/shard_map/ppermute | solution.py:400
  89.5 4.0 %collective-permute-start.14 = (f32[2,768,128]{2,1,0:T(8,128)S(1)}, f32[2,768,128]{2,1,0:T(8,128)S(1)}, u32[]{:S(2)}, u32[]{:S(2)}) collective-permute-start(f32[2,768,128]{2,1,0:T(8,128)S(1)} %copy-done.5), channel_id=1, source_target_pairs={{0,2},{3,1},{4,6},{7,5},{8,10},{11,9},{12,14},{15,13},{16,18},{19,... | collective-permute-start | bytes 2359304 | tf_op jit(solution)/shard_map/ppermute | solution.py:400
  93.5 1.3 copy-done.22
  94.9 34.6 %shard_map.72 = (f32[2,1024,512]{2,1,0:T(8,128)}, f32[512,512]{1,0:T(8,128)}, f32[3,1024,128]{2,1,0:T(8,128)}, f32[3,768,128]{2,1,0:T(8,128)}) custom-call(s32[20]{0:T(128)} %concatenate.9.s, f32[3,768,128]{2,1,0:T(8,128)} %get-tuple-element.42.refs_0_, f32[3,768,128]{2,1,0:T(8,128)} %copy-done, f32[3,768,128]{2,1,0:T(8,128)} %copy-done.1, ...), custom_call_target="tpu_custom_call" | custom-call | flops 60000002048 | bytes 1 | tf_op jit(solution)/shard_map/pallas_call | solution.py:100
  130.9 3.3 %shard_map.73 = f32[4,768,128]{2,1,0:T(8,128)} custom-call(s32[20]{0:T(128)} %concatenate.9.s, f32[2,768,128]{2,1,0:T(8,128)} %get-tuple-element.51.refs_0_.x0, f32[2,768,128]{2,1,0:T(8,128)} %copy-done.6, f32[2,768,128]{2,1,0:T(8,128)} %copy-done.7, f32[2,768,128]{2,1,0:T(8,128)} %copy-done.9), custom_call_target="tpu_custom_call" | custom-call | flops 1000000000 | bytes 1 | tf_op jit(solution)/shard_map/pallas_call | solution.py:100
  134.3 1.8 collective-permute-start.15
  138.0 1.3 collective-permute-start.19
  140.1 3.3 %collective-permute-start.21 = (f32[2,768,128]{2,1,0:T(8,128)S(1)}, f32[2,768,128]{2,1,0:T(8,128)S(1)}, u32[]{:S(2)}, u32[]{:S(2)}) collective-permute-start(f32[2,768,128]{2,1,0:T(8,128)S(1)} %copy-done.4), channel_id=1, source_target_pairs={{0,2},{3,1},{4,6},{7,5},{8,10},{11,9},{12,14},{15,13},{16,18},{19,... | collective-permute-start | bytes 2359304 | tf_op jit(solution)/shard_map/ppermute | solution.py:400
  143.4 1.5 collective-permute-start.11
  144.9 9.0 %shard_map.74 = (f32[1024,128]{1,0:T(8,128)}, f32[1024,128]{1,0:T(8,128)}, f32[768,128]{1,0:T(8,128)}, f32[768,128]{1,0:T(8,128)}) custom-call(s32[12]{0:T(128)} %concatenate.10.s, f32[2,768,128]{2,1,0:T(8,128)} %get-tuple-element.51.refs_0_.x0, f32[2,768,128]{2,1,0:T(8,128)} %copy-done.6, f32[2,768,128]{2,1,0:T(8,128)} %copy-done.7, ...), custom_call_target="tpu_custom_call" | custom-call | flops 10000000000 | bytes 1 | tf_op jit(solution)/shard_map/pallas_call | solution.py:100
  155.2 2.0 collective-permute-done.19.refs_1_.x1
  158.6 14.3 %collective-permute-done.21.refs_3_.x3 = f32[2,768,128]{2,1,0:T(8,128)S(1)} collective-permute-done((f32[2,768,128]{2,1,0:T(8,128)S(1)}, f32[2,768,128]{2,1,0:T(8,128)S(1)}, u32[]{:S(2)}, u32[]{:S(2)}) %collective-permute-start.21) | collective-permute-done | bytes 786464 | tf_op jit(solution)/shard_map/ppermute | solution.py:400
  172.9 1.4 collective-permute-done.11.upper.refs_1_
  174.3 8.4 %collective-permute-done.16.end.refs_3_ = f32[768,128]{1,0:T(8,128)S(1)} collective-permute-done((f32[768,128]{1,0:T(8,128)}, f32[768,128]{1,0:T(8,128)S(1)}, u32[]{:S(2)}, u32[]{:S(2)}) %collective-permute-start.16) | collective-permute-done | bytes 393248 | tf_op jit(solution)/shard_map/ppermute | solution.py:456
  182.7 6.0 %collective-permute-done.17.cross.refs_4_ = f32[768,128]{1,0:T(8,128)S(1)} collective-permute-done((f32[768,128]{1,0:T(8,128)}, f32[768,128]{1,0:T(8,128)S(1)}, u32[]{:S(2)}, u32[]{:S(2)}) %collective-permute-start.17) | collective-permute-done | bytes 393248 | tf_op jit(solution)/shard_map/ppermute | solution.py:456
  188.8 3.2 %shard_map.76 = f32[4,768,128]{2,1,0:T(8,128)} custom-call(s32[20]{0:T(128)} %concatenate.9.s, f32[2,768,128]{2,1,0:T(8,128)} %get-tuple-element.62.refs_0_.x0, f32[2,768,128]{2,1,0:T(8,128)} %copy-done.8, f32[2,768,128]{2,1,0:T(8,128)} %copy-done.10, f32[2,768,128]{2,1,0:T(8,128)} %copy-done.11), custom_call_target="tpu_custom_call" | custom-call | flops 1000000000 | bytes 1 | tf_op jit(solution)/shard_map/pallas_call | solution.py:100
  194.0 2.7 %shard_map.75 = f32[1280,128]{1,0:T(8,128)} custom-call(s32[20]{0:T(128)} %concatenate.9.s, f32[3,768,128]{2,1,0:T(8,128)} %copy-done.3, f32[768,128]{1,0:T(8,128)} %copy-done.19, f32[768,128]{1,0:T(8,128)} %copy-done.20, f32[1024,128]{1,0:T(8,128)} %get-tuple-element.59.core), custom_call_target="tpu_custom_call" | custom-call | flops 1000000000 | bytes 1 | tf_op jit(solution)/shard_map/pallas_call | solution.py:100
  199.0 9.1 %shard_map.77 = (f32[1024,128]{1,0:T(8,128)}, f32[1024,128]{1,0:T(8,128)}, f32[1024,128]{1,0:T(8,128)}, f32[1024,128]{1,0:T(8,128)}) custom-call(s32[12]{0:T(128)} %concatenate.11.s, f32[2,768,128]{2,1,0:T(8,128)} %get-tuple-element.62.refs_0_.x0, f32[2,768,128]{2,1,0:T(8,128)} %copy-done.8, f32[2,768,128]{2,1,0:T(8,128)} %copy-done.10, ...), custom_call_target="tpu_custom_call" | custom-call | flops 10000000000 | bytes 1 | tf_op jit(solution)/shard_map/pallas_call | solution.py:100
  211.5 14.3 %collective-permute-done.24.refs_8_ = f32[1024,128]{1,0:T(8,128)S(1)} collective-permute-done((f32[1024,128]{1,0:T(8,128)}, f32[1024,128]{1,0:T(8,128)S(1)}, u32[]{:S(2)}, u32[]{:S(2)}) %collective-permute-start.24) | collective-permute-done | bytes 524320 | tf_op jit(solution)/shard_map/ppermute | solution.py:456
  225.7 10.7 %collective-permute-done.25.refs_9_ = f32[1024,128]{1,0:T(8,128)S(1)} collective-permute-done((f32[1024,128]{1,0:T(8,128)}, f32[1024,128]{1,0:T(8,128)S(1)}, u32[]{:S(2)}, u32[]{:S(2)}) %collective-permute-start.25) | collective-permute-done | bytes 524320 | tf_op jit(solution)/shard_map/ppermute | solution.py:456
  237.3 4.7 %shard_map.78 = (f32[7,512,128]{2,1,0:T(8,128)}, f32[7,512,128]{2,1,0:T(8,128)}) custom-call(s32[20]{0:T(128)} %concatenate.9.s, f32[3,1024,128]{2,1,0:T(8,128)} %get-tuple-element.46.refs_0_, f32[3,768,128]{2,1,0:T(8,128)} %copy-done.3, f32[1024,128]{1,0:T(8,128)} %get-tuple-element.56.refs_2_, f32[768,128]{1,0:T(8,128)} %copy-done.19, ...), custom_call_target="tpu_custom_call" | custom-call | flops 1000000000 | bytes 1 | tf_op jit(solution)/shard_map/pallas_call | solution.py:100
  (90 shorter events, 23.8 us)
Async XLA Ops:
  0.6 17.5 %collective-permute-start.3 = (f32[128,256]{1,0:T(8,128)}, f32[128,256]{1,0:T(8,128)S(1)}, u32[]{:S(2)}, u32[]{:S(2)}) collective-permute-start(f32[128,256]{1,0:T(8,128)} %refs_0_), channel_id=1, source_target_pairs={{0,1},{3,2},{4,5},{7,6},{8,9},{11,10},{12,13},{15,14},{16,17},{19,... | collective-permute-start | bytes 393224 | tf_op jit(solution)/shard_map/ppermute | solution.py:400
  5.6 16.5 %collective-permute-start.4 = (f32[128,256]{1,0:T(8,128)}, f32[128,256]{1,0:T(8,128)S(1)}, u32[]{:S(2)}, u32[]{:S(2)}) collective-permute-start(f32[128,256]{1,0:T(8,128)} %refs_0_), channel_id=1, source_target_pairs={{1,2},{2,1},{5,6},{6,5},{9,10},{10,9},{13,14},{14,13},{17,18},{18,... | collective-permute-start | bytes 393224 | tf_op jit(solution)/shard_map/ppermute | solution.py:400
  6.3 15.8 %collective-permute-start.5 = (f32[128,256]{1,0:T(8,128)}, f32[128,256]{1,0:T(8,128)S(1)}, u32[]{:S(2)}, u32[]{:S(2)}) collective-permute-start(f32[128,256]{1,0:T(8,128)} %refs_0_), channel_id=1, source_target_pairs={{0,2},{3,1},{4,6},{7,5},{8,10},{11,9},{12,14},{15,13},{16,18},{19,... | collective-permute-start | bytes 393224 | tf_op jit(solution)/shard_map/ppermute | solution.py:400
  15.9 28.1 %collective-permute-start = (f32[3,768,128]{2,1,0:T(8,128)}, f32[3,768,128]{2,1,0:T(8,128)S(1)}, u32[]{:S(2)}, u32[]{:S(2)}) collective-permute-start(f32[3,768,128]{2,1,0:T(8,128)} %get-tuple-element.42.refs_0_), channel_id=1, source_target_pairs={{0,1},{3,2},{4,5},{7,6},{8,9},{11,10},{12,13},{15,14},{16,17},{19,... | collective-permute-start | bytes 3538952 | tf_op jit(solution)/shard_map/ppermute | solution.py:400
  17.4 26.6 %collective-permute-start.1 = (f32[3,768,128]{2,1,0:T(8,128)}, f32[3,768,128]{2,1,0:T(8,128)S(1)}, u32[]{:S(2)}, u32[]{:S(2)}) collective-permute-start(f32[3,768,128]{2,1,0:T(8,128)} %get-tuple-element.42.refs_0_), channel_id=1, source_target_pairs={{1,2},{2,1},{5,6},{6,5},{9,10},{10,9},{13,14},{14,13},{17,18},{18,... | collective-permute-start | bytes 3538952 | tf_op jit(solution)/shard_map/ppermute | solution.py:400
  18.1 49.7 %collective-permute-start.2 = (f32[3,768,128]{2,1,0:T(8,128)}, f32[3,768,128]{2,1,0:T(8,128)S(1)}, u32[]{:S(2)}, u32[]{:S(2)}) collective-permute-start(f32[3,768,128]{2,1,0:T(8,128)} %get-tuple-element.42.refs_0_), channel_id=1, source_target_pairs={{0,2},{3,1},{4,6},{7,5},{8,10},{11,9},{12,14},{15,13},{16,18},{19,... | collective-permute-start | bytes 3538952 | tf_op jit(solution)/shard_map/ppermute | solution.py:400
  26.0 1.4 collective-permute-start.6
  26.7 1.4 collective-permute-start.7
  27.4 46.7 %copy-start.13 = (f32[128,1024]{1,0:T(8,128)}, f32[128,1024]{1,0:T(8,128)S(1)}, u32[]{:S(2)}) copy-start(f32[128,1024]{1,0:T(8,128)S(1)} %collective-permute-done.6.refs_1_.refs_6_) | copy-start | bytes 1572868
  27.4 0.7 collective-permute-start.8
  28.1 46.0 %copy-start.14 = (f32[128,1024]{1,0:T(8,128)}, f32[128,1024]{1,0:T(8,128)S(1)}, u32[]{:S(2)}) copy-start(f32[128,1024]{1,0:T(8,128)S(1)} %collective-permute-done.7.refs_2_.refs_7_) | copy-start | bytes 1572868
  28.1 46.0 %copy-start.15 = (f32[128,1024]{1,0:T(8,128)}, f32[128,1024]{1,0:T(8,128)S(1)}, u32[]{:S(2)}) copy-start(f32[128,1024]{1,0:T(8,128)S(1)} %collective-permute-done.8.refs_3_.refs_8_) | copy-start | bytes 1572868
  74.2 19.4 %collective-permute-start.9 = (f32[4,3,768,128]{3,2,1,0:T(8,128)}, f32[4,3,768,128]{3,2,1,0:T(8,128)}, u32[]{:S(2)}, u32[]{:S(2)}) collective-permute-start(f32[4,3,768,128]{3,2,1,0:T(8,128)} %shard_map.70), channel_id=1, source_target_pairs={{1,5},{2,6},{5,1},{6,2},{9,13},{10,14},{13,9},{14,10},{17,21},{18,... | collective-permute-start | bytes 14155784 | tf_op jit(solution)/shard_map/ppermute | solution.py:403
  80.7 12.8 %collective-permute-start.10 = (f32[4,128,1024]{2,1,0:T(8,128)}, f32[4,128,1024]{2,1,0:T(8,128)S(1)}, u32[]{:S(2)}, u32[]{:S(2)}) collective-permute-start(f32[4,128,1024]{2,1,0:T(8,128)} %shard_map.71), channel_id=1, source_target_pairs={{1,5},{2,6},{5,1},{6,2},{9,13},{10,14},{13,9},{14,10},{17,21},{18,... | collective-permute-start | bytes 6291464 | tf_op jit(solution)/shard_map/ppermute | solution.py:403
  81.5 48.0 %collective-permute-start.12 = (f32[2,768,128]{2,1,0:T(8,128)S(1)}, f32[2,768,128]{2,1,0:T(8,128)S(1)}, u32[]{:S(2)}, u32[]{:S(2)}) collective-permute-start(f32[2,768,128]{2,1,0:T(8,128)S(1)} %copy-done.5), channel_id=1, source_target_pairs={{0,1},{3,2},{4,5},{7,6},{8,9},{11,10},{12,13},{15,14},{16,17},{19,... | collective-permute-start | bytes 2359304 | tf_op jit(solution)/shard_map/ppermute | solution.py:400
  88.8 40.7 %collective-permute-start.13 = (f32[2,768,128]{2,1,0:T(8,128)S(1)}, f32[2,768,128]{2,1,0:T(8,128)S(1)}, u32[]{:S(2)}, u32[]{:S(2)}) collective-permute-start(f32[2,768,128]{2,1,0:T(8,128)S(1)} %copy-done.5), channel_id=1, source_target_pairs={{1,2},{2,1},{5,6},{6,5},{9,10},{10,9},{13,14},{14,13},{17,18},{18,... | collective-permute-start | bytes 2359304 | tf_op jit(solution)/shard_map/ppermute | solution.py:400
  89.5 40.0 %collective-permute-start.14 = (f32[2,768,128]{2,1,0:T(8,128)S(1)}, f32[2,768,128]{2,1,0:T(8,128)S(1)}, u32[]{:S(2)}, u32[]{:S(2)}) collective-permute-start(f32[2,768,128]{2,1,0:T(8,128)S(1)} %copy-done.5), channel_id=1, source_target_pairs={{0,2},{3,1},{4,6},{7,5},{8,10},{11,9},{12,14},{15,13},{16,18},{19,... | collective-permute-start | bytes 2359304 | tf_op jit(solution)/shard_map/ppermute | solution.py:400
  134.3 10.6 %collective-permute-start.15 = (f32[4,768,128]{2,1,0:T(8,128)}, f32[4,768,128]{2,1,0:T(8,128)}, u32[]{:S(2)}, u32[]{:S(2)}) collective-permute-start(f32[4,768,128]{2,1,0:T(8,128)} %shard_map.73), channel_id=1, source_target_pairs={{1,5},{2,6},{5,1},{6,2},{9,13},{10,14},{13,9},{14,10},{17,21},{18,... | collective-permute-start | bytes 4718600 | tf_op jit(solution)/shard_map/ppermute | solution.py:403
  138.0 19.2 %collective-permute-start.19 = (f32[2,768,128]{2,1,0:T(8,128)S(1)}, f32[2,768,128]{2,1,0:T(8,128)S(1)}, u32[]{:S(2)}, u32[]{:S(2)}) collective-permute-start(f32[2,768,128]{2,1,0:T(8,128)S(1)} %copy-done.4), channel_id=1, source_target_pairs={{0,1},{3,2},{4,5},{7,6},{8,9},{11,10},{12,13},{15,14},{16,17},{19,... | collective-permute-start | bytes 2359304 | tf_op jit(solution)/shard_map/ppermute | solution.py:400
  139.4 19.2 %collective-permute-start.20 = (f32[2,768,128]{2,1,0:T(8,128)S(1)}, f32[2,768,128]{2,1,0:T(8,128)S(1)}, u32[]{:S(2)}, u32[]{:S(2)}) collective-permute-start(f32[2,768,128]{2,1,0:T(8,128)S(1)} %copy-done.4), channel_id=1, source_target_pairs={{1,2},{2,1},{5,6},{6,5},{9,10},{10,9},{13,14},{14,13},{17,18},{18,... | collective-permute-start | bytes 2359304 | tf_op jit(solution)/shard_map/ppermute | solution.py:400
  140.1 32.8 %collective-permute-start.21 = (f32[2,768,128]{2,1,0:T(8,128)S(1)}, f32[2,768,128]{2,1,0:T(8,128)S(1)}, u32[]{:S(2)}, u32[]{:S(2)}) collective-permute-start(f32[2,768,128]{2,1,0:T(8,128)S(1)} %copy-done.4), channel_id=1, source_target_pairs={{0,2},{3,1},{4,6},{7,5},{8,10},{11,9},{12,14},{15,13},{16,18},{19,... | collective-permute-start | bytes 2359304 | tf_op jit(solution)/shard_map/ppermute | solution.py:400
  143.4 31.0 %collective-permute-start.11 = (f32[3,768,128]{2,1,0:T(8,128)}, f32[3,768,128]{2,1,0:T(8,128)S(1)}, u32[]{:S(2)}, u32[]{:S(2)}) collective-permute-start(f32[3,768,128]{2,1,0:T(8,128)} %get-tuple-element.47), channel_id=1, source_target_pairs={{1,0},{2,3},{5,4},{6,7},{9,8},{10,11},{13,12},{14,15},{17,16},{18,... | collective-permute-start | bytes 3538952 | tf_op jit(solution)/shard_map/ppermute | solution.py:437
  153.9 28.8 %collective-permute-start.16 = (f32[768,128]{1,0:T(8,128)}, f32[768,128]{1,0:T(8,128)S(1)}, u32[]{:S(2)}, u32[]{:S(2)}) collective-permute-start(f32[768,128]{1,0:T(8,128)} %get-tuple-element.57), channel_id=1, source_target_pairs={{1,0},{2,3},{5,4},{6,7},{9,8},{10,11},{13,12},{14,15},{17,16},{18,... | collective-permute-start | bytes 1179656 | tf_op jit(solution)/shard_map/ppermute | solution.py:456
  157.3 31.5 %copy-start.8 = (f32[2,768,128]{2,1,0:T(8,128)}, f32[2,768,128]{2,1,0:T(8,128)S(1)}, u32[]{:S(2)}) copy-start(f32[2,768,128]{2,1,0:T(8,128)S(1)} %collective-permute-done.19.refs_1_.x1) | copy-start | bytes 2359300
  157.3 31.5 %collective-permute-start.17 = (f32[768,128]{1,0:T(8,128)}, f32[768,128]{1,0:T(8,128)S(1)}, u32[]{:S(2)}, u32[]{:S(2)}) collective-permute-start(f32[768,128]{1,0:T(8,128)} %get-tuple-element.58), channel_id=1, source_target_pairs={{1,4},{2,7},{5,0},{6,3},{9,12},{10,15},{13,8},{14,11},{17,20},{18,... | collective-permute-start | bytes 1179656 | tf_op jit(solution)/shard_map/ppermute | solution.py:456
  158.6 30.2 %copy-start.10 = (f32[2,768,128]{2,1,0:T(8,128)}, f32[2,768,128]{2,1,0:T(8,128)S(1)}, u32[]{:S(2)}) copy-start(f32[2,768,128]{2,1,0:T(8,128)S(1)} %collective-permute-done.20.refs_2_.x2) | copy-start | bytes 2359300
  192.0 5.8 %collective-permute-start.22 = (f32[4,768,128]{2,1,0:T(8,128)}, f32[4,768,128]{2,1,0:T(8,128)S(1)}, u32[]{:S(2)}, u32[]{:S(2)}) collective-permute-start(f32[4,768,128]{2,1,0:T(8,128)} %shard_map.76), channel_id=1, source_target_pairs={{1,5},{2,6},{5,1},{6,2},{9,13},{10,14},{13,9},{14,10},{17,21},{18,... | collective-permute-start | bytes 4718600 | tf_op jit(solution)/shard_map/ppermute | solution.py:403
  196.7 14.7 %collective-permute-start.18 = (f32[1280,128]{1,0:T(8,128)}, f32[1280,128]{1,0:T(8,128)S(1)}, u32[]{:S(2)}, u32[]{:S(2)}) collective-permute-start(f32[1280,128]{1,0:T(8,128)} %shard_map.75), channel_id=1, source_target_pairs={{0,4},{1,5},{2,6},{3,7},{4,0},{5,1},{6,2},{7,3},{8,12},{9,13},{10,... | collective-permute-start | bytes 1966088 | tf_op jit(solution)/shard_map/ppermute | solution.py:462
  208.1 3.3 %collective-permute-start.23 = (f32[1024,128]{1,0:T(8,128)}, f32[1024,128]{1,0:T(8,128)S(1)}, u32[]{:S(2)}, u32[]{:S(2)}) collective-permute-start(f32[1024,128]{1,0:T(8,128)} %get-tuple-element.67), channel_id=1, source_target_pairs={{1,5},{2,6},{5,1},{6,2},{9,13},{10,14},{13,9},{14,10},{17,21},{18,... | collective-permute-start | bytes 1572872 | tf_op jit(solution)/shard_map/ppermute | solution.py:403
  208.8 16.9 %collective-permute-start.24 = (f32[1024,128]{1,0:T(8,128)}, f32[1024,128]{1,0:T(8,128)S(1)}, u32[]{:S(2)}, u32[]{:S(2)}) collective-permute-start(f32[1024,128]{1,0:T(8,128)} %get-tuple-element.68), channel_id=1, source_target_pairs={{1,0},{2,3},{5,4},{6,7},{9,8},{10,11},{13,12},{14,15},{17,16},{18,... | collective-permute-start | bytes 1572872 | tf_op jit(solution)/shard_map/ppermute | solution.py:456
  210.1 26.3 %collective-permute-start.25 = (f32[1024,128]{1,0:T(8,128)}, f32[1024,128]{1,0:T(8,128)S(1)}, u32[]{:S(2)}, u32[]{:S(2)}) collective-permute-start(f32[1024,128]{1,0:T(8,128)} %get-tuple-element.69), channel_id=1, source_target_pairs={{1,4},{2,7},{5,0},{6,3},{9,12},{10,15},{13,8},{14,11},{17,20},{18,... | collective-permute-start | bytes 1572872 | tf_op jit(solution)/shard_map/ppermute | solution.py:456
  211.4 25.0 %copy-start.12 = (f32[1280,128]{1,0:T(8,128)}, f32[1280,128]{1,0:T(8,128)S(1)}, u32[]{:S(2)}) copy-start(f32[1280,128]{1,0:T(8,128)S(1)} %collective-permute-done.18.refs_5_) | copy-start | bytes 1966084
  (21 other events, 162.2 us)

commit v4 on v3

--- a/solution.py
+++ b/solution.py
@@ -10,6 +10,7 @@
 TILE = 128
 STEP = 2 * TILE
 QUARTER = TILE // 2
+ROWS = 4 * TILE
 F32 = jnp.float32
 BF16 = jnp.bfloat16
 VMEM_LIMIT = 56 * 2**20
@@ -69,22 +70,22 @@
 
 def solve(p, pt, dt, a, dc, f, w, t, weights, emit_ab, emit_dg, join):
     width = dc[0].shape[1]
-    for rows in tiles(p[0].shape[0]):
+    for rows in tiles(p[0].shape[0], ROWS):
         k = rows.start // TILE
         for cols in tiles(width):
             value = dot3(get(p, (rows, ALL)), get(dc, (ALL, cols)))
-            value = jnp.concatenate([value[:TILE] * weights[k], value[TILE:] * weights[k + 1]], axis=0)
-            put(f, (rows, cols), value)
+            parts = [value[i * TILE:(i + 1) * TILE] * weights[k + i] for i in range(ROWS // TILE)]
+            put(f, (rows, cols), jnp.concatenate(parts, axis=0))
     join()
     for cols in tiles(width):
-        for rows in tiles(a[0].shape[0]):
+        for rows in tiles(a[0].shape[0], ROWS):
             value = dot3(get(a, (rows, ALL)), get(f, (ALL, cols)))
             emit_ab(rows, cols, -value)
             put(w, (rows, cols), value)
-        for rows in tiles(pt[0].shape[0]):
+        for rows in tiles(pt[0].shape[0], ROWS):
             value = dot3(get(pt, (rows, ALL)), get(w, (ALL, cols)))
             put(t, (rows, cols), value + dc[0][rows, cols].astype(F32) + dc[1][rows, cols].astype(F32))
-        for rows in tiles(dt[0].shape[0]):
+        for rows in tiles(dt[0].shape[0], ROWS):
             emit_dg(rows, cols, dot3(get(dt, (rows, ALL)), get(t, (ALL, cols))))
 
 
@@ -134,11 +135,11 @@
     return [(s[LIST + j] >= 0).astype(F32) for j in range(order // TILE)]
 
 
-def pack_kernel(s, panels, inverse, *rest):
+def pack_kernel(first, s, panels, inverse, *rest):
     outs, sems = rest[:-1], rest[-1]
     half = panels.shape[1]
     copies = []
-    node = 0
+    node = first
     for out in outs:
         for i in range(out.shape[0]):
             copies.append((panels.at[node], out.at[i, pl.ds(0, half)]))
@@ -178,100 +179,112 @@
             put(a, (place, slice(own + j * TILE, own + (j + 1) * TILE)), corner(i, j) * (weight[i] * weight[j]))
 
 
-def trunk_kernel(s, *refs):
-    mine, theirs, sigmas = refs[:4], refs[4], refs[5:10]
-    ext, grand, self_out, end_out = refs[10:14]
-    stage, sigma, sems, corners, ab, dg = refs[14:20]
-    p, d, a, f, w, t, pt, dt = pairs(refs[20:-1])
+def emitters(ab, dg):
+    def emit_ab(rows, cols, value):
+        ab[rows, cols] = value
+
+    def emit_dg(rows, cols, value):
+        dg[rows, cols] = value
+
+    return emit_ab, emit_dg
+
+
+def columns_out(s, ab, dg, self_out, end_out):
+    r, c = s[0], s[1]
+    half = ab.shape[0] // 2
+    own = dg.shape[0]
+    share = own // 2
+    end_cols = at(3 * (c // 2) * TILE, TILE)
+    self_out[0:half, :] = ab[at(r * half, half), at(c * TILE, TILE)]
+    self_out[half:, :] = dg[:, at(c * TILE, TILE)]
+    end_out[0:half, :] = ab[at(r * half, half), end_cols]
+    end_out[half:, :] = dg[at(r * share, share), end_cols]
+
+
+def root_kernel(s, *refs):
+    mine, theirs, sigmas = refs[:4], refs[4], refs[5:13]
+    ext, corners, self_out, end_out = refs[13:17]
+    stage, sigma, sems = refs[17:20]
+    p, d, a, f, w, t, pt, dt = pairs(refs[20:])
     r, c, leaf = s[0], s[1], s[2]
     order = a[0].shape[0]
     own = d[0].shape[0]
     half = order // 2
     far = c // 2
-    count = 3
-
-    def fetch(node, slot):
-        found = []
-        for k in range(4):
-            found.append(pltpu.make_async_copy(mine[k].at[node], stage.at[slot, 2 * k], sems.at[slot, 2 * k]))
-            found.append(pltpu.make_async_copy(theirs.at[k, node], stage.at[slot, 2 * k + 1], sems.at[slot, 2 * k + 1]))
-        return found
-
-    sigma_copies = [
-        pltpu.make_async_copy(ref, sigma.at[k], sems.at[2, k])
-        for k, ref in enumerate(list(sigmas[:4]) + [sigmas[4].at[m] for m in range(4)])
-    ]
-    for one in fetch(0, 0) + sigma_copies + fetch(1, 1):
+    blocks = [x for k in range(4) for x in (mine[k].at[0], theirs.at[k, 0])]
+    copies = [pltpu.make_async_copy(ref, stage.at[k], sems.at[0, k]) for k, ref in enumerate(blocks)]
+    later = [pltpu.make_async_copy(ref, sigma.at[k], sems.at[1, k]) for k, ref in enumerate(sigmas)]
+    for one in copies + later:
         one.start()
-
-    def panels_of(node, slot):
-        for one in fetch(node, slot):
-            one.wait()
-        load_panels([stage.at[slot, k] for k in range(8)], r, p, d, pt, dt, half)
-
-    def emit_ab(rows, cols, value):
-        ab[rows, cols] = value
-
-    def emit_dg(rows, cols, value):
-        dg[rows, cols] = value
-
-    def columns_out(node):
-        for out, col in ((self_out, c), (end_out, 3 * far)):
-            out[node, 0:half, :] = ab[at(r * half, half), at(col * TILE, TILE)]
-        self_out[node, half:, :] = dg[:, at(c * TILE, TILE)]
-        end_out[node, half:, :] = dg[at(r * (own // 2), own // 2), at(3 * far * TILE, TILE)]
-
-    panels_of(0, 0)
-
-    def join_root():
+    for one in copies:
+        one.wait()
+    load_panels([stage.at[k] for k in range(8)], r, p, d, pt, dt, half)
+
+    def join():
         places = (c, 3 * far, 3 - c, 3 - 3 * far)
         span = order // 4
-        for one in sigma_copies:
+        for one in later:
             one.wait()
         for m in range(4):
             for turn in range(2):
                 side = r if turn == 0 else 1 - r
                 rows = at(((leaf ^ m) * 2 + side) * TILE, TILE)
                 for k in range(4):
-                    value = sigma[4 * turn + m, :, k * span:(k + 1) * span]
-                    put(a, (rows, at(places[k] * span, span)), value)
-
-    solve(p, pt, dt, a, d, f, w, t, [1.0] * (order // TILE), emit_ab, emit_dg, join_root)
-    columns_out(0)
-    grand[...] = dg[...]
-    for node in (1, 2):
-        index, weight = tail_of(s, LIST + (node - 1) * (order // TILE), own, order)
+                    put(a, (rows, at(places[k] * span, span)), sigma[4 * turn + m, :, k * span:(k + 1) * span])
+
+    ab, dg = ext.at[pl.ds(0, order)], ext.at[pl.ds(order, own)]
+    solve(p, pt, dt, a, d, f, w, t, [1.0] * (order // TILE), *emitters(ab, dg), join)
+    columns_out(s, ab, dg, self_out, end_out)
+    for node in range(2):
+        index, weight = tail_of(s, LIST + node * (order // TILE), own, order)
         for i in range(len(index)):
             for j in range(len(index)):
                 high, low = get(a, (at(index[i] * TILE, TILE), at(index[j] * TILE, TILE)))
                 value = high.astype(F32) + low.astype(F32)
-                corners[node - 1, i * TILE:(i + 1) * TILE, j * TILE:(j + 1) * TILE] = value
-    for one in fetch(2, 0):
+                corners[node, i * TILE:(i + 1) * TILE, j * TILE:(j + 1) * TILE] = value
+
+
+def middle_kernel(s, *refs):
+    mine, theirs, root, corners_in = refs[:4], refs[4], refs[5], refs[6]
+    ext, self_out, end_out = refs[7:10]
+    stage, root_in, corners, sems, ab, dg = refs[10:16]
+    p, d, a, f, w, t, pt, dt = pairs(refs[16:])
+    r = s[0]
+    order = a[0].shape[0]
+    own = d[0].shape[0]
+    half = order // 2
+    blocks = [[x for k in range(4) for x in (mine[k].at[node], theirs.at[k, node])] for node in (1, 2)]
+    copies = [
+        pltpu.make_async_copy(ref, stage.at[node, k], sems.at[node, k])
+        for node in range(2) for k, ref in enumerate(blocks[node])
+    ]
+    later = [pltpu.make_async_copy(root, root_in, sems.at[2, 0]), pltpu.make_async_copy(corners_in, corners, sems.at[2, 1])]
+    for one in copies[:8] + later + copies[8:]:
         one.start()
-    root_ab = refs[-1]
-    root_ab[...] = ab[...]
-
-    @pl.loop(1, count)
+    for one in copies + later:
+        one.wait()
+
+    @pl.loop(0, 2)
     def _(node):
-        start = LIST + (node - 1) * (order // TILE)
+        start = LIST + node * (order // TILE)
         index, weight = tail_of(s, start, own, order)
-        panels_of(node, node % 2)
+        load_panels([stage.at[node, k] for k in range(8)], r, p, d, pt, dt, half)
 
         def join():
             join_block(
                 a, own,
-                lambda i, j: corners[node - 1, i * TILE:(i + 1) * TILE, j * TILE:(j + 1) * TILE],
-                lambda i: root_ab[at(index[i] * TILE, TILE), :], grand[...], index, weight,
+                lambda i, j: corners[node, i * TILE:(i + 1) * TILE, j * TILE:(j + 1) * TILE],
+                lambda i: root_in[at(index[i] * TILE, TILE), :], root_in[order:, :], index, weight,
             )
 
         weights = [(s[start + k] >= 0).astype(F32) for k in range(order // TILE)]
-        solve(p, pt, dt, a, d, f, w, t, weights, emit_ab, emit_dg, join)
-        columns_out(node)
-        ext[node - 1, 0:half, :] = ab[0:half, :]
-        ext[node - 1, half:, :] = dg[...]
-
-
-def leaf_kernel(s, x0, x1, x2, x3, ex, ext, grand, self_out, core_out, end_out, cross_out, *rest):
+        solve(p, pt, dt, a, d, f, w, t, weights, *emitters(ab, dg), join)
+        columns_out(s, ab, dg, self_out.at[node], end_out.at[node])
+        ext[node, 0:half, :] = ab[0:half, :]
+        ext[node, half:, :] = dg[...]
+
+
+def leaf_kernel(s, x0, x1, x2, x3, ex, ext, root, self_out, core_out, end_out, cross_out, *rest):
     stage, sems, tails, top, grand_in, ab, dg = rest[:7]
     p, d, a, dc, f, w, t, pt, dt = pairs(rest[7:])
     r, c = s[0], s[1]
@@ -285,7 +298,7 @@
     copies = [pltpu.make_async_copy(ref, stage.at[k], sems.at[k]) for k, ref in enumerate(blocks)]
     later = [
         pltpu.make_async_copy(ext.at[parent, pl.ds(half, own)], top, sems.at[8]),
-        pltpu.make_async_copy(grand, grand_in, sems.at[9]),
+        pltpu.make_async_copy(root.at[pl.ds(order, own)], grand_in, sems.at[9]),
     ]
     for j, pick in enumerate(index):
         later.append(pltpu.make_async_copy(ext.at[parent, at(pick * TILE, TILE)], tails.at[j], sems.at[10 + j]))
@@ -305,13 +318,7 @@
             top[...], index, weight,
         )
 
-    def emit_ab(rows, cols, value):
-        ab[rows, cols] = value
-
-    def emit_dg(rows, cols, value):
-        dg[rows, cols] = value
-
-    solve(p, pt, dt, a, dc, f, w, t, weights_of(s, order), emit_ab, emit_dg, join)
+    solve(p, pt, dt, a, dc, f, w, t, weights_of(s, order), *emitters(ab, dg), join)
     near_cols, end_cols = at((1 - far) * TILE, TILE), at(far * TILE, TILE)
     for out, side, cols in (
         (self_out, r, near_cols), (core_out, 1 - r, near_cols), (end_out, r, end_cols), (cross_out, 1 - r, end_cols)
@@ -321,7 +328,7 @@
         out[half:, :] = dg[:, cols] if share == own else dg[at(side * share, share), cols]
 
 
-def shares_kernel(s, upper, end, cross, core, out, sems):
+def shares_kernel(s, root, upper, end, cross, core, out, sems):
     c = s[1]
     middle = (c == 1) | (c == 2)
     half = core.shape[0] // 2
@@ -333,14 +340,15 @@
 
     @pl.when(jnp.logical_not(middle))
     def _():
-        found = [upper.at[k] for k in range(3)] + [end, cross]
+        found = [root, upper.at[0], upper.at[1], end, cross]
         copy_all([
             (ref.at[pl.ds(half, share)], out.at[pl.ds(k * share, share)]) for k, ref in enumerate(found)
         ], sems)
 
 
 def output_kernel(s, *refs):
-    upper_self, upper_end, self_34, end_34, cross_34, shares, self_56, core_56, end_56, cross_56 = refs[:10]
+    root_self, root_end, upper_self, upper_end, self_34, end_34, cross_34, shares = refs[:8]
+    self_56, core_56, end_56, cross_56 = refs[8:12]
     ab, dg, sems = refs[-3:]
     r, c = s[0], s[1]
     half = ab.shape[1]
@@ -352,7 +360,7 @@
             pair = [self_34, shares] if core == 0 else [shares, self_34]
             last = [self_56, core_56] if core == 0 else [core_56, self_56]
             copies = []
-            for node, ref in enumerate([upper_self.at[k] for k in range(3)] + pair + last):
+            for node, ref in enumerate([root_self, upper_self.at[0], upper_self.at[1]] + pair + last):
                 copies.append((ref.at[pl.ds(0, half)], ab.at[node]))
                 copies.append((ref.at[pl.ds(half, half)], dg.at[node]))
             copy_all(copies, sems)
@@ -362,7 +370,8 @@
             same, swapped = (3, 4) if core == 0 else (4, 3)
             last = [end_56, cross_56] if core == 0 else [cross_56, end_56]
             copies = []
-            for node, ref, k in [(k, upper_end.at[k], k) for k in range(3)] + [(same, end_34, 4), (swapped, cross_34, 3)]:
+            found = [(0, root_end, 0), (1, upper_end.at[0], 1), (2, upper_end.at[1], 2)]
+            for node, ref, k in found + [(same, end_34, 4), (swapped, cross_34, 3)]:
                 copies.append((ref.at[pl.ds(0, half)], ab.at[node]))
                 copies.append((ref.at[pl.ds(half, share)], dg.at[node, pl.ds(core * share, share)]))
                 copies.append((shares.at[pl.ds(k * share, share)], dg.at[node, pl.ds((1 - core) * share, share)]))
@@ -406,32 +415,40 @@
         head = jnp.stack([r, c, leaf, parent]).astype(jnp.int32)
         return jnp.concatenate([head] + [lists[row] for row in rows])
 
-    trunk = 3
     here = scalars(jnp.int32(0), 0, 1)
     packed = half + own // 2
+
+    pack_t, pack_34, pack_56 = move(
+        functools.partial(pack_kernel, 0), here, [panels, inverse], [(k, packed, TILE) for k in (3, 2, 2)], 35
+    )
     sigma_parts = straight(sigma_top)
-    pack_t, pack_34, pack_56 = move(
-        pack_kernel, here, [panels, inverse], [(k, packed, TILE) for k in (trunk, 2, 2)], 35
-    )
     blocks_t = straight(pack_t)
     sigma_cols = move(join_columns_kernel, here, after(sigma_parts, pack_t), [(TILE, order)], 4)[0]
     sigma_rows = [sigma_cols] + [
         lax.ppermute(sigma_cols, ("leaf", "row", "col"), leaf_routes[m]) for m in range(1, 4)
     ]
-    sigma_other = swapped(move(stack_kernel, here, sigma_rows, [(4, TILE, order)], 4)[0])
-    gathered = after(blocks_t, sigma_rows[1:])
-    other_t = swapped(move(stack_kernel, here, gathered, [(4, trunk, packed, TILE)], 4)[0])
+    sigma_other = [swapped(x) for x in sigma_rows]
+    gathered = after(blocks_t, sigma_other)
+    other_t = swapped(move(stack_kernel, here, gathered, [(4, 3, packed, TILE)], 4)[0])
     blocks_34 = straight(after(pack_34, blocks_t[1:]))
-    ext, grand, upper_self, upper_end = call(
-        trunk_kernel, here, blocks_t + [other_t] + sigma_rows + [sigma_other],
-        [(2, half + own, own), (own, own), (trunk, half + own, TILE), (trunk, packed, TILE)],
+    node_scratch = scratch_pairs(
+        (order, own), (own, own), (order, order), (order, own), (order, own), (own, own), (own, order), (own, own)
+    )
+    root, corners, root_self, root_end = call(
+        root_kernel, here, blocks_t + [other_t] + sigma_rows + sigma_other,
+        [(order + own, own), (2, order - own, order - own), (half + own, TILE), (packed, TILE)],
+        [pltpu.VMEM((8, packed, TILE), F32), pltpu.VMEM((8, TILE, order), F32), pltpu.SemaphoreType.DMA((2, 8))]
+        + node_scratch, [ANY] * 13, micros=10,
+    )
+    root_home = lax.ppermute(root_end, "col", home)
+    ext, upper_self, upper_end = call(
+        middle_kernel, here, blocks_t + [other_t, root, corners],
+        [(2, half + own, own), (2, half + own, TILE), (2, packed, TILE)],
         [
-            pltpu.VMEM((2, 8, packed, TILE), F32), pltpu.VMEM((8, TILE, order), F32), pltpu.SemaphoreType.DMA((3, 8)),
-            pltpu.VMEM((2, order - own, order - own), F32), pltpu.VMEM((order, own), F32), pltpu.VMEM((own, own), F32),
-        ] + scratch_pairs(
-            (order, own), (own, own), (order, order), (order, own), (order, own), (own, own), (own, order), (own, own)
-        ) + [pltpu.VMEM((order, own), F32)],
-        [ANY] * 10, micros=60,
+            pltpu.VMEM((2, 8, packed, TILE), F32), pltpu.VMEM((order + own, own), F32),
+            pltpu.VMEM((2, order - own, order - own), F32), pltpu.SemaphoreType.DMA((3, 8)),
+            pltpu.VMEM((order, own), F32), pltpu.VMEM((own, own), F32),
+        ] + node_scratch, [ANY] * 7, micros=25,
     )
     blocks_56 = straight(after(pack_56, (blocks_34[1:], ext)))
     upper_home = lax.ppermute(upper_end, "col", home)
@@ -450,21 +467,24 @@
         parent = lax.dynamic_index_in_dim(links, node - 3, 0, keepdims=False)
         theirs = swapped(move(swap_kernel, here, after(blocks, earlier), [(4, packed, TILE)], 4)[0])
         self_out, core_out, end_out, cross_out = call(
-            leaf_kernel, scalars(parent, node - 1), blocks + [theirs, ext, grand],
+            leaf_kernel, scalars(parent, node - 1), blocks + [theirs, ext, root],
             [(half + own, TILE)] * 2 + [(end_rows, TILE)] * 2, leaf_scratch, [ANY] * 7, micros=10,
         )
         return self_out, core_out, lax.ppermute(end_out, "col", home), lax.ppermute(cross_out, both, home_cross)
 
-    self_34, core_34, end_34, cross_34 = leaves(blocks_34, 3, ext, packed)
+    self_34, core_34, end_34, cross_34 = leaves(blocks_34, 3, (ext, root_home), packed)
     shares = move(
-        shares_kernel, here, [upper_home, end_34, cross_34, core_34], [((trunk + 2) * (own // 2), TILE)], trunk + 2
+        shares_kernel, here, [root_home, upper_home, end_34, cross_34, core_34], [(5 * (own // 2), TILE)], 5
     )[0]
     shares = lax.ppermute(shares, both, swap_all)
     self_56, core_56, end_56, cross_56 = leaves(blocks_56, 5, (upper_home, end_34, cross_34), half + own)
     count = panels.shape[0]
     ancestor_block, diagonal_block = move(
         output_kernel, here,
-        [upper_self, upper_home, self_34, end_34, cross_34, shares, self_56, swapped(core_56), end_56, cross_56],
+        [
+            root_self, root_home, upper_self, upper_home, self_34, end_34, cross_34, shares, self_56, swapped(core_56),
+            end_56, cross_56,
+        ],
         [(count, half, TILE), (count, own, TILE)], 3 * count,
     )
     return (ancestor_block[None], diagonal_block[None])

time: 243 us -> 263 us (1.082)
  starting transfers between devices: 49.9 us -> 63.4 us
  Pallas kernels: 82.3 us -> 94.8 us
  waiting for transfers between devices: 96.9 us -> 90.5 us
    pallas_call x11, Pallas kernels: 82.3 us -> 94.8 us  [call(): pl.pallas_call(kernel, out_shape=[jax.ShapeDtypeStruct(o, F32) for o in o...]
    ppermute x12, starting transfers between devices: 33 us -> 45.1 us  [straight(): return [x] + [lax.ppermute(x, 'col', route) for route in routes]]
    ppermute x1, waiting for transfers between devices: 1.41 us -> 9.14 us  [chip_body(): upper_home = lax.ppermute(upper_end, 'col', home)]
    ppermute x12, waiting for transfers between devices: 56.1 us -> 48.7 us  [straight(): return [x] + [lax.ppermute(x, 'col', route) for route in routes]]
    ppermute x2, waiting for transfers between devices: 22.7 us -> 15.6 us  [leaves(): lax.ppermute(end_out, 'col', home)]
    ppermute x5 -> x8, starting transfers between devices: 7.01 us -> 7.2 us  [swapped(): return lax.ppermute(x, both, swap)]
    unnamed x54 -> x66, local copies, waits for them, and re-layouts: 7.11 us -> 7.29 us
  transfers between devices with their start and end apart: 26 -> 30, of which waited for: 9 -> 8; matrix products, arithmetic and copies ran while one was open for 2% -> 2% of each run, Pallas kernels for 27% -> 29%
where the time goes in v4:
time: 263 us; the launch traced here: 262 us
  Pallas kernels  94.8 us (36%)
  waiting for transfers between devices  90.5 us (34%)
  starting transfers between devices  63.4 us (24%)
  local copies, waits for them, and re-layouts  11.7 us (4%)
    pallas_call x11, Pallas kernels, call(): pl.pallas_call(kernel, out_shape=[jax.ShapeDtypeStruct(o, F32) for o in o...  94.8 us
    ppermute x12, waiting for transfers between devices, straight(): return [x] + [lax.ppermute(x, 'col', route) for route in routes]  48.7 us
    ppermute x12, starting transfers between devices, straight(): return [x] + [lax.ppermute(x, 'col', route) for route in routes]  45.1 us
    ppermute x2, waiting for transfers between devices, leaves(): lax.ppermute(cross_out, both, home_cross)  17.1 us
    ppermute x2, waiting for transfers between devices, leaves(): lax.ppermute(end_out, 'col', home)  15.6 us
    ppermute x1, waiting for transfers between devices, chip_body(): upper_home = lax.ppermute(upper_end, 'col', home)  9.14 us
    unnamed x66, local copies, waits for them, and re-layouts  7.29 us
    ppermute x8, starting transfers between devices, swapped(): return lax.ppermute(x, both, swap)  7.2 us
  transfers between devices with their start and end apart: 30, of which 8 were waited for; matrix products, arithmetic and copies ran while one was open for 2% of the time, Pallas kernels for 29%

profile of v4, /device:TPU:0, one launch (start us, length us, event | category | flops | bytes accessed | tf_op | source)
XLA Modules:
  0.0 262.1 jit_solution(7271696926352778854)
XLA Ops:
  0.6 4.9 %collective-permute-start.3 = (f32[128,256]{1,0:T(8,128)}, f32[128,256]{1,0:T(8,128)S(1)}, u32[]{:S(2)}, u32[]{:S(2)}) collective-permute-start(f32[128,256]{1,0:T(8,128)} %refs_0_), channel_id=1, source_target_pairs={{0,1},{3,2},{4,5},{7,6},{8,9},{11,10},{12,13},{15,14},{16,17},{19,... | collective-permute-start | bytes 393224 | tf_op jit(solution)/shard_map/ppermute | solution.py:409
  6.3 4.0 %collective-permute-start.5 = (f32[128,256]{1,0:T(8,128)}, f32[128,256]{1,0:T(8,128)S(1)}, u32[]{:S(2)}, u32[]{:S(2)}) collective-permute-start(f32[128,256]{1,0:T(8,128)} %refs_0_), channel_id=1, source_target_pairs={{0,2},{3,1},{4,6},{7,5},{8,10},{11,9},{12,14},{15,13},{16,18},{19,... | collective-permute-start | bytes 393224 | tf_op jit(solution)/shard_map/ppermute | solution.py:409
  11.6 4.2 %shard_map.68 = (f32[3,768,128]{2,1,0:T(8,128)}, f32[2,768,128]{2,1,0:T(8,128)}, f32[2,768,128]{2,1,0:T(8,128)}) custom-call(s32[20]{0:T(128)} %concatenate.9.s, f32[7,512,128]{2,1,0:T(8,128)} %bitcast.17, f32[7,128,512]{2,1,0:T(8,128)} %bitcast.18), custom_call_target="tpu_custom_call" | custom-call | flops 1000000000 | bytes 1 | tf_op jit(solution)/shard_map/pallas_call | solution.py:101
  16.6 2.7 %shard_map.69.refs_5_ = f32[128,1024]{1,0:T(8,128)} custom-call(s32[20]{0:T(128)} %concatenate.9.s, f32[128,256]{1,0:T(8,128)} %refs_0_, f32[128,256]{1,0:T(8,128)} %copy-done.30, f32[128,256]{1,0:T(8,128)} %copy-done.31, f32[128,256]{1,0:T(8,128)} %copy-done.32), custom_call_target="tpu_custom_call" | custom-call | flops 1000000000 | bytes 1 | tf_op jit(solution)/shard_map/pallas_call | solution.py:101
  21.6 9.1 %collective-permute-start = (f32[3,768,128]{2,1,0:T(8,128)S(1)}, f32[3,768,128]{2,1,0:T(8,128)S(1)}, u32[]{:S(2)}, u32[]{:S(2)}) collective-permute-start(f32[3,768,128]{2,1,0:T(8,128)S(1)} %copy-done), channel_id=1, source_target_pairs={{0,1},{3,2},{4,5},{7,6},{8,9},{11,10},{12,13},{15,14},{16,17},{19,... | collective-permute-start | bytes 3538952 | tf_op jit(solution)/shard_map/ppermute | solution.py:409
  31.5 3.9 %collective-permute-start.2 = (f32[3,768,128]{2,1,0:T(8,128)S(1)}, f32[3,768,128]{2,1,0:T(8,128)S(1)}, u32[]{:S(2)}, u32[]{:S(2)}) collective-permute-start(f32[3,768,128]{2,1,0:T(8,128)S(1)} %copy-done), channel_id=1, source_target_pairs={{0,2},{3,1},{4,6},{7,5},{8,10},{11,9},{12,14},{15,13},{16,18},{19,... | collective-permute-start | bytes 3538952 | tf_op jit(solution)/shard_map/ppermute | solution.py:409
  38.3 18.6 %collective-permute-done.refs_1_ = f32[3,768,128]{2,1,0:T(8,128)S(1)} collective-permute-done((f32[3,768,128]{2,1,0:T(8,128)S(1)}, f32[3,768,128]{2,1,0:T(8,128)S(1)}, u32[]{:S(2)}, u32[]{:S(2)}) %collective-permute-start) | collective-permute-done | bytes 1179680 | tf_op jit(solution)/shard_map/ppermute | solution.py:409
  57.0 24.3 %collective-permute-done.2.refs_3_ = f32[3,768,128]{2,1,0:T(8,128)S(1)} collective-permute-done((f32[3,768,128]{2,1,0:T(8,128)S(1)}, f32[3,768,128]{2,1,0:T(8,128)S(1)}, u32[]{:S(2)}, u32[]{:S(2)}) %collective-permute-start.2) | collective-permute-done | bytes 1179680 | tf_op jit(solution)/shard_map/ppermute | solution.py:409
  82.3 5.2 %shard_map.70 = f32[4,3,768,128]{3,2,1,0:T(8,128)} custom-call(s32[20]{0:T(128)} %concatenate.9.s, f32[3,768,128]{2,1,0:T(8,128)} %get-tuple-element.45.refs_0_, f32[3,768,128]{2,1,0:T(8,128)} %copy-done.1, f32[3,768,128]{2,1,0:T(8,128)} %copy-done.2, f32[3,768,128]{2,1,0:T(8,128)} %copy-done.3), custom_call_target="tpu_custom_call" | custom-call | flops 1000000000 | bytes 1 | tf_op jit(solution)/shard_map/pallas_call | solution.py:101
  88.5 7.7 %collective-permute-start.16 = (f32[2,768,128]{2,1,0:T(8,128)S(1)}, f32[2,768,128]{2,1,0:T(8,128)S(1)}, u32[]{:S(2)}, u32[]{:S(2)}) collective-permute-start(f32[2,768,128]{2,1,0:T(8,128)S(1)} %copy-done.5), channel_id=1, source_target_pairs={{0,1},{3,2},{4,5},{7,6},{8,9},{11,10},{12,13},{15,14},{16,17},{19,... | collective-permute-start | bytes 2359304 | tf_op jit(solution)/shard_map/ppermute | solution.py:409
  97.0 4.0 %collective-permute-start.18 = (f32[2,768,128]{2,1,0:T(8,128)S(1)}, f32[2,768,128]{2,1,0:T(8,128)S(1)}, u32[]{:S(2)}, u32[]{:S(2)}) collective-permute-start(f32[2,768,128]{2,1,0:T(8,128)S(1)} %copy-done.5), channel_id=1, source_target_pairs={{0,2},{3,1},{4,6},{7,5},{8,10},{11,9},{12,14},{15,13},{16,18},{19,... | collective-permute-start | bytes 2359304 | tf_op jit(solution)/shard_map/ppermute | solution.py:409
  101.0 2.2 copy-done.21
  103.1 17.3 %shard_map.71 = (f32[1536,512]{1,0:T(8,128)}, f32[2,512,512]{2,1,0:T(8,128)}, f32[1024,128]{1,0:T(8,128)}, f32[768,128]{1,0:T(8,128)}) custom-call(s32[20]{0:T(128)} %concatenate.9.s, f32[3,768,128]{2,1,0:T(8,128)} %get-tuple-element.45.refs_0_, f32[3,768,128]{2,1,0:T(8,128)} %copy-done.1, f32[3,768,128]{2,1,0:T(8,128)} %copy-done.2, ...), custom_call_target="tpu_custom_call" | custom-call | flops 10000000000 | bytes 1 | tf_op jit(solution)/shard_map/pallas_call | solution.py:101
  120.4 1.5 collective-permute-start.14
  121.9 30.2 %shard_map.72 = (f32[2,1024,512]{2,1,0:T(8,128)}, f32[2,1024,128]{2,1,0:T(8,128)}, f32[2,768,128]{2,1,0:T(8,128)}) custom-call(s32[20]{0:T(128)} %concatenate.9.s, f32[3,768,128]{2,1,0:T(8,128)} %get-tuple-element.45.refs_0_, f32[3,768,128]{2,1,0:T(8,128)} %copy-done.1, f32[3,768,128]{2,1,0:T(8,128)} %copy-done.2, f32[3,768,128]{2,1,0:T(8,128)} %copy-done.3, ...), custom_call_target="tpu_custom_call" | custom-call | flops 24999999488 | bytes 1 | tf_op jit(solution)/shard_map/pallas_call | solution.py:101
  153.6 3.3 %shard_map.73 = f32[4,768,128]{2,1,0:T(8,128)} custom-call(s32[20]{0:T(128)} %concatenate.9.s, f32[2,768,128]{2,1,0:T(8,128)} %get-tuple-element.58.refs_0_.x0, f32[2,768,128]{2,1,0:T(8,128)} %copy-done.6, f32[2,768,128]{2,1,0:T(8,128)} %copy-done.7, f32[2,768,128]{2,1,0:T(8,128)} %copy-done.8), custom_call_target="tpu_custom_call" | custom-call | flops 1000000000 | bytes 1 | tf_op jit(solution)/shard_map/pallas_call | solution.py:101
  156.9 1.9 collective-permute-start.19
  160.6 4.7 %collective-permute-start.23 = (f32[2,768,128]{2,1,0:T(8,128)S(1)}, f32[2,768,128]{2,1,0:T(8,128)S(1)}, u32[]{:S(2)}, u32[]{:S(2)}) collective-permute-start(f32[2,768,128]{2,1,0:T(8,128)S(1)} %copy-done.4), channel_id=1, source_target_pairs={{0,1},{3,2},{4,5},{7,6},{8,9},{11,10},{12,13},{15,14},{16,17},{19,... | collective-permute-start | bytes 2359304 | tf_op jit(solution)/shard_map/ppermute | solution.py:409
  166.1 4.0 %collective-permute-start.25 = (f32[2,768,128]{2,1,0:T(8,128)S(1)}, f32[2,768,128]{2,1,0:T(8,128)S(1)}, u32[]{:S(2)}, u32[]{:S(2)}) collective-permute-start(f32[2,768,128]{2,1,0:T(8,128)S(1)} %copy-done.4), channel_id=1, source_target_pairs={{0,2},{3,1},{4,6},{7,5},{8,10},{11,9},{12,14},{15,13},{16,18},{19,... | collective-permute-start | bytes 2359304 | tf_op jit(solution)/shard_map/ppermute | solution.py:409
  170.0 1.5 collective-permute-start.15
  171.5 10.5 %shard_map.74 = (f32[1024,128]{1,0:T(8,128)}, f32[1024,128]{1,0:T(8,128)}, f32[768,128]{1,0:T(8,128)}, f32[768,128]{1,0:T(8,128)}) custom-call(s32[12]{0:T(128)} %concatenate.10.s, f32[2,768,128]{2,1,0:T(8,128)} %get-tuple-element.58.refs_0_.x0, f32[2,768,128]{2,1,0:T(8,128)} %copy-done.6, f32[2,768,128]{2,1,0:T(8,128)} %copy-done.7, ...), custom_call_target="tpu_custom_call" | custom-call | flops 10000000000 | bytes 1 | tf_op jit(solution)/shard_map/pallas_call | solution.py:101
  182.1 1.3 collective-permute-start.20
  183.4 9.1 %collective-permute-done.15.upper.refs_3_ = f32[2,768,128]{2,1,0:T(8,128)S(1)} collective-permute-done((f32[2,768,128]{2,1,0:T(8,128)}, f32[2,768,128]{2,1,0:T(8,128)S(1)}, u32[]{:S(2)}, u32[]{:S(2)}) %collective-permute-start.15) | collective-permute-done | bytes 786464 | tf_op jit(solution)/shard_map/ppermute | solution.py:454
  193.9 5.8 %collective-permute-done.25.refs_3_.x3 = f32[2,768,128]{2,1,0:T(8,128)S(1)} collective-permute-done((f32[2,768,128]{2,1,0:T(8,128)S(1)}, f32[2,768,128]{2,1,0:T(8,128)S(1)}, u32[]{:S(2)}, u32[]{:S(2)}) %collective-permute-start.25) | collective-permute-done | bytes 786464 | tf_op jit(solution)/shard_map/ppermute | solution.py:409
  199.6 1.3 collective-permute-done.20.end.refs_5_
  201.0 6.4 %collective-permute-done.21.cross.refs_6_ = f32[768,128]{1,0:T(8,128)S(1)} collective-permute-done((f32[768,128]{1,0:T(8,128)}, f32[768,128]{1,0:T(8,128)S(1)}, u32[]{:S(2)}, u32[]{:S(2)}) %collective-permute-start.21) | collective-permute-done | bytes 393248 | tf_op jit(solution)/shard_map/ppermute | solution.py:473
  207.3 3.2 %shard_map.76 = f32[4,768,128]{2,1,0:T(8,128)} custom-call(s32[20]{0:T(128)} %concatenate.9.s, f32[2,768,128]{2,1,0:T(8,128)} %get-tuple-element.68.refs_0_.x0, f32[2,768,128]{2,1,0:T(8,128)} %copy-done.9, f32[2,768,128]{2,1,0:T(8,128)} %copy-done.10, f32[2,768,128]{2,1,0:T(8,128)} %copy-done.11), custom_call_target="tpu_custom_call" | custom-call | flops 1000000000 | bytes 1 | tf_op jit(solution)/shard_map/pallas_call | solution.py:101
  212.6 2.7 %shard_map.75 = f32[1280,128]{1,0:T(8,128)} custom-call(s32[20]{0:T(128)} %concatenate.9.s, f32[768,128]{1,0:T(8,128)} %copy-done.17, f32[2,768,128]{2,1,0:T(8,128)} %copy-done.12, f32[768,128]{1,0:T(8,128)} %copy-done.18, f32[768,128]{1,0:T(8,128)} %copy-done.19, f32[1024,128]{1,0:T(8,128)} %get-tuple-element.65.core), custom_call_target="tpu_custom_call" | custom-call | flops 1000000000 | bytes 1 | tf_op jit(solution)/shard_map/pallas_call | solution.py:101
  217.4 10.6 %shard_map.77 = (f32[1024,128]{1,0:T(8,128)}, f32[1024,128]{1,0:T(8,128)}, f32[1024,128]{1,0:T(8,128)}, f32[1024,128]{1,0:T(8,128)}) custom-call(s32[12]{0:T(128)} %concatenate.11.s, f32[2,768,128]{2,1,0:T(8,128)} %get-tuple-element.68.refs_0_.x0, f32[2,768,128]{2,1,0:T(8,128)} %copy-done.9, f32[2,768,128]{2,1,0:T(8,128)} %copy-done.10, ...), custom_call_target="tpu_custom_call" | custom-call | flops 10000000000 | bytes 1 | tf_op jit(solution)/shard_map/pallas_call | solution.py:101
  231.4 14.3 %collective-permute-done.28.refs_10_ = f32[1024,128]{1,0:T(8,128)S(1)} collective-permute-done((f32[1024,128]{1,0:T(8,128)}, f32[1024,128]{1,0:T(8,128)S(1)}, u32[]{:S(2)}, u32[]{:S(2)}) %collective-permute-start.28) | collective-permute-done | bytes 524320 | tf_op jit(solution)/shard_map/ppermute | solution.py:473
  245.6 10.7 %collective-permute-done.29.refs_11_ = f32[1024,128]{1,0:T(8,128)S(1)} collective-permute-done((f32[1024,128]{1,0:T(8,128)}, f32[1024,128]{1,0:T(8,128)S(1)}, u32[]{:S(2)}, u32[]{:S(2)}) %collective-permute-start.29) | collective-permute-done | bytes 524320 | tf_op jit(solution)/shard_map/ppermute | solution.py:473
  257.2 4.7 %shard_map.78 = (f32[7,512,128]{2,1,0:T(8,128)}, f32[7,512,128]{2,1,0:T(8,128)}) custom-call(s32[20]{0:T(128)} %concatenate.9.s, f32[1024,128]{1,0:T(8,128)} %get-tuple-element.49.refs_0_, f32[768,128]{1,0:T(8,128)} %copy-done.17, f32[2,1024,128]{2,1,0:T(8,128)} %get-tuple-element.53.refs_2_, f32[2,768,128]{2,1,0:T(8,128)} %copy-done.12, ...), custom_call_target="tpu_custom_call" | custom-call | flops 1000000000 | bytes 1 | tf_op jit(solution)/shard_map/pallas_call | solution.py:101
  (110 shorter events, 24.7 us)
Async XLA Ops:
  0.6 15.2 %collective-permute-start.3 = (f32[128,256]{1,0:T(8,128)}, f32[128,256]{1,0:T(8,128)S(1)}, u32[]{:S(2)}, u32[]{:S(2)}) collective-permute-start(f32[128,256]{1,0:T(8,128)} %refs_0_), channel_id=1, source_target_pairs={{0,1},{3,2},{4,5},{7,6},{8,9},{11,10},{12,13},{15,14},{16,17},{19,... | collective-permute-start | bytes 393224 | tf_op jit(solution)/shard_map/ppermute | solution.py:409
  5.6 10.3 %collective-permute-start.4 = (f32[128,256]{1,0:T(8,128)}, f32[128,256]{1,0:T(8,128)S(1)}, u32[]{:S(2)}, u32[]{:S(2)}) collective-permute-start(f32[128,256]{1,0:T(8,128)} %refs_0_), channel_id=1, source_target_pairs={{1,2},{2,1},{5,6},{6,5},{9,10},{10,9},{13,14},{14,13},{17,18},{18,... | collective-permute-start | bytes 393224 | tf_op jit(solution)/shard_map/ppermute | solution.py:409
  6.3 9.7 %collective-permute-start.5 = (f32[128,256]{1,0:T(8,128)}, f32[128,256]{1,0:T(8,128)S(1)}, u32[]{:S(2)}, u32[]{:S(2)}) collective-permute-start(f32[128,256]{1,0:T(8,128)} %refs_0_), channel_id=1, source_target_pairs={{0,2},{3,1},{4,6},{7,5},{8,10},{11,9},{12,14},{15,13},{16,18},{19,... | collective-permute-start | bytes 393224 | tf_op jit(solution)/shard_map/ppermute | solution.py:409
  19.4 69.2 %copy-start.5 = (f32[2,768,128]{2,1,0:T(8,128)S(1)}, f32[2,768,128]{2,1,0:T(8,128)}, u32[]{:S(2)}) copy-start(f32[2,768,128]{2,1,0:T(8,128)} %get-tuple-element.58.refs_0_.x0) | copy-start | bytes 2359300
  19.4 12.1 %collective-permute-start.6 = (f32[128,1024]{1,0:T(8,128)}, f32[128,1024]{1,0:T(8,128)S(1)}, u32[]{:S(2)}, u32[]{:S(2)}) collective-permute-start(f32[128,1024]{1,0:T(8,128)} %shard_map.69.refs_5_), channel_id=1, source_target_pairs={{1,5},{2,6},{5,1},{6,2},{9,13},{10,14},{13,9},{14,10},{17,21},{18,... | collective-permute-start | bytes 1572872 | tf_op jit(solution)/shard_map/ppermute | solution.py:412
  20.2 15.2 %collective-permute-start.7 = (f32[128,1024]{1,0:T(8,128)}, f32[128,1024]{1,0:T(8,128)S(1)}, u32[]{:S(2)}, u32[]{:S(2)}) collective-permute-start(f32[128,1024]{1,0:T(8,128)} %shard_map.69.refs_5_), channel_id=1, source_target_pairs={{1,9},{2,10},{5,13},{6,14},{9,1},{10,2},{13,5},{14,6},{17,25},{18,... | collective-permute-start | bytes 1572872 | tf_op jit(solution)/shard_map/ppermute | solution.py:428
  20.9 15.2 %collective-permute-start.9 = (f32[128,1024]{1,0:T(8,128)}, f32[128,1024]{1,0:T(8,128)S(1)}, u32[]{:S(2)}, u32[]{:S(2)}) collective-permute-start(f32[128,1024]{1,0:T(8,128)} %shard_map.69.refs_5_), channel_id=1, source_target_pairs={{1,17},{2,18},{5,21},{6,22},{9,25},{10,26},{13,29},{14,30},{17,1},... | collective-permute-start | bytes 1572872 | tf_op jit(solution)/shard_map/ppermute | solution.py:428
  21.6 35.4 %collective-permute-start = (f32[3,768,128]{2,1,0:T(8,128)S(1)}, f32[3,768,128]{2,1,0:T(8,128)S(1)}, u32[]{:S(2)}, u32[]{:S(2)}) collective-permute-start(f32[3,768,128]{2,1,0:T(8,128)S(1)} %copy-done), channel_id=1, source_target_pairs={{0,1},{3,2},{4,5},{7,6},{8,9},{11,10},{12,13},{15,14},{16,17},{19,... | collective-permute-start | bytes 3538952 | tf_op jit(solution)/shard_map/ppermute | solution.py:409
  30.7 26.3 %collective-permute-start.1 = (f32[3,768,128]{2,1,0:T(8,128)S(1)}, f32[3,768,128]{2,1,0:T(8,128)S(1)}, u32[]{:S(2)}, u32[]{:S(2)}) collective-permute-start(f32[3,768,128]{2,1,0:T(8,128)S(1)} %copy-done), channel_id=1, source_target_pairs={{1,2},{2,1},{5,6},{6,5},{9,10},{10,9},{13,14},{14,13},{17,18},{18,... | collective-permute-start | bytes 3538952 | tf_op jit(solution)/shard_map/ppermute | solution.py:409
  31.5 57.0 %copy-start.23 = (f32[128,1024]{1,0:T(8,128)}, f32[128,1024]{1,0:T(8,128)S(1)}, u32[]{:S(2)}) copy-start(f32[128,1024]{1,0:T(8,128)S(1)} %collective-permute-done.6.refs_9_) | copy-start | bytes 1572868
  31.5 49.8 %collective-permute-start.2 = (f32[3,768,128]{2,1,0:T(8,128)S(1)}, f32[3,768,128]{2,1,0:T(8,128)S(1)}, u32[]{:S(2)}, u32[]{:S(2)}) collective-permute-start(f32[3,768,128]{2,1,0:T(8,128)S(1)} %copy-done), channel_id=1, source_target_pairs={{0,2},{3,1},{4,6},{7,5},{8,10},{11,9},{12,14},{15,13},{16,18},{19,... | collective-permute-start | bytes 3538952 | tf_op jit(solution)/shard_map/ppermute | solution.py:409
  35.4 1.4 collective-permute-start.11
  36.2 1.4 collective-permute-start.8
  36.9 1.4 collective-permute-start.10
  37.6 0.7 collective-permute-start.12
  87.5 13.4 %collective-permute-start.13 = (f32[4,3,768,128]{3,2,1,0:T(8,128)}, f32[4,3,768,128]{3,2,1,0:T(8,128)S(1)}, u32[]{:S(2)}, u32[]{:S(2)}) collective-permute-start(f32[4,3,768,128]{3,2,1,0:T(8,128)} %shard_map.70), channel_id=1, source_target_pairs={{1,5},{2,6},{5,1},{6,2},{9,13},{10,14},{13,9},{14,10},{17,21},{18,... | collective-permute-start | bytes 14155784 | tf_op jit(solution)/shard_map/ppermute | solution.py:412
  88.5 63.6 %collective-permute-start.16 = (f32[2,768,128]{2,1,0:T(8,128)S(1)}, f32[2,768,128]{2,1,0:T(8,128)S(1)}, u32[]{:S(2)}, u32[]{:S(2)}) collective-permute-start(f32[2,768,128]{2,1,0:T(8,128)S(1)} %copy-done.5), channel_id=1, source_target_pairs={{0,1},{3,2},{4,5},{7,6},{8,9},{11,10},{12,13},{15,14},{16,17},{19,... | collective-permute-start | bytes 2359304 | tf_op jit(solution)/shard_map/ppermute | solution.py:409
  96.3 55.9 %collective-permute-start.17 = (f32[2,768,128]{2,1,0:T(8,128)S(1)}, f32[2,768,128]{2,1,0:T(8,128)S(1)}, u32[]{:S(2)}, u32[]{:S(2)}) collective-permute-start(f32[2,768,128]{2,1,0:T(8,128)S(1)} %copy-done.5), channel_id=1, source_target_pairs={{1,2},{2,1},{5,6},{6,5},{9,10},{10,9},{13,14},{14,13},{17,18},{18,... | collective-permute-start | bytes 2359304 | tf_op jit(solution)/shard_map/ppermute | solution.py:409
  97.0 55.2 %collective-permute-start.18 = (f32[2,768,128]{2,1,0:T(8,128)S(1)}, f32[2,768,128]{2,1,0:T(8,128)S(1)}, u32[]{:S(2)}, u32[]{:S(2)}) collective-permute-start(f32[2,768,128]{2,1,0:T(8,128)S(1)} %copy-done.5), channel_id=1, source_target_pairs={{0,2},{3,1},{4,6},{7,5},{8,10},{11,9},{12,14},{15,13},{16,18},{19,... | collective-permute-start | bytes 2359304 | tf_op jit(solution)/shard_map/ppermute | solution.py:409
  120.4 31.8 %collective-permute-start.14 = (f32[768,128]{1,0:T(8,128)}, f32[768,128]{1,0:T(8,128)S(1)}, u32[]{:S(2)}, u32[]{:S(2)}) collective-permute-start(f32[768,128]{1,0:T(8,128)} %get-tuple-element.50), channel_id=1, source_target_pairs={{1,0},{2,3},{5,4},{6,7},{9,8},{10,11},{13,12},{14,15},{17,16},{18,... | collective-permute-start | bytes 1179656 | tf_op jit(solution)/shard_map/ppermute | solution.py:443
  156.9 14.6 %collective-permute-start.19 = (f32[4,768,128]{2,1,0:T(8,128)}, f32[4,768,128]{2,1,0:T(8,128)}, u32[]{:S(2)}, u32[]{:S(2)}) collective-permute-start(f32[4,768,128]{2,1,0:T(8,128)} %shard_map.73), channel_id=1, source_target_pairs={{1,5},{2,6},{5,1},{6,2},{9,13},{10,14},{13,9},{14,10},{17,21},{18,... | collective-permute-start | bytes 4718600 | tf_op jit(solution)/shard_map/ppermute | solution.py:412
  160.6 33.2 %collective-permute-start.23 = (f32[2,768,128]{2,1,0:T(8,128)S(1)}, f32[2,768,128]{2,1,0:T(8,128)S(1)}, u32[]{:S(2)}, u32[]{:S(2)}) collective-permute-start(f32[2,768,128]{2,1,0:T(8,128)S(1)} %copy-done.4), channel_id=1, source_target_pairs={{0,1},{3,2},{4,5},{7,6},{8,9},{11,10},{12,13},{15,14},{16,17},{19,... | collective-permute-start | bytes 2359304 | tf_op jit(solution)/shard_map/ppermute | solution.py:409
  165.3 28.5 %collective-permute-start.24 = (f32[2,768,128]{2,1,0:T(8,128)S(1)}, f32[2,768,128]{2,1,0:T(8,128)S(1)}, u32[]{:S(2)}, u32[]{:S(2)}) collective-permute-start(f32[2,768,128]{2,1,0:T(8,128)S(1)} %copy-done.4), channel_id=1, source_target_pairs={{1,2},{2,1},{5,6},{6,5},{9,10},{10,9},{13,14},{14,13},{17,18},{18,... | collective-permute-start | bytes 2359304 | tf_op jit(solution)/shard_map/ppermute | solution.py:409
  166.1 33.6 %collective-permute-start.25 = (f32[2,768,128]{2,1,0:T(8,128)S(1)}, f32[2,768,128]{2,1,0:T(8,128)S(1)}, u32[]{:S(2)}, u32[]{:S(2)}) collective-permute-start(f32[2,768,128]{2,1,0:T(8,128)S(1)} %copy-done.4), channel_id=1, source_target_pairs={{0,2},{3,1},{4,6},{7,5},{8,10},{11,9},{12,14},{15,13},{16,18},{19,... | collective-permute-start | bytes 2359304 | tf_op jit(solution)/shard_map/ppermute | solution.py:409
  170.0 22.5 %collective-permute-start.15 = (f32[2,768,128]{2,1,0:T(8,128)}, f32[2,768,128]{2,1,0:T(8,128)S(1)}, u32[]{:S(2)}, u32[]{:S(2)}) collective-permute-start(f32[2,768,128]{2,1,0:T(8,128)} %get-tuple-element.54), channel_id=1, source_target_pairs={{1,0},{2,3},{5,4},{6,7},{9,8},{10,11},{13,12},{14,15},{17,16},{18,... | collective-permute-start | bytes 2359304 | tf_op jit(solution)/shard_map/ppermute | solution.py:454
  182.1 18.9 %collective-permute-start.20 = (f32[768,128]{1,0:T(8,128)}, f32[768,128]{1,0:T(8,128)S(1)}, u32[]{:S(2)}, u32[]{:S(2)}) collective-permute-start(f32[768,128]{1,0:T(8,128)} %get-tuple-element.63), channel_id=1, source_target_pairs={{1,0},{2,3},{5,4},{6,7},{9,8},{10,11},{13,12},{14,15},{17,16},{18,... | collective-permute-start | bytes 1179656 | tf_op jit(solution)/shard_map/ppermute | solution.py:473
  192.5 14.8 %collective-permute-start.21 = (f32[768,128]{1,0:T(8,128)}, f32[768,128]{1,0:T(8,128)S(1)}, u32[]{:S(2)}, u32[]{:S(2)}) collective-permute-start(f32[768,128]{1,0:T(8,128)} %get-tuple-element.64), channel_id=1, source_target_pairs={{1,4},{2,7},{5,0},{6,3},{9,12},{10,15},{13,8},{14,11},{17,20},{18,... | collective-permute-start | bytes 1179656 | tf_op jit(solution)/shard_map/ppermute | solution.py:473
  210.6 5.7 %collective-permute-start.26 = (f32[4,768,128]{2,1,0:T(8,128)}, f32[4,768,128]{2,1,0:T(8,128)S(1)}, u32[]{:S(2)}, u32[]{:S(2)}) collective-permute-start(f32[4,768,128]{2,1,0:T(8,128)} %shard_map.76), channel_id=1, source_target_pairs={{1,5},{2,6},{5,1},{6,2},{9,13},{10,14},{13,9},{14,10},{17,21},{18,... | collective-permute-start | bytes 4718600 | tf_op jit(solution)/shard_map/ppermute | solution.py:412
  215.3 16.0 %collective-permute-start.22 = (f32[1280,128]{1,0:T(8,128)}, f32[1280,128]{1,0:T(8,128)S(1)}, u32[]{:S(2)}, u32[]{:S(2)}) collective-permute-start(f32[1280,128]{1,0:T(8,128)} %shard_map.75), channel_id=1, source_target_pairs={{0,4},{1,5},{2,6},{3,7},{4,0},{5,1},{6,2},{7,3},{8,12},{9,13},{10,... | collective-permute-start | bytes 1966088 | tf_op jit(solution)/shard_map/ppermute | solution.py:479
  228.0 3.3 %collective-permute-start.27 = (f32[1024,128]{1,0:T(8,128)}, f32[1024,128]{1,0:T(8,128)S(1)}, u32[]{:S(2)}, u32[]{:S(2)}) collective-permute-start(f32[1024,128]{1,0:T(8,128)} %get-tuple-element.73), channel_id=1, source_target_pairs={{1,5},{2,6},{5,1},{6,2},{9,13},{10,14},{13,9},{14,10},{17,21},{18,... | collective-permute-start | bytes 1572872 | tf_op jit(solution)/shard_map/ppermute | solution.py:412
  228.7 16.9 %collective-permute-start.28 = (f32[1024,128]{1,0:T(8,128)}, f32[1024,128]{1,0:T(8,128)S(1)}, u32[]{:S(2)}, u32[]{:S(2)}) collective-permute-start(f32[1024,128]{1,0:T(8,128)} %get-tuple-element.74), channel_id=1, source_target_pairs={{1,0},{2,3},{5,4},{6,7},{9,8},{10,11},{13,12},{14,15},{17,16},{18,... | collective-permute-start | bytes 1572872 | tf_op jit(solution)/shard_map/ppermute | solution.py:473
  230.0 26.3 %collective-permute-start.29 = (f32[1024,128]{1,0:T(8,128)}, f32[1024,128]{1,0:T(8,128)S(1)}, u32[]{:S(2)}, u32[]{:S(2)}) collective-permute-start(f32[1024,128]{1,0:T(8,128)} %get-tuple-element.75), channel_id=1, source_target_pairs={{1,4},{2,7},{5,0},{6,3},{9,12},{10,15},{13,8},{14,11},{17,20},{18,... | collective-permute-start | bytes 1572872 | tf_op jit(solution)/shard_map/ppermute | solution.py:473
  (31 other events, 414.0 us)

commit v5 on v3

--- a/solution.py
+++ b/solution.py
@@ -122,7 +122,7 @@
     )
 
 
-LIST = 4
+LINKS, LIST = 4, 8
 
 
 def tail_of(s, start, own, order):
@@ -130,15 +130,15 @@
     return [jnp.maximum(s[k], 0) for k in spots], [(s[k] >= 0).astype(F32) for k in spots]
 
 
-def weights_of(s, order):
-    return [(s[LIST + j] >= 0).astype(F32) for j in range(order // TILE)]
-
-
-def pack_kernel(s, panels, inverse, *rest):
+def weights_of(s, start, order):
+    return [(s[start + j] >= 0).astype(F32) for j in range(order // TILE)]
+
+
+def pack_kernel(first, s, panels, inverse, *rest):
     outs, sems = rest[:-1], rest[-1]
     half = panels.shape[1]
     copies = []
-    node = 0
+    node = first
     for out in outs:
         for i in range(out.shape[0]):
             copies.append((panels.at[node], out.at[i, pl.ds(0, half)]))
@@ -151,6 +151,21 @@
     copy_all(copies, sems)
 
 
+def leaf_pack_kernel(s, panels, inverse, pair, every, last, sems):
+    half = panels.shape[1]
+    targets = [(3 + k, pair.at[k]) for k in range(2)] + [(3 + k, every.at[k]) for k in range(4)]
+    targets += [(5 + k, last.at[k]) for k in range(2)]
+    copies = []
+    for node, out in targets:
+        copies.append((panels.at[node], out.at[pl.ds(0, half)]))
+        for j in range(inverse.shape[2] // TILE):
+            copies.append((
+                inverse.at[node, at(s[0] * QUARTER, QUARTER, QUARTER), pl.ds(j * TILE, TILE)],
+                out.at[pl.ds(half + j * QUARTER, QUARTER)],
+            ))
+    copy_all(copies, sems)
+
+
 def join_columns_kernel(s, *refs):
     out, sems = refs[-2:]
     width = refs[0].shape[1]
@@ -162,9 +177,9 @@
     copy_all([(ref, out.at[k]) for k, ref in enumerate(refs[:-2])], sems)
 
 
-def swap_kernel(s, *refs):
+def swap_kernel(skips, s, *refs):
     out, sems = refs[-2:]
-    copy_all([(ref.at[1 - s[0]], out.at[k]) for k, ref in enumerate(refs[:-2])], sems)
+    copy_all([(ref.at[skips[k] + 1 - s[0]], out.at[k]) for k, ref in enumerate(refs[:-2])], sems)
 
 
 def join_block(a, own, corner, rows_of, top, index, weight):
@@ -264,24 +279,25 @@
                 lambda i: root_ab[at(index[i] * TILE, TILE), :], grand[...], index, weight,
             )
 
-        weights = [(s[start + k] >= 0).astype(F32) for k in range(order // TILE)]
-        solve(p, pt, dt, a, d, f, w, t, weights, emit_ab, emit_dg, join)
+        solve(p, pt, dt, a, d, f, w, t, weights_of(s, start, order), emit_ab, emit_dg, join)
         columns_out(node)
         ext[node - 1, 0:half, :] = ab[0:half, :]
         ext[node - 1, half:, :] = dg[...]
 
 
-def leaf_kernel(s, x0, x1, x2, x3, ex, ext, grand, self_out, core_out, end_out, cross_out, *rest):
+def leaf_kernel(first, skips, s, x0, x1, x2, x3, ex, ext, grand, self_out, core_out, end_out, cross_out, *rest):
     stage, sems, tails, top, grand_in, ab, dg = rest[:7]
     p, d, a, dc, f, w, t, pt, dt = pairs(rest[7:])
     r, c = s[0], s[1]
-    blocks = [x for k, ref in enumerate((x0, x1, x2, x3)) for x in (ref.at[r], ex.at[k])]
+    blocks = [x for k, ref in enumerate((x0, x1, x2, x3)) for x in (ref.at[skips[k] + r], ex.at[k])]
     order = a[0].shape[0]
     own = d[0].shape[0]
     half = order // 2
     far = c // 2
-    index, weight = tail_of(s, LIST, own, order)
-    parent = s[3] - 1
+    node = first + r
+    start = LIST + (node - 1) * (order // TILE)
+    index, weight = tail_of(s, start, own, order)
+    parent = s[LINKS + node - 3] - 1
     copies = [pltpu.make_async_copy(ref, stage.at[k], sems.at[k]) for k, ref in enumerate(blocks)]
     later = [
         pltpu.make_async_copy(ext.at[parent, pl.ds(half, own)], top, sems.at[8]),
@@ -311,7 +327,7 @@
     def emit_dg(rows, cols, value):
         dg[rows, cols] = value
 
-    solve(p, pt, dt, a, dc, f, w, t, weights_of(s, order), emit_ab, emit_dg, join)
+    solve(p, pt, dt, a, dc, f, w, t, weights_of(s, start, order), emit_ab, emit_dg, join)
     near_cols, end_cols = at((1 - far) * TILE, TILE), at(far * TILE, TILE)
     for out, side, cols in (
         (self_out, r, near_cols), (core_out, 1 - r, near_cols), (end_out, r, end_cols), (cross_out, 1 - r, end_cols)
@@ -402,26 +418,35 @@
     def swapped(x):
         return lax.ppermute(x, both, swap)
 
-    def scalars(parent, *rows):
-        head = jnp.stack([r, c, leaf, parent]).astype(jnp.int32)
-        return jnp.concatenate([head] + [lists[row] for row in rows])
-
+    here = jnp.concatenate([jnp.stack([r, c, leaf, jnp.int32(0)]).astype(jnp.int32), links, lists.reshape(-1)])
     trunk = 3
-    here = scalars(jnp.int32(0), 0, 1)
     packed = half + own // 2
+
+    def pack(first, *counts):
+        return move(
+            functools.partial(pack_kernel, first), here, [panels, inverse], [(k, packed, TILE) for k in counts],
+            5 * sum(counts),
+        )
+
+    def pack_leaves(sources):
+        return move(leaf_pack_kernel, here, sources, [(k, packed, TILE) for k in (2, 4, 2)], 40)
+
     sigma_parts = straight(sigma_top)
-    pack_t, pack_34, pack_56 = move(
-        pack_kernel, here, [panels, inverse], [(k, packed, TILE) for k in (trunk, 2, 2)], 35
-    )
+    pack_t = pack(0, trunk)[0]
     blocks_t = straight(pack_t)
     sigma_cols = move(join_columns_kernel, here, after(sigma_parts, pack_t), [(TILE, order)], 4)[0]
     sigma_rows = [sigma_cols] + [
         lax.ppermute(sigma_cols, ("leaf", "row", "col"), leaf_routes[m]) for m in range(1, 4)
     ]
-    sigma_other = swapped(move(stack_kernel, here, sigma_rows, [(4, TILE, order)], 4)[0])
-    gathered = after(blocks_t, sigma_rows[1:])
+    sigma_mine = move(stack_kernel, here, sigma_rows, [(4, TILE, order)], 4)[0]
+    sigma_other = swapped(sigma_mine)
+    pack_34, pack_all, pack_56 = pack_leaves(after((panels, inverse), pack_t))
+    gathered = after(blocks_t, (sigma_mine, pack_34))
     other_t = swapped(move(stack_kernel, here, gathered, [(4, trunk, packed, TILE)], 4)[0])
-    blocks_34 = straight(after(pack_34, blocks_t[1:]))
+    pack_34, pack_all = after((pack_34, pack_all), blocks_t[1:])
+    near, between, far = routes
+    across = lax.ppermute(pack_all, "col", between)
+    blocks_34 = [pack_34, lax.ppermute(pack_34, "col", near), across, lax.ppermute(pack_34, "col", far)]
     ext, grand, upper_self, upper_end = call(
         trunk_kernel, here, blocks_t + [other_t] + sigma_rows + [sigma_other],
         [(2, half + own, own), (own, own), (trunk, half + own, TILE), (trunk, packed, TILE)],
@@ -433,7 +458,8 @@
         ) + [pltpu.VMEM((order, own), F32)],
         [ANY] * 10, micros=60,
     )
-    blocks_56 = straight(after(pack_56, (blocks_34[1:], ext)))
+    last = after(pack_56, ext)
+    blocks_56 = [pack_56, lax.ppermute(last, "col", near), across, lax.ppermute(last, "col", far)]
     upper_home = lax.ppermute(upper_end, "col", home)
     tails = (order - own) // TILE
     leaf_scratch = [
@@ -445,22 +471,21 @@
         (own, own),
     )
 
-    def leaves(blocks, first, earlier, end_rows):
-        node = first + r
-        parent = lax.dynamic_index_in_dim(links, node - 3, 0, keepdims=False)
-        theirs = swapped(move(swap_kernel, here, after(blocks, earlier), [(4, packed, TILE)], 4)[0])
+    def leaves(blocks, first, skips, earlier, end_rows):
+        chosen = after(blocks, earlier)
+        theirs = swapped(move(functools.partial(swap_kernel, skips), here, chosen, [(4, packed, TILE)], 4)[0])
         self_out, core_out, end_out, cross_out = call(
-            leaf_kernel, scalars(parent, node - 1), blocks + [theirs, ext, grand],
+            functools.partial(leaf_kernel, first, skips), here, blocks + [theirs, ext, grand],
             [(half + own, TILE)] * 2 + [(end_rows, TILE)] * 2, leaf_scratch, [ANY] * 7, micros=10,
         )
         return self_out, core_out, lax.ppermute(end_out, "col", home), lax.ppermute(cross_out, both, home_cross)
 
-    self_34, core_34, end_34, cross_34 = leaves(blocks_34, 3, ext, packed)
+    self_34, core_34, end_34, cross_34 = leaves(blocks_34, 3, (0, 0, 0, 0), ext, packed)
+    self_56, core_56, end_56, cross_56 = leaves(blocks_56, 5, (0, 0, 2, 0), (upper_home, self_34), half + own)
     shares = move(
-        shares_kernel, here, [upper_home, end_34, cross_34, core_34], [((trunk + 2) * (own // 2), TILE)], trunk + 2
+        shares_kernel, here, after([upper_home, end_34, cross_34, core_34], self_56), [((trunk + 2) * (own // 2), TILE)], trunk + 2
     )[0]
     shares = lax.ppermute(shares, both, swap_all)
-    self_56, core_56, end_56, cross_56 = leaves(blocks_56, 5, (upper_home, end_34, cross_34), half + own)
     count = panels.shape[0]
     ancestor_block, diagonal_block = move(
         output_kernel, here,

time: 243 us -> 250 us (1.029)
  starting transfers between devices: 49.9 us -> 61 us
  waiting for transfers between devices: 96.9 us -> 86.6 us
  Pallas kernels: 82.3 us -> 86.2 us
    ppermute x0 -> x5, starting transfers between devices: none -> 30.8 us  [the longest x1 20.4 us: chip_body(): lax.ppermute(last, 'col', near)]
    ppermute x12 -> x6, waiting for transfers between devices: 56.1 us -> 30 us  [straight(): return [x] + [lax.ppermute(x, 'col', route) for route in routes]]
    ppermute x0 -> x5, waiting for transfers between devices: none -> 22.5 us  [the longest x1 16.5 us: chip_body(): lax.ppermute(last, 'col', far)]
    ppermute x12 -> x6, starting transfers between devices: 33 us -> 15.7 us  [straight(): return [x] + [lax.ppermute(x, 'col', route) for route in routes]]
    ppermute x2, waiting for transfers between devices: 22.7 us -> 15.9 us  [leaves(): lax.ppermute(end_out, 'col', home)]
    unnamed x54 -> x66, local copies, waits for them, and re-layouts: 7.11 us -> 11.8 us
    pallas_call x11 -> x12, Pallas kernels: 82.3 us -> 86.2 us  [call(): pl.pallas_call(kernel, out_shape=[jax.ShapeDtypeStruct(o, F32) for o in o...]
  transfers between devices with their start and end apart: 26 -> 25, of which waited for: 9 -> 8; matrix products, arithmetic and copies ran while one was open for 2% -> 1% of each run, Pallas kernels for 27% -> 27%
where the time goes in v5:
time: 250 us; the launch traced here: 249 us
  waiting for transfers between devices  86.6 us (35%)
  Pallas kernels  86.2 us (34%)
  starting transfers between devices  61 us (24%)
  local copies, waits for them, and re-layouts  13.1 us (5%)
    pallas_call x12, Pallas kernels, call(): pl.pallas_call(kernel, out_shape=[jax.ShapeDtypeStruct(o, F32) for o in o...  86.2 us
    ppermute x6, waiting for transfers between devices, straight(): return [x] + [lax.ppermute(x, 'col', route) for route in routes]  30 us
    ppermute x1, starting transfers between devices, chip_body(): lax.ppermute(last, 'col', near)  20.4 us
    ppermute x2, waiting for transfers between devices, leaves(): lax.ppermute(cross_out, both, home_cross)  18.2 us
    ppermute x1, waiting for transfers between devices, chip_body(): lax.ppermute(last, 'col', far)  16.5 us
    ppermute x2, waiting for transfers between devices, leaves(): lax.ppermute(end_out, 'col', home)  15.9 us
    ppermute x6, starting transfers between devices, straight(): return [x] + [lax.ppermute(x, 'col', route) for route in routes]  15.7 us
    unnamed x66, local copies, waits for them, and re-layouts  11.8 us
  transfers between devices with their start and end apart: 25, of which 8 were waited for; matrix products, arithmetic and copies ran while one was open for 1% of the time, Pallas kernels for 27%

profile of v5, /device:TPU:0, one launch (start us, length us, event | category | flops | bytes accessed | tf_op | source)
XLA Modules:
  0.0 249.1 jit_solution(823153591630109986)
XLA Ops:
  0.6 4.9 %collective-permute-start.3 = (f32[128,256]{1,0:T(8,128)}, f32[128,256]{1,0:T(8,128)S(1)}, u32[]{:S(2)}, u32[]{:S(2)}) collective-permute-start(f32[128,256]{1,0:T(8,128)} %refs_0_), channel_id=1, source_target_pairs={{0,1},{3,2},{4,5},{7,6},{8,9},{11,10},{12,13},{15,14},{16,17},{19,... | collective-permute-start | bytes 393224 | tf_op jit(solution)/shard_map/ppermute | solution.py:416
  6.3 4.0 %collective-permute-start.5 = (f32[128,256]{1,0:T(8,128)}, f32[128,256]{1,0:T(8,128)S(1)}, u32[]{:S(2)}, u32[]{:S(2)}) collective-permute-start(f32[128,256]{1,0:T(8,128)} %refs_0_), channel_id=1, source_target_pairs={{0,2},{3,1},{4,6},{7,5},{8,10},{11,9},{12,14},{15,13},{16,18},{19,... | collective-permute-start | bytes 393224 | tf_op jit(solution)/shard_map/ppermute | solution.py:416
  12.3 3.1 %shard_map.68.refs_0_ = f32[3,768,128]{2,1,0:T(8,128)} custom-call(s32[56]{0:T(128)} %concatenate.3.s, f32[7,512,128]{2,1,0:T(8,128)} %bitcast.8, f32[7,128,512]{2,1,0:T(8,128)} %bitcast.10), custom_call_target="tpu_custom_call" | custom-call | flops 1000000000 | bytes 1 | tf_op jit(solution)/shard_map/pallas_call | solution.py:100
  15.4 1.5 collective-permute-start
  17.6 3.9 %collective-permute-start.2 = (f32[3,768,128]{2,1,0:T(8,128)}, f32[3,768,128]{2,1,0:T(8,128)S(1)}, u32[]{:S(2)}, u32[]{:S(2)}) collective-permute-start(f32[3,768,128]{2,1,0:T(8,128)} %shard_map.68.refs_0_), channel_id=1, source_target_pairs={{0,2},{3,1},{4,6},{7,5},{8,10},{11,9},{12,14},{15,13},{16,18},{19,... | collective-permute-start | bytes 3538952 | tf_op jit(solution)/shard_map/ppermute | solution.py:416
  22.9 2.6 %shard_map.69.refs_0_.refs_5_ = f32[128,1024]{1,0:T(8,128)} custom-call(s32[56]{0:T(128)} %concatenate.3.s, f32[128,256]{1,0:T(8,128)} %refs_0_, f32[128,256]{1,0:T(8,128)} %copy-done.30, f32[128,256]{1,0:T(8,128)} %copy-done.31, f32[128,256]{1,0:T(8,128)} %copy-done.32), custom_call_target="tpu_custom_call" | custom-call | flops 1000000000 | bytes 1 | tf_op jit(solution)/shard_map/pallas_call | solution.py:100
  27.6 4.5 %shard_map.71 = (f32[2,768,128]{2,1,0:T(8,128)}, f32[4,768,128]{2,1,0:T(8,128)}, f32[2,768,128]{2,1,0:T(8,128)}) custom-call(s32[56]{0:T(128)} %concatenate.3.s, f32[7,512,128]{2,1,0:T(8,128)} %bitcast.9, f32[7,128,512]{2,1,0:T(8,128)} %bitcast.11), custom_call_target="tpu_custom_call" | custom-call | flops 1000000000 | bytes 1 | tf_op jit(solution)/shard_map/pallas_call | solution.py:100
  33.8 3.5 %shard_map.70 = f32[4,128,1024]{2,1,0:T(8,128)} custom-call(s32[56]{0:T(128)} %concatenate.3.s, f32[128,1024]{1,0:T(8,128)} %shard_map.69.refs_0_.refs_5_, f32[128,1024]{1,0:T(8,128)} %copy-done.13, f32[128,1024]{1,0:T(8,128)} %copy-done.14, f32[128,1024]{1,0:T(8,128)} %copy-done.15), custom_call_target="tpu_custom_call" | custom-call | flops 1000000000 | bytes 1 | tf_op jit(solution)/shard_map/pallas_call | solution.py:100
  37.3 6.2 %collective-permute-done.refs_1_ = f32[3,768,128]{2,1,0:T(8,128)S(1)} collective-permute-done((f32[3,768,128]{2,1,0:T(8,128)}, f32[3,768,128]{2,1,0:T(8,128)S(1)}, u32[]{:S(2)}, u32[]{:S(2)}) %collective-permute-start) | collective-permute-done | bytes 1179680 | tf_op jit(solution)/shard_map/ppermute | solution.py:416
  43.5 23.9 %collective-permute-done.2.refs_3_ = f32[3,768,128]{2,1,0:T(8,128)S(1)} collective-permute-done((f32[3,768,128]{2,1,0:T(8,128)}, f32[3,768,128]{2,1,0:T(8,128)S(1)}, u32[]{:S(2)}, u32[]{:S(2)}) %collective-permute-start.2) | collective-permute-done | bytes 1179680 | tf_op jit(solution)/shard_map/ppermute | solution.py:416
  68.4 5.4 %shard_map.72 = f32[4,3,768,128]{3,2,1,0:T(8,128)} custom-call(s32[56]{0:T(128)} %concatenate.3.s, f32[3,768,128]{2,1,0:T(8,128)} %shard_map.68.refs_0_, f32[3,768,128]{2,1,0:T(8,128)} %copy-done.2, f32[3,768,128]{2,1,0:T(8,128)} %copy-done.3, f32[3,768,128]{2,1,0:T(8,128)} %copy-done.4), custom_call_target="tpu_custom_call" | custom-call | flops 1000000000 | bytes 1 | tf_op jit(solution)/shard_map/pallas_call | solution.py:100
  73.8 2.8 %collective-permute-start.9 = (f32[4,3,768,128]{3,2,1,0:T(8,128)}, f32[4,3,768,128]{3,2,1,0:T(8,128)}, u32[]{:S(2)}, u32[]{:S(2)}) collective-permute-start(f32[4,3,768,128]{3,2,1,0:T(8,128)} %shard_map.72), channel_id=1, source_target_pairs={{1,5},{2,6},{5,1},{6,2},{9,13},{10,14},{13,9},{14,10},{17,21},{18,... | collective-permute-start | bytes 14155784 | tf_op jit(solution)/shard_map/ppermute | solution.py:419
  77.5 6.6 %collective-permute-start.12 = (f32[2,768,128]{2,1,0:T(8,128)S(1)}, f32[2,768,128]{2,1,0:T(8,128)S(1)}, u32[]{:S(2)}, u32[]{:S(2)}) collective-permute-start(f32[2,768,128]{2,1,0:T(8,128)S(1)} %copy-done.7), channel_id=1, source_target_pairs={{0,1},{3,2},{4,5},{7,6},{8,9},{11,10},{12,13},{15,14},{16,17},{19,... | collective-permute-start | bytes 2359304 | tf_op jit(solution)/shard_map/ppermute | solution.py:449
  84.1 1.3 collective-permute-start.14
  87.5 34.7 %shard_map.73 = (f32[2,1024,512]{2,1,0:T(8,128)}, f32[512,512]{1,0:T(8,128)}, f32[3,1024,128]{2,1,0:T(8,128)}, f32[3,768,128]{2,1,0:T(8,128)}) custom-call(s32[56]{0:T(128)} %concatenate.3.s, f32[3,768,128]{2,1,0:T(8,128)} %shard_map.68.refs_0_, f32[3,768,128]{2,1,0:T(8,128)} %copy-done.2, f32[3,768,128]{2,1,0:T(8,128)} %copy-done.3, ...), custom_call_target="tpu_custom_call" | custom-call | flops 60000002048 | bytes 1 | tf_op jit(solution)/shard_map/pallas_call | solution.py:100
  123.9 3.3 %shard_map.74 = f32[4,768,128]{2,1,0:T(8,128)} custom-call(s32[56]{0:T(128)} %concatenate.3.s, f32[2,768,128]{2,1,0:T(8,128)} %get-tuple-element.61.refs_0_.x0, f32[2,768,128]{2,1,0:T(8,128)} %copy-done.8, f32[4,768,128]{2,1,0:T(8,128)} %copy-done, f32[2,768,128]{2,1,0:T(8,128)} %copy-done.9), custom_call_target="tpu_custom_call" | custom-call | flops 1000000000 | bytes 1 | tf_op jit(solution)/shard_map/pallas_call | solution.py:100
  128.0 1.3 collective-permute-start.11
  129.3 20.4 %collective-permute-start.18 = (f32[2,768,128]{2,1,0:T(8,128)S(1)}, f32[2,768,128]{2,1,0:T(8,128)S(1)}, u32[]{:S(2)}, u32[]{:S(2)}) collective-permute-start(f32[2,768,128]{2,1,0:T(8,128)S(1)} %copy-done.6), channel_id=1, source_target_pairs={{0,1},{3,2},{4,5},{7,6},{8,9},{11,10},{12,13},{15,14},{16,17},{19,... | collective-permute-start | bytes 2359304 | tf_op jit(solution)/shard_map/ppermute | solution.py:462
  149.8 1.6 collective-permute-start.19
  152.5 9.0 %shard_map.75 = (f32[1024,128]{1,0:T(8,128)}, f32[1024,128]{1,0:T(8,128)}, f32[768,128]{1,0:T(8,128)}, f32[768,128]{1,0:T(8,128)}) custom-call(s32[56]{0:T(128)} %concatenate.3.s, f32[2,768,128]{2,1,0:T(8,128)} %get-tuple-element.61.refs_0_.x0, f32[2,768,128]{2,1,0:T(8,128)} %copy-done.8, f32[4,768,128]{2,1,0:T(8,128)} %copy-done, f32[2,768,128]{2,1,0:T(8,128)} %copy-done.9, ...), custom_call_target="tpu_custom_call" | custom-call | flops 10000000000 | bytes 1 | tf_op jit(solution)/shard_map/pallas_call | solution.py:100
  161.5 6.0 %collective-permute-done.18.refs_1_.x1 = f32[2,768,128]{2,1,0:T(8,128)S(1)} collective-permute-done((f32[2,768,128]{2,1,0:T(8,128)S(1)}, f32[2,768,128]{2,1,0:T(8,128)S(1)}, u32[]{:S(2)}, u32[]{:S(2)}) %collective-permute-start.18) | collective-permute-done | bytes 786464 | tf_op jit(solution)/shard_map/ppermute | solution.py:462
  167.6 16.5 %collective-permute-done.19.refs_3_.x3 = f32[2,768,128]{2,1,0:T(8,128)S(1)} collective-permute-done((f32[2,768,128]{2,1,0:T(8,128)S(1)}, f32[2,768,128]{2,1,0:T(8,128)S(1)}, u32[]{:S(2)}, u32[]{:S(2)}) %collective-permute-start.19) | collective-permute-done | bytes 786464 | tf_op jit(solution)/shard_map/ppermute | solution.py:462
  184.9 3.3 %shard_map.76 = f32[4,768,128]{2,1,0:T(8,128)} custom-call(s32[56]{0:T(128)} %concatenate.3.s, f32[2,768,128]{2,1,0:T(8,128)} %get-tuple-element.72.refs_0_.x0, f32[2,768,128]{2,1,0:T(8,128)} %copy-done.10, f32[4,768,128]{2,1,0:T(8,128)} %copy-done, f32[2,768,128]{2,1,0:T(8,128)} %copy-done.11), custom_call_target="tpu_custom_call" | custom-call | flops 1000000000 | bytes 1 | tf_op jit(solution)/shard_map/pallas_call | solution.py:100
  189.1 1.3 collective-permute-start.16
  190.4 1.3 collective-permute-start.17
  192.8 9.1 %shard_map.77 = (f32[1024,128]{1,0:T(8,128)}, f32[1024,128]{1,0:T(8,128)}, f32[1024,128]{1,0:T(8,128)}, f32[1024,128]{1,0:T(8,128)}) custom-call(s32[56]{0:T(128)} %concatenate.3.s, f32[2,768,128]{2,1,0:T(8,128)} %get-tuple-element.72.refs_0_.x0, f32[2,768,128]{2,1,0:T(8,128)} %copy-done.10, f32[4,768,128]{2,1,0:T(8,128)} %copy-done, ...), custom_call_target="tpu_custom_call" | custom-call | flops 10000000000 | bytes 1 | tf_op jit(solution)/shard_map/pallas_call | solution.py:100
  201.9 1.9 collective-permute-done.16.end.refs_3_
  203.8 8.0 %collective-permute-done.17.cross.refs_4_ = f32[768,128]{1,0:T(8,128)S(1)} collective-permute-done((f32[768,128]{1,0:T(8,128)S(1)}, f32[768,128]{1,0:T(8,128)S(1)}, u32[]{:S(2)}, u32[]{:S(2)}) %collective-permute-start.17) | collective-permute-done | bytes 393248 | tf_op jit(solution)/shard_map/ppermute | solution.py:481
  212.6 2.8 %shard_map.78 = f32[1280,128]{1,0:T(8,128)} custom-call(s32[56]{0:T(128)} %concatenate.3.s, f32[3,768,128]{2,1,0:T(8,128)} %copy-done.5, f32[768,128]{1,0:T(8,128)} %copy-done.19, f32[768,128]{1,0:T(8,128)} %copy-done.20, f32[1024,128]{1,0:T(8,128)} %get-tuple-element.80.core), custom_call_target="tpu_custom_call" | custom-call | flops 1000000000 | bytes 1 | tf_op jit(solution)/shard_map/pallas_call | solution.py:100
  219.0 14.0 %collective-permute-done.23.refs_8_ = f32[1024,128]{1,0:T(8,128)S(1)} collective-permute-done((f32[1024,128]{1,0:T(8,128)S(1)}, f32[1024,128]{1,0:T(8,128)S(1)}, u32[]{:S(2)}, u32[]{:S(2)}) %collective-permute-start.23) | collective-permute-done | bytes 524320 | tf_op jit(solution)/shard_map/ppermute | solution.py:481
  233.0 10.1 %collective-permute-done.24.refs_9_ = f32[1024,128]{1,0:T(8,128)S(1)} collective-permute-done((f32[1024,128]{1,0:T(8,128)S(1)}, f32[1024,128]{1,0:T(8,128)S(1)}, u32[]{:S(2)}, u32[]{:S(2)}) %collective-permute-start.24) | collective-permute-done | bytes 524320 | tf_op jit(solution)/shard_map/ppermute | solution.py:481
  244.2 4.7 %shard_map.79 = (f32[7,512,128]{2,1,0:T(8,128)}, f32[7,512,128]{2,1,0:T(8,128)}) custom-call(s32[56]{0:T(128)} %concatenate.3.s, f32[3,1024,128]{2,1,0:T(8,128)} %get-tuple-element.55.refs_0_, f32[3,768,128]{2,1,0:T(8,128)} %copy-done.5, f32[1024,128]{1,0:T(8,128)} %get-tuple-element.66.refs_2_, f32[768,128]{1,0:T(8,128)} %copy-done.19, ...), custom_call_target="tpu_custom_call" | custom-call | flops 1000000000 | bytes 1 | tf_op jit(solution)/shard_map/pallas_call | solution.py:100
  (99 shorter events, 23.9 us)
Async XLA Ops:
  0.6 17.0 %collective-permute-start.3 = (f32[128,256]{1,0:T(8,128)}, f32[128,256]{1,0:T(8,128)S(1)}, u32[]{:S(2)}, u32[]{:S(2)}) collective-permute-start(f32[128,256]{1,0:T(8,128)} %refs_0_), channel_id=1, source_target_pairs={{0,1},{3,2},{4,5},{7,6},{8,9},{11,10},{12,13},{15,14},{16,17},{19,... | collective-permute-start | bytes 393224 | tf_op jit(solution)/shard_map/ppermute | solution.py:416
  5.6 16.0 %collective-permute-start.4 = (f32[128,256]{1,0:T(8,128)}, f32[128,256]{1,0:T(8,128)S(1)}, u32[]{:S(2)}, u32[]{:S(2)}) collective-permute-start(f32[128,256]{1,0:T(8,128)} %refs_0_), channel_id=1, source_target_pairs={{1,2},{2,1},{5,6},{6,5},{9,10},{10,9},{13,14},{14,13},{17,18},{18,... | collective-permute-start | bytes 393224 | tf_op jit(solution)/shard_map/ppermute | solution.py:416
  6.3 15.3 %collective-permute-start.5 = (f32[128,256]{1,0:T(8,128)}, f32[128,256]{1,0:T(8,128)S(1)}, u32[]{:S(2)}, u32[]{:S(2)}) collective-permute-start(f32[128,256]{1,0:T(8,128)} %refs_0_), channel_id=1, source_target_pairs={{0,2},{3,1},{4,6},{7,5},{8,10},{11,9},{12,14},{15,13},{16,18},{19,... | collective-permute-start | bytes 393224 | tf_op jit(solution)/shard_map/ppermute | solution.py:416
  15.4 28.1 %collective-permute-start = (f32[3,768,128]{2,1,0:T(8,128)}, f32[3,768,128]{2,1,0:T(8,128)S(1)}, u32[]{:S(2)}, u32[]{:S(2)}) collective-permute-start(f32[3,768,128]{2,1,0:T(8,128)} %shard_map.68.refs_0_), channel_id=1, source_target_pairs={{0,1},{3,2},{4,5},{7,6},{8,9},{11,10},{12,13},{15,14},{16,17},{19,... | collective-permute-start | bytes 3538952 | tf_op jit(solution)/shard_map/ppermute | solution.py:416
  16.8 26.6 %collective-permute-start.1 = (f32[3,768,128]{2,1,0:T(8,128)}, f32[3,768,128]{2,1,0:T(8,128)S(1)}, u32[]{:S(2)}, u32[]{:S(2)}) collective-permute-start(f32[3,768,128]{2,1,0:T(8,128)} %shard_map.68.refs_0_), channel_id=1, source_target_pairs={{1,2},{2,1},{5,6},{6,5},{9,10},{10,9},{13,14},{14,13},{17,18},{18,... | collective-permute-start | bytes 3538952 | tf_op jit(solution)/shard_map/ppermute | solution.py:416
  17.6 49.7 %collective-permute-start.2 = (f32[3,768,128]{2,1,0:T(8,128)}, f32[3,768,128]{2,1,0:T(8,128)S(1)}, u32[]{:S(2)}, u32[]{:S(2)}) collective-permute-start(f32[3,768,128]{2,1,0:T(8,128)} %shard_map.68.refs_0_), channel_id=1, source_target_pairs={{0,2},{3,1},{4,6},{7,5},{8,10},{11,9},{12,14},{15,13},{16,18},{19,... | collective-permute-start | bytes 3538952 | tf_op jit(solution)/shard_map/ppermute | solution.py:416
  25.5 1.4 collective-permute-start.6
  26.2 6.0 %collective-permute-start.7 = (f32[128,1024]{1,0:T(8,128)}, f32[128,1024]{1,0:T(8,128)S(1)}, u32[]{:S(2)}, u32[]{:S(2)}) collective-permute-start(f32[128,1024]{1,0:T(8,128)} %shard_map.69.refs_0_.refs_5_), channel_id=1, source_target_pairs={{1,17},{2,18},{5,21},{6,22},{9,25},{10,26},{13,29},{14,30},{17,1},... | collective-permute-start | bytes 1572872 | tf_op jit(solution)/shard_map/ppermute | solution.py:439
  26.9 5.3 %collective-permute-start.8 = (f32[128,1024]{1,0:T(8,128)}, f32[128,1024]{1,0:T(8,128)S(1)}, u32[]{:S(2)}, u32[]{:S(2)}) collective-permute-start(f32[128,1024]{1,0:T(8,128)} %shard_map.69.refs_0_.refs_5_), channel_id=1, source_target_pairs={{1,25},{2,26},{5,29},{6,30},{9,17},{10,18},{13,21},{14,22},{17,9},... | collective-permute-start | bytes 1572872 | tf_op jit(solution)/shard_map/ppermute | solution.py:439
  43.5 23.9 %copy-start.2 = (f32[3,768,128]{2,1,0:T(8,128)}, f32[3,768,128]{2,1,0:T(8,128)S(1)}, u32[]{:S(2)}) copy-start(f32[3,768,128]{2,1,0:T(8,128)S(1)} %collective-permute-done.refs_1_) | copy-start | bytes 3538948
  43.5 23.9 %copy-start.3 = (f32[3,768,128]{2,1,0:T(8,128)}, f32[3,768,128]{2,1,0:T(8,128)S(1)}, u32[]{:S(2)}) copy-start(f32[3,768,128]{2,1,0:T(8,128)S(1)} %collective-permute-done.1.refs_2_) | copy-start | bytes 3538948
  68.4 8.3 %copy-start.1 = (f32[4,128,1024]{2,1,0:T(8,128)S(1)}, f32[4,128,1024]{2,1,0:T(8,128)}, u32[]{:S(2)}) copy-start(f32[4,128,1024]{2,1,0:T(8,128)} %shard_map.70) | copy-start | bytes 6291460
  68.4 9.1 %copy-start.7 = (f32[2,768,128]{2,1,0:T(8,128)S(1)}, f32[2,768,128]{2,1,0:T(8,128)}, u32[]{:S(2)}) copy-start(f32[2,768,128]{2,1,0:T(8,128)} %get-tuple-element.61.refs_0_.x0) | copy-start | bytes 2359300
  73.8 13.7 %collective-permute-start.9 = (f32[4,3,768,128]{3,2,1,0:T(8,128)}, f32[4,3,768,128]{3,2,1,0:T(8,128)}, u32[]{:S(2)}, u32[]{:S(2)}) collective-permute-start(f32[4,3,768,128]{3,2,1,0:T(8,128)} %shard_map.72), channel_id=1, source_target_pairs={{1,5},{2,6},{5,1},{6,2},{9,13},{10,14},{13,9},{14,10},{17,21},{18,... | collective-permute-start | bytes 14155784 | tf_op jit(solution)/shard_map/ppermute | solution.py:419
  76.7 9.6 %collective-permute-start.10 = (f32[4,128,1024]{2,1,0:T(8,128)S(1)}, f32[4,128,1024]{2,1,0:T(8,128)S(1)}, u32[]{:S(2)}, u32[]{:S(2)}) collective-permute-start(f32[4,128,1024]{2,1,0:T(8,128)S(1)} %copy-done.1), channel_id=1, source_target_pairs={{1,5},{2,6},{5,1},{6,2},{9,13},{10,14},{13,9},{14,10},{17,21},{18,... | collective-permute-start | bytes 6291464 | tf_op jit(solution)/shard_map/ppermute | solution.py:419
  77.5 44.8 %collective-permute-start.12 = (f32[2,768,128]{2,1,0:T(8,128)S(1)}, f32[2,768,128]{2,1,0:T(8,128)S(1)}, u32[]{:S(2)}, u32[]{:S(2)}) collective-permute-start(f32[2,768,128]{2,1,0:T(8,128)S(1)} %copy-done.7), channel_id=1, source_target_pairs={{0,1},{3,2},{4,5},{7,6},{8,9},{11,10},{12,13},{15,14},{16,17},{19,... | collective-permute-start | bytes 2359304 | tf_op jit(solution)/shard_map/ppermute | solution.py:449
  84.1 38.1 %collective-permute-start.14 = (f32[2,768,128]{2,1,0:T(8,128)S(1)}, f32[2,768,128]{2,1,0:T(8,128)S(1)}, u32[]{:S(2)}, u32[]{:S(2)}) collective-permute-start(f32[2,768,128]{2,1,0:T(8,128)S(1)} %copy-done.7), channel_id=1, source_target_pairs={{0,2},{3,1},{4,6},{7,5},{8,10},{11,9},{12,14},{15,13},{16,18},{19,... | collective-permute-start | bytes 2359304 | tf_op jit(solution)/shard_map/ppermute | solution.py:449
  85.5 36.8 %collective-permute-start.13 = (f32[4,768,128]{2,1,0:T(8,128)}, f32[4,768,128]{2,1,0:T(8,128)S(1)}, u32[]{:S(2)}, u32[]{:S(2)}) collective-permute-start(f32[4,768,128]{2,1,0:T(8,128)} %get-tuple-element.59), channel_id=1, source_target_pairs={{1,2},{2,1},{5,6},{6,5},{9,10},{10,9},{13,14},{14,13},{17,18},{18,... | collective-permute-start | bytes 4718600 | tf_op jit(solution)/shard_map/ppermute | solution.py:448
  127.2 24.1 %collective-permute-start.15 = (f32[4,768,128]{2,1,0:T(8,128)}, f32[4,768,128]{2,1,0:T(8,128)S(1)}, u32[]{:S(2)}, u32[]{:S(2)}) collective-permute-start(f32[4,768,128]{2,1,0:T(8,128)} %shard_map.74), channel_id=1, source_target_pairs={{1,5},{2,6},{5,1},{6,2},{9,13},{10,14},{13,9},{14,10},{17,21},{18,... | collective-permute-start | bytes 4718600 | tf_op jit(solution)/shard_map/ppermute | solution.py:419
  128.0 56.0 %collective-permute-start.11 = (f32[3,768,128]{2,1,0:T(8,128)S(1)}, f32[3,768,128]{2,1,0:T(8,128)S(1)}, u32[]{:S(2)}, u32[]{:S(2)}) collective-permute-start(f32[3,768,128]{2,1,0:T(8,128)S(1)} %copy-done.24), channel_id=1, source_target_pairs={{1,0},{2,3},{5,4},{6,7},{9,8},{10,11},{13,12},{14,15},{17,16},{18,... | collective-permute-start | bytes 3538952 | tf_op jit(solution)/shard_map/ppermute | solution.py:463
  129.3 38.2 %collective-permute-start.18 = (f32[2,768,128]{2,1,0:T(8,128)S(1)}, f32[2,768,128]{2,1,0:T(8,128)S(1)}, u32[]{:S(2)}, u32[]{:S(2)}) collective-permute-start(f32[2,768,128]{2,1,0:T(8,128)S(1)} %copy-done.6), channel_id=1, source_target_pairs={{0,1},{3,2},{4,5},{7,6},{8,9},{11,10},{12,13},{15,14},{16,17},{19,... | collective-permute-start | bytes 2359304 | tf_op jit(solution)/shard_map/ppermute | solution.py:462
  149.8 34.2 %collective-permute-start.19 = (f32[2,768,128]{2,1,0:T(8,128)S(1)}, f32[2,768,128]{2,1,0:T(8,128)S(1)}, u32[]{:S(2)}, u32[]{:S(2)}) collective-permute-start(f32[2,768,128]{2,1,0:T(8,128)S(1)} %copy-done.6), channel_id=1, source_target_pairs={{0,2},{3,1},{4,6},{7,5},{8,10},{11,9},{12,14},{15,13},{16,18},{19,... | collective-permute-start | bytes 2359304 | tf_op jit(solution)/shard_map/ppermute | solution.py:462
  167.6 16.5 %copy-start.10 = (f32[2,768,128]{2,1,0:T(8,128)}, f32[2,768,128]{2,1,0:T(8,128)S(1)}, u32[]{:S(2)}) copy-start(f32[2,768,128]{2,1,0:T(8,128)S(1)} %collective-permute-done.18.refs_1_.x1) | copy-start | bytes 2359300
  188.3 3.4 %collective-permute-start.20 = (f32[4,768,128]{2,1,0:T(8,128)}, f32[4,768,128]{2,1,0:T(8,128)S(1)}, u32[]{:S(2)}, u32[]{:S(2)}) collective-permute-start(f32[4,768,128]{2,1,0:T(8,128)} %shard_map.76), channel_id=1, source_target_pairs={{1,5},{2,6},{5,1},{6,2},{9,13},{10,14},{13,9},{14,10},{17,21},{18,... | collective-permute-start | bytes 4718600 | tf_op jit(solution)/shard_map/ppermute | solution.py:419
  189.1 14.8 %collective-permute-start.16 = (f32[768,128]{1,0:T(8,128)S(1)}, f32[768,128]{1,0:T(8,128)S(1)}, u32[]{:S(2)}, u32[]{:S(2)}) collective-permute-start(f32[768,128]{1,0:T(8,128)S(1)} %copy-done.29), channel_id=1, source_target_pairs={{1,0},{2,3},{5,4},{6,7},{9,8},{10,11},{13,12},{14,15},{17,16},{18,... | collective-permute-start | bytes 1179656 | tf_op jit(solution)/shard_map/ppermute | solution.py:481
  190.4 21.5 %collective-permute-start.17 = (f32[768,128]{1,0:T(8,128)S(1)}, f32[768,128]{1,0:T(8,128)S(1)}, u32[]{:S(2)}, u32[]{:S(2)}) collective-permute-start(f32[768,128]{1,0:T(8,128)S(1)} %copy-done.28), channel_id=1, source_target_pairs={{1,4},{2,7},{5,0},{6,3},{9,12},{10,15},{13,8},{14,11},{17,20},{18,... | collective-permute-start | bytes 1179656 | tf_op jit(solution)/shard_map/ppermute | solution.py:481
  215.5 27.7 %collective-permute-start.21 = (f32[1280,128]{1,0:T(8,128)}, f32[1280,128]{1,0:T(8,128)S(1)}, u32[]{:S(2)}, u32[]{:S(2)}) collective-permute-start(f32[1280,128]{1,0:T(8,128)} %shard_map.78), channel_id=1, source_target_pairs={{0,4},{1,5},{2,6},{3,7},{4,0},{5,1},{6,2},{7,3},{8,12},{9,13},{10,... | collective-permute-start | bytes 1966088 | tf_op jit(solution)/shard_map/ppermute | solution.py:488
  215.7 3.3 %collective-permute-start.22 = (f32[1024,128]{1,0:T(8,128)S(1)}, f32[1024,128]{1,0:T(8,128)S(1)}, u32[]{:S(2)}, u32[]{:S(2)}) collective-permute-start(f32[1024,128]{1,0:T(8,128)S(1)} %copy-done.27), channel_id=1, source_target_pairs={{1,5},{2,6},{5,1},{6,2},{9,13},{10,14},{13,9},{14,10},{17,21},{18,... | collective-permute-start | bytes 1572872 | tf_op jit(solution)/shard_map/ppermute | solution.py:419
  216.4 16.7 %collective-permute-start.23 = (f32[1024,128]{1,0:T(8,128)S(1)}, f32[1024,128]{1,0:T(8,128)S(1)}, u32[]{:S(2)}, u32[]{:S(2)}) collective-permute-start(f32[1024,128]{1,0:T(8,128)S(1)} %copy-done.26), channel_id=1, source_target_pairs={{1,0},{2,3},{5,4},{6,7},{9,8},{10,11},{13,12},{14,15},{17,16},{18,... | collective-permute-start | bytes 1572872 | tf_op jit(solution)/shard_map/ppermute | solution.py:481
  217.7 25.5 %collective-permute-start.24 = (f32[1024,128]{1,0:T(8,128)S(1)}, f32[1024,128]{1,0:T(8,128)S(1)}, u32[]{:S(2)}, u32[]{:S(2)}) collective-permute-start(f32[1024,128]{1,0:T(8,128)S(1)} %copy-done.25), channel_id=1, source_target_pairs={{1,4},{2,7},{5,0},{6,3},{9,12},{10,15},{13,8},{14,11},{17,20},{18,... | collective-permute-start | bytes 1572872 | tf_op jit(solution)/shard_map/ppermute | solution.py:481
  219.0 24.2 %copy-start.16 = (f32[1024,128]{1,0:T(8,128)}, f32[1024,128]{1,0:T(8,128)S(1)}, u32[]{:S(2)}) copy-start(f32[1024,128]{1,0:T(8,128)S(1)} %collective-permute-done.22.refs_7_) | copy-start | bytes 1572868
  233.0 10.1 %copy-start.17 = (f32[1024,128]{1,0:T(8,128)}, f32[1024,128]{1,0:T(8,128)S(1)}, u32[]{:S(2)}) copy-start(f32[1024,128]{1,0:T(8,128)S(1)} %collective-permute-done.23.refs_8_) | copy-start | bytes 1572868
  (26 other events, 67.1 us)

commit v6 on v5

--- a/solution.py
+++ b/solution.py
@@ -151,21 +151,6 @@
     copy_all(copies, sems)
 
 
-def leaf_pack_kernel(s, panels, inverse, pair, every, last, sems):
-    half = panels.shape[1]
-    targets = [(3 + k, pair.at[k]) for k in range(2)] + [(3 + k, every.at[k]) for k in range(4)]
-    targets += [(5 + k, last.at[k]) for k in range(2)]
-    copies = []
-    for node, out in targets:
-        copies.append((panels.at[node], out.at[pl.ds(0, half)]))
-        for j in range(inverse.shape[2] // TILE):
-            copies.append((
-                inverse.at[node, at(s[0] * QUARTER, QUARTER, QUARTER), pl.ds(j * TILE, TILE)],
-                out.at[pl.ds(half + j * QUARTER, QUARTER)],
-            ))
-    copy_all(copies, sems)
-
-
 def join_columns_kernel(s, *refs):
     out, sems = refs[-2:]
     width = refs[0].shape[1]
@@ -177,9 +162,12 @@
     copy_all([(ref, out.at[k]) for k, ref in enumerate(refs[:-2])], sems)
 
 
-def swap_kernel(skips, s, *refs):
+def swap_kernel(s, *refs):
     out, sems = refs[-2:]
-    copy_all([(ref.at[skips[k] + 1 - s[0]], out.at[k]) for k, ref in enumerate(refs[:-2])], sems)
+    copies = [
+        (ref.at[2 * pair + 1 - s[0]], out.at[pair, k]) for pair in range(2) for k, ref in enumerate(refs[:-2])
+    ]
+    copy_all(copies, sems)
 
 
 def join_block(a, own, corner, rows_of, top, index, weight):
@@ -216,7 +204,7 @@
         pltpu.make_async_copy(ref, sigma.at[k], sems.at[2, k])
         for k, ref in enumerate(list(sigmas[:4]) + [sigmas[4].at[m] for m in range(4)])
     ]
-    for one in fetch(0, 0) + sigma_copies + fetch(1, 1):
+    for one in fetch(0, 0) + sigma_copies:
         one.start()
 
     def panels_of(node, slot):
@@ -237,6 +225,8 @@
         end_out[node, half:, :] = dg[at(r * (own // 2), own // 2), at(3 * far * TILE, TILE)]
 
     panels_of(0, 0)
+    for one in fetch(1, 1):
+        one.start()
 
     def join_root():
         places = (c, 3 * far, 3 - c, 3 - 3 * far)
@@ -285,11 +275,11 @@
         ext[node - 1, half:, :] = dg[...]
 
 
-def leaf_kernel(first, skips, s, x0, x1, x2, x3, ex, ext, grand, self_out, core_out, end_out, cross_out, *rest):
+def leaf_kernel(first, s, x0, x1, x2, x3, ex, ext, grand, self_out, core_out, end_out, cross_out, *rest):
     stage, sems, tails, top, grand_in, ab, dg = rest[:7]
     p, d, a, dc, f, w, t, pt, dt = pairs(rest[7:])
     r, c = s[0], s[1]
-    blocks = [x for k, ref in enumerate((x0, x1, x2, x3)) for x in (ref.at[skips[k] + r], ex.at[k])]
+    blocks = [x for k, ref in enumerate((x0, x1, x2, x3)) for x in (ref.at[first - 3 + r], ex.at[(first - 3) // 2, k])]
     order = a[0].shape[0]
     own = d[0].shape[0]
     half = order // 2
@@ -337,26 +327,21 @@
         out[half:, :] = dg[:, cols] if share == own else dg[at(side * share, share), cols]
 
 
-def shares_kernel(s, upper, end, cross, core, out, sems):
-    c = s[1]
-    middle = (c == 1) | (c == 2)
-    half = core.shape[0] // 2
-    share = upper.shape[1] - half
-
-    @pl.when(middle)
-    def _():
-        copy_all([(core, out.at[pl.ds(0, 2 * half)])], sems)
-
-    @pl.when(jnp.logical_not(middle))
-    def _():
-        found = [upper.at[k] for k in range(3)] + [end, cross]
-        copy_all([
-            (ref.at[pl.ds(half, share)], out.at[pl.ds(k * share, share)]) for k, ref in enumerate(found)
-        ], sems)
+def shares_kernel(s, *refs):
+    out, sems = refs[-2:]
+    share = out.shape[0] // len(refs[:-2])
+    copy_all([
+        (ref.at[pl.ds(ref.shape[0] - share, share)], out.at[pl.ds(k * share, share)]) for k, ref in enumerate(refs[:-2])
+    ], sems)
+
+
+def upper_shares_kernel(s, upper, out, sems):
+    shares_kernel(s, upper.at[0], upper.at[1], upper.at[2], out, sems)
 
 
 def output_kernel(s, *refs):
-    upper_self, upper_end, self_34, end_34, cross_34, shares, self_56, core_56, end_56, cross_56 = refs[:10]
+    upper_self, upper_end, upper_shares, self_34, core_34, end_34, cross_34, shares_34 = refs[:8]
+    self_56, core_56, end_56, cross_56 = refs[8:12]
     ab, dg, sems = refs[-3:]
     r, c = s[0], s[1]
     half = ab.shape[1]
@@ -365,7 +350,7 @@
     for core in range(2):
         @pl.when((r == core) & middle)
         def _():
-            pair = [self_34, shares] if core == 0 else [shares, self_34]
+            pair = [self_34, core_34] if core == 0 else [core_34, self_34]
             last = [self_56, core_56] if core == 0 else [core_56, self_56]
             copies = []
             for node, ref in enumerate([upper_self.at[k] for k in range(3)] + pair + last):
@@ -377,8 +362,10 @@
         def _():
             same, swapped = (3, 4) if core == 0 else (4, 3)
             last = [end_56, cross_56] if core == 0 else [cross_56, end_56]
+            found = [(k, upper_end.at[k], upper_shares, k) for k in range(3)]
+            found += [(same, end_34, shares_34, 1), (swapped, cross_34, shares_34, 0)]
             copies = []
-            for node, ref, k in [(k, upper_end.at[k], k) for k in range(3)] + [(same, end_34, 4), (swapped, cross_34, 3)]:
+            for node, ref, shares, k in found:
                 copies.append((ref.at[pl.ds(0, half)], ab.at[node]))
                 copies.append((ref.at[pl.ds(half, share)], dg.at[node, pl.ds(core * share, share)]))
                 copies.append((shares.at[pl.ds(k * share, share)], dg.at[node, pl.ds((1 - core) * share, share)]))
@@ -404,7 +391,7 @@
     routes = (((0, 1), (3, 2)), ((1, 2), (2, 1)), ((0, 2), (3, 1)))
     middles = (1, 2)
     swap = [(row * 4 + a, (1 - row) * 4 + a) for row in range(2) for a in middles]
-    swap_all = [(row * 4 + a, (1 - row) * 4 + a) for row in range(2) for a in range(4)]
+    swap_ends = [(row * 4 + a, (1 - row) * 4 + a) for row in range(2) for a in (0, 3)]
     home = ((1, 0), (2, 3))
     home_cross = [(row * 4 + a, (1 - row) * 4 + b) for row in range(2) for a, b in home]
     leaf_routes = [
@@ -422,17 +409,11 @@
     trunk = 3
     packed = half + own // 2
 
-    def pack(first, *counts):
-        return move(
-            functools.partial(pack_kernel, first), here, [panels, inverse], [(k, packed, TILE) for k in counts],
-            5 * sum(counts),
-        )
-
-    def pack_leaves(sources):
-        return move(leaf_pack_kernel, here, sources, [(k, packed, TILE) for k in (2, 4, 2)], 40)
+    def pack(first, count, sources):
+        return move(functools.partial(pack_kernel, first), here, sources, [(count, packed, TILE)], 5 * count)[0]
 
     sigma_parts = straight(sigma_top)
-    pack_t = pack(0, trunk)[0]
+    pack_t = pack(0, trunk, [panels, inverse])
     blocks_t = straight(pack_t)
     sigma_cols = move(join_columns_kernel, here, after(sigma_parts, pack_t), [(TILE, order)], 4)[0]
     sigma_rows = [sigma_cols] + [
@@ -440,13 +421,10 @@
     ]
     sigma_mine = move(stack_kernel, here, sigma_rows, [(4, TILE, order)], 4)[0]
     sigma_other = swapped(sigma_mine)
-    pack_34, pack_all, pack_56 = pack_leaves(after((panels, inverse), pack_t))
-    gathered = after(blocks_t, (sigma_mine, pack_34))
+    pack_l = pack(trunk, 4, after([panels, inverse], pack_t))
+    gathered = after(blocks_t, (sigma_mine, pack_l))
     other_t = swapped(move(stack_kernel, here, gathered, [(4, trunk, packed, TILE)], 4)[0])
-    pack_34, pack_all = after((pack_34, pack_all), blocks_t[1:])
-    near, between, far = routes
-    across = lax.ppermute(pack_all, "col", between)
-    blocks_34 = [pack_34, lax.ppermute(pack_34, "col", near), across, lax.ppermute(pack_34, "col", far)]
+    blocks_l = straight(after(pack_l, blocks_t[1:]))
     ext, grand, upper_self, upper_end = call(
         trunk_kernel, here, blocks_t + [other_t] + sigma_rows + [sigma_other],
         [(2, half + own, own), (own, own), (trunk, half + own, TILE), (trunk, packed, TILE)],
@@ -456,10 +434,8 @@
         ] + scratch_pairs(
             (order, own), (own, own), (order, order), (order, own), (order, own), (own, own), (own, order), (own, own)
         ) + [pltpu.VMEM((order, own), F32)],
-        [ANY] * 10, micros=60,
+        [ANY] * 10, micros=1,
     )
-    last = after(pack_56, ext)
-    blocks_56 = [pack_56, lax.ppermute(last, "col", near), across, lax.ppermute(last, "col", far)]
     upper_home = lax.ppermute(upper_end, "col", home)
     tails = (order - own) // TILE
     leaf_scratch = [
@@ -471,25 +447,31 @@
         (own, own),
     )
 
-    def leaves(blocks, first, skips, earlier, end_rows):
-        chosen = after(blocks, earlier)
-        theirs = swapped(move(functools.partial(swap_kernel, skips), here, chosen, [(4, packed, TILE)], 4)[0])
+    def leaves(first, theirs, end_rows):
         self_out, core_out, end_out, cross_out = call(
-            functools.partial(leaf_kernel, first, skips), here, blocks + [theirs, ext, grand],
+            functools.partial(leaf_kernel, first), here, blocks_l + [theirs, ext, grand],
             [(half + own, TILE)] * 2 + [(end_rows, TILE)] * 2, leaf_scratch, [ANY] * 7, micros=10,
         )
         return self_out, core_out, lax.ppermute(end_out, "col", home), lax.ppermute(cross_out, both, home_cross)
 
-    self_34, core_34, end_34, cross_34 = leaves(blocks_34, 3, (0, 0, 0, 0), ext, packed)
-    self_56, core_56, end_56, cross_56 = leaves(blocks_56, 5, (0, 0, 2, 0), (upper_home, self_34), half + own)
-    shares = move(
-        shares_kernel, here, after([upper_home, end_34, cross_34, core_34], self_56), [((trunk + 2) * (own // 2), TILE)], trunk + 2
-    )[0]
-    shares = lax.ppermute(shares, both, swap_all)
+    chosen = after(blocks_l, (ext, upper_home))
+    others = swapped(move(swap_kernel, here, chosen, [(2, 4, packed, TILE)], 8)[0])
+    self_34, core_34, end_34, cross_34 = leaves(3, others, packed)
+    self_56, core_56, end_56, cross_56 = leaves(5, after(others, self_34), half + own)
+
+    def shared(kernel, parts, count):
+        out = move(kernel, here, parts, [(count * (own // 2), TILE)], count)[0]
+        return lax.ppermute(out, both, swap_ends)
+
+    upper_shares = shared(upper_shares_kernel, [upper_home], 3)
+    shares_34 = shared(shares_kernel, [end_34, cross_34], 2)
     count = panels.shape[0]
     ancestor_block, diagonal_block = move(
         output_kernel, here,
-        [upper_self, upper_home, self_34, end_34, cross_34, shares, self_56, swapped(core_56), end_56, cross_56],
+        [
+            upper_self, upper_home, upper_shares, self_34, swapped(core_34), end_34, cross_34, shares_34, self_56,
+            swapped(core_56), end_56, cross_56,
+        ],
         [(count, half, TILE), (count, own, TILE)], 3 * count,
     )
     return (ancestor_block[None], diagonal_block[None])

time: 250 us -> 227 us (0.908)
  starting transfers between devices: 61 us -> 48.1 us
  waiting for transfers between devices: 86.6 us -> 82.6 us
  local copies, waits for them, and re-layouts: 13.1 us -> 9.26 us
    ppermute x6 -> x2, starting transfers between devices: 30.9 us -> 4.69 us  [shared(): return lax.ppermute(out, both, swap_ends)]
    ppermute x6 -> x9, waiting for transfers between devices: 30 us -> 55.7 us  [straight(): return [x] + [lax.ppermute(x, 'col', route) for route in routes]]
    ppermute x6 -> x2, waiting for transfers between devices: 22.5 us -> 0.01 us  [shared(): return lax.ppermute(out, both, swap_ends)]
    ppermute x6 -> x9, starting transfers between devices: 15.7 us -> 28.8 us  [straight(): return [x] + [lax.ppermute(x, 'col', route) for route in routes]]
    ppermute x2, waiting for transfers between devices: 15.9 us -> 6.49 us  [leaves(): lax.ppermute(end_out, 'col', home)]
    unnamed x66 -> x46, local copies, waits for them, and re-layouts: 11.8 us -> 7.96 us
    ppermute x1, waiting for transfers between devices: 0.01 us -> 3.59 us  [chip_body(): upper_home = lax.ppermute(upper_end, 'col', home)]
  transfers between devices with their start and end apart: 25 -> 24, of which waited for: 8 -> 8; matrix products, arithmetic and copies ran while one was open for 1% -> 1% of each run, Pallas kernels for 27% -> 31%
where the time goes in v6:
time: 227 us; the launch traced here: 226 us
  Pallas kernels  84.2 us (37%)
  waiting for transfers between devices  82.6 us (36%)
  starting transfers between devices  48.1 us (21%)
  local copies, waits for them, and re-layouts  9.26 us (4%)
    pallas_call x12, Pallas kernels, call(): pl.pallas_call(kernel, out_shape=[jax.ShapeDtypeStruct(o, F32) for o in o...  84.2 us
    ppermute x9, waiting for transfers between devices, straight(): return [x] + [lax.ppermute(x, 'col', route) for route in routes]  55.7 us
    ppermute x9, starting transfers between devices, straight(): return [x] + [lax.ppermute(x, 'col', route) for route in routes]  28.8 us
    ppermute x2, waiting for transfers between devices, leaves(): lax.ppermute(cross_out, both, home_cross)  16.7 us
    unnamed x46, local copies, waits for them, and re-layouts  7.96 us
    ppermute x2, waiting for transfers between devices, leaves(): lax.ppermute(end_out, 'col', home)  6.49 us
    ppermute x5, starting transfers between devices, swapped(): return lax.ppermute(x, both, swap)  5.88 us
    ppermute x2, starting transfers between devices, shared(): return lax.ppermute(out, both, swap_ends)  4.69 us
  transfers between devices with their start and end apart: 24, of which 8 were waited for; matrix products, arithmetic and copies ran while one was open for 1% of the time, Pallas kernels for 31%

profile of v6, /device:TPU:0, one launch (start us, length us, event | category | flops | bytes accessed | tf_op | source)
XLA Modules:
  0.0 226.1 jit_solution(12800842731044259193)
XLA Ops:
  0.6 4.9 %collective-permute-start.3 = (f32[128,256]{1,0:T(8,128)}, f32[128,256]{1,0:T(8,128)S(1)}, u32[]{:S(2)}, u32[]{:S(2)}) collective-permute-start(f32[128,256]{1,0:T(8,128)} %refs_0_), channel_id=1, source_target_pairs={{0,1},{3,2},{4,5},{7,6},{8,9},{11,10},{12,13},{15,14},{16,17},{19,... | collective-permute-start | bytes 393224 | tf_op jit(solution)/shard_map/ppermute | solution.py:403
  6.3 4.0 %collective-permute-start.5 = (f32[128,256]{1,0:T(8,128)}, f32[128,256]{1,0:T(8,128)S(1)}, u32[]{:S(2)}, u32[]{:S(2)}) collective-permute-start(f32[128,256]{1,0:T(8,128)} %refs_0_), channel_id=1, source_target_pairs={{0,2},{3,1},{4,6},{7,5},{8,10},{11,9},{12,14},{15,13},{16,18},{19,... | collective-permute-start | bytes 393224 | tf_op jit(solution)/shard_map/ppermute | solution.py:403
  12.3 3.1 %shard_map.68.refs_0_ = f32[3,768,128]{2,1,0:T(8,128)} custom-call(s32[56]{0:T(128)} %concatenate.3.s, f32[7,512,128]{2,1,0:T(8,128)} %bitcast.8, f32[7,128,512]{2,1,0:T(8,128)} %bitcast.10), custom_call_target="tpu_custom_call" | custom-call | flops 1000000000 | bytes 1 | tf_op jit(solution)/shard_map/pallas_call | solution.py:100
  15.3 1.5 collective-permute-start
  17.6 3.9 %collective-permute-start.2 = (f32[3,768,128]{2,1,0:T(8,128)}, f32[3,768,128]{2,1,0:T(8,128)S(1)}, u32[]{:S(2)}, u32[]{:S(2)}) collective-permute-start(f32[3,768,128]{2,1,0:T(8,128)} %shard_map.68.refs_0_), channel_id=1, source_target_pairs={{0,2},{3,1},{4,6},{7,5},{8,10},{11,9},{12,14},{15,13},{16,18},{19,... | collective-permute-start | bytes 3538952 | tf_op jit(solution)/shard_map/ppermute | solution.py:403
  22.8 2.6 %shard_map.69.refs_0_.refs_5_ = f32[128,1024]{1,0:T(8,128)} custom-call(s32[56]{0:T(128)} %concatenate.3.s, f32[128,256]{1,0:T(8,128)} %refs_0_, f32[128,256]{1,0:T(8,128)} %copy-done.20, f32[128,256]{1,0:T(8,128)} %copy-done.21, f32[128,256]{1,0:T(8,128)} %copy-done.22), custom_call_target="tpu_custom_call" | custom-call | flops 1000000000 | bytes 1 | tf_op jit(solution)/shard_map/pallas_call | solution.py:100
  27.6 3.3 %shard_map.71.refs_0_.x0 = f32[4,768,128]{2,1,0:T(8,128)} custom-call(s32[56]{0:T(128)} %concatenate.3.s, f32[7,512,128]{2,1,0:T(8,128)} %bitcast.9, f32[7,128,512]{2,1,0:T(8,128)} %bitcast.11), custom_call_target="tpu_custom_call" | custom-call | flops 1000000000 | bytes 1 | tf_op jit(solution)/shard_map/pallas_call | solution.py:100
  32.5 3.6 %shard_map.70 = f32[4,128,1024]{2,1,0:T(8,128)} custom-call(s32[56]{0:T(128)} %concatenate.3.s, f32[128,1024]{1,0:T(8,128)} %shard_map.69.refs_0_.refs_5_, f32[128,1024]{1,0:T(8,128)} %copy-done.6, f32[128,1024]{1,0:T(8,128)} %copy-done.7, f32[128,1024]{1,0:T(8,128)} %copy-done.8), custom_call_target="tpu_custom_call" | custom-call | flops 1000000000 | bytes 1 | tf_op jit(solution)/shard_map/pallas_call | solution.py:100
  36.1 7.3 %collective-permute-done.refs_1_ = f32[3,768,128]{2,1,0:T(8,128)S(1)} collective-permute-done((f32[3,768,128]{2,1,0:T(8,128)}, f32[3,768,128]{2,1,0:T(8,128)S(1)}, u32[]{:S(2)}, u32[]{:S(2)}) %collective-permute-start) | collective-permute-done | bytes 1179680 | tf_op jit(solution)/shard_map/ppermute | solution.py:403
  43.5 23.9 %collective-permute-done.2.refs_3_ = f32[3,768,128]{2,1,0:T(8,128)S(1)} collective-permute-done((f32[3,768,128]{2,1,0:T(8,128)}, f32[3,768,128]{2,1,0:T(8,128)S(1)}, u32[]{:S(2)}, u32[]{:S(2)}) %collective-permute-start.2) | collective-permute-done | bytes 1179680 | tf_op jit(solution)/shard_map/ppermute | solution.py:403
  68.3 5.2 %shard_map.72 = f32[4,3,768,128]{3,2,1,0:T(8,128)} custom-call(s32[56]{0:T(128)} %concatenate.3.s, f32[3,768,128]{2,1,0:T(8,128)} %shard_map.68.refs_0_, f32[3,768,128]{2,1,0:T(8,128)} %copy-done.1, f32[3,768,128]{2,1,0:T(8,128)} %copy-done.2, f32[3,768,128]{2,1,0:T(8,128)} %copy-done.3), custom_call_target="tpu_custom_call" | custom-call | flops 1000000000 | bytes 1 | tf_op jit(solution)/shard_map/pallas_call | solution.py:100
  73.5 2.9 %collective-permute-start.9 = (f32[4,3,768,128]{3,2,1,0:T(8,128)}, f32[4,3,768,128]{3,2,1,0:T(8,128)}, u32[]{:S(2)}, u32[]{:S(2)}) collective-permute-start(f32[4,3,768,128]{3,2,1,0:T(8,128)} %shard_map.72), channel_id=1, source_target_pairs={{1,5},{2,6},{5,1},{6,2},{9,13},{10,14},{13,9},{14,10},{17,21},{18,... | collective-permute-start | bytes 14155784 | tf_op jit(solution)/shard_map/ppermute | solution.py:406
  77.2 8.4 %collective-permute-start.13 = (f32[4,768,128]{2,1,0:T(8,128)S(1)}, f32[4,768,128]{2,1,0:T(8,128)}, u32[]{:S(2)}, u32[]{:S(2)}) collective-permute-start(f32[4,768,128]{2,1,0:T(8,128)S(1)} %copy-done), channel_id=1, source_target_pairs={{0,1},{3,2},{4,5},{7,6},{8,9},{11,10},{12,13},{15,14},{16,17},{19,... | collective-permute-start | bytes 4718600 | tf_op jit(solution)/shard_map/ppermute | solution.py:403
  85.6 1.8 collective-permute-start.14
  87.4 2.8 %collective-permute-start.15 = (f32[4,768,128]{2,1,0:T(8,128)S(1)}, f32[4,768,128]{2,1,0:T(8,128)}, u32[]{:S(2)}, u32[]{:S(2)}) collective-permute-start(f32[4,768,128]{2,1,0:T(8,128)S(1)} %copy-done), channel_id=1, source_target_pairs={{0,2},{3,1},{4,6},{7,5},{8,10},{11,9},{12,14},{15,13},{16,18},{19,... | collective-permute-start | bytes 4718600 | tf_op jit(solution)/shard_map/ppermute | solution.py:403
  90.3 1.3 copy-done.5
  91.6 34.6 %shard_map.73 = (f32[2,1024,512]{2,1,0:T(8,128)}, f32[512,512]{1,0:T(8,128)}, f32[3,1024,128]{2,1,0:T(8,128)}, f32[3,768,128]{2,1,0:T(8,128)}) custom-call(s32[56]{0:T(128)} %concatenate.3.s, f32[3,768,128]{2,1,0:T(8,128)} %shard_map.68.refs_0_, f32[3,768,128]{2,1,0:T(8,128)} %copy-done.1, f32[3,768,128]{2,1,0:T(8,128)} %copy-done.2, ...), custom_call_target="tpu_custom_call" | custom-call | flops 1000000000 | bytes 1 | tf_op jit(solution)/shard_map/pallas_call | solution.py:100
  127.5 24.5 %collective-permute-done.15.refs_3_.x3 = f32[4,768,128]{2,1,0:T(8,128)} collective-permute-done((f32[4,768,128]{2,1,0:T(8,128)S(1)}, f32[4,768,128]{2,1,0:T(8,128)}, u32[]{:S(2)}, u32[]{:S(2)}) %collective-permute-start.15) | collective-permute-done | bytes 1572896 | tf_op jit(solution)/shard_map/ppermute | solution.py:403
  152.0 3.6 %collective-permute-done.11.upper.refs_1_ = f32[3,768,128]{2,1,0:T(8,128)S(1)} collective-permute-done((f32[3,768,128]{2,1,0:T(8,128)}, f32[3,768,128]{2,1,0:T(8,128)S(1)}, u32[]{:S(2)}, u32[]{:S(2)}) %collective-permute-start.11) | collective-permute-done | bytes 1179680 | tf_op jit(solution)/shard_map/ppermute | solution.py:439
  155.6 4.2 %shard_map.75 = f32[2,4,768,128]{3,2,1,0:T(8,128)} custom-call(s32[56]{0:T(128)} %concatenate.3.s, f32[4,768,128]{2,1,0:T(8,128)} %shard_map.71.refs_0_.x0, f32[4,768,128]{2,1,0:T(8,128)} %collective-permute-done.13.refs_1_.x1, f32[4,768,128]{2,1,0:T(8,128)} %collective-permute-done.14.refs_2_.x2, f32[4,768,128]{2,1,0:T(8,128)} %collective-permute-done.15.refs_3_.x3), custom_call_target="tpu_custom_call" | custom-call | flops 1000000000 | bytes 1 | tf_op jit(solution)/shard_map/pallas_call | solution.py:100
  160.7 2.5 %shard_map.74 = f32[768,128]{1,0:T(8,128)} custom-call(s32[56]{0:T(128)} %concatenate.3.s, f32[3,768,128]{2,1,0:T(8,128)} %copy-done.9), custom_call_target="tpu_custom_call" | custom-call | flops 1000000000 | bytes 1 | tf_op jit(solution)/shard_map/pallas_call | solution.py:100
  163.2 2.1 collective-permute-start.12
  165.3 1.6 copy-done.18
  167.0 9.1 %shard_map.76 = (f32[1024,128]{1,0:T(8,128)}, f32[1024,128]{1,0:T(8,128)}, f32[768,128]{1,0:T(8,128)}, f32[768,128]{1,0:T(8,128)}) custom-call(s32[56]{0:T(128)} %concatenate.3.s, f32[4,768,128]{2,1,0:T(8,128)} %shard_map.71.refs_0_.x0, f32[4,768,128]{2,1,0:T(8,128)} %collective-permute-done.13.refs_1_.x1, ...), custom_call_target="tpu_custom_call" | custom-call | flops 10000000000 | bytes 1 | tf_op jit(solution)/shard_map/pallas_call | solution.py:100
  177.3 1.4 collective-permute-start.19
  178.8 9.1 %shard_map.78 = (f32[1024,128]{1,0:T(8,128)}, f32[1024,128]{1,0:T(8,128)}, f32[1024,128]{1,0:T(8,128)}, f32[1024,128]{1,0:T(8,128)}) custom-call(s32[56]{0:T(128)} %concatenate.3.s, f32[4,768,128]{2,1,0:T(8,128)} %shard_map.71.refs_0_.x0, f32[4,768,128]{2,1,0:T(8,128)} %collective-permute-done.13.refs_1_.x1, ...), custom_call_target="tpu_custom_call" | custom-call | flops 10000000000 | bytes 1 | tf_op jit(solution)/shard_map/pallas_call | solution.py:100
  191.3 6.3 %collective-permute-done.19.refs_1_.refs_6_ = f32[768,128]{1,0:T(8,128)S(1)} collective-permute-done((f32[768,128]{1,0:T(8,128)}, f32[768,128]{1,0:T(8,128)S(1)}, u32[]{:S(2)}, u32[]{:S(2)}) %collective-permute-start.19) | collective-permute-done | bytes 393248 | tf_op jit(solution)/shard_map/ppermute | solution.py:455
  198.4 2.3 %shard_map.77 = f32[512,128]{1,0:T(8,128)} custom-call(s32[56]{0:T(128)} %concatenate.3.s, f32[768,128]{1,0:T(8,128)} %copy-done.15, f32[768,128]{1,0:T(8,128)} %copy-done.16), custom_call_target="tpu_custom_call" | custom-call | flops 1000000000 | bytes 1 | tf_op jit(solution)/shard_map/pallas_call | solution.py:100
  200.8 2.5 %collective-permute-start.20 = (f32[512,128]{1,0:T(8,128)}, f32[512,128]{1,0:T(8,128)S(1)}, u32[]{:S(2)}, u32[]{:S(2)}) collective-permute-start(f32[512,128]{1,0:T(8,128)} %shard_map.77), channel_id=1, source_target_pairs={{0,4},{3,7},{4,0},{7,3},{8,12},{11,15},{12,8},{15,11},{16,20},{19,... | collective-permute-start | bytes 786440 | tf_op jit(solution)/shard_map/ppermute | solution.py:464
  203.4 6.4 %collective-permute-done.22.refs_10_ = f32[1024,128]{1,0:T(8,128)S(1)} collective-permute-done((f32[1024,128]{1,0:T(8,128)}, f32[1024,128]{1,0:T(8,128)S(1)}, u32[]{:S(2)}, u32[]{:S(2)}) %collective-permute-start.22) | collective-permute-done | bytes 524320 | tf_op jit(solution)/shard_map/ppermute | solution.py:455
  209.7 10.4 %collective-permute-done.23.refs_11_ = f32[1024,128]{1,0:T(8,128)S(1)} collective-permute-done((f32[1024,128]{1,0:T(8,128)}, f32[1024,128]{1,0:T(8,128)S(1)}, u32[]{:S(2)}, u32[]{:S(2)}) %collective-permute-start.23) | collective-permute-done | bytes 524320 | tf_op jit(solution)/shard_map/ppermute | solution.py:455
  221.2 4.7 %shard_map.79 = (f32[7,512,128]{2,1,0:T(8,128)}, f32[7,512,128]{2,1,0:T(8,128)}) custom-call(s32[56]{0:T(128)} %concatenate.3.s, f32[3,1024,128]{2,1,0:T(8,128)} %get-tuple-element.42.refs_0_, f32[3,768,128]{2,1,0:T(8,128)} %copy-done.9, f32[768,128]{1,0:T(8,128)} %copy-done.14, f32[1024,128]{1,0:T(8,128)} %get-tuple-element.51.refs_3_, ...), custom_call_target="tpu_custom_call" | custom-call | flops 1000000000 | bytes 1 | tf_op jit(solution)/shard_map/pallas_call | solution.py:100
  (77 shorter events, 18.9 us)
Async XLA Ops:
  0.6 16.9 %collective-permute-start.3 = (f32[128,256]{1,0:T(8,128)}, f32[128,256]{1,0:T(8,128)S(1)}, u32[]{:S(2)}, u32[]{:S(2)}) collective-permute-start(f32[128,256]{1,0:T(8,128)} %refs_0_), channel_id=1, source_target_pairs={{0,1},{3,2},{4,5},{7,6},{8,9},{11,10},{12,13},{15,14},{16,17},{19,... | collective-permute-start | bytes 393224 | tf_op jit(solution)/shard_map/ppermute | solution.py:403
  5.6 15.9 %collective-permute-start.4 = (f32[128,256]{1,0:T(8,128)}, f32[128,256]{1,0:T(8,128)S(1)}, u32[]{:S(2)}, u32[]{:S(2)}) collective-permute-start(f32[128,256]{1,0:T(8,128)} %refs_0_), channel_id=1, source_target_pairs={{1,2},{2,1},{5,6},{6,5},{9,10},{10,9},{13,14},{14,13},{17,18},{18,... | collective-permute-start | bytes 393224 | tf_op jit(solution)/shard_map/ppermute | solution.py:403
  6.3 15.3 %collective-permute-start.5 = (f32[128,256]{1,0:T(8,128)}, f32[128,256]{1,0:T(8,128)S(1)}, u32[]{:S(2)}, u32[]{:S(2)}) collective-permute-start(f32[128,256]{1,0:T(8,128)} %refs_0_), channel_id=1, source_target_pairs={{0,2},{3,1},{4,6},{7,5},{8,10},{11,9},{12,14},{15,13},{16,18},{19,... | collective-permute-start | bytes 393224 | tf_op jit(solution)/shard_map/ppermute | solution.py:403
  15.3 28.1 %collective-permute-start = (f32[3,768,128]{2,1,0:T(8,128)}, f32[3,768,128]{2,1,0:T(8,128)S(1)}, u32[]{:S(2)}, u32[]{:S(2)}) collective-permute-start(f32[3,768,128]{2,1,0:T(8,128)} %shard_map.68.refs_0_), channel_id=1, source_target_pairs={{0,1},{3,2},{4,5},{7,6},{8,9},{11,10},{12,13},{15,14},{16,17},{19,... | collective-permute-start | bytes 3538952 | tf_op jit(solution)/shard_map/ppermute | solution.py:403
  16.8 26.6 %collective-permute-start.1 = (f32[3,768,128]{2,1,0:T(8,128)}, f32[3,768,128]{2,1,0:T(8,128)S(1)}, u32[]{:S(2)}, u32[]{:S(2)}) collective-permute-start(f32[3,768,128]{2,1,0:T(8,128)} %shard_map.68.refs_0_), channel_id=1, source_target_pairs={{1,2},{2,1},{5,6},{6,5},{9,10},{10,9},{13,14},{14,13},{17,18},{18,... | collective-permute-start | bytes 3538952 | tf_op jit(solution)/shard_map/ppermute | solution.py:403
  17.6 49.7 %collective-permute-start.2 = (f32[3,768,128]{2,1,0:T(8,128)}, f32[3,768,128]{2,1,0:T(8,128)S(1)}, u32[]{:S(2)}, u32[]{:S(2)}) collective-permute-start(f32[3,768,128]{2,1,0:T(8,128)} %shard_map.68.refs_0_), channel_id=1, source_target_pairs={{0,2},{3,1},{4,6},{7,5},{8,10},{11,9},{12,14},{15,13},{16,18},{19,... | collective-permute-start | bytes 3538952 | tf_op jit(solution)/shard_map/ppermute | solution.py:403
  25.4 1.4 collective-permute-start.6
  26.1 4.8 %collective-permute-start.7 = (f32[128,1024]{1,0:T(8,128)}, f32[128,1024]{1,0:T(8,128)S(1)}, u32[]{:S(2)}, u32[]{:S(2)}) collective-permute-start(f32[128,1024]{1,0:T(8,128)} %shard_map.69.refs_0_.refs_5_), channel_id=1, source_target_pairs={{1,17},{2,18},{5,21},{6,22},{9,25},{10,26},{13,29},{14,30},{17,1},... | collective-permute-start | bytes 1572872 | tf_op jit(solution)/shard_map/ppermute | solution.py:420
  26.9 4.1 %collective-permute-start.8 = (f32[128,1024]{1,0:T(8,128)}, f32[128,1024]{1,0:T(8,128)S(1)}, u32[]{:S(2)}, u32[]{:S(2)}) collective-permute-start(f32[128,1024]{1,0:T(8,128)} %shard_map.69.refs_0_.refs_5_), channel_id=1, source_target_pairs={{1,25},{2,26},{5,29},{6,30},{9,17},{10,18},{13,21},{14,22},{17,9},... | collective-permute-start | bytes 1572872 | tf_op jit(solution)/shard_map/ppermute | solution.py:420
  36.1 40.3 %copy-start.4 = (f32[4,128,1024]{2,1,0:T(8,128)S(1)}, f32[4,128,1024]{2,1,0:T(8,128)}, u32[]{:S(2)}) copy-start(f32[4,128,1024]{2,1,0:T(8,128)} %shard_map.70) | copy-start | bytes 6291460
  36.1 41.0 %copy-start = (f32[4,768,128]{2,1,0:T(8,128)S(1)}, f32[4,768,128]{2,1,0:T(8,128)}, u32[]{:S(2)}) copy-start(f32[4,768,128]{2,1,0:T(8,128)} %shard_map.71.refs_0_.x0) | copy-start | bytes 4718596
  43.4 23.9 %copy-start.1 = (f32[3,768,128]{2,1,0:T(8,128)}, f32[3,768,128]{2,1,0:T(8,128)S(1)}, u32[]{:S(2)}) copy-start(f32[3,768,128]{2,1,0:T(8,128)S(1)} %collective-permute-done.refs_1_) | copy-start | bytes 3538948
  43.4 23.9 %copy-start.2 = (f32[3,768,128]{2,1,0:T(8,128)}, f32[3,768,128]{2,1,0:T(8,128)S(1)}, u32[]{:S(2)}) copy-start(f32[3,768,128]{2,1,0:T(8,128)S(1)} %collective-permute-done.1.refs_2_) | copy-start | bytes 3538948
  73.5 16.8 %collective-permute-start.9 = (f32[4,3,768,128]{3,2,1,0:T(8,128)}, f32[4,3,768,128]{3,2,1,0:T(8,128)}, u32[]{:S(2)}, u32[]{:S(2)}) collective-permute-start(f32[4,3,768,128]{3,2,1,0:T(8,128)} %shard_map.72), channel_id=1, source_target_pairs={{1,5},{2,6},{5,1},{6,2},{9,13},{10,14},{13,9},{14,10},{17,21},{18,... | collective-permute-start | bytes 14155784 | tf_op jit(solution)/shard_map/ppermute | solution.py:406
  76.4 13.9 %collective-permute-start.10 = (f32[4,128,1024]{2,1,0:T(8,128)S(1)}, f32[4,128,1024]{2,1,0:T(8,128)S(1)}, u32[]{:S(2)}, u32[]{:S(2)}) collective-permute-start(f32[4,128,1024]{2,1,0:T(8,128)S(1)} %copy-done.4), channel_id=1, source_target_pairs={{1,5},{2,6},{5,1},{6,2},{9,13},{10,14},{13,9},{14,10},{17,21},{18,... | collective-permute-start | bytes 6291464 | tf_op jit(solution)/shard_map/ppermute | solution.py:406
  77.2 50.3 %collective-permute-start.13 = (f32[4,768,128]{2,1,0:T(8,128)S(1)}, f32[4,768,128]{2,1,0:T(8,128)}, u32[]{:S(2)}, u32[]{:S(2)}) collective-permute-start(f32[4,768,128]{2,1,0:T(8,128)S(1)} %copy-done), channel_id=1, source_target_pairs={{0,1},{3,2},{4,5},{7,6},{8,9},{11,10},{12,13},{15,14},{16,17},{19,... | collective-permute-start | bytes 4718600 | tf_op jit(solution)/shard_map/ppermute | solution.py:403
  85.6 41.9 %collective-permute-start.14 = (f32[4,768,128]{2,1,0:T(8,128)S(1)}, f32[4,768,128]{2,1,0:T(8,128)}, u32[]{:S(2)}, u32[]{:S(2)}) collective-permute-start(f32[4,768,128]{2,1,0:T(8,128)S(1)} %copy-done), channel_id=1, source_target_pairs={{1,2},{2,1},{5,6},{6,5},{9,10},{10,9},{13,14},{14,13},{17,18},{18,... | collective-permute-start | bytes 4718600 | tf_op jit(solution)/shard_map/ppermute | solution.py:403
  87.4 64.5 %collective-permute-start.15 = (f32[4,768,128]{2,1,0:T(8,128)S(1)}, f32[4,768,128]{2,1,0:T(8,128)}, u32[]{:S(2)}, u32[]{:S(2)}) collective-permute-start(f32[4,768,128]{2,1,0:T(8,128)S(1)} %copy-done), channel_id=1, source_target_pairs={{0,2},{3,1},{4,6},{7,5},{8,10},{11,9},{12,14},{15,13},{16,18},{19,... | collective-permute-start | bytes 4718600 | tf_op jit(solution)/shard_map/ppermute | solution.py:403
  126.1 29.5 %collective-permute-start.11 = (f32[3,768,128]{2,1,0:T(8,128)}, f32[3,768,128]{2,1,0:T(8,128)S(1)}, u32[]{:S(2)}, u32[]{:S(2)}) collective-permute-start(f32[3,768,128]{2,1,0:T(8,128)} %get-tuple-element.43), channel_id=1, source_target_pairs={{1,0},{2,3},{5,4},{6,7},{9,8},{10,11},{13,12},{14,15},{17,16},{18,... | collective-permute-start | bytes 3538952 | tf_op jit(solution)/shard_map/ppermute | solution.py:439
  159.8 5.5 %collective-permute-start.16 = (f32[2,4,768,128]{3,2,1,0:T(8,128)}, f32[2,4,768,128]{3,2,1,0:T(8,128)S(1)}, u32[]{:S(2)}, u32[]{:S(2)}) collective-permute-start(f32[2,4,768,128]{3,2,1,0:T(8,128)} %shard_map.75), channel_id=1, source_target_pairs={{1,5},{2,6},{5,1},{6,2},{9,13},{10,14},{13,9},{14,10},{17,21},{18,... | collective-permute-start | bytes 9437192 | tf_op jit(solution)/shard_map/ppermute | solution.py:406
  163.2 37.6 %collective-permute-start.12 = (f32[768,128]{1,0:T(8,128)}, f32[768,128]{1,0:T(8,128)S(1)}, u32[]{:S(2)}, u32[]{:S(2)}) collective-permute-start(f32[768,128]{1,0:T(8,128)} %shard_map.74), channel_id=1, source_target_pairs={{0,4},{3,7},{4,0},{7,3},{8,12},{11,15},{12,8},{15,11},{16,20},{19,... | collective-permute-start | bytes 1179656 | tf_op jit(solution)/shard_map/ppermute | solution.py:464
  176.0 14.0 %collective-permute-start.18 = (f32[768,128]{1,0:T(8,128)}, f32[768,128]{1,0:T(8,128)S(1)}, u32[]{:S(2)}, u32[]{:S(2)}) collective-permute-start(f32[768,128]{1,0:T(8,128)} %get-tuple-element.53), channel_id=1, source_target_pairs={{1,0},{2,3},{5,4},{6,7},{9,8},{10,11},{13,12},{14,15},{17,16},{18,... | collective-permute-start | bytes 1179656 | tf_op jit(solution)/shard_map/ppermute | solution.py:455
  177.3 20.3 %copy-start.19 = (f32[1024,128]{1,0:T(8,128)S(1)}, f32[1024,128]{1,0:T(8,128)}, u32[]{:S(2)}) copy-start(f32[1024,128]{1,0:T(8,128)} %get-tuple-element.52) | copy-start | bytes 1572868
  177.3 20.3 %collective-permute-start.19 = (f32[768,128]{1,0:T(8,128)}, f32[768,128]{1,0:T(8,128)S(1)}, u32[]{:S(2)}, u32[]{:S(2)}) collective-permute-start(f32[768,128]{1,0:T(8,128)} %get-tuple-element.54), channel_id=1, source_target_pairs={{1,4},{2,7},{5,0},{6,3},{9,12},{10,15},{13,8},{14,11},{17,20},{18,... | collective-permute-start | bytes 1179656 | tf_op jit(solution)/shard_map/ppermute | solution.py:455
  187.9 15.4 %collective-permute-start.21 = (f32[1024,128]{1,0:T(8,128)}, f32[1024,128]{1,0:T(8,128)S(1)}, u32[]{:S(2)}, u32[]{:S(2)}) collective-permute-start(f32[1024,128]{1,0:T(8,128)} %get-tuple-element.57), channel_id=1, source_target_pairs={{1,5},{2,6},{5,1},{6,2},{9,13},{10,14},{13,9},{14,10},{17,21},{18,... | collective-permute-start | bytes 1572872 | tf_op jit(solution)/shard_map/ppermute | solution.py:406
  188.6 21.1 %collective-permute-start.22 = (f32[1024,128]{1,0:T(8,128)}, f32[1024,128]{1,0:T(8,128)S(1)}, u32[]{:S(2)}, u32[]{:S(2)}) collective-permute-start(f32[1024,128]{1,0:T(8,128)} %get-tuple-element.58), channel_id=1, source_target_pairs={{1,0},{2,3},{5,4},{6,7},{9,8},{10,11},{13,12},{14,15},{17,16},{18,... | collective-permute-start | bytes 1572872 | tf_op jit(solution)/shard_map/ppermute | solution.py:455
  190.0 30.1 %collective-permute-start.23 = (f32[1024,128]{1,0:T(8,128)}, f32[1024,128]{1,0:T(8,128)S(1)}, u32[]{:S(2)}, u32[]{:S(2)}) collective-permute-start(f32[1024,128]{1,0:T(8,128)} %get-tuple-element.59), channel_id=1, source_target_pairs={{1,4},{2,7},{5,0},{6,3},{9,12},{10,15},{13,8},{14,11},{17,20},{18,... | collective-permute-start | bytes 1572872 | tf_op jit(solution)/shard_map/ppermute | solution.py:455
  197.7 22.5 %collective-permute-start.17 = (f32[1024,128]{1,0:T(8,128)S(1)}, f32[1024,128]{1,0:T(8,128)S(1)}, u32[]{:S(2)}, u32[]{:S(2)}) collective-permute-start(f32[1024,128]{1,0:T(8,128)S(1)} %copy-done.19), channel_id=1, source_target_pairs={{1,5},{2,6},{5,1},{6,2},{9,13},{10,14},{13,9},{14,10},{17,21},{18,... | collective-permute-start | bytes 1572872 | tf_op jit(solution)/shard_map/ppermute | solution.py:406
  200.8 19.4 %copy-start.14 = (f32[768,128]{1,0:T(8,128)}, f32[768,128]{1,0:T(8,128)S(1)}, u32[]{:S(2)}) copy-start(f32[768,128]{1,0:T(8,128)S(1)} %collective-permute-done.12.refs_2_) | copy-start | bytes 1179652
  200.8 19.4 %collective-permute-start.20 = (f32[512,128]{1,0:T(8,128)}, f32[512,128]{1,0:T(8,128)S(1)}, u32[]{:S(2)}, u32[]{:S(2)}) collective-permute-start(f32[512,128]{1,0:T(8,128)} %shard_map.77), channel_id=1, source_target_pairs={{0,4},{3,7},{4,0},{7,3},{8,12},{11,15},{12,8},{15,11},{16,20},{19,... | collective-permute-start | bytes 786440 | tf_op jit(solution)/shard_map/ppermute | solution.py:464
  203.3 16.8 %copy-start.10 = (f32[1024,128]{1,0:T(8,128)}, f32[1024,128]{1,0:T(8,128)S(1)}, u32[]{:S(2)}) copy-start(f32[1024,128]{1,0:T(8,128)S(1)} %collective-permute-done.21.refs_9_) | copy-start | bytes 1572868
  209.7 10.5 %copy-start.11 = (f32[1024,128]{1,0:T(8,128)}, f32[1024,128]{1,0:T(8,128)S(1)}, u32[]{:S(2)}) copy-start(f32[1024,128]{1,0:T(8,128)S(1)} %collective-permute-done.22.refs_10_) | copy-start | bytes 1572868
  (15 other events, 31.1 us)

commit v7 on v4

--- a/solution.py
+++ b/solution.py
@@ -10,7 +10,6 @@
 TILE = 128
 STEP = 2 * TILE
 QUARTER = TILE // 2
-ROWS = 4 * TILE
 F32 = jnp.float32
 BF16 = jnp.bfloat16
 VMEM_LIMIT = 56 * 2**20
@@ -70,22 +69,22 @@
 
 def solve(p, pt, dt, a, dc, f, w, t, weights, emit_ab, emit_dg, join):
     width = dc[0].shape[1]
-    for rows in tiles(p[0].shape[0], ROWS):
+    for rows in tiles(p[0].shape[0]):
         k = rows.start // TILE
         for cols in tiles(width):
             value = dot3(get(p, (rows, ALL)), get(dc, (ALL, cols)))
-            parts = [value[i * TILE:(i + 1) * TILE] * weights[k + i] for i in range(ROWS // TILE)]
-            put(f, (rows, cols), jnp.concatenate(parts, axis=0))
+            value = jnp.concatenate([value[:TILE] * weights[k], value[TILE:] * weights[k + 1]], axis=0)
+            put(f, (rows, cols), value)
     join()
     for cols in tiles(width):
-        for rows in tiles(a[0].shape[0], ROWS):
+        for rows in tiles(a[0].shape[0]):
             value = dot3(get(a, (rows, ALL)), get(f, (ALL, cols)))
             emit_ab(rows, cols, -value)
             put(w, (rows, cols), value)
-        for rows in tiles(pt[0].shape[0], ROWS):
+        for rows in tiles(pt[0].shape[0]):
             value = dot3(get(pt, (rows, ALL)), get(w, (ALL, cols)))
             put(t, (rows, cols), value + dc[0][rows, cols].astype(F32) + dc[1][rows, cols].astype(F32))
-        for rows in tiles(dt[0].shape[0], ROWS):
+        for rows in tiles(dt[0].shape[0]):
             emit_dg(rows, cols, dot3(get(dt, (rows, ALL)), get(t, (ALL, cols))))
 
 
@@ -123,7 +122,7 @@
     )
 
 
-LIST = 4
+LINKS, LIST = 4, 8
 
 
 def tail_of(s, start, own, order):
@@ -131,8 +130,8 @@
     return [jnp.maximum(s[k], 0) for k in spots], [(s[k] >= 0).astype(F32) for k in spots]
 
 
-def weights_of(s, order):
-    return [(s[LIST + j] >= 0).astype(F32) for j in range(order // TILE)]
+def weights_of(s, start, order):
+    return [(s[start + j] >= 0).astype(F32) for j in range(order // TILE)]
 
 
 def pack_kernel(first, s, panels, inverse, *rest):
@@ -163,9 +162,9 @@
     copy_all([(ref, out.at[k]) for k, ref in enumerate(refs[:-2])], sems)
 
 
-def swap_kernel(s, *refs):
+def swap_kernel(skips, s, *refs):
     out, sems = refs[-2:]
-    copy_all([(ref.at[1 - s[0]], out.at[k]) for k, ref in enumerate(refs[:-2])], sems)
+    copy_all([(ref.at[skips[k] + 1 - s[0]], out.at[k]) for k, ref in enumerate(refs[:-2])], sems)
 
 
 def join_block(a, own, corner, rows_of, top, index, weight):
@@ -202,10 +201,10 @@
 
 
 def root_kernel(s, *refs):
-    mine, theirs, sigmas = refs[:4], refs[4], refs[5:13]
-    ext, corners, self_out, end_out = refs[13:17]
-    stage, sigma, sems = refs[17:20]
-    p, d, a, f, w, t, pt, dt = pairs(refs[20:])
+    mine, theirs, sigmas = refs[:4], refs[4], refs[5:10]
+    ext, corners, self_out, end_out = refs[10:14]
+    stage, sigma, sems = refs[14:17]
+    p, d, a, f, w, t, pt, dt = pairs(refs[17:])
     r, c, leaf = s[0], s[1], s[2]
     order = a[0].shape[0]
     own = d[0].shape[0]
@@ -213,7 +212,8 @@
     far = c // 2
     blocks = [x for k in range(4) for x in (mine[k].at[0], theirs.at[k, 0])]
     copies = [pltpu.make_async_copy(ref, stage.at[k], sems.at[0, k]) for k, ref in enumerate(blocks)]
-    later = [pltpu.make_async_copy(ref, sigma.at[k], sems.at[1, k]) for k, ref in enumerate(sigmas)]
+    pieces = list(sigmas[:4]) + [sigmas[4].at[m] for m in range(4)]
+    later = [pltpu.make_async_copy(ref, sigma.at[k], sems.at[1, k]) for k, ref in enumerate(pieces)]
     for one in copies + later:
         one.start()
     for one in copies:
@@ -261,13 +261,18 @@
     later = [pltpu.make_async_copy(root, root_in, sems.at[2, 0]), pltpu.make_async_copy(corners_in, corners, sems.at[2, 1])]
     for one in copies[:8] + later + copies[8:]:
         one.start()
-    for one in copies + later:
+    for one in copies[:8] + later:
         one.wait()
 
     @pl.loop(0, 2)
     def _(node):
         start = LIST + node * (order // TILE)
         index, weight = tail_of(s, start, own, order)
+        @pl.when(node == 1)
+        def _():
+            for one in copies[8:]:
+                one.wait()
+
         load_panels([stage.at[node, k] for k in range(8)], r, p, d, pt, dt, half)
 
         def join():
@@ -277,24 +282,25 @@
                 lambda i: root_in[at(index[i] * TILE, TILE), :], root_in[order:, :], index, weight,
             )
 
-        weights = [(s[start + k] >= 0).astype(F32) for k in range(order // TILE)]
-        solve(p, pt, dt, a, d, f, w, t, weights, *emitters(ab, dg), join)
+        solve(p, pt, dt, a, d, f, w, t, weights_of(s, start, order), *emitters(ab, dg), join)
         columns_out(s, ab, dg, self_out.at[node], end_out.at[node])
         ext[node, 0:half, :] = ab[0:half, :]
         ext[node, half:, :] = dg[...]
 
 
-def leaf_kernel(s, x0, x1, x2, x3, ex, ext, root, self_out, core_out, end_out, cross_out, *rest):
+def leaf_kernel(first, skips, s, x0, x1, x2, x3, ex, ext, root, self_out, core_out, end_out, cross_out, *rest):
     stage, sems, tails, top, grand_in, ab, dg = rest[:7]
     p, d, a, dc, f, w, t, pt, dt = pairs(rest[7:])
     r, c = s[0], s[1]
-    blocks = [x for k, ref in enumerate((x0, x1, x2, x3)) for x in (ref.at[r], ex.at[k])]
+    blocks = [x for k, ref in enumerate((x0, x1, x2, x3)) for x in (ref.at[skips[k] + r], ex.at[k])]
     order = a[0].shape[0]
     own = d[0].shape[0]
     half = order // 2
     far = c // 2
-    index, weight = tail_of(s, LIST, own, order)
-    parent = s[3] - 1
+    node = first + r
+    start = LIST + (node - 1) * (order // TILE)
+    index, weight = tail_of(s, start, own, order)
+    parent = s[LINKS + node - 3] - 1
     copies = [pltpu.make_async_copy(ref, stage.at[k], sems.at[k]) for k, ref in enumerate(blocks)]
     later = [
         pltpu.make_async_copy(ext.at[parent, pl.ds(half, own)], top, sems.at[8]),
@@ -318,7 +324,7 @@
             top[...], index, weight,
         )
 
-    solve(p, pt, dt, a, dc, f, w, t, weights_of(s, order), *emitters(ab, dg), join)
+    solve(p, pt, dt, a, dc, f, w, t, weights_of(s, start, order), *emitters(ab, dg), join)
     near_cols, end_cols = at((1 - far) * TILE, TILE), at(far * TILE, TILE)
     for out, side, cols in (
         (self_out, r, near_cols), (core_out, 1 - r, near_cols), (end_out, r, end_cols), (cross_out, 1 - r, end_cols)
@@ -328,27 +334,21 @@
         out[half:, :] = dg[:, cols] if share == own else dg[at(side * share, share), cols]
 
 
-def shares_kernel(s, root, upper, end, cross, core, out, sems):
-    c = s[1]
-    middle = (c == 1) | (c == 2)
-    half = core.shape[0] // 2
-    share = upper.shape[1] - half
-
-    @pl.when(middle)
-    def _():
-        copy_all([(core, out.at[pl.ds(0, 2 * half)])], sems)
-
-    @pl.when(jnp.logical_not(middle))
-    def _():
-        found = [root, upper.at[0], upper.at[1], end, cross]
-        copy_all([
-            (ref.at[pl.ds(half, share)], out.at[pl.ds(k * share, share)]) for k, ref in enumerate(found)
-        ], sems)
+def shares_kernel(s, *refs):
+    out, sems = refs[-2:]
+    share = out.shape[0] // len(refs[:-2])
+    copy_all([
+        (ref.at[pl.ds(ref.shape[0] - share, share)], out.at[pl.ds(k * share, share)]) for k, ref in enumerate(refs[:-2])
+    ], sems)
+
+
+def upper_shares_kernel(s, root, upper, out, sems):
+    shares_kernel(s, root, upper.at[0], upper.at[1], out, sems)
 
 
 def output_kernel(s, *refs):
-    root_self, root_end, upper_self, upper_end, self_34, end_34, cross_34, shares = refs[:8]
-    self_56, core_56, end_56, cross_56 = refs[8:12]
+    root_self, root_end, upper_self, upper_end, upper_shares, self_34, core_34, end_34, cross_34, shares_34 = refs[:10]
+    self_56, core_56, end_56, cross_56 = refs[10:14]
     ab, dg, sems = refs[-3:]
     r, c = s[0], s[1]
     half = ab.shape[1]
@@ -357,7 +357,7 @@
     for core in range(2):
         @pl.when((r == core) & middle)
         def _():
-            pair = [self_34, shares] if core == 0 else [shares, self_34]
+            pair = [self_34, core_34] if core == 0 else [core_34, self_34]
             last = [self_56, core_56] if core == 0 else [core_56, self_56]
             copies = []
             for node, ref in enumerate([root_self, upper_self.at[0], upper_self.at[1]] + pair + last):
@@ -369,9 +369,10 @@
         def _():
             same, swapped = (3, 4) if core == 0 else (4, 3)
             last = [end_56, cross_56] if core == 0 else [cross_56, end_56]
+            found = [(0, root_end, upper_shares, 0)] + [(k, upper_end.at[k - 1], upper_shares, k) for k in (1, 2)]
+            found += [(same, end_34, shares_34, 1), (swapped, cross_34, shares_34, 0)]
             copies = []
-            found = [(0, root_end, 0), (1, upper_end.at[0], 1), (2, upper_end.at[1], 2)]
-            for node, ref, k in found + [(same, end_34, 4), (swapped, cross_34, 3)]:
+            for node, ref, shares, k in found:
                 copies.append((ref.at[pl.ds(0, half)], ab.at[node]))
                 copies.append((ref.at[pl.ds(half, share)], dg.at[node, pl.ds(core * share, share)]))
                 copies.append((shares.at[pl.ds(k * share, share)], dg.at[node, pl.ds((1 - core) * share, share)]))
@@ -397,7 +398,7 @@
     routes = (((0, 1), (3, 2)), ((1, 2), (2, 1)), ((0, 2), (3, 1)))
     middles = (1, 2)
     swap = [(row * 4 + a, (1 - row) * 4 + a) for row in range(2) for a in middles]
-    swap_all = [(row * 4 + a, (1 - row) * 4 + a) for row in range(2) for a in range(4)]
+    swap_ends = [(row * 4 + a, (1 - row) * 4 + a) for row in range(2) for a in (0, 3)]
     home = ((1, 0), (2, 3))
     home_cross = [(row * 4 + a, (1 - row) * 4 + b) for row in range(2) for a, b in home]
     leaf_routes = [
@@ -411,34 +412,37 @@
     def swapped(x):
         return lax.ppermute(x, both, swap)
 
-    def scalars(parent, *rows):
-        head = jnp.stack([r, c, leaf, parent]).astype(jnp.int32)
-        return jnp.concatenate([head] + [lists[row] for row in rows])
-
-    here = scalars(jnp.int32(0), 0, 1)
+    here = jnp.concatenate([jnp.stack([r, c, leaf, jnp.int32(0)]).astype(jnp.int32), links, lists.reshape(-1)])
+    trunk = 3
     packed = half + own // 2
 
-    pack_t, pack_34, pack_56 = move(
-        functools.partial(pack_kernel, 0), here, [panels, inverse], [(k, packed, TILE) for k in (3, 2, 2)], 35
-    )
+    def pack(first, count, sources):
+        return move(functools.partial(pack_kernel, first), here, sources, [(count, packed, TILE)], 5 * count)[0]
+
     sigma_parts = straight(sigma_top)
+    pack_t = pack(0, trunk, [panels, inverse])
     blocks_t = straight(pack_t)
     sigma_cols = move(join_columns_kernel, here, after(sigma_parts, pack_t), [(TILE, order)], 4)[0]
     sigma_rows = [sigma_cols] + [
         lax.ppermute(sigma_cols, ("leaf", "row", "col"), leaf_routes[m]) for m in range(1, 4)
     ]
-    sigma_other = [swapped(x) for x in sigma_rows]
-    gathered = after(blocks_t, sigma_other)
-    other_t = swapped(move(stack_kernel, here, gathered, [(4, 3, packed, TILE)], 4)[0])
-    blocks_34 = straight(after(pack_34, blocks_t[1:]))
+    sigma_mine = move(stack_kernel, here, sigma_rows, [(4, TILE, order)], 4)[0]
+    sigma_other = swapped(sigma_mine)
+    pack_l = pack(trunk, 4, after([panels, inverse], pack_t))
+    gathered = after(blocks_t, (sigma_mine, pack_l))
+    other_t = swapped(move(stack_kernel, here, gathered, [(4, trunk, packed, TILE)], 4)[0])
+    near, between, far = routes
+    queued = after(pack_l, blocks_t[1:])
+    blocks_l = [pack_l, lax.ppermute(queued, "col", near), lax.ppermute(queued, "col", between)]
+    far_34 = lax.ppermute(queued[:2], "col", far)
     node_scratch = scratch_pairs(
         (order, own), (own, own), (order, order), (order, own), (order, own), (own, own), (own, order), (own, own)
     )
     root, corners, root_self, root_end = call(
-        root_kernel, here, blocks_t + [other_t] + sigma_rows + sigma_other,
+        root_kernel, here, blocks_t + [other_t] + sigma_rows + [sigma_other],
         [(order + own, own), (2, order - own, order - own), (half + own, TILE), (packed, TILE)],
         [pltpu.VMEM((8, packed, TILE), F32), pltpu.VMEM((8, TILE, order), F32), pltpu.SemaphoreType.DMA((2, 8))]
-        + node_scratch, [ANY] * 13, micros=10,
+        + node_scratch, [ANY] * 10,
     )
     root_home = lax.ppermute(root_end, "col", home)
     ext, upper_self, upper_end = call(
@@ -448,9 +452,9 @@
             pltpu.VMEM((2, 8, packed, TILE), F32), pltpu.VMEM((order + own, own), F32),
             pltpu.VMEM((2, order - own, order - own), F32), pltpu.SemaphoreType.DMA((3, 8)),
             pltpu.VMEM((order, own), F32), pltpu.VMEM((own, own), F32),
-        ] + node_scratch, [ANY] * 7, micros=25,
+        ] + node_scratch, [ANY] * 7,
     )
-    blocks_56 = straight(after(pack_56, (blocks_34[1:], ext)))
+    far_56 = lax.ppermute(after(pack_l[2:], ext), "col", far)
     upper_home = lax.ppermute(upper_end, "col", home)
     tails = (order - own) // TILE
     leaf_scratch = [
@@ -462,28 +466,30 @@
         (own, own),
     )
 
-    def leaves(blocks, first, earlier, end_rows):
-        node = first + r
-        parent = lax.dynamic_index_in_dim(links, node - 3, 0, keepdims=False)
-        theirs = swapped(move(swap_kernel, here, after(blocks, earlier), [(4, packed, TILE)], 4)[0])
+    def leaves(first, last, skips, earlier, end_rows):
+        blocks = after(blocks_l + [last], earlier)
+        theirs = swapped(move(functools.partial(swap_kernel, skips), here, blocks, [(4, packed, TILE)], 4)[0])
         self_out, core_out, end_out, cross_out = call(
-            leaf_kernel, scalars(parent, node - 1), blocks + [theirs, ext, root],
+            functools.partial(leaf_kernel, first, skips), here, blocks + [theirs, ext, root],
             [(half + own, TILE)] * 2 + [(end_rows, TILE)] * 2, leaf_scratch, [ANY] * 7, micros=10,
         )
         return self_out, core_out, lax.ppermute(end_out, "col", home), lax.ppermute(cross_out, both, home_cross)
 
-    self_34, core_34, end_34, cross_34 = leaves(blocks_34, 3, (ext, root_home), packed)
-    shares = move(
-        shares_kernel, here, [root_home, upper_home, end_34, cross_34, core_34], [(5 * (own // 2), TILE)], 5
-    )[0]
-    shares = lax.ppermute(shares, both, swap_all)
-    self_56, core_56, end_56, cross_56 = leaves(blocks_56, 5, (upper_home, end_34, cross_34), half + own)
+    self_34, core_34, end_34, cross_34 = leaves(3, far_34, (0, 0, 0, 0), (ext, root_home), packed)
+    self_56, core_56, end_56, cross_56 = leaves(5, far_56, (2, 2, 2, 0), (self_34, upper_home), half + own)
+
+    def shared(kernel, parts, count):
+        out = move(kernel, here, parts, [(count * (own // 2), TILE)], count)[0]
+        return lax.ppermute(out, both, swap_ends)
+
+    upper_shares = shared(upper_shares_kernel, after([root_home, upper_home], self_56), 3)
+    shares_34 = shared(shares_kernel, [end_34, cross_34], 2)
     count = panels.shape[0]
     ancestor_block, diagonal_block = move(
         output_kernel, here,
         [
-            root_self, root_home, upper_self, upper_home, self_34, end_34, cross_34, shares, self_56, swapped(core_56),
-            end_56, cross_56,
+            root_self, root_home, upper_self, upper_home, upper_shares, self_34, swapped(core_34), end_34, cross_34, shares_34, self_56,
+            swapped(core_56), end_56, cross_56,
         ],
         [(count, half, TILE), (count, own, TILE)], 3 * count,
     )

time: 263 us -> 225 us (0.86)
  waiting for transfers between devices: 90.5 us -> 58.5 us
  starting transfers between devices: 63.4 us -> 56.8 us
    ppermute x12 -> x6, starting transfers between devices: 45.1 us -> 15.7 us  [straight(): return [x] + [lax.ppermute(x, 'col', route) for route in routes]]
    ppermute x1 -> x6, starting transfers between devices: 0.92 us -> 25.2 us  [the longest x1 8.07 us: chip_body(): lax.ppermute(queued, 'col', near)]
    ppermute x12 -> x6, waiting for transfers between devices: 48.7 us -> 31.2 us  [straight(): return [x] + [lax.ppermute(x, 'col', route) for route in routes]]
    ppermute x2, waiting for transfers between devices: 15.6 us -> 5.25 us  [leaves(): lax.ppermute(end_out, 'col', home)]
    ppermute x1, waiting for transfers between devices: 9.14 us -> 5.03 us  [chip_body(): upper_home = lax.ppermute(upper_end, 'col', home)]
    unnamed x66 -> x60, local copies, waits for them, and re-layouts: 7.29 us -> 11.2 us
    ppermute x2, waiting for transfers between devices: 17.1 us -> 13.4 us  [leaves(): lax.ppermute(cross_out, both, home_cross)]
    ppermute x1 -> x6, waiting for transfers between devices: 0.01 us -> 3.64 us  [the longest x1 1.92 us: chip_body(): far_56 = lax.ppermute(after(pack_l[2:], ext), 'col', far)]
  transfers between devices with their start and end apart: 30 -> 27, of which waited for: 8 -> 9; matrix products, arithmetic and copies ran while one was open for 2% -> 1% of each run, Pallas kernels for 29% -> 34%
where the time goes in v7:
time: 225 us; the launch traced here: 224 us
  Pallas kernels  92.9 us (41%)
  waiting for transfers between devices  58.5 us (26%)
  starting transfers between devices  56.8 us (25%)
  local copies, waits for them, and re-layouts  13.6 us (6%)
    pallas_call x14, Pallas kernels, call(): pl.pallas_call(kernel, out_shape=[jax.ShapeDtypeStruct(o, F32) for o in o...  92.9 us
    ppermute x6, waiting for transfers between devices, straight(): return [x] + [lax.ppermute(x, 'col', route) for route in routes]  31.2 us
    ppermute x6, starting transfers between devices, straight(): return [x] + [lax.ppermute(x, 'col', route) for route in routes]  15.7 us
    ppermute x2, waiting for transfers between devices, leaves(): lax.ppermute(cross_out, both, home_cross)  13.4 us
    unnamed x60, local copies, waits for them, and re-layouts  11.2 us
    ppermute x1, starting transfers between devices, chip_body(): lax.ppermute(queued, 'col', near)  8.07 us
    ppermute x1, starting transfers between devices, chip_body(): far_56 = lax.ppermute(after(pack_l[2:], ext), 'col', far)  6.77 us
    ppermute x6, starting transfers between devices, swapped(): return lax.ppermute(x, both, swap)  5.87 us
  transfers between devices with their start and end apart: 27, of which 9 were waited for; matrix products, arithmetic and copies ran while one was open for 1% of the time, Pallas kernels for 34%

profile of v7, /device:TPU:0, one launch (start us, length us, event | category | flops | bytes accessed | tf_op | source)
XLA Modules:
  0.0 223.9 jit_solution(12952516428478800545)
XLA Ops:
  0.6 4.9 %collective-permute-start.3 = (f32[128,256]{1,0:T(8,128)}, f32[128,256]{1,0:T(8,128)S(1)}, u32[]{:S(2)}, u32[]{:S(2)}) collective-permute-start(f32[128,256]{1,0:T(8,128)} %refs_0_), channel_id=1, source_target_pairs={{0,1},{3,2},{4,5},{7,6},{8,9},{11,10},{12,13},{15,14},{16,17},{19,... | collective-permute-start | bytes 393224 | tf_op jit(solution)/shard_map/ppermute | solution.py:410
  6.3 4.0 %collective-permute-start.5 = (f32[128,256]{1,0:T(8,128)}, f32[128,256]{1,0:T(8,128)S(1)}, u32[]{:S(2)}, u32[]{:S(2)}) collective-permute-start(f32[128,256]{1,0:T(8,128)} %refs_0_), channel_id=1, source_target_pairs={{0,2},{3,1},{4,6},{7,5},{8,10},{11,9},{12,14},{15,13},{16,18},{19,... | collective-permute-start | bytes 393224 | tf_op jit(solution)/shard_map/ppermute | solution.py:410
  12.3 3.1 %shard_map.68.refs_0_ = f32[3,768,128]{2,1,0:T(8,128)} custom-call(s32[56]{0:T(128)} %concatenate.3.s, f32[7,512,128]{2,1,0:T(8,128)} %bitcast.8, f32[7,128,512]{2,1,0:T(8,128)} %bitcast.10), custom_call_target="tpu_custom_call" | custom-call | flops 1000000000 | bytes 1 | tf_op jit(solution)/shard_map/pallas_call | solution.py:100
  17.6 3.9 %collective-permute-start.2 = (f32[3,768,128]{2,1,0:T(8,128)}, f32[3,768,128]{2,1,0:T(8,128)S(1)}, u32[]{:S(2)}, u32[]{:S(2)}) collective-permute-start(f32[3,768,128]{2,1,0:T(8,128)} %shard_map.68.refs_0_), channel_id=1, source_target_pairs={{0,2},{3,1},{4,6},{7,5},{8,10},{11,9},{12,14},{15,13},{16,18},{19,... | collective-permute-start | bytes 3538952 | tf_op jit(solution)/shard_map/ppermute | solution.py:410
  22.9 2.6 %shard_map.69.refs_0_.refs_5_ = f32[128,1024]{1,0:T(8,128)} custom-call(s32[56]{0:T(128)} %concatenate.3.s, f32[128,256]{1,0:T(8,128)} %refs_0_, f32[128,256]{1,0:T(8,128)} %copy-done.27, f32[128,256]{1,0:T(8,128)} %copy-done.28, f32[128,256]{1,0:T(8,128)} %copy-done.29), custom_call_target="tpu_custom_call" | custom-call | flops 1000000000 | bytes 1 | tf_op jit(solution)/shard_map/pallas_call | solution.py:100
  27.6 3.4 %shard_map.71.refs_0_.x0 = f32[4,768,128]{2,1,0:T(8,128)} custom-call(s32[56]{0:T(128)} %concatenate.3.s, f32[7,512,128]{2,1,0:T(8,128)} %bitcast.9, f32[7,128,512]{2,1,0:T(8,128)} %bitcast.11), custom_call_target="tpu_custom_call" | custom-call | flops 1000000000 | bytes 1 | tf_op jit(solution)/shard_map/pallas_call | solution.py:100
  32.6 3.6 %shard_map.70 = f32[4,128,1024]{2,1,0:T(8,128)} custom-call(s32[56]{0:T(128)} %concatenate.3.s, f32[128,1024]{1,0:T(8,128)} %shard_map.69.refs_0_.refs_5_, f32[128,1024]{1,0:T(8,128)} %copy-done.7, f32[128,1024]{1,0:T(8,128)} %copy-done.8, f32[128,1024]{1,0:T(8,128)} %copy-done.9), custom_call_target="tpu_custom_call" | custom-call | flops 1000000000 | bytes 1 | tf_op jit(solution)/shard_map/pallas_call | solution.py:100
  36.2 7.3 %collective-permute-done.refs_1_ = f32[3,768,128]{2,1,0:T(8,128)S(1)} collective-permute-done((f32[3,768,128]{2,1,0:T(8,128)}, f32[3,768,128]{2,1,0:T(8,128)S(1)}, u32[]{:S(2)}, u32[]{:S(2)}) %collective-permute-start) | collective-permute-done | bytes 1179680 | tf_op jit(solution)/shard_map/ppermute | solution.py:410
  43.5 23.9 %collective-permute-done.2.refs_3_ = f32[3,768,128]{2,1,0:T(8,128)S(1)} collective-permute-done((f32[3,768,128]{2,1,0:T(8,128)}, f32[3,768,128]{2,1,0:T(8,128)S(1)}, u32[]{:S(2)}, u32[]{:S(2)}) %collective-permute-start.2) | collective-permute-done | bytes 1179680 | tf_op jit(solution)/shard_map/ppermute | solution.py:410
  68.4 5.2 %shard_map.72 = f32[4,3,768,128]{3,2,1,0:T(8,128)} custom-call(s32[56]{0:T(128)} %concatenate.3.s, f32[3,768,128]{2,1,0:T(8,128)} %shard_map.68.refs_0_, f32[3,768,128]{2,1,0:T(8,128)} %copy-done.3, f32[3,768,128]{2,1,0:T(8,128)} %copy-done.4, f32[3,768,128]{2,1,0:T(8,128)} %copy-done.5), custom_call_target="tpu_custom_call" | custom-call | flops 1000000000 | bytes 1 | tf_op jit(solution)/shard_map/pallas_call | solution.py:100
  74.6 2.0 collective-permute-start.10
  76.6 8.1 %collective-permute-start.13 = (f32[4,768,128]{2,1,0:T(8,128)S(1)}, f32[4,768,128]{2,1,0:T(8,128)S(1)}, u32[]{:S(2)}, u32[]{:S(2)}) collective-permute-start(f32[4,768,128]{2,1,0:T(8,128)S(1)} %copy-done), channel_id=1, source_target_pairs={{0,1},{3,2},{4,5},{7,6},{8,9},{11,10},{12,13},{15,14},{16,17},{19,... | collective-permute-start | bytes 4718600 | tf_op jit(solution)/shard_map/ppermute | solution.py:436
  84.6 1.8 collective-permute-start.14
  87.5 3.6 %collective-permute-start.16 = (f32[2,768,128]{2,1,0:T(8,128)}, f32[2,768,128]{2,1,0:T(8,128)}, u32[]{:S(2)}, u32[]{:S(2)}) collective-permute-start(f32[2,768,128]{2,1,0:T(8,128)} %slice.7), channel_id=1, source_target_pairs={{0,2},{3,1},{4,6},{7,5},{8,10},{11,9},{12,14},{15,13},{16,18},{19,... | collective-permute-start | bytes 2359304 | tf_op jit(solution)/shard_map/ppermute | solution.py:437
  91.1 2.2 copy-done.2
  93.3 15.3 %shard_map.73 = (f32[1536,512]{1,0:T(8,128)}, f32[2,512,512]{2,1,0:T(8,128)}, f32[1024,128]{1,0:T(8,128)}, f32[768,128]{1,0:T(8,128)}) custom-call(s32[56]{0:T(128)} %concatenate.3.s, f32[3,768,128]{2,1,0:T(8,128)} %shard_map.68.refs_0_, f32[3,768,128]{2,1,0:T(8,128)} %copy-done.3, f32[3,768,128]{2,1,0:T(8,128)} %copy-done.4, f32[3,768,128]{2,1,0:T(8,128)} %copy-done.5, ...), custom_call_target="tpu_custom_call" | custom-call | flops 1000000000 | bytes 1 | tf_op jit(solution)/shard_map/pallas_call | solution.py:100
  110.0 25.4 %shard_map.74 = (f32[2,1024,512]{2,1,0:T(8,128)}, f32[2,1024,128]{2,1,0:T(8,128)}, f32[2,768,128]{2,1,0:T(8,128)}) custom-call(s32[56]{0:T(128)} %concatenate.3.s, f32[3,768,128]{2,1,0:T(8,128)} %shard_map.68.refs_0_, f32[3,768,128]{2,1,0:T(8,128)} %copy-done.3, f32[3,768,128]{2,1,0:T(8,128)} %copy-done.4, f32[3,768,128]{2,1,0:T(8,128)} %copy-done.5, ...), custom_call_target="tpu_custom_call" | custom-call | flops 1000000000 | bytes 1 | tf_op jit(solution)/shard_map/pallas_call | solution.py:100
  136.6 3.4 %shard_map.75 = f32[4,768,128]{2,1,0:T(8,128)} custom-call(s32[56]{0:T(128)} %concatenate.3.s, f32[4,768,128]{2,1,0:T(8,128)} %shard_map.71.refs_0_.x0, f32[4,768,128]{2,1,0:T(8,128)} %copy-done.6, f32[4,768,128]{2,1,0:T(8,128)} %collective-permute-done.14.refs_2_.x2, f32[2,768,128]{2,1,0:T(8,128)} %collective-permute-done.16.refs_3_.x3), custom_call_target="tpu_custom_call" | custom-call | flops 1000000000 | bytes 1 | tf_op jit(solution)/shard_map/pallas_call | solution.py:100
  142.1 6.8 %collective-permute-start.15 = (f32[2,768,128]{2,1,0:T(8,128)S(1)}, f32[2,768,128]{2,1,0:T(8,128)S(1)}, u32[]{:S(2)}, u32[]{:S(2)}) collective-permute-start(f32[2,768,128]{2,1,0:T(8,128)S(1)} %slice.8), channel_id=1, source_target_pairs={{0,2},{3,1},{4,6},{7,5},{8,10},{11,9},{12,14},{15,13},{16,18},{19,... | collective-permute-start | bytes 2359304 | tf_op jit(solution)/shard_map/ppermute | solution.py:457
  150.0 9.0 %shard_map.76 = (f32[1024,128]{1,0:T(8,128)}, f32[1024,128]{1,0:T(8,128)}, f32[768,128]{1,0:T(8,128)}, f32[768,128]{1,0:T(8,128)}) custom-call(s32[56]{0:T(128)} %concatenate.3.s, f32[4,768,128]{2,1,0:T(8,128)} %shard_map.71.refs_0_.x0, f32[4,768,128]{2,1,0:T(8,128)} %copy-done.6, f32[4,768,128]{2,1,0:T(8,128)} %collective-permute-done.14.refs_2_.x2, ...), custom_call_target="tpu_custom_call" | custom-call | flops 10000000000 | bytes 1 | tf_op jit(solution)/shard_map/pallas_call | solution.py:100
  159.1 5.0 %collective-permute-done.12.upper.refs_3_ = f32[2,768,128]{2,1,0:T(8,128)S(1)} collective-permute-done((f32[2,768,128]{2,1,0:T(8,128)S(1)}, f32[2,768,128]{2,1,0:T(8,128)S(1)}, u32[]{:S(2)}, u32[]{:S(2)}) %collective-permute-start.12) | collective-permute-done | bytes 786464 | tf_op jit(solution)/shard_map/ppermute | solution.py:458
  164.1 1.9 collective-permute-done.15.refs_3_.x3
  166.9 3.4 %shard_map.77 = f32[4,768,128]{2,1,0:T(8,128)} custom-call(s32[56]{0:T(128)} %concatenate.3.s, f32[4,768,128]{2,1,0:T(8,128)} %shard_map.71.refs_0_.x0, f32[4,768,128]{2,1,0:T(8,128)} %copy-done.6, f32[4,768,128]{2,1,0:T(8,128)} %collective-permute-done.14.refs_2_.x2, f32[2,768,128]{2,1,0:T(8,128)} %copy-done.10), custom_call_target="tpu_custom_call" | custom-call | flops 1000000000 | bytes 1 | tf_op jit(solution)/shard_map/pallas_call | solution.py:100
  175.6 9.1 %shard_map.78 = (f32[1024,128]{1,0:T(8,128)}, f32[1024,128]{1,0:T(8,128)}, f32[1024,128]{1,0:T(8,128)}, f32[1024,128]{1,0:T(8,128)}) custom-call(s32[56]{0:T(128)} %concatenate.3.s, f32[4,768,128]{2,1,0:T(8,128)} %shard_map.71.refs_0_.x0, f32[4,768,128]{2,1,0:T(8,128)} %copy-done.6, f32[4,768,128]{2,1,0:T(8,128)} %collective-permute-done.14.refs_2_.x2, ...), custom_call_target="tpu_custom_call" | custom-call | flops 10000000000 | bytes 1 | tf_op jit(solution)/shard_map/pallas_call | solution.py:100
  189.8 2.5 %shard_map.79 = f32[768,128]{1,0:T(8,128)} custom-call(s32[56]{0:T(128)} %concatenate.3.s, f32[768,128]{1,0:T(8,128)} %copy-done.16, f32[2,768,128]{2,1,0:T(8,128)} %copy-done.11), custom_call_target="tpu_custom_call" | custom-call | flops 1000000000 | bytes 1 | tf_op jit(solution)/shard_map/pallas_call | solution.py:100
  192.3 3.4 %collective-permute-done.22.refs_1_.refs_8_ = f32[768,128]{1,0:T(8,128)S(1)} collective-permute-done((f32[768,128]{1,0:T(8,128)S(1)}, f32[768,128]{1,0:T(8,128)S(1)}, u32[]{:S(2)}, u32[]{:S(2)}) %collective-permute-start.22) | collective-permute-done | bytes 393248 | tf_op jit(solution)/shard_map/ppermute | solution.py:476
  195.7 3.0 %collective-permute-start.19 = (f32[768,128]{1,0:T(8,128)}, f32[768,128]{1,0:T(8,128)S(1)}, u32[]{:S(2)}, u32[]{:S(2)}) collective-permute-start(f32[768,128]{1,0:T(8,128)} %shard_map.79), channel_id=1, source_target_pairs={{0,4},{3,7},{4,0},{7,3},{8,12},{11,15},{12,8},{15,11},{16,20},{19,... | collective-permute-start | bytes 1179656 | tf_op jit(solution)/shard_map/ppermute | solution.py:483
  198.7 2.3 %shard_map.80 = f32[512,128]{1,0:T(8,128)} custom-call(s32[56]{0:T(128)} %concatenate.3.s, f32[768,128]{1,0:T(8,128)} %copy-done.17, f32[768,128]{1,0:T(8,128)} %copy-done.18), custom_call_target="tpu_custom_call" | custom-call | flops 1000000000 | bytes 1 | tf_op jit(solution)/shard_map/pallas_call | solution.py:100
  201.1 1.9 collective-permute-start.23
  204.7 3.5 %collective-permute-done.25.refs_12_ = f32[1024,128]{1,0:T(8,128)S(1)} collective-permute-done((f32[1024,128]{1,0:T(8,128)}, f32[1024,128]{1,0:T(8,128)S(1)}, u32[]{:S(2)}, u32[]{:S(2)}) %collective-permute-start.25) | collective-permute-done | bytes 524320 | tf_op jit(solution)/shard_map/ppermute | solution.py:476
  208.2 10.0 %collective-permute-done.26.refs_13_ = f32[1024,128]{1,0:T(8,128)S(1)} collective-permute-done((f32[1024,128]{1,0:T(8,128)}, f32[1024,128]{1,0:T(8,128)S(1)}, u32[]{:S(2)}, u32[]{:S(2)}) %collective-permute-start.26) | collective-permute-done | bytes 524320 | tf_op jit(solution)/shard_map/ppermute | solution.py:476
  219.0 4.7 %shard_map.81 = (f32[7,512,128]{2,1,0:T(8,128)}, f32[7,512,128]{2,1,0:T(8,128)}) custom-call(s32[56]{0:T(128)} %concatenate.3.s, f32[1024,128]{1,0:T(8,128)} %get-tuple-element.51.refs_0_, f32[768,128]{1,0:T(8,128)} %copy-done.16, f32[2,1024,128]{2,1,0:T(8,128)} %get-tuple-element.55.refs_2_, f32[2,768,128]{2,1,0:T(8,128)} %copy-done.11, ...), custom_call_target="tpu_custom_call" | custom-call | flops 1000000000 | bytes 1 | tf_op jit(solution)/shard_map/pallas_call | solution.py:100
  (101 shorter events, 32.4 us)
Async XLA Ops:
  0.6 17.0 %collective-permute-start.3 = (f32[128,256]{1,0:T(8,128)}, f32[128,256]{1,0:T(8,128)S(1)}, u32[]{:S(2)}, u32[]{:S(2)}) collective-permute-start(f32[128,256]{1,0:T(8,128)} %refs_0_), channel_id=1, source_target_pairs={{0,1},{3,2},{4,5},{7,6},{8,9},{11,10},{12,13},{15,14},{16,17},{19,... | collective-permute-start | bytes 393224 | tf_op jit(solution)/shard_map/ppermute | solution.py:410
  5.6 16.0 %collective-permute-start.4 = (f32[128,256]{1,0:T(8,128)}, f32[128,256]{1,0:T(8,128)S(1)}, u32[]{:S(2)}, u32[]{:S(2)}) collective-permute-start(f32[128,256]{1,0:T(8,128)} %refs_0_), channel_id=1, source_target_pairs={{1,2},{2,1},{5,6},{6,5},{9,10},{10,9},{13,14},{14,13},{17,18},{18,... | collective-permute-start | bytes 393224 | tf_op jit(solution)/shard_map/ppermute | solution.py:410
  6.3 15.3 %collective-permute-start.5 = (f32[128,256]{1,0:T(8,128)}, f32[128,256]{1,0:T(8,128)S(1)}, u32[]{:S(2)}, u32[]{:S(2)}) collective-permute-start(f32[128,256]{1,0:T(8,128)} %refs_0_), channel_id=1, source_target_pairs={{0,2},{3,1},{4,6},{7,5},{8,10},{11,9},{12,14},{15,13},{16,18},{19,... | collective-permute-start | bytes 393224 | tf_op jit(solution)/shard_map/ppermute | solution.py:410
  15.4 28.1 %collective-permute-start = (f32[3,768,128]{2,1,0:T(8,128)}, f32[3,768,128]{2,1,0:T(8,128)S(1)}, u32[]{:S(2)}, u32[]{:S(2)}) collective-permute-start(f32[3,768,128]{2,1,0:T(8,128)} %shard_map.68.refs_0_), channel_id=1, source_target_pairs={{0,1},{3,2},{4,5},{7,6},{8,9},{11,10},{12,13},{15,14},{16,17},{19,... | collective-permute-start | bytes 3538952 | tf_op jit(solution)/shard_map/ppermute | solution.py:410
  16.9 26.6 %collective-permute-start.1 = (f32[3,768,128]{2,1,0:T(8,128)}, f32[3,768,128]{2,1,0:T(8,128)S(1)}, u32[]{:S(2)}, u32[]{:S(2)}) collective-permute-start(f32[3,768,128]{2,1,0:T(8,128)} %shard_map.68.refs_0_), channel_id=1, source_target_pairs={{1,2},{2,1},{5,6},{6,5},{9,10},{10,9},{13,14},{14,13},{17,18},{18,... | collective-permute-start | bytes 3538952 | tf_op jit(solution)/shard_map/ppermute | solution.py:410
  17.6 49.7 %collective-permute-start.2 = (f32[3,768,128]{2,1,0:T(8,128)}, f32[3,768,128]{2,1,0:T(8,128)S(1)}, u32[]{:S(2)}, u32[]{:S(2)}) collective-permute-start(f32[3,768,128]{2,1,0:T(8,128)} %shard_map.68.refs_0_), channel_id=1, source_target_pairs={{0,2},{3,1},{4,6},{7,5},{8,10},{11,9},{12,14},{15,13},{16,18},{19,... | collective-permute-start | bytes 3538952 | tf_op jit(solution)/shard_map/ppermute | solution.py:410
  25.5 1.4 collective-permute-start.6
  26.2 4.8 %collective-permute-start.7 = (f32[128,1024]{1,0:T(8,128)}, f32[128,1024]{1,0:T(8,128)S(1)}, u32[]{:S(2)}, u32[]{:S(2)}) collective-permute-start(f32[128,1024]{1,0:T(8,128)} %shard_map.69.refs_0_.refs_5_), channel_id=1, source_target_pairs={{1,17},{2,18},{5,21},{6,22},{9,25},{10,26},{13,29},{14,30},{17,1},... | collective-permute-start | bytes 1572872 | tf_op jit(solution)/shard_map/ppermute | solution.py:427
  26.9 4.1 %collective-permute-start.8 = (f32[128,1024]{1,0:T(8,128)}, f32[128,1024]{1,0:T(8,128)S(1)}, u32[]{:S(2)}, u32[]{:S(2)}) collective-permute-start(f32[128,1024]{1,0:T(8,128)} %shard_map.69.refs_0_.refs_5_), channel_id=1, source_target_pairs={{1,25},{2,26},{5,29},{6,30},{9,17},{10,18},{13,21},{14,22},{17,9},... | collective-permute-start | bytes 1572872 | tf_op jit(solution)/shard_map/ppermute | solution.py:427
  36.2 40.4 %copy-start = (f32[4,768,128]{2,1,0:T(8,128)S(1)}, f32[4,768,128]{2,1,0:T(8,128)}, u32[]{:S(2)}) copy-start(f32[4,768,128]{2,1,0:T(8,128)} %shard_map.71.refs_0_.x0) | copy-start | bytes 4718596
  43.5 23.9 %copy-start.3 = (f32[3,768,128]{2,1,0:T(8,128)}, f32[3,768,128]{2,1,0:T(8,128)S(1)}, u32[]{:S(2)}) copy-start(f32[3,768,128]{2,1,0:T(8,128)S(1)} %collective-permute-done.refs_1_) | copy-start | bytes 3538948
  43.5 23.9 %copy-start.4 = (f32[3,768,128]{2,1,0:T(8,128)}, f32[3,768,128]{2,1,0:T(8,128)S(1)}, u32[]{:S(2)}) copy-start(f32[3,768,128]{2,1,0:T(8,128)S(1)} %collective-permute-done.1.refs_2_) | copy-start | bytes 3538948
  73.6 17.5 %collective-permute-start.9 = (f32[4,3,768,128]{3,2,1,0:T(8,128)}, f32[4,3,768,128]{3,2,1,0:T(8,128)S(1)}, u32[]{:S(2)}, u32[]{:S(2)}) collective-permute-start(f32[4,3,768,128]{3,2,1,0:T(8,128)} %shard_map.72), channel_id=1, source_target_pairs={{1,5},{2,6},{5,1},{6,2},{9,13},{10,14},{13,9},{14,10},{17,21},{18,... | collective-permute-start | bytes 14155784 | tf_op jit(solution)/shard_map/ppermute | solution.py:413
  74.6 16.5 %collective-permute-start.10 = (f32[4,128,1024]{2,1,0:T(8,128)}, f32[4,128,1024]{2,1,0:T(8,128)}, u32[]{:S(2)}, u32[]{:S(2)}) collective-permute-start(f32[4,128,1024]{2,1,0:T(8,128)} %shard_map.70), channel_id=1, source_target_pairs={{1,5},{2,6},{5,1},{6,2},{9,13},{10,14},{13,9},{14,10},{17,21},{18,... | collective-permute-start | bytes 6291464 | tf_op jit(solution)/shard_map/ppermute | solution.py:413
  76.6 58.8 %collective-permute-start.13 = (f32[4,768,128]{2,1,0:T(8,128)S(1)}, f32[4,768,128]{2,1,0:T(8,128)S(1)}, u32[]{:S(2)}, u32[]{:S(2)}) collective-permute-start(f32[4,768,128]{2,1,0:T(8,128)S(1)} %copy-done), channel_id=1, source_target_pairs={{0,1},{3,2},{4,5},{7,6},{8,9},{11,10},{12,13},{15,14},{16,17},{19,... | collective-permute-start | bytes 4718600 | tf_op jit(solution)/shard_map/ppermute | solution.py:436
  84.6 50.8 %collective-permute-start.14 = (f32[4,768,128]{2,1,0:T(8,128)S(1)}, f32[4,768,128]{2,1,0:T(8,128)}, u32[]{:S(2)}, u32[]{:S(2)}) collective-permute-start(f32[4,768,128]{2,1,0:T(8,128)S(1)} %copy-done), channel_id=1, source_target_pairs={{1,2},{2,1},{5,6},{6,5},{9,10},{10,9},{13,14},{14,13},{17,18},{18,... | collective-permute-start | bytes 4718600 | tf_op jit(solution)/shard_map/ppermute | solution.py:436
  87.5 47.9 %collective-permute-start.16 = (f32[2,768,128]{2,1,0:T(8,128)}, f32[2,768,128]{2,1,0:T(8,128)}, u32[]{:S(2)}, u32[]{:S(2)}) collective-permute-start(f32[2,768,128]{2,1,0:T(8,128)} %slice.7), channel_id=1, source_target_pairs={{0,2},{3,1},{4,6},{7,5},{8,10},{11,9},{12,14},{15,13},{16,18},{19,... | collective-permute-start | bytes 2359304 | tf_op jit(solution)/shard_map/ppermute | solution.py:437
  108.5 26.9 %collective-permute-start.11 = (f32[768,128]{1,0:T(8,128)}, f32[768,128]{1,0:T(8,128)S(1)}, u32[]{:S(2)}, u32[]{:S(2)}) collective-permute-start(f32[768,128]{1,0:T(8,128)} %get-tuple-element.52), channel_id=1, source_target_pairs={{1,0},{2,3},{5,4},{6,7},{9,8},{10,11},{13,12},{14,15},{17,16},{18,... | collective-permute-start | bytes 1179656 | tf_op jit(solution)/shard_map/ppermute | solution.py:447
  139.9 8.9 %collective-permute-start.17 = (f32[4,768,128]{2,1,0:T(8,128)}, f32[4,768,128]{2,1,0:T(8,128)S(1)}, u32[]{:S(2)}, u32[]{:S(2)}) collective-permute-start(f32[4,768,128]{2,1,0:T(8,128)} %shard_map.75), channel_id=1, source_target_pairs={{1,5},{2,6},{5,1},{6,2},{9,13},{10,14},{13,9},{14,10},{17,21},{18,... | collective-permute-start | bytes 4718600 | tf_op jit(solution)/shard_map/ppermute | solution.py:413
  140.8 23.3 %collective-permute-start.12 = (f32[2,768,128]{2,1,0:T(8,128)S(1)}, f32[2,768,128]{2,1,0:T(8,128)S(1)}, u32[]{:S(2)}, u32[]{:S(2)}) collective-permute-start(f32[2,768,128]{2,1,0:T(8,128)S(1)} %copy-done.23), channel_id=1, source_target_pairs={{1,0},{2,3},{5,4},{6,7},{9,8},{10,11},{13,12},{14,15},{17,16},{18,... | collective-permute-start | bytes 2359304 | tf_op jit(solution)/shard_map/ppermute | solution.py:458
  142.1 24.0 %collective-permute-start.15 = (f32[2,768,128]{2,1,0:T(8,128)S(1)}, f32[2,768,128]{2,1,0:T(8,128)S(1)}, u32[]{:S(2)}, u32[]{:S(2)}) collective-permute-start(f32[2,768,128]{2,1,0:T(8,128)S(1)} %slice.8), channel_id=1, source_target_pairs={{0,2},{3,1},{4,6},{7,5},{8,10},{11,9},{12,14},{15,13},{16,18},{19,... | collective-permute-start | bytes 2359304 | tf_op jit(solution)/shard_map/ppermute | solution.py:457
  164.1 20.6 %copy-start.11 = (f32[2,768,128]{2,1,0:T(8,128)}, f32[2,768,128]{2,1,0:T(8,128)S(1)}, u32[]{:S(2)}) copy-start(f32[2,768,128]{2,1,0:T(8,128)S(1)} %collective-permute-done.12.upper.refs_3_) | copy-start | bytes 2359300
  170.3 4.1 %collective-permute-start.18 = (f32[4,768,128]{2,1,0:T(8,128)}, f32[4,768,128]{2,1,0:T(8,128)S(1)}, u32[]{:S(2)}, u32[]{:S(2)}) collective-permute-start(f32[4,768,128]{2,1,0:T(8,128)} %shard_map.77), channel_id=1, source_target_pairs={{1,5},{2,6},{5,1},{6,2},{9,13},{10,14},{13,9},{14,10},{17,21},{18,... | collective-permute-start | bytes 4718600 | tf_op jit(solution)/shard_map/ppermute | solution.py:413
  171.1 30.0 %collective-permute-start.20 = (f32[1024,128]{1,0:T(8,128)S(1)}, f32[1024,128]{1,0:T(8,128)S(1)}, u32[]{:S(2)}, u32[]{:S(2)}) collective-permute-start(f32[1024,128]{1,0:T(8,128)S(1)} %copy-done.24), channel_id=1, source_target_pairs={{1,5},{2,6},{5,1},{6,2},{9,13},{10,14},{13,9},{14,10},{17,21},{18,... | collective-permute-start | bytes 1572872 | tf_op jit(solution)/shard_map/ppermute | solution.py:413
  171.8 16.7 %collective-permute-start.21 = (f32[768,128]{1,0:T(8,128)S(1)}, f32[768,128]{1,0:T(8,128)S(1)}, u32[]{:S(2)}, u32[]{:S(2)}) collective-permute-start(f32[768,128]{1,0:T(8,128)S(1)} %copy-done.26), channel_id=1, source_target_pairs={{1,0},{2,3},{5,4},{6,7},{9,8},{10,11},{13,12},{14,15},{17,16},{18,... | collective-permute-start | bytes 1179656 | tf_op jit(solution)/shard_map/ppermute | solution.py:476
  173.1 22.6 %collective-permute-start.22 = (f32[768,128]{1,0:T(8,128)S(1)}, f32[768,128]{1,0:T(8,128)S(1)}, u32[]{:S(2)}, u32[]{:S(2)}) collective-permute-start(f32[768,128]{1,0:T(8,128)S(1)} %copy-done.25), channel_id=1, source_target_pairs={{1,4},{2,7},{5,0},{6,3},{9,12},{10,15},{13,8},{14,11},{17,20},{18,... | collective-permute-start | bytes 1179656 | tf_op jit(solution)/shard_map/ppermute | solution.py:476
  184.7 20.0 %collective-permute-start.24 = (f32[1024,128]{1,0:T(8,128)}, f32[1024,128]{1,0:T(8,128)S(1)}, u32[]{:S(2)}, u32[]{:S(2)}) collective-permute-start(f32[1024,128]{1,0:T(8,128)} %get-tuple-element.75), channel_id=1, source_target_pairs={{1,5},{2,6},{5,1},{6,2},{9,13},{10,14},{13,9},{14,10},{17,21},{18,... | collective-permute-start | bytes 1572872 | tf_op jit(solution)/shard_map/ppermute | solution.py:413
  185.4 22.8 %collective-permute-start.25 = (f32[1024,128]{1,0:T(8,128)}, f32[1024,128]{1,0:T(8,128)S(1)}, u32[]{:S(2)}, u32[]{:S(2)}) collective-permute-start(f32[1024,128]{1,0:T(8,128)} %get-tuple-element.76), channel_id=1, source_target_pairs={{1,0},{2,3},{5,4},{6,7},{9,8},{10,11},{13,12},{14,15},{17,16},{18,... | collective-permute-start | bytes 1572872 | tf_op jit(solution)/shard_map/ppermute | solution.py:476
  188.5 29.6 %collective-permute-start.26 = (f32[1024,128]{1,0:T(8,128)}, f32[1024,128]{1,0:T(8,128)S(1)}, u32[]{:S(2)}, u32[]{:S(2)}) collective-permute-start(f32[1024,128]{1,0:T(8,128)} %get-tuple-element.77), channel_id=1, source_target_pairs={{1,4},{2,7},{5,0},{6,3},{9,12},{10,15},{13,8},{14,11},{17,20},{18,... | collective-permute-start | bytes 1572872 | tf_op jit(solution)/shard_map/ppermute | solution.py:476
  195.7 9.0 %collective-permute-start.19 = (f32[768,128]{1,0:T(8,128)}, f32[768,128]{1,0:T(8,128)S(1)}, u32[]{:S(2)}, u32[]{:S(2)}) collective-permute-start(f32[768,128]{1,0:T(8,128)} %shard_map.79), channel_id=1, source_target_pairs={{0,4},{3,7},{4,0},{7,3},{8,12},{11,15},{12,8},{15,11},{16,20},{19,... | collective-permute-start | bytes 1179656 | tf_op jit(solution)/shard_map/ppermute | solution.py:483
  201.1 17.1 %copy-start.12 = (f32[1024,128]{1,0:T(8,128)}, f32[1024,128]{1,0:T(8,128)S(1)}, u32[]{:S(2)}) copy-start(f32[1024,128]{1,0:T(8,128)S(1)} %collective-permute-done.20.refs_6_) | copy-start | bytes 1572868
  201.1 3.6 %collective-permute-start.23 = (f32[512,128]{1,0:T(8,128)}, f32[512,128]{1,0:T(8,128)S(1)}, u32[]{:S(2)}, u32[]{:S(2)}) collective-permute-start(f32[512,128]{1,0:T(8,128)} %shard_map.80), channel_id=1, source_target_pairs={{0,4},{3,7},{4,0},{7,3},{8,12},{11,15},{12,8},{15,11},{16,20},{19,... | collective-permute-start | bytes 786440 | tf_op jit(solution)/shard_map/ppermute | solution.py:483
  (25 other events, 104.5 us)

commit v8 on v7

--- a/solution.py
+++ b/solution.py
@@ -151,12 +151,6 @@
     copy_all(copies, sems)
 
 
-def join_columns_kernel(s, *refs):
-    out, sems = refs[-2:]
-    width = refs[0].shape[1]
-    copy_all([(ref, out.at[:, pl.ds(k * width, width)]) for k, ref in enumerate(refs[:-2])], sems)
-
-
 def stack_kernel(s, *refs):
     out, sems = refs[-2:]
     copy_all([(ref, out.at[k]) for k, ref in enumerate(refs[:-2])], sems)
@@ -205,11 +199,10 @@
     ext, corners, self_out, end_out = refs[10:14]
     stage, sigma, sems = refs[14:17]
     p, d, a, f, w, t, pt, dt = pairs(refs[17:])
-    r, c, leaf = s[0], s[1], s[2]
+    r, leaf = s[0], s[2]
     order = a[0].shape[0]
     own = d[0].shape[0]
     half = order // 2
-    far = c // 2
     blocks = [x for k in range(4) for x in (mine[k].at[0], theirs.at[k, 0])]
     copies = [pltpu.make_async_copy(ref, stage.at[k], sems.at[0, k]) for k, ref in enumerate(blocks)]
     pieces = list(sigmas[:4]) + [sigmas[4].at[m] for m in range(4)]
@@ -221,16 +214,13 @@
     load_panels([stage.at[k] for k in range(8)], r, p, d, pt, dt, half)
 
     def join():
-        places = (c, 3 * far, 3 - c, 3 - 3 * far)
-        span = order // 4
         for one in later:
             one.wait()
         for m in range(4):
             for turn in range(2):
                 side = r if turn == 0 else 1 - r
                 rows = at(((leaf ^ m) * 2 + side) * TILE, TILE)
-                for k in range(4):
-                    put(a, (rows, at(places[k] * span, span)), sigma[4 * turn + m, :, k * span:(k + 1) * span])
+                put(a, (rows, ALL), sigma[4 * turn + m])
 
     ab, dg = ext.at[pl.ds(0, order)], ext.at[pl.ds(order, own)]
     solve(p, pt, dt, a, d, f, w, t, [1.0] * (order // TILE), *emitters(ab, dg), join)
@@ -346,9 +336,8 @@
     shares_kernel(s, root, upper.at[0], upper.at[1], out, sems)
 
 
-def output_kernel(s, *refs):
+def first_output_kernel(s, *refs):
     root_self, root_end, upper_self, upper_end, upper_shares, self_34, core_34, end_34, cross_34, shares_34 = refs[:10]
-    self_56, core_56, end_56, cross_56 = refs[10:14]
     ab, dg, sems = refs[-3:]
     r, c = s[0], s[1]
     half = ab.shape[1]
@@ -358,9 +347,8 @@
         @pl.when((r == core) & middle)
         def _():
             pair = [self_34, core_34] if core == 0 else [core_34, self_34]
-            last = [self_56, core_56] if core == 0 else [core_56, self_56]
             copies = []
-            for node, ref in enumerate([root_self, upper_self.at[0], upper_self.at[1]] + pair + last):
+            for node, ref in enumerate([root_self, upper_self.at[0], upper_self.at[1]] + pair):
                 copies.append((ref.at[pl.ds(0, half)], ab.at[node]))
                 copies.append((ref.at[pl.ds(half, half)], dg.at[node]))
             copy_all(copies, sems)
@@ -368,7 +356,6 @@
         @pl.when((r == core) & jnp.logical_not(middle))
         def _():
             same, swapped = (3, 4) if core == 0 else (4, 3)
-            last = [end_56, cross_56] if core == 0 else [cross_56, end_56]
             found = [(0, root_end, upper_shares, 0)] + [(k, upper_end.at[k - 1], upper_shares, k) for k in (1, 2)]
             found += [(same, end_34, shares_34, 1), (swapped, cross_34, shares_34, 0)]
             copies = []
@@ -376,10 +363,26 @@
                 copies.append((ref.at[pl.ds(0, half)], ab.at[node]))
                 copies.append((ref.at[pl.ds(half, share)], dg.at[node, pl.ds(core * share, share)]))
                 copies.append((shares.at[pl.ds(k * share, share)], dg.at[node, pl.ds((1 - core) * share, share)]))
-            for node, ref in ((5, last[0]), (6, last[1])):
-                copies.append((ref.at[pl.ds(0, half)], ab.at[node]))
-                copies.append((ref.at[pl.ds(half, half)], dg.at[node]))
             copy_all(copies, sems)
+
+
+def last_output_kernel(s, ab_in, dg_in, self_56, core_56, end_56, cross_56, ab, dg, stage, sems):
+    r, c = s[0], s[1]
+    half = ab.shape[1]
+    middle = (c == 1) | (c == 2)
+    for core in range(2):
+        for inner in range(2):
+            @pl.when((r == core) & (middle == (inner == 1)))
+            def _():
+                pair = [self_56, core_56] if inner else [end_56, cross_56]
+                if core == 1:
+                    pair = pair[::-1]
+                copy_all([(ref, stage.at[k]) for k, ref in enumerate(pair)], sems)
+    copies = []
+    for k in range(2):
+        copies.append((stage.at[k, pl.ds(0, half)], ab.at[5 + k]))
+        copies.append((stage.at[k, pl.ds(half, half)], dg.at[5 + k]))
+    copy_all(copies, sems)
 
 
 def after(x, earlier):
@@ -419,10 +422,9 @@
     def pack(first, count, sources):
         return move(functools.partial(pack_kernel, first), here, sources, [(count, packed, TILE)], 5 * count)[0]
 
-    sigma_parts = straight(sigma_top)
+    sigma_cols = lax.all_gather(sigma_top, "col", axis=1, tiled=True)
     pack_t = pack(0, trunk, [panels, inverse])
     blocks_t = straight(pack_t)
-    sigma_cols = move(join_columns_kernel, here, after(sigma_parts, pack_t), [(TILE, order)], 4)[0]
     sigma_rows = [sigma_cols] + [
         lax.ppermute(sigma_cols, ("leaf", "row", "col"), leaf_routes[m]) for m in range(1, 4)
     ]
@@ -476,7 +478,7 @@
         return self_out, core_out, lax.ppermute(end_out, "col", home), lax.ppermute(cross_out, both, home_cross)
 
     self_34, core_34, end_34, cross_34 = leaves(3, far_34, (0, 0, 0, 0), (ext, root_home), packed)
-    self_56, core_56, end_56, cross_56 = leaves(5, far_56, (2, 2, 2, 0), (self_34, upper_home), half + own)
+    self_56, core_56, end_56, cross_56 = leaves(5, far_56, (2, 2, 2, 0), (self_34, upper_home, end_34), half + own)
 
     def shared(kernel, parts, count):
         out = move(kernel, here, parts, [(count * (own // 2), TILE)], count)[0]
@@ -485,14 +487,24 @@
     upper_shares = shared(upper_shares_kernel, after([root_home, upper_home], self_56), 3)
     shares_34 = shared(shares_kernel, [end_34, cross_34], 2)
     count = panels.shape[0]
-    ancestor_block, diagonal_block = move(
-        output_kernel, here,
+    shapes = [(count, half, TILE), (count, own, TILE)]
+    first_outputs = move(
+        first_output_kernel, here,
         [
-            root_self, root_home, upper_self, upper_home, upper_shares, self_34, swapped(core_34), end_34, cross_34, shares_34, self_56,
-            swapped(core_56), end_56, cross_56,
+            root_self, root_home, upper_self, upper_home, upper_shares, self_34, swapped(core_34), end_34, cross_34,
+            shares_34,
         ],
-        [(count, half, TILE), (count, own, TILE)], 3 * count,
+        shapes, 15,
     )
+    ancestor_block, diagonal_block = pl.pallas_call(
+        last_output_kernel,
+        out_shape=[jax.ShapeDtypeStruct(shape, F32) for shape in shapes],
+        in_specs=[pl.BlockSpec(memory_space=pltpu.SMEM)] + [ANY] * 6,
+        out_specs=[ANY] * 2,
+        scratch_shapes=[pltpu.VMEM((2, half + own, TILE), F32), pltpu.SemaphoreType.DMA((4,))],
+        input_output_aliases={1: 0, 2: 1},
+        compiler_params=pltpu.CompilerParams(vmem_limit_bytes=VMEM_LIMIT),
+    )(here, *first_outputs, self_56, swapped(core_56), end_56, cross_56)
     return (ancestor_block[None], diagonal_block[None])
 
 

time: 225 us -> 261 us (1.16)
  blocking collectives: 0 us -> 60.4 us
  waiting for transfers between devices: 58.5 us -> 24.6 us
  starting transfers between devices: 56.8 us -> 66.6 us
    all_gather x0 -> x1, blocking collectives: none -> 60.4 us  [chip_body(): sigma_cols = lax.all_gather(sigma_top, 'col', axis=1, tiled=True)]
    ppermute x6 -> x3, waiting for transfers between devices: 31.2 us -> 0.01 us  [straight(): return [x] + [lax.ppermute(x, 'col', route) for route in routes]]
    ppermute x1, starting transfers between devices: 8.07 us -> 23.9 us  [chip_body(): lax.ppermute(queued, 'col', near)]
    ppermute x6 -> x3, starting transfers between devices: 15.7 us -> 9.66 us  [straight(): return [x] + [lax.ppermute(x, 'col', route) for route in routes]]
    pallas_call x14 -> x13, Pallas kernels: 92.9 us -> 89.8 us  [call(): pl.pallas_call(kernel, out_shape=[jax.ShapeDtypeStruct(o, F32) for o in o...]
    ppermute x2, waiting for transfers between devices: 13.4 us -> 10.3 us  [leaves(): lax.ppermute(cross_out, both, home_cross)]
    pallas_call x0 -> x1, Pallas kernels: none -> 2.86 us  [chip_body(): pl.pallas_call(last_output_kernel, out_shape=[jax.ShapeDtypeStruct(shape,...]
    unnamed x60 -> x56, local copies, waits for them, and re-layouts: 11.2 us -> 11.3 us
  transfers between devices with their start and end apart: 27 -> 24, of which waited for: 9 -> 6; matrix products, arithmetic and copies ran while one was open for 1% -> 0% of each run, Pallas kernels for 34% -> 29%
where the time goes in v8:
time: 261 us; the launch traced here: 260 us
  Pallas kernels  92.7 us (36%)
  starting transfers between devices  66.6 us (26%)
  blocking collectives  60.4 us (23%)
  waiting for transfers between devices  24.6 us (9%)
  local copies, waits for them, and re-layouts  13.6 us (5%)
    pallas_call x13, Pallas kernels, call(): pl.pallas_call(kernel, out_shape=[jax.ShapeDtypeStruct(o, F32) for o in o...  89.8 us
    all_gather x1, blocking collectives, chip_body(): sigma_cols = lax.all_gather(sigma_top, 'col', axis=1, tiled=True)  60.4 us
    ppermute x1, starting transfers between devices, chip_body(): lax.ppermute(queued, 'col', near)  23.9 us
    unnamed x56, local copies, waits for them, and re-layouts  11.3 us
    ppermute x2, waiting for transfers between devices, leaves(): lax.ppermute(cross_out, both, home_cross)  10.3 us
    ppermute x3, starting transfers between devices, straight(): return [x] + [lax.ppermute(x, 'col', route) for route in routes]  9.66 us
    ppermute x1, starting transfers between devices, chip_body(): far_56 = lax.ppermute(after(pack_l[2:], ext), 'col', far)  7.29 us
    ppermute x2, waiting for transfers between devices, leaves(): lax.ppermute(end_out, 'col', home)  7.09 us
  transfers between devices with their start and end apart: 24, of which 6 were waited for; matrix products, arithmetic and copies ran while one was open for 0% of the time, Pallas kernels for 29%

profile of v8, /device:TPU:0, one launch (start us, length us, event | category | flops | bytes accessed | tf_op | source)
XLA Modules:
  0.0 260.0 jit_solution(3373376460262795757)
XLA Ops:
  2.7 3.2 %shard_map.68.refs_0_ = f32[3,768,128]{2,1,0:T(8,128)} custom-call(s32[56]{0:T(128)} %concatenate.3.s, f32[7,512,128]{2,1,0:T(8,128)} %bitcast.8, f32[7,128,512]{2,1,0:T(8,128)} %bitcast.10), custom_call_target="tpu_custom_call" | custom-call | flops 1000000000 | bytes 1 | tf_op jit(solution)/shard_map/pallas_call | solution.py:100
  5.9 5.0 %collective-permute-start = (f32[3,768,128]{2,1,0:T(8,128)}, f32[3,768,128]{2,1,0:T(8,128)S(1)}, u32[]{:S(2)}, u32[]{:S(2)}) collective-permute-start(f32[3,768,128]{2,1,0:T(8,128)} %shard_map.68.refs_0_), channel_id=1, source_target_pairs={{0,1},{3,2},{4,5},{7,6},{8,9},{11,10},{12,13},{15,14},{16,17},{19,... | collective-permute-start | bytes 3538952 | tf_op jit(solution)/shard_map/ppermute | solution.py:413
  11.6 3.9 %collective-permute-start.2 = (f32[3,768,128]{2,1,0:T(8,128)}, f32[3,768,128]{2,1,0:T(8,128)S(1)}, u32[]{:S(2)}, u32[]{:S(2)}) collective-permute-start(f32[3,768,128]{2,1,0:T(8,128)} %shard_map.68.refs_0_), channel_id=1, source_target_pairs={{0,2},{3,1},{4,6},{7,5},{8,10},{11,9},{12,14},{15,13},{16,18},{19,... | collective-permute-start | bytes 3538952 | tf_op jit(solution)/shard_map/ppermute | solution.py:413
  15.6 60.4 %all_gather.3.refs_0_.refs_5_ = f32[128,1024]{1,0:T(8,128)S(1)} all-gather(f32[128,256]{1,0:T(8,128)S(1)} %copy-done.22), channel_id=1, replica_groups=mesh['leaf'=4,'row'=2,'col'=4] {'col'}, dimensions={1}, use_global_device_ids=true | all-gather | bytes 655360 | tf_op jit(solution)/shard_map/all_gather | solution.py:425
  78.1 3.4 %shard_map.70.refs_0_.x0 = f32[4,768,128]{2,1,0:T(8,128)} custom-call(s32[56]{0:T(128)} %concatenate.3.s, f32[7,512,128]{2,1,0:T(8,128)} %bitcast.9, f32[7,128,512]{2,1,0:T(8,128)} %bitcast.11), custom_call_target="tpu_custom_call" | custom-call | flops 1000000000 | bytes 1 | tf_op jit(solution)/shard_map/pallas_call | solution.py:100
  83.1 3.5 %shard_map.69 = f32[4,128,1024]{2,1,0:T(8,128)} custom-call(s32[56]{0:T(128)} %concatenate.3.s, f32[128,1024]{1,0:T(8,128)} %copy-done.7, f32[128,1024]{1,0:T(8,128)} %copy-done.8, f32[128,1024]{1,0:T(8,128)} %copy-done.9, f32[128,1024]{1,0:T(8,128)} %copy-done.10), custom_call_target="tpu_custom_call" | custom-call | flops 1000000000 | bytes 1 | tf_op jit(solution)/shard_map/pallas_call | solution.py:100
  89.1 5.2 %shard_map.71 = f32[4,3,768,128]{3,2,1,0:T(8,128)} custom-call(s32[56]{0:T(128)} %concatenate.3.s, f32[3,768,128]{2,1,0:T(8,128)} %shard_map.68.refs_0_, f32[3,768,128]{2,1,0:T(8,128)} %copy-done.3, f32[3,768,128]{2,1,0:T(8,128)} %copy-done.4, f32[3,768,128]{2,1,0:T(8,128)} %copy-done.5), custom_call_target="tpu_custom_call" | custom-call | flops 1000000000 | bytes 1 | tf_op jit(solution)/shard_map/pallas_call | solution.py:100
  95.3 2.1 collective-permute-start.7
  97.3 23.9 %collective-permute-start.10 = (f32[4,768,128]{2,1,0:T(8,128)S(1)}, f32[4,768,128]{2,1,0:T(8,128)S(1)}, u32[]{:S(2)}, u32[]{:S(2)}) collective-permute-start(f32[4,768,128]{2,1,0:T(8,128)S(1)} %copy-done), channel_id=1, source_target_pairs={{0,1},{3,2},{4,5},{7,6},{8,9},{11,10},{12,13},{15,14},{16,17},{19,... | collective-permute-start | bytes 4718600 | tf_op jit(solution)/shard_map/ppermute | solution.py:438
  121.2 1.9 collective-permute-start.11
  124.0 3.6 %collective-permute-start.13 = (f32[2,768,128]{2,1,0:T(8,128)}, f32[2,768,128]{2,1,0:T(8,128)}, u32[]{:S(2)}, u32[]{:S(2)}) collective-permute-start(f32[2,768,128]{2,1,0:T(8,128)} %slice.7), channel_id=1, source_target_pairs={{0,2},{3,1},{4,6},{7,5},{8,10},{11,9},{12,14},{15,13},{16,18},{19,... | collective-permute-start | bytes 2359304 | tf_op jit(solution)/shard_map/ppermute | solution.py:439
  127.6 2.1 copy-done.2
  129.8 15.2 %shard_map.72 = (f32[1536,512]{1,0:T(8,128)}, f32[2,512,512]{2,1,0:T(8,128)}, f32[1024,128]{1,0:T(8,128)}, f32[768,128]{1,0:T(8,128)}) custom-call(s32[56]{0:T(128)} %concatenate.3.s, f32[3,768,128]{2,1,0:T(8,128)} %shard_map.68.refs_0_, f32[3,768,128]{2,1,0:T(8,128)} %copy-done.3, f32[3,768,128]{2,1,0:T(8,128)} %copy-done.4, f32[3,768,128]{2,1,0:T(8,128)} %copy-done.5, ...), custom_call_target="tpu_custom_call" | custom-call | flops 1000000000 | bytes 1 | tf_op jit(solution)/shard_map/pallas_call | solution.py:100
  144.9 1.5 collective-permute-start.8
  146.4 25.4 %shard_map.73 = (f32[2,1024,512]{2,1,0:T(8,128)}, f32[2,1024,128]{2,1,0:T(8,128)}, f32[2,768,128]{2,1,0:T(8,128)}) custom-call(s32[56]{0:T(128)} %concatenate.3.s, f32[3,768,128]{2,1,0:T(8,128)} %shard_map.68.refs_0_, f32[3,768,128]{2,1,0:T(8,128)} %copy-done.3, f32[3,768,128]{2,1,0:T(8,128)} %copy-done.4, f32[3,768,128]{2,1,0:T(8,128)} %copy-done.5, ...), custom_call_target="tpu_custom_call" | custom-call | flops 1000000000 | bytes 1 | tf_op jit(solution)/shard_map/pallas_call | solution.py:100
  173.1 3.4 %shard_map.74 = f32[4,768,128]{2,1,0:T(8,128)} custom-call(s32[56]{0:T(128)} %concatenate.3.s, f32[4,768,128]{2,1,0:T(8,128)} %shard_map.70.refs_0_.x0, f32[4,768,128]{2,1,0:T(8,128)} %copy-done.6, f32[4,768,128]{2,1,0:T(8,128)} %collective-permute-done.11.refs_2_.x2, f32[2,768,128]{2,1,0:T(8,128)} %collective-permute-done.13.refs_3_.x3), custom_call_target="tpu_custom_call" | custom-call | flops 1000000000 | bytes 1 | tf_op jit(solution)/shard_map/pallas_call | solution.py:100
  177.3 1.3 collective-permute-start.9
  178.6 7.3 %collective-permute-start.12 = (f32[2,768,128]{2,1,0:T(8,128)S(1)}, f32[2,768,128]{2,1,0:T(8,128)S(1)}, u32[]{:S(2)}, u32[]{:S(2)}) collective-permute-start(f32[2,768,128]{2,1,0:T(8,128)S(1)} %slice.8), channel_id=1, source_target_pairs={{0,2},{3,1},{4,6},{7,5},{8,10},{11,9},{12,14},{15,13},{16,18},{19,... | collective-permute-start | bytes 2359304 | tf_op jit(solution)/shard_map/ppermute | solution.py:459
  187.1 9.1 %shard_map.75 = (f32[1024,128]{1,0:T(8,128)}, f32[1024,128]{1,0:T(8,128)}, f32[768,128]{1,0:T(8,128)}, f32[768,128]{1,0:T(8,128)}) custom-call(s32[56]{0:T(128)} %concatenate.3.s, f32[4,768,128]{2,1,0:T(8,128)} %shard_map.70.refs_0_.x0, f32[4,768,128]{2,1,0:T(8,128)} %copy-done.6, f32[4,768,128]{2,1,0:T(8,128)} %collective-permute-done.11.refs_2_.x2, ...), custom_call_target="tpu_custom_call" | custom-call | flops 10000000000 | bytes 1 | tf_op jit(solution)/shard_map/pallas_call | solution.py:100
  196.2 1.3 collective-permute-start.15
  197.5 4.5 %collective-permute-done.9.upper.refs_3_ = f32[2,768,128]{2,1,0:T(8,128)S(1)} collective-permute-done((f32[2,768,128]{2,1,0:T(8,128)S(1)}, f32[2,768,128]{2,1,0:T(8,128)S(1)}, u32[]{:S(2)}, u32[]{:S(2)}) %collective-permute-start.9) | collective-permute-done | bytes 786464 | tf_op jit(solution)/shard_map/ppermute | solution.py:460
  203.1 7.1 %collective-permute-done.15.refs_0_.refs_7_ = f32[768,128]{1,0:T(8,128)S(1)} collective-permute-done((f32[768,128]{1,0:T(8,128)}, f32[768,128]{1,0:T(8,128)S(1)}, u32[]{:S(2)}, u32[]{:S(2)}) %collective-permute-start.15) | collective-permute-done | bytes 393248 | tf_op jit(solution)/shard_map/ppermute | solution.py:478
  210.2 3.3 %shard_map.76 = f32[4,768,128]{2,1,0:T(8,128)} custom-call(s32[56]{0:T(128)} %concatenate.3.s, f32[4,768,128]{2,1,0:T(8,128)} %shard_map.70.refs_0_.x0, f32[4,768,128]{2,1,0:T(8,128)} %copy-done.6, f32[4,768,128]{2,1,0:T(8,128)} %collective-permute-done.11.refs_2_.x2, f32[2,768,128]{2,1,0:T(8,128)} %copy-done.11), custom_call_target="tpu_custom_call" | custom-call | flops 1000000000 | bytes 1 | tf_op jit(solution)/shard_map/pallas_call | solution.py:100
  217.5 9.1 %shard_map.77 = (f32[1024,128]{1,0:T(8,128)}, f32[1024,128]{1,0:T(8,128)}, f32[1024,128]{1,0:T(8,128)}, f32[1024,128]{1,0:T(8,128)}) custom-call(s32[56]{0:T(128)} %concatenate.3.s, f32[4,768,128]{2,1,0:T(8,128)} %shard_map.70.refs_0_.x0, f32[4,768,128]{2,1,0:T(8,128)} %copy-done.6, f32[4,768,128]{2,1,0:T(8,128)} %collective-permute-done.11.refs_2_.x2, ...), custom_call_target="tpu_custom_call" | custom-call | flops 10000000000 | bytes 1 | tf_op jit(solution)/shard_map/pallas_call | solution.py:100
  230.0 2.5 shard_map.78
  232.5 1.9 collective-permute-start.17
  234.4 2.3 shard_map.79
  236.8 2.4 collective-permute-start.20
  239.2 1.4 collective-permute-done.20.refs_9_
  241.4 4.3 %shard_map.80 = (f32[7,512,128]{2,1,0:T(8,128)}, f32[7,512,128]{2,1,0:T(8,128)}) custom-call(s32[56]{0:T(128)} %concatenate.3.s, f32[1024,128]{1,0:T(8,128)} %get-tuple-element.45.refs_0_, f32[768,128]{1,0:T(8,128)} %copy-done.17, f32[2,1024,128]{2,1,0:T(8,128)} %get-tuple-element.49.refs_2_, f32[2,768,128]{2,1,0:T(8,128)} %copy-done.12, ...), custom_call_target="tpu_custom_call" | custom-call | flops 1000000000 | bytes 1 | tf_op jit(solution)/shard_map/pallas_call | solution.py:100
  245.8 10.3 %collective-permute-done.23.cross_56 = f32[1024,128]{1,0:T(8,128)S(1)} collective-permute-done((f32[1024,128]{1,0:T(8,128)}, f32[1024,128]{1,0:T(8,128)S(1)}, u32[]{:S(2)}, u32[]{:S(2)}) %collective-permute-start.23) | collective-permute-done | bytes 524320 | tf_op jit(solution)/shard_map/ppermute | solution.py:478
  256.9 2.9 %shard_map.81 = (f32[7,512,128]{2,1,0:T(8,128)}, f32[7,512,128]{2,1,0:T(8,128)}) custom-call(s32[56]{0:T(128)} %concatenate.3.s, f32[7,512,128]{2,1,0:T(8,128)} %get-tuple-element.69.ab_in, f32[7,512,128]{2,1,0:T(8,128)} %get-tuple-element.70.dg_in, f32[1024,128]{1,0:T(8,128)} %get-tuple-element.64.self_56, ...), custom_call_target="tpu_custom_call", output_to_operand_aliasing={{0}: (1, {}), {1}: (2, {})} | custom-call | tf_op jit(solution)/shard_map/pallas_call | solution.py:499
  (92 shorter events, 24.1 us)
Async XLA Ops:
  2.7 12.9 %copy-start.22 = (f32[128,256]{1,0:T(8,128)S(1)}, f32[128,256]{1,0:T(8,128)}, u32[]{:S(2)}) copy-start(f32[128,256]{1,0:T(8,128)} %param.5) | copy-start | bytes 393220
  5.9 80.7 %collective-permute-start = (f32[3,768,128]{2,1,0:T(8,128)}, f32[3,768,128]{2,1,0:T(8,128)S(1)}, u32[]{:S(2)}, u32[]{:S(2)}) collective-permute-start(f32[3,768,128]{2,1,0:T(8,128)} %shard_map.68.refs_0_), channel_id=1, source_target_pairs={{0,1},{3,2},{4,5},{7,6},{8,9},{11,10},{12,13},{15,14},{16,17},{19,... | collective-permute-start | bytes 3538952 | tf_op jit(solution)/shard_map/ppermute | solution.py:413
  10.9 75.7 %collective-permute-start.1 = (f32[3,768,128]{2,1,0:T(8,128)}, f32[3,768,128]{2,1,0:T(8,128)S(1)}, u32[]{:S(2)}, u32[]{:S(2)}) collective-permute-start(f32[3,768,128]{2,1,0:T(8,128)} %shard_map.68.refs_0_), channel_id=1, source_target_pairs={{1,2},{2,1},{5,6},{6,5},{9,10},{10,9},{13,14},{14,13},{17,18},{18,... | collective-permute-start | bytes 3538952 | tf_op jit(solution)/shard_map/ppermute | solution.py:413
  11.6 75.0 %collective-permute-start.2 = (f32[3,768,128]{2,1,0:T(8,128)}, f32[3,768,128]{2,1,0:T(8,128)S(1)}, u32[]{:S(2)}, u32[]{:S(2)}) collective-permute-start(f32[3,768,128]{2,1,0:T(8,128)} %shard_map.68.refs_0_), channel_id=1, source_target_pairs={{0,2},{3,1},{4,6},{7,5},{8,10},{11,9},{12,14},{15,13},{16,18},{19,... | collective-permute-start | bytes 3538952 | tf_op jit(solution)/shard_map/ppermute | solution.py:413
  76.0 5.5 %copy-start.7 = (f32[128,1024]{1,0:T(8,128)}, f32[128,1024]{1,0:T(8,128)S(1)}, u32[]{:S(2)}) copy-start(f32[128,1024]{1,0:T(8,128)S(1)} %all_gather.3.refs_0_.refs_5_) | copy-start | bytes 1572868
  76.0 1.4 collective-permute-start.3
  76.7 4.8 %collective-permute-start.4 = (f32[128,1024]{1,0:T(8,128)S(1)}, f32[128,1024]{1,0:T(8,128)S(1)}, u32[]{:S(2)}, u32[]{:S(2)}) collective-permute-start(f32[128,1024]{1,0:T(8,128)S(1)} %all_gather.3.refs_0_.refs_5_), channel_id=1, source_target_pairs={{1,17},{2,18},{5,21},{6,22},{9,25},{10,26},{13,29},{14,30},{17,1},... | collective-permute-start | bytes 1572872 | tf_op jit(solution)/shard_map/ppermute | solution.py:429
  77.4 4.1 %collective-permute-start.5 = (f32[128,1024]{1,0:T(8,128)S(1)}, f32[128,1024]{1,0:T(8,128)S(1)}, u32[]{:S(2)}, u32[]{:S(2)}) collective-permute-start(f32[128,1024]{1,0:T(8,128)S(1)} %all_gather.3.refs_0_.refs_5_), channel_id=1, source_target_pairs={{1,25},{2,26},{5,29},{6,30},{9,17},{10,18},{13,21},{14,22},{17,9},... | collective-permute-start | bytes 1572872 | tf_op jit(solution)/shard_map/ppermute | solution.py:429
  86.6 10.7 %copy-start = (f32[4,768,128]{2,1,0:T(8,128)S(1)}, f32[4,768,128]{2,1,0:T(8,128)}, u32[]{:S(2)}) copy-start(f32[4,768,128]{2,1,0:T(8,128)} %shard_map.70.refs_0_.x0) | copy-start | bytes 4718596
  94.3 33.3 %collective-permute-start.6 = (f32[4,3,768,128]{3,2,1,0:T(8,128)}, f32[4,3,768,128]{3,2,1,0:T(8,128)S(1)}, u32[]{:S(2)}, u32[]{:S(2)}) collective-permute-start(f32[4,3,768,128]{3,2,1,0:T(8,128)} %shard_map.71), channel_id=1, source_target_pairs={{1,5},{2,6},{5,1},{6,2},{9,13},{10,14},{13,9},{14,10},{17,21},{18,... | collective-permute-start | bytes 14155784 | tf_op jit(solution)/shard_map/ppermute | solution.py:416
  95.3 32.4 %collective-permute-start.7 = (f32[4,128,1024]{2,1,0:T(8,128)}, f32[4,128,1024]{2,1,0:T(8,128)}, u32[]{:S(2)}, u32[]{:S(2)}) collective-permute-start(f32[4,128,1024]{2,1,0:T(8,128)} %shard_map.69), channel_id=1, source_target_pairs={{1,5},{2,6},{5,1},{6,2},{9,13},{10,14},{13,9},{14,10},{17,21},{18,... | collective-permute-start | bytes 6291464 | tf_op jit(solution)/shard_map/ppermute | solution.py:416
  97.3 74.6 %collective-permute-start.10 = (f32[4,768,128]{2,1,0:T(8,128)S(1)}, f32[4,768,128]{2,1,0:T(8,128)S(1)}, u32[]{:S(2)}, u32[]{:S(2)}) collective-permute-start(f32[4,768,128]{2,1,0:T(8,128)S(1)} %copy-done), channel_id=1, source_target_pairs={{0,1},{3,2},{4,5},{7,6},{8,9},{11,10},{12,13},{15,14},{16,17},{19,... | collective-permute-start | bytes 4718600 | tf_op jit(solution)/shard_map/ppermute | solution.py:438
  121.2 50.7 %collective-permute-start.11 = (f32[4,768,128]{2,1,0:T(8,128)S(1)}, f32[4,768,128]{2,1,0:T(8,128)}, u32[]{:S(2)}, u32[]{:S(2)}) collective-permute-start(f32[4,768,128]{2,1,0:T(8,128)S(1)} %copy-done), channel_id=1, source_target_pairs={{1,2},{2,1},{5,6},{6,5},{9,10},{10,9},{13,14},{14,13},{17,18},{18,... | collective-permute-start | bytes 4718600 | tf_op jit(solution)/shard_map/ppermute | solution.py:438
  124.0 47.9 %collective-permute-start.13 = (f32[2,768,128]{2,1,0:T(8,128)}, f32[2,768,128]{2,1,0:T(8,128)}, u32[]{:S(2)}, u32[]{:S(2)}) collective-permute-start(f32[2,768,128]{2,1,0:T(8,128)} %slice.7), channel_id=1, source_target_pairs={{0,2},{3,1},{4,6},{7,5},{8,10},{11,9},{12,14},{15,13},{16,18},{19,... | collective-permute-start | bytes 2359304 | tf_op jit(solution)/shard_map/ppermute | solution.py:439
  144.9 27.0 %collective-permute-start.8 = (f32[768,128]{1,0:T(8,128)}, f32[768,128]{1,0:T(8,128)S(1)}, u32[]{:S(2)}, u32[]{:S(2)}) collective-permute-start(f32[768,128]{1,0:T(8,128)} %get-tuple-element.46), channel_id=1, source_target_pairs={{1,0},{2,3},{5,4},{6,7},{9,8},{10,11},{13,12},{14,15},{17,16},{18,... | collective-permute-start | bytes 1179656 | tf_op jit(solution)/shard_map/ppermute | solution.py:449
  176.5 9.5 %collective-permute-start.14 = (f32[4,768,128]{2,1,0:T(8,128)}, f32[4,768,128]{2,1,0:T(8,128)S(1)}, u32[]{:S(2)}, u32[]{:S(2)}) collective-permute-start(f32[4,768,128]{2,1,0:T(8,128)} %shard_map.74), channel_id=1, source_target_pairs={{1,5},{2,6},{5,1},{6,2},{9,13},{10,14},{13,9},{14,10},{17,21},{18,... | collective-permute-start | bytes 4718600 | tf_op jit(solution)/shard_map/ppermute | solution.py:416
  177.3 24.6 %collective-permute-start.9 = (f32[2,768,128]{2,1,0:T(8,128)S(1)}, f32[2,768,128]{2,1,0:T(8,128)S(1)}, u32[]{:S(2)}, u32[]{:S(2)}) collective-permute-start(f32[2,768,128]{2,1,0:T(8,128)S(1)} %copy-done.25), channel_id=1, source_target_pairs={{1,0},{2,3},{5,4},{6,7},{9,8},{10,11},{13,12},{14,15},{17,16},{18,... | collective-permute-start | bytes 2359304 | tf_op jit(solution)/shard_map/ppermute | solution.py:460
  178.6 24.5 %collective-permute-start.12 = (f32[2,768,128]{2,1,0:T(8,128)S(1)}, f32[2,768,128]{2,1,0:T(8,128)S(1)}, u32[]{:S(2)}, u32[]{:S(2)}) collective-permute-start(f32[2,768,128]{2,1,0:T(8,128)S(1)} %slice.8), channel_id=1, source_target_pairs={{0,2},{3,1},{4,6},{7,5},{8,10},{11,9},{12,14},{15,13},{16,18},{19,... | collective-permute-start | bytes 2359304 | tf_op jit(solution)/shard_map/ppermute | solution.py:459
  196.2 14.0 %collective-permute-start.15 = (f32[768,128]{1,0:T(8,128)}, f32[768,128]{1,0:T(8,128)S(1)}, u32[]{:S(2)}, u32[]{:S(2)}) collective-permute-start(f32[768,128]{1,0:T(8,128)} %get-tuple-element.59), channel_id=1, source_target_pairs={{1,0},{2,3},{5,4},{6,7},{9,8},{10,11},{13,12},{14,15},{17,16},{18,... | collective-permute-start | bytes 1179656 | tf_op jit(solution)/shard_map/ppermute | solution.py:478
  202.0 24.7 %copy-start.12 = (f32[2,768,128]{2,1,0:T(8,128)}, f32[2,768,128]{2,1,0:T(8,128)S(1)}, u32[]{:S(2)}) copy-start(f32[2,768,128]{2,1,0:T(8,128)S(1)} %collective-permute-done.9.upper.refs_3_) | copy-start | bytes 2359300
  203.1 7.1 %copy-start.11 = (f32[2,768,128]{2,1,0:T(8,128)}, f32[2,768,128]{2,1,0:T(8,128)S(1)}, u32[]{:S(2)}) copy-start(f32[2,768,128]{2,1,0:T(8,128)S(1)} %collective-permute-done.12.refs_3_.x3) | copy-start | bytes 2359300
  210.2 4.8 %copy-start.27 = (f32[768,128]{1,0:T(8,128)S(1)}, f32[768,128]{1,0:T(8,128)}, u32[]{:S(2)}) copy-start(f32[768,128]{1,0:T(8,128)} %get-tuple-element.68) | copy-start | bytes 1179652
  213.6 2.8 %collective-permute-start.16 = (f32[4,768,128]{2,1,0:T(8,128)}, f32[4,768,128]{2,1,0:T(8,128)S(1)}, u32[]{:S(2)}, u32[]{:S(2)}) collective-permute-start(f32[4,768,128]{2,1,0:T(8,128)} %shard_map.76), channel_id=1, source_target_pairs={{1,5},{2,6},{5,1},{6,2},{9,13},{10,14},{13,9},{14,10},{17,21},{18,... | collective-permute-start | bytes 4718600 | tf_op jit(solution)/shard_map/ppermute | solution.py:416
  214.3 22.4 %collective-permute-start.18 = (f32[1024,128]{1,0:T(8,128)S(1)}, f32[1024,128]{1,0:T(8,128)S(1)}, u32[]{:S(2)}, u32[]{:S(2)}) collective-permute-start(f32[1024,128]{1,0:T(8,128)S(1)} %copy-done.26), channel_id=1, source_target_pairs={{1,5},{2,6},{5,1},{6,2},{9,13},{10,14},{13,9},{14,10},{17,21},{18,... | collective-permute-start | bytes 1572872 | tf_op jit(solution)/shard_map/ppermute | solution.py:416
  215.1 17.4 %collective-permute-start.19 = (f32[768,128]{1,0:T(8,128)S(1)}, f32[768,128]{1,0:T(8,128)S(1)}, u32[]{:S(2)}, u32[]{:S(2)}) collective-permute-start(f32[768,128]{1,0:T(8,128)S(1)} %copy-done.27), channel_id=1, source_target_pairs={{1,4},{2,7},{5,0},{6,3},{9,12},{10,15},{13,8},{14,11},{17,20},{18,... | collective-permute-start | bytes 1179656 | tf_op jit(solution)/shard_map/ppermute | solution.py:478
  226.7 19.1 %collective-permute-start.21 = (f32[1024,128]{1,0:T(8,128)}, f32[1024,128]{1,0:T(8,128)S(1)}, u32[]{:S(2)}, u32[]{:S(2)}) collective-permute-start(f32[1024,128]{1,0:T(8,128)} %get-tuple-element.71), channel_id=1, source_target_pairs={{1,5},{2,6},{5,1},{6,2},{9,13},{10,14},{13,9},{14,10},{17,21},{18,... | collective-permute-start | bytes 1572872 | tf_op jit(solution)/shard_map/ppermute | solution.py:416
  227.4 18.4 %collective-permute-start.22 = (f32[1024,128]{1,0:T(8,128)}, f32[1024,128]{1,0:T(8,128)S(1)}, u32[]{:S(2)}, u32[]{:S(2)}) collective-permute-start(f32[1024,128]{1,0:T(8,128)} %get-tuple-element.72), channel_id=1, source_target_pairs={{1,0},{2,3},{5,4},{6,7},{9,8},{10,11},{13,12},{14,15},{17,16},{18,... | collective-permute-start | bytes 1572872 | tf_op jit(solution)/shard_map/ppermute | solution.py:478
  228.7 27.4 %collective-permute-start.23 = (f32[1024,128]{1,0:T(8,128)}, f32[1024,128]{1,0:T(8,128)S(1)}, u32[]{:S(2)}, u32[]{:S(2)}) collective-permute-start(f32[1024,128]{1,0:T(8,128)} %get-tuple-element.73), channel_id=1, source_target_pairs={{1,4},{2,7},{5,0},{6,3},{9,12},{10,15},{13,8},{14,11},{17,20},{18,... | collective-permute-start | bytes 1572872 | tf_op jit(solution)/shard_map/ppermute | solution.py:478
  232.5 8.1 %collective-permute-start.17 = (f32[768,128]{1,0:T(8,128)}, f32[768,128]{1,0:T(8,128)S(1)}, u32[]{:S(2)}, u32[]{:S(2)}) collective-permute-start(f32[768,128]{1,0:T(8,128)} %shard_map.78), channel_id=1, source_target_pairs={{0,4},{3,7},{4,0},{7,3},{8,12},{11,15},{12,8},{15,11},{16,20},{19,... | collective-permute-start | bytes 1179656 | tf_op jit(solution)/shard_map/ppermute | solution.py:485
  236.8 3.8 %collective-permute-start.20 = (f32[512,128]{1,0:T(8,128)}, f32[512,128]{1,0:T(8,128)S(1)}, u32[]{:S(2)}, u32[]{:S(2)}) collective-permute-start(f32[512,128]{1,0:T(8,128)} %shard_map.79), channel_id=1, source_target_pairs={{0,4},{3,7},{4,0},{7,3},{8,12},{11,15},{12,8},{15,11},{16,20},{19,... | collective-permute-start | bytes 786440 | tf_op jit(solution)/shard_map/ppermute | solution.py:485
  245.8 10.3 %copy-start.13 = (f32[1024,128]{1,0:T(8,128)}, f32[1024,128]{1,0:T(8,128)S(1)}, u32[]{:S(2)}) copy-start(f32[1024,128]{1,0:T(8,128)S(1)} %collective-permute-done.21.core_56) | copy-start | bytes 1572868
  245.8 10.3 %copy-start.14 = (f32[1024,128]{1,0:T(8,128)}, f32[1024,128]{1,0:T(8,128)S(1)}, u32[]{:S(2)}) copy-start(f32[1024,128]{1,0:T(8,128)S(1)} %collective-permute-done.22.end_56) | copy-start | bytes 1572868
  (20 other events, 43.3 us)

commit v9 on v8

--- a/solution.py
+++ b/solution.py
@@ -151,14 +151,23 @@
     copy_all(copies, sems)
 
 
+def join_columns_kernel(s, *refs):
+    out, sems = refs[-2:]
+    width = refs[0].shape[1]
+    copy_all([(ref, out.at[:, pl.ds(k * width, width)]) for k, ref in enumerate(refs[:-2])], sems)
+
+
 def stack_kernel(s, *refs):
     out, sems = refs[-2:]
     copy_all([(ref, out.at[k]) for k, ref in enumerate(refs[:-2])], sems)
 
 
 def swap_kernel(skips, s, *refs):
-    out, sems = refs[-2:]
-    copy_all([(ref.at[skips[k] + 1 - s[0]], out.at[k]) for k, ref in enumerate(refs[:-2])], sems)
+    blocks, outs, sems = refs[:4], refs[4:6], refs[6]
+    copies = []
+    for k, ref in enumerate(blocks):
+        copies.append((ref.at[skips[k] + 1 - s[0], pl.ds(0, outs[0].shape[1])], outs[k // 2].at[k % 2]))
+    copy_all(copies, sems)
 
 
 def join_block(a, own, corner, rows_of, top, index, weight):
@@ -195,11 +204,13 @@
 
 
 def root_kernel(s, *refs):
-    mine, theirs, sigmas = refs[:4], refs[4], refs[5:10]
-    ext, corners, self_out, end_out = refs[10:14]
-    stage, sigma, sems = refs[14:17]
-    p, d, a, f, w, t, pt, dt = pairs(refs[17:])
-    r, leaf = s[0], s[2]
+    mine, theirs, sigmas, leaves = refs[:4], refs[4], refs[5:10], refs[10]
+    ext, corners, self_out, sent = refs[11:15]
+    stage, sigma, end_out, sems = refs[15:19]
+    p, d, a, f, w, t, pt, dt = pairs(refs[19:])
+    r, c, leaf = s[0], s[1], s[2]
+    far = c // 2
+    middle = (c == 1) | (c == 2)
     order = a[0].shape[0]
     own = d[0].shape[0]
     half = order // 2
@@ -214,17 +225,30 @@
     load_panels([stage.at[k] for k in range(8)], r, p, d, pt, dt, half)
 
     def join():
+        places = (c, 3 * far, 3 - c, 3 - 3 * far)
+        span = order // 4
         for one in later:
             one.wait()
         for m in range(4):
             for turn in range(2):
                 side = r if turn == 0 else 1 - r
                 rows = at(((leaf ^ m) * 2 + side) * TILE, TILE)
-                put(a, (rows, ALL), sigma[4 * turn + m])
+                for k in range(4):
+                    put(a, (rows, at(places[k] * span, span)), sigma[4 * turn + m, :, k * span:(k + 1) * span])
 
     ab, dg = ext.at[pl.ds(0, order)], ext.at[pl.ds(order, own)]
     solve(p, pt, dt, a, d, f, w, t, [1.0] * (order // TILE), *emitters(ab, dg), join)
     columns_out(s, ab, dg, self_out, end_out)
+    packed = end_out.shape[0]
+
+    @pl.when(middle)
+    def _():
+        sent[0, 0:packed, :] = end_out[...]
+
+    @pl.when(jnp.logical_not(middle))
+    def _():
+        copy_all([(leaves.at[2 + i], sent.at[i, pl.ds(0, packed)]) for i in range(2)], sems.at[2])
+
     for node in range(2):
         index, weight = tail_of(s, LIST + node * (order // TILE), own, order)
         for i in range(len(index)):
@@ -278,11 +302,12 @@
         ext[node, half:, :] = dg[...]
 
 
-def leaf_kernel(first, skips, s, x0, x1, x2, x3, ex, ext, root, self_out, core_out, end_out, cross_out, *rest):
+def leaf_kernel(first, skips, s, x0, x1, x2, x3, ex0, ex1, ext, root, self_out, core_out, end_out, cross_out, *rest):
     stage, sems, tails, top, grand_in, ab, dg = rest[:7]
     p, d, a, dc, f, w, t, pt, dt = pairs(rest[7:])
     r, c = s[0], s[1]
-    blocks = [x for k, ref in enumerate((x0, x1, x2, x3)) for x in (ref.at[skips[k] + r], ex.at[k])]
+    packed = stage.shape[1]
+    blocks = [x for k, ref in enumerate((x0, x1, x2, x3)) for x in (ref.at[skips[k] + r, pl.ds(0, packed)], (ex0, ex1)[k // 2].at[k % 2])]
     order = a[0].shape[0]
     own = d[0].shape[0]
     half = order // 2
@@ -328,12 +353,12 @@
     out, sems = refs[-2:]
     share = out.shape[0] // len(refs[:-2])
     copy_all([
-        (ref.at[pl.ds(ref.shape[0] - share, share)], out.at[pl.ds(k * share, share)]) for k, ref in enumerate(refs[:-2])
+        (ref.at[pl.ds(2 * share, share)], out.at[pl.ds(k * share, share)]) for k, ref in enumerate(refs[:-2])
     ], sems)
 
 
 def upper_shares_kernel(s, root, upper, out, sems):
-    shares_kernel(s, root, upper.at[0], upper.at[1], out, sems)
+    shares_kernel(s, root.at[0], upper.at[0], upper.at[1], out, sems)
 
 
 def first_output_kernel(s, *refs):
@@ -356,7 +381,7 @@
         @pl.when((r == core) & jnp.logical_not(middle))
         def _():
             same, swapped = (3, 4) if core == 0 else (4, 3)
-            found = [(0, root_end, upper_shares, 0)] + [(k, upper_end.at[k - 1], upper_shares, k) for k in (1, 2)]
+            found = [(0, root_end.at[0], upper_shares, 0)] + [(k, upper_end.at[k - 1], upper_shares, k) for k in (1, 2)]
             found += [(same, end_34, shares_34, 1), (swapped, cross_34, shares_34, 0)]
             copies = []
             for node, ref, shares, k in found:
@@ -422,9 +447,10 @@
     def pack(first, count, sources):
         return move(functools.partial(pack_kernel, first), here, sources, [(count, packed, TILE)], 5 * count)[0]
 
-    sigma_cols = lax.all_gather(sigma_top, "col", axis=1, tiled=True)
+    sigma_parts = straight(sigma_top)
     pack_t = pack(0, trunk, [panels, inverse])
     blocks_t = straight(pack_t)
+    sigma_cols = move(join_columns_kernel, here, after(sigma_parts, pack_t), [(TILE, order)], 4)[0]
     sigma_rows = [sigma_cols] + [
         lax.ppermute(sigma_cols, ("leaf", "row", "col"), leaf_routes[m]) for m in range(1, 4)
     ]
@@ -440,13 +466,15 @@
     node_scratch = scratch_pairs(
         (order, own), (own, own), (order, order), (order, own), (order, own), (own, own), (own, order), (own, own)
     )
-    root, corners, root_self, root_end = call(
-        root_kernel, here, blocks_t + [other_t] + sigma_rows + [sigma_other],
-        [(order + own, own), (2, order - own, order - own), (half + own, TILE), (packed, TILE)],
-        [pltpu.VMEM((8, packed, TILE), F32), pltpu.VMEM((8, TILE, order), F32), pltpu.SemaphoreType.DMA((2, 8))]
-        + node_scratch, [ANY] * 10,
+    root, corners, root_self, sent = call(
+        root_kernel, here, blocks_t + [other_t] + sigma_rows + [sigma_other, pack_l],
+        [(order + own, own), (2, order - own, order - own), (half + own, TILE), (2, packed + QUARTER, TILE)],
+        [
+            pltpu.VMEM((8, packed, TILE), F32), pltpu.VMEM((8, TILE, order), F32), pltpu.VMEM((packed, TILE), F32),
+            pltpu.SemaphoreType.DMA((3, 8)),
+        ] + node_scratch, [ANY] * 11,
     )
-    root_home = lax.ppermute(root_end, "col", home)
+    mixed = lax.ppermute(sent, "col", home + far)
     ext, upper_self, upper_end = call(
         middle_kernel, here, blocks_t + [other_t, root, corners],
         [(2, half + own, own), (2, half + own, TILE), (2, packed, TILE)],
@@ -456,7 +484,6 @@
             pltpu.VMEM((order, own), F32), pltpu.VMEM((own, own), F32),
         ] + node_scratch, [ANY] * 7,
     )
-    far_56 = lax.ppermute(after(pack_l[2:], ext), "col", far)
     upper_home = lax.ppermute(upper_end, "col", home)
     tails = (order - own) // TILE
     leaf_scratch = [
@@ -468,30 +495,31 @@
         (own, own),
     )
 
-    def leaves(first, last, skips, earlier, end_rows):
-        blocks = after(blocks_l + [last], earlier)
-        theirs = swapped(move(functools.partial(swap_kernel, skips), here, blocks, [(4, packed, TILE)], 4)[0])
+    def leaves(first, last, skips, earlier, latest, end_rows):
+        blocks = after(blocks_l, earlier) + [last]
+        picked = move(functools.partial(swap_kernel, skips), here, blocks, [(2, packed, TILE)] * 2, 4)
+        theirs = after([swapped(x) for x in picked], latest)
         self_out, core_out, end_out, cross_out = call(
-            functools.partial(leaf_kernel, first, skips), here, blocks + [theirs, ext, root],
-            [(half + own, TILE)] * 2 + [(end_rows, TILE)] * 2, leaf_scratch, [ANY] * 7, micros=10,
+            functools.partial(leaf_kernel, first, skips), here, blocks + theirs + [ext, root],
+            [(half + own, TILE)] * 2 + [(end_rows, TILE)] * 2, leaf_scratch, [ANY] * 8, micros=10,
         )
         return self_out, core_out, lax.ppermute(end_out, "col", home), lax.ppermute(cross_out, both, home_cross)
 
-    self_34, core_34, end_34, cross_34 = leaves(3, far_34, (0, 0, 0, 0), (ext, root_home), packed)
-    self_56, core_56, end_56, cross_56 = leaves(5, far_56, (2, 2, 2, 0), (self_34, upper_home, end_34), half + own)
+    self_34, core_34, end_34, cross_34 = leaves(3, far_34, (0, 0, 0, 0), ext, mixed, packed)
+    self_56, core_56, end_56, cross_56 = leaves(5, mixed, (2, 2, 2, 0), (self_34, upper_home), ext, half + own)
 
     def shared(kernel, parts, count):
         out = move(kernel, here, parts, [(count * (own // 2), TILE)], count)[0]
         return lax.ppermute(out, both, swap_ends)
 
-    upper_shares = shared(upper_shares_kernel, after([root_home, upper_home], self_56), 3)
+    upper_shares = shared(upper_shares_kernel, after([mixed, upper_home], self_56), 3)
     shares_34 = shared(shares_kernel, [end_34, cross_34], 2)
     count = panels.shape[0]
     shapes = [(count, half, TILE), (count, own, TILE)]
     first_outputs = move(
         first_output_kernel, here,
         [
-            root_self, root_home, upper_self, upper_home, upper_shares, self_34, swapped(core_34), end_34, cross_34,
+            root_self, mixed, upper_self, upper_home, upper_shares, self_34, swapped(core_34), end_34, cross_34,
             shares_34,
         ],
         shapes, 15,

time: 261 us -> 240 us (0.920)
  blocking collectives: 60.4 us -> 0 us
  waiting for transfers between devices: 24.6 us -> 77.6 us
  starting transfers between devices: 66.6 us -> 49.7 us
  Pallas kernels: 92.7 us -> 96.7 us
    all_gather x1 -> x0, blocking collectives: 60.4 us -> none  [chip_body(): sigma_cols = lax.all_gather(sigma_top, 'col', axis=1, tiled=True)]
    ppermute x3 -> x6, waiting for transfers between devices: 0.01 us -> 31.2 us  [straight(): return [x] + [lax.ppermute(x, 'col', route) for route in routes]]
    ppermute x1, waiting for transfers between devices: 4.5 us -> 21.4 us  [chip_body(): upper_home = lax.ppermute(upper_end, 'col', home)]
    ppermute x1, starting transfers between devices: 23.9 us -> 7.96 us  [chip_body(): lax.ppermute(queued, 'col', near)]
    ppermute x2 -> x1, waiting for transfers between devices: 1.14 us -> 10.5 us  [chip_body(): mixed = lax.ppermute(sent, 'col', home + far)]
    ppermute x2 -> x1, starting transfers between devices: 8.76 us -> 0.24 us  [chip_body(): mixed = lax.ppermute(sent, 'col', home + far)]
    ppermute x2, waiting for transfers between devices: 7.09 us -> 0.01 us  [leaves(): lax.ppermute(end_out, 'col', home)]
    ppermute x3 -> x6, starting transfers between devices: 9.66 us -> 15.7 us  [straight(): return [x] + [lax.ppermute(x, 'col', route) for route in routes]]
  transfers between devices with their start and end apart: 24 -> 28, of which waited for: 6 -> 8; matrix products, arithmetic and copies ran while one was open for 0% -> 1% of each run, Pallas kernels for 29% -> 36%
where the time goes in v9:
time: 240 us; the launch traced here: 239 us
  Pallas kernels  96.7 us (40%)
  waiting for transfers between devices  77.6 us (32%)
  starting transfers between devices  49.7 us (21%)
  local copies, waits for them, and re-layouts  12.6 us (5%)
    pallas_call x14, Pallas kernels, call(): pl.pallas_call(kernel, out_shape=[jax.ShapeDtypeStruct(o, F32) for o in o...  93.9 us
    ppermute x6, waiting for transfers between devices, straight(): return [x] + [lax.ppermute(x, 'col', route) for route in routes]  31.2 us
    ppermute x1, waiting for transfers between devices, chip_body(): upper_home = lax.ppermute(upper_end, 'col', home)  21.4 us
    ppermute x6, starting transfers between devices, straight(): return [x] + [lax.ppermute(x, 'col', route) for route in routes]  15.7 us
    ppermute x2, waiting for transfers between devices, leaves(): lax.ppermute(cross_out, both, home_cross)  12.6 us
    ppermute x1, waiting for transfers between devices, chip_body(): mixed = lax.ppermute(sent, 'col', home + far)  10.5 us
    unnamed x60, local copies, waits for them, and re-layouts  10.3 us
    ppermute x1, starting transfers between devices, chip_body(): lax.ppermute(queued, 'col', near)  7.96 us
  transfers between devices with their start and end apart: 28, of which 8 were waited for; matrix products, arithmetic and copies ran while one was open for 1% of the time, Pallas kernels for 36%

profile of v9, /device:TPU:0, one launch (start us, length us, event | category | flops | bytes accessed | tf_op | source)
XLA Modules:
  0.0 238.9 jit_solution(9331040059228998753)
XLA Ops:
  0.6 4.9 %collective-permute-start.3 = (f32[128,256]{1,0:T(8,128)}, f32[128,256]{1,0:T(8,128)S(1)}, u32[]{:S(2)}, u32[]{:S(2)}) collective-permute-start(f32[128,256]{1,0:T(8,128)} %refs_0_), channel_id=1, source_target_pairs={{0,1},{3,2},{4,5},{7,6},{8,9},{11,10},{12,13},{15,14},{16,17},{19,... | collective-permute-start | bytes 393224 | tf_op jit(solution)/shard_map/ppermute | solution.py:438
  6.3 4.0 %collective-permute-start.5 = (f32[128,256]{1,0:T(8,128)}, f32[128,256]{1,0:T(8,128)S(1)}, u32[]{:S(2)}, u32[]{:S(2)}) collective-permute-start(f32[128,256]{1,0:T(8,128)} %refs_0_), channel_id=1, source_target_pairs={{0,2},{3,1},{4,6},{7,5},{8,10},{11,9},{12,14},{15,13},{16,18},{19,... | collective-permute-start | bytes 393224 | tf_op jit(solution)/shard_map/ppermute | solution.py:438
  12.4 3.1 %shard_map.68.refs_0_ = f32[3,768,128]{2,1,0:T(8,128)} custom-call(s32[56]{0:T(128)} %concatenate.3.s, f32[7,512,128]{2,1,0:T(8,128)} %bitcast.8, f32[7,128,512]{2,1,0:T(8,128)} %bitcast.10), custom_call_target="tpu_custom_call" | custom-call | flops 1000000000 | bytes 1 | tf_op jit(solution)/shard_map/pallas_call | solution.py:100
  17.7 3.9 %collective-permute-start.2 = (f32[3,768,128]{2,1,0:T(8,128)}, f32[3,768,128]{2,1,0:T(8,128)S(1)}, u32[]{:S(2)}, u32[]{:S(2)}) collective-permute-start(f32[3,768,128]{2,1,0:T(8,128)} %shard_map.68.refs_0_), channel_id=1, source_target_pairs={{0,2},{3,1},{4,6},{7,5},{8,10},{11,9},{12,14},{15,13},{16,18},{19,... | collective-permute-start | bytes 3538952 | tf_op jit(solution)/shard_map/ppermute | solution.py:438
  22.9 2.6 %shard_map.69.refs_0_.refs_5_ = f32[128,1024]{1,0:T(8,128)} custom-call(s32[56]{0:T(128)} %concatenate.3.s, f32[128,256]{1,0:T(8,128)} %refs_0_, f32[128,256]{1,0:T(8,128)} %copy-done.27, f32[128,256]{1,0:T(8,128)} %copy-done.28, f32[128,256]{1,0:T(8,128)} %copy-done.29), custom_call_target="tpu_custom_call" | custom-call | flops 1000000000 | bytes 1 | tf_op jit(solution)/shard_map/pallas_call | solution.py:100
  27.6 3.4 %shard_map.71.refs_10_.refs_0_.x0 = f32[4,768,128]{2,1,0:T(8,128)} custom-call(s32[56]{0:T(128)} %concatenate.3.s, f32[7,512,128]{2,1,0:T(8,128)} %bitcast.9, f32[7,128,512]{2,1,0:T(8,128)} %bitcast.11), custom_call_target="tpu_custom_call" | custom-call | flops 1000000000 | bytes 1 | tf_op jit(solution)/shard_map/pallas_call | solution.py:100
  32.6 3.5 %shard_map.70 = f32[4,128,1024]{2,1,0:T(8,128)} custom-call(s32[56]{0:T(128)} %concatenate.3.s, f32[128,1024]{1,0:T(8,128)} %shard_map.69.refs_0_.refs_5_, f32[128,1024]{1,0:T(8,128)} %copy-done.7, f32[128,1024]{1,0:T(8,128)} %copy-done.8, f32[128,1024]{1,0:T(8,128)} %copy-done.9), custom_call_target="tpu_custom_call" | custom-call | flops 1000000000 | bytes 1 | tf_op jit(solution)/shard_map/pallas_call | solution.py:100
  36.2 7.4 %collective-permute-done.refs_1_ = f32[3,768,128]{2,1,0:T(8,128)S(1)} collective-permute-done((f32[3,768,128]{2,1,0:T(8,128)}, f32[3,768,128]{2,1,0:T(8,128)S(1)}, u32[]{:S(2)}, u32[]{:S(2)}) %collective-permute-start) | collective-permute-done | bytes 1179680 | tf_op jit(solution)/shard_map/ppermute | solution.py:438
  43.6 23.9 %collective-permute-done.2.refs_3_ = f32[3,768,128]{2,1,0:T(8,128)S(1)} collective-permute-done((f32[3,768,128]{2,1,0:T(8,128)}, f32[3,768,128]{2,1,0:T(8,128)S(1)}, u32[]{:S(2)}, u32[]{:S(2)}) %collective-permute-start.2) | collective-permute-done | bytes 1179680 | tf_op jit(solution)/shard_map/ppermute | solution.py:438
  68.5 5.2 %shard_map.72 = f32[4,3,768,128]{3,2,1,0:T(8,128)} custom-call(s32[56]{0:T(128)} %concatenate.3.s, f32[3,768,128]{2,1,0:T(8,128)} %shard_map.68.refs_0_, f32[3,768,128]{2,1,0:T(8,128)} %copy-done.2, f32[3,768,128]{2,1,0:T(8,128)} %copy-done.3, f32[3,768,128]{2,1,0:T(8,128)} %copy-done.4), custom_call_target="tpu_custom_call" | custom-call | flops 1000000000 | bytes 1 | tf_op jit(solution)/shard_map/pallas_call | solution.py:100
  74.6 2.1 collective-permute-start.10
  76.7 8.0 %collective-permute-start.13 = (f32[4,768,128]{2,1,0:T(8,128)S(1)}, f32[4,768,128]{2,1,0:T(8,128)S(1)}, u32[]{:S(2)}, u32[]{:S(2)}) collective-permute-start(f32[4,768,128]{2,1,0:T(8,128)S(1)} %copy-done), channel_id=1, source_target_pairs={{0,1},{3,2},{4,5},{7,6},{8,9},{11,10},{12,13},{15,14},{16,17},{19,... | collective-permute-start | bytes 4718600 | tf_op jit(solution)/shard_map/ppermute | solution.py:464
  84.7 1.8 collective-permute-start.14
  87.4 3.6 %collective-permute-start.15 = (f32[2,768,128]{2,1,0:T(8,128)}, f32[2,768,128]{2,1,0:T(8,128)}, u32[]{:S(2)}, u32[]{:S(2)}) collective-permute-start(f32[2,768,128]{2,1,0:T(8,128)} %slice.3), channel_id=1, source_target_pairs={{0,2},{3,1},{4,6},{7,5},{8,10},{11,9},{12,14},{15,13},{16,18},{19,... | collective-permute-start | bytes 2359304 | tf_op jit(solution)/shard_map/ppermute | solution.py:465
  91.1 2.1 copy-done.1
  93.2 16.9 %shard_map.73 = (f32[1536,512]{1,0:T(8,128)}, f32[2,512,512]{2,1,0:T(8,128)}, f32[1024,128]{1,0:T(8,128)}, f32[2,832,128]{2,1,0:T(8,128)}) custom-call(s32[56]{0:T(128)} %concatenate.3.s, f32[3,768,128]{2,1,0:T(8,128)} %shard_map.68.refs_0_, f32[3,768,128]{2,1,0:T(8,128)} %copy-done.2, f32[3,768,128]{2,1,0:T(8,128)} %copy-done.3, f32[3,768,128]{2,1,0:T(8,128)} %copy-done.4, ...), custom_call_target="tpu_custom_call" | custom-call | flops 1000000000 | bytes 1 | tf_op jit(solution)/shard_map/pallas_call | solution.py:100
  110.4 25.4 %shard_map.74 = (f32[2,1024,512]{2,1,0:T(8,128)}, f32[2,1024,128]{2,1,0:T(8,128)}, f32[2,768,128]{2,1,0:T(8,128)}) custom-call(s32[56]{0:T(128)} %concatenate.3.s, f32[3,768,128]{2,1,0:T(8,128)} %shard_map.68.refs_0_, f32[3,768,128]{2,1,0:T(8,128)} %copy-done.2, f32[3,768,128]{2,1,0:T(8,128)} %copy-done.3, f32[3,768,128]{2,1,0:T(8,128)} %copy-done.4, ...), custom_call_target="tpu_custom_call" | custom-call | flops 1000000000 | bytes 1 | tf_op jit(solution)/shard_map/pallas_call | solution.py:100
  137.0 3.2 %shard_map.75 = (f32[2,768,128]{2,1,0:T(8,128)}, f32[2,768,128]{2,1,0:T(8,128)}) custom-call(s32[56]{0:T(128)} %concatenate.3.s, f32[4,768,128]{2,1,0:T(8,128)} %shard_map.71.refs_10_.refs_0_.x0, f32[4,768,128]{2,1,0:T(8,128)} %copy-done.5, f32[4,768,128]{2,1,0:T(8,128)} %collective-permute-done.14.refs_2_.x2, f32[2,768,128]{2,1,0:T(8,128)} %collective-permute-done.15.refs_3_.x3), custom_call_target="tpu_custom_call" | custom-call | flops 1000000000 | bytes 1 | tf_op jit(solution)/shard_map/pallas_call | solution.py:100
  141.6 1.5 collective-permute-start.12
  143.2 10.5 %collective-permute-done.11.refs_3_.x3.root.refs_1_ = f32[2,832,128]{2,1,0:T(8,128)S(1)} collective-permute-done((f32[2,832,128]{2,1,0:T(8,128)}, f32[2,832,128]{2,1,0:T(8,128)S(1)}, u32[]{:S(2)}, u32[]{:S(2)}) %collective-permute-start.11) | collective-permute-done | bytes 852000 | tf_op jit(solution)/shard_map/ppermute | solution.py:477
  153.7 9.0 %shard_map.76 = (f32[1024,128]{1,0:T(8,128)}, f32[1024,128]{1,0:T(8,128)}, f32[768,128]{1,0:T(8,128)}, f32[768,128]{1,0:T(8,128)}) custom-call(s32[56]{0:T(128)} %concatenate.3.s, f32[4,768,128]{2,1,0:T(8,128)} %shard_map.71.refs_10_.refs_0_.x0, f32[4,768,128]{2,1,0:T(8,128)} %copy-done.5, f32[4,768,128]{2,1,0:T(8,128)} %collective-permute-done.14.refs_2_.x2, ...), custom_call_target="tpu_custom_call" | custom-call | flops 10000000000 | bytes 1 | tf_op jit(solution)/shard_map/pallas_call | solution.py:100
  162.7 21.4 %collective-permute-done.12.upper.refs_3_ = f32[2,768,128]{2,1,0:T(8,128)S(1)} collective-permute-done((f32[2,768,128]{2,1,0:T(8,128)S(1)}, f32[2,768,128]{2,1,0:T(8,128)S(1)}, u32[]{:S(2)}, u32[]{:S(2)}) %collective-permute-start.12) | collective-permute-done | bytes 786464 | tf_op jit(solution)/shard_map/ppermute | solution.py:487
  184.1 3.3 %shard_map.77 = (f32[2,768,128]{2,1,0:T(8,128)}, f32[2,768,128]{2,1,0:T(8,128)}) custom-call(s32[56]{0:T(128)} %concatenate.3.s, f32[4,768,128]{2,1,0:T(8,128)} %shard_map.71.refs_10_.refs_0_.x0, f32[4,768,128]{2,1,0:T(8,128)} %copy-done.5, f32[4,768,128]{2,1,0:T(8,128)} %collective-permute-done.14.refs_2_.x2, f32[2,832,128]{2,1,0:T(8,128)} %copy-done.6), custom_call_target="tpu_custom_call" | custom-call | flops 1000000000 | bytes 1 | tf_op jit(solution)/shard_map/pallas_call | solution.py:100
  194.1 9.1 %shard_map.78 = (f32[1024,128]{1,0:T(8,128)}, f32[1024,128]{1,0:T(8,128)}, f32[1024,128]{1,0:T(8,128)}, f32[1024,128]{1,0:T(8,128)}) custom-call(s32[56]{0:T(128)} %concatenate.3.s, f32[4,768,128]{2,1,0:T(8,128)} %shard_map.71.refs_10_.refs_0_.x0, f32[4,768,128]{2,1,0:T(8,128)} %copy-done.5, f32[4,768,128]{2,1,0:T(8,128)} %collective-permute-done.14.refs_2_.x2, ...), custom_call_target="tpu_custom_call" | custom-call | flops 10000000000 | bytes 1 | tf_op jit(solution)/shard_map/pallas_call | solution.py:100
  206.5 2.5 %shard_map.79 = f32[768,128]{1,0:T(8,128)} custom-call(s32[56]{0:T(128)} %concatenate.3.s, f32[2,832,128]{2,1,0:T(8,128)} %copy-done.6, f32[2,768,128]{2,1,0:T(8,128)} %copy-done.10), custom_call_target="tpu_custom_call" | custom-call | flops 1000000000 | bytes 1 | tf_op jit(solution)/shard_map/pallas_call | solution.py:100
  209.0 3.6 %collective-permute-done.23.refs_1_.refs_8_ = f32[768,128]{1,0:T(8,128)S(1)} collective-permute-done((f32[768,128]{1,0:T(8,128)S(1)}, f32[768,128]{1,0:T(8,128)S(1)}, u32[]{:S(2)}, u32[]{:S(2)}) %collective-permute-start.23) | collective-permute-done | bytes 393248 | tf_op jit(solution)/shard_map/ppermute | solution.py:506
  212.6 2.1 collective-permute-start.20
  214.7 2.3 shard_map.80
  217.1 2.2 collective-permute-start.24
  221.6 4.3 %shard_map.81 = (f32[7,512,128]{2,1,0:T(8,128)}, f32[7,512,128]{2,1,0:T(8,128)}) custom-call(s32[56]{0:T(128)} %concatenate.3.s, f32[1024,128]{1,0:T(8,128)} %get-tuple-element.58.refs_0_, f32[2,832,128]{2,1,0:T(8,128)} %copy-done.6, f32[2,1024,128]{2,1,0:T(8,128)} %get-tuple-element.62.refs_2_, f32[2,768,128]{2,1,0:T(8,128)} %copy-done.10, ...), custom_call_target="tpu_custom_call" | custom-call | flops 1000000000 | bytes 1 | tf_op jit(solution)/shard_map/pallas_call | solution.py:100
  226.0 9.1 %collective-permute-done.27.cross_56 = f32[1024,128]{1,0:T(8,128)S(1)} collective-permute-done((f32[1024,128]{1,0:T(8,128)}, f32[1024,128]{1,0:T(8,128)S(1)}, u32[]{:S(2)}, u32[]{:S(2)}) %collective-permute-start.27) | collective-permute-done | bytes 524320 | tf_op jit(solution)/shard_map/ppermute | solution.py:506
  235.8 2.9 %shard_map.82 = (f32[7,512,128]{2,1,0:T(8,128)}, f32[7,512,128]{2,1,0:T(8,128)}) custom-call(s32[56]{0:T(128)} %concatenate.3.s, f32[7,512,128]{2,1,0:T(8,128)} %get-tuple-element.87.ab_in, f32[7,512,128]{2,1,0:T(8,128)} %get-tuple-element.88.dg_in, f32[1024,128]{1,0:T(8,128)} %get-tuple-element.81.self_56, ...), custom_call_target="tpu_custom_call", output_to_operand_aliasing={{0}: (1, {}), {1}: (2, {})} | custom-call | tf_op jit(solution)/shard_map/pallas_call | solution.py:527
  (103 shorter events, 28.7 us)
Async XLA Ops:
  0.6 17.0 %collective-permute-start.3 = (f32[128,256]{1,0:T(8,128)}, f32[128,256]{1,0:T(8,128)S(1)}, u32[]{:S(2)}, u32[]{:S(2)}) collective-permute-start(f32[128,256]{1,0:T(8,128)} %refs_0_), channel_id=1, source_target_pairs={{0,1},{3,2},{4,5},{7,6},{8,9},{11,10},{12,13},{15,14},{16,17},{19,... | collective-permute-start | bytes 393224 | tf_op jit(solution)/shard_map/ppermute | solution.py:438
  5.6 16.0 %collective-permute-start.4 = (f32[128,256]{1,0:T(8,128)}, f32[128,256]{1,0:T(8,128)S(1)}, u32[]{:S(2)}, u32[]{:S(2)}) collective-permute-start(f32[128,256]{1,0:T(8,128)} %refs_0_), channel_id=1, source_target_pairs={{1,2},{2,1},{5,6},{6,5},{9,10},{10,9},{13,14},{14,13},{17,18},{18,... | collective-permute-start | bytes 393224 | tf_op jit(solution)/shard_map/ppermute | solution.py:438
  6.3 15.4 %collective-permute-start.5 = (f32[128,256]{1,0:T(8,128)}, f32[128,256]{1,0:T(8,128)S(1)}, u32[]{:S(2)}, u32[]{:S(2)}) collective-permute-start(f32[128,256]{1,0:T(8,128)} %refs_0_), channel_id=1, source_target_pairs={{0,2},{3,1},{4,6},{7,5},{8,10},{11,9},{12,14},{15,13},{16,18},{19,... | collective-permute-start | bytes 393224 | tf_op jit(solution)/shard_map/ppermute | solution.py:438
  15.4 28.1 %collective-permute-start = (f32[3,768,128]{2,1,0:T(8,128)}, f32[3,768,128]{2,1,0:T(8,128)S(1)}, u32[]{:S(2)}, u32[]{:S(2)}) collective-permute-start(f32[3,768,128]{2,1,0:T(8,128)} %shard_map.68.refs_0_), channel_id=1, source_target_pairs={{0,1},{3,2},{4,5},{7,6},{8,9},{11,10},{12,13},{15,14},{16,17},{19,... | collective-permute-start | bytes 3538952 | tf_op jit(solution)/shard_map/ppermute | solution.py:438
  16.9 26.6 %collective-permute-start.1 = (f32[3,768,128]{2,1,0:T(8,128)}, f32[3,768,128]{2,1,0:T(8,128)S(1)}, u32[]{:S(2)}, u32[]{:S(2)}) collective-permute-start(f32[3,768,128]{2,1,0:T(8,128)} %shard_map.68.refs_0_), channel_id=1, source_target_pairs={{1,2},{2,1},{5,6},{6,5},{9,10},{10,9},{13,14},{14,13},{17,18},{18,... | collective-permute-start | bytes 3538952 | tf_op jit(solution)/shard_map/ppermute | solution.py:438
  17.7 49.7 %collective-permute-start.2 = (f32[3,768,128]{2,1,0:T(8,128)}, f32[3,768,128]{2,1,0:T(8,128)S(1)}, u32[]{:S(2)}, u32[]{:S(2)}) collective-permute-start(f32[3,768,128]{2,1,0:T(8,128)} %shard_map.68.refs_0_), channel_id=1, source_target_pairs={{0,2},{3,1},{4,6},{7,5},{8,10},{11,9},{12,14},{15,13},{16,18},{19,... | collective-permute-start | bytes 3538952 | tf_op jit(solution)/shard_map/ppermute | solution.py:438
  25.5 1.4 collective-permute-start.6
  26.2 4.8 %collective-permute-start.7 = (f32[128,1024]{1,0:T(8,128)}, f32[128,1024]{1,0:T(8,128)S(1)}, u32[]{:S(2)}, u32[]{:S(2)}) collective-permute-start(f32[128,1024]{1,0:T(8,128)} %shard_map.69.refs_0_.refs_5_), channel_id=1, source_target_pairs={{1,17},{2,18},{5,21},{6,22},{9,25},{10,26},{13,29},{14,30},{17,1},... | collective-permute-start | bytes 1572872 | tf_op jit(solution)/shard_map/ppermute | solution.py:455
  26.9 4.1 %collective-permute-start.8 = (f32[128,1024]{1,0:T(8,128)}, f32[128,1024]{1,0:T(8,128)S(1)}, u32[]{:S(2)}, u32[]{:S(2)}) collective-permute-start(f32[128,1024]{1,0:T(8,128)} %shard_map.69.refs_0_.refs_5_), channel_id=1, source_target_pairs={{1,25},{2,26},{5,29},{6,30},{9,17},{10,18},{13,21},{14,22},{17,9},... | collective-permute-start | bytes 1572872 | tf_op jit(solution)/shard_map/ppermute | solution.py:455
  36.2 40.5 %copy-start = (f32[4,768,128]{2,1,0:T(8,128)S(1)}, f32[4,768,128]{2,1,0:T(8,128)}, u32[]{:S(2)}) copy-start(f32[4,768,128]{2,1,0:T(8,128)} %shard_map.71.refs_10_.refs_0_.x0) | copy-start | bytes 4718596
  43.5 23.9 %copy-start.2 = (f32[3,768,128]{2,1,0:T(8,128)}, f32[3,768,128]{2,1,0:T(8,128)S(1)}, u32[]{:S(2)}) copy-start(f32[3,768,128]{2,1,0:T(8,128)S(1)} %collective-permute-done.refs_1_) | copy-start | bytes 3538948
  43.6 23.9 %copy-start.3 = (f32[3,768,128]{2,1,0:T(8,128)}, f32[3,768,128]{2,1,0:T(8,128)S(1)}, u32[]{:S(2)}) copy-start(f32[3,768,128]{2,1,0:T(8,128)S(1)} %collective-permute-done.1.refs_2_) | copy-start | bytes 3538948
  73.7 17.4 %collective-permute-start.9 = (f32[4,3,768,128]{3,2,1,0:T(8,128)}, f32[4,3,768,128]{3,2,1,0:T(8,128)S(1)}, u32[]{:S(2)}, u32[]{:S(2)}) collective-permute-start(f32[4,3,768,128]{3,2,1,0:T(8,128)} %shard_map.72), channel_id=1, source_target_pairs={{1,5},{2,6},{5,1},{6,2},{9,13},{10,14},{13,9},{14,10},{17,21},{18,... | collective-permute-start | bytes 14155784 | tf_op jit(solution)/shard_map/ppermute | solution.py:441
  74.6 16.4 %collective-permute-start.10 = (f32[4,128,1024]{2,1,0:T(8,128)}, f32[4,128,1024]{2,1,0:T(8,128)}, u32[]{:S(2)}, u32[]{:S(2)}) collective-permute-start(f32[4,128,1024]{2,1,0:T(8,128)} %shard_map.70), channel_id=1, source_target_pairs={{1,5},{2,6},{5,1},{6,2},{9,13},{10,14},{13,9},{14,10},{17,21},{18,... | collective-permute-start | bytes 6291464 | tf_op jit(solution)/shard_map/ppermute | solution.py:441
  76.7 59.1 %collective-permute-start.13 = (f32[4,768,128]{2,1,0:T(8,128)S(1)}, f32[4,768,128]{2,1,0:T(8,128)S(1)}, u32[]{:S(2)}, u32[]{:S(2)}) collective-permute-start(f32[4,768,128]{2,1,0:T(8,128)S(1)} %copy-done), channel_id=1, source_target_pairs={{0,1},{3,2},{4,5},{7,6},{8,9},{11,10},{12,13},{15,14},{16,17},{19,... | collective-permute-start | bytes 4718600 | tf_op jit(solution)/shard_map/ppermute | solution.py:464
  84.7 51.2 %collective-permute-start.14 = (f32[4,768,128]{2,1,0:T(8,128)S(1)}, f32[4,768,128]{2,1,0:T(8,128)}, u32[]{:S(2)}, u32[]{:S(2)}) collective-permute-start(f32[4,768,128]{2,1,0:T(8,128)S(1)} %copy-done), channel_id=1, source_target_pairs={{1,2},{2,1},{5,6},{6,5},{9,10},{10,9},{13,14},{14,13},{17,18},{18,... | collective-permute-start | bytes 4718600 | tf_op jit(solution)/shard_map/ppermute | solution.py:464
  87.4 48.9 %collective-permute-start.15 = (f32[2,768,128]{2,1,0:T(8,128)}, f32[2,768,128]{2,1,0:T(8,128)}, u32[]{:S(2)}, u32[]{:S(2)}) collective-permute-start(f32[2,768,128]{2,1,0:T(8,128)} %slice.3), channel_id=1, source_target_pairs={{0,2},{3,1},{4,6},{7,5},{8,10},{11,9},{12,14},{15,13},{16,18},{19,... | collective-permute-start | bytes 2359304 | tf_op jit(solution)/shard_map/ppermute | solution.py:465
  110.1 43.5 %collective-permute-start.11 = (f32[2,832,128]{2,1,0:T(8,128)}, f32[2,832,128]{2,1,0:T(8,128)S(1)}, u32[]{:S(2)}, u32[]{:S(2)}) collective-permute-start(f32[2,832,128]{2,1,0:T(8,128)} %get-tuple-element.59), channel_id=1, source_target_pairs={{1,0},{2,3},{0,2},{3,1},{5,4},{6,7},{4,6},{7,5},{9,8},{10,11},{8,1... | collective-permute-start | bytes 2555912 | tf_op jit(solution)/shard_map/ppermute | solution.py:477
  140.2 3.0 %collective-permute-start.16 = (f32[2,768,128]{2,1,0:T(8,128)}, f32[2,768,128]{2,1,0:T(8,128)S(1)}, u32[]{:S(2)}, u32[]{:S(2)}) collective-permute-start(f32[2,768,128]{2,1,0:T(8,128)} %get-tuple-element.69), channel_id=1, source_target_pairs={{1,5},{2,6},{5,1},{6,2},{9,13},{10,14},{13,9},{14,10},{17,21},{18,... | collective-permute-start | bytes 2359304 | tf_op jit(solution)/shard_map/ppermute | solution.py:441
  140.9 2.3 collective-permute-start.17
  141.6 42.5 %collective-permute-start.12 = (f32[2,768,128]{2,1,0:T(8,128)S(1)}, f32[2,768,128]{2,1,0:T(8,128)S(1)}, u32[]{:S(2)}, u32[]{:S(2)}) collective-permute-start(f32[2,768,128]{2,1,0:T(8,128)S(1)} %copy-done.19), channel_id=1, source_target_pairs={{1,0},{2,3},{5,4},{6,7},{9,8},{10,11},{13,12},{14,15},{17,16},{18,... | collective-permute-start | bytes 2359304 | tf_op jit(solution)/shard_map/ppermute | solution.py:487
  143.2 10.5 %copy-start.22 = (f32[2,768,128]{2,1,0:T(8,128)}, f32[2,768,128]{2,1,0:T(8,128)S(1)}, u32[]{:S(2)}) copy-start(f32[2,768,128]{2,1,0:T(8,128)S(1)} %collective-permute-done.16.ex0) | copy-start | bytes 2359300
  187.5 4.8 %collective-permute-start.18 = (f32[2,768,128]{2,1,0:T(8,128)}, f32[2,768,128]{2,1,0:T(8,128)S(1)}, u32[]{:S(2)}, u32[]{:S(2)}) collective-permute-start(f32[2,768,128]{2,1,0:T(8,128)} %get-tuple-element.77), channel_id=1, source_target_pairs={{1,5},{2,6},{5,1},{6,2},{9,13},{10,14},{13,9},{14,10},{17,21},{18,... | collective-permute-start | bytes 2359304 | tf_op jit(solution)/shard_map/ppermute | solution.py:441
  188.2 4.1 %collective-permute-start.19 = (f32[2,768,128]{2,1,0:T(8,128)}, f32[2,768,128]{2,1,0:T(8,128)S(1)}, u32[]{:S(2)}, u32[]{:S(2)}) collective-permute-start(f32[2,768,128]{2,1,0:T(8,128)} %get-tuple-element.78), channel_id=1, source_target_pairs={{1,5},{2,6},{5,1},{6,2},{9,13},{10,14},{13,9},{14,10},{17,21},{18,... | collective-permute-start | bytes 2359304 | tf_op jit(solution)/shard_map/ppermute | solution.py:441
  188.9 28.1 %collective-permute-start.21 = (f32[1024,128]{1,0:T(8,128)S(1)}, f32[1024,128]{1,0:T(8,128)S(1)}, u32[]{:S(2)}, u32[]{:S(2)}) collective-permute-start(f32[1024,128]{1,0:T(8,128)S(1)} %copy-done.24), channel_id=1, source_target_pairs={{1,5},{2,6},{5,1},{6,2},{9,13},{10,14},{13,9},{14,10},{17,21},{18,... | collective-permute-start | bytes 1572872 | tf_op jit(solution)/shard_map/ppermute | solution.py:441
  189.6 15.6 %collective-permute-start.22 = (f32[768,128]{1,0:T(8,128)S(1)}, f32[768,128]{1,0:T(8,128)S(1)}, u32[]{:S(2)}, u32[]{:S(2)}) collective-permute-start(f32[768,128]{1,0:T(8,128)S(1)} %copy-done.26), channel_id=1, source_target_pairs={{1,0},{2,3},{5,4},{6,7},{9,8},{10,11},{13,12},{14,15},{17,16},{18,... | collective-permute-start | bytes 1179656 | tf_op jit(solution)/shard_map/ppermute | solution.py:506
  190.9 21.6 %collective-permute-start.23 = (f32[768,128]{1,0:T(8,128)S(1)}, f32[768,128]{1,0:T(8,128)S(1)}, u32[]{:S(2)}, u32[]{:S(2)}) collective-permute-start(f32[768,128]{1,0:T(8,128)S(1)} %copy-done.25), channel_id=1, source_target_pairs={{1,4},{2,7},{5,0},{6,3},{9,12},{10,15},{13,8},{14,11},{17,20},{18,... | collective-permute-start | bytes 1179656 | tf_op jit(solution)/shard_map/ppermute | solution.py:506
  203.2 22.8 %collective-permute-start.25 = (f32[1024,128]{1,0:T(8,128)}, f32[1024,128]{1,0:T(8,128)S(1)}, u32[]{:S(2)}, u32[]{:S(2)}) collective-permute-start(f32[1024,128]{1,0:T(8,128)} %get-tuple-element.89), channel_id=1, source_target_pairs={{1,5},{2,6},{5,1},{6,2},{9,13},{10,14},{13,9},{14,10},{17,21},{18,... | collective-permute-start | bytes 1572872 | tf_op jit(solution)/shard_map/ppermute | solution.py:441
  203.9 22.1 %collective-permute-start.26 = (f32[1024,128]{1,0:T(8,128)}, f32[1024,128]{1,0:T(8,128)S(1)}, u32[]{:S(2)}, u32[]{:S(2)}) collective-permute-start(f32[1024,128]{1,0:T(8,128)} %get-tuple-element.90), channel_id=1, source_target_pairs={{1,0},{2,3},{5,4},{6,7},{9,8},{10,11},{13,12},{14,15},{17,16},{18,... | collective-permute-start | bytes 1572872 | tf_op jit(solution)/shard_map/ppermute | solution.py:506
  205.2 29.8 %collective-permute-start.27 = (f32[1024,128]{1,0:T(8,128)}, f32[1024,128]{1,0:T(8,128)S(1)}, u32[]{:S(2)}, u32[]{:S(2)}) collective-permute-start(f32[1024,128]{1,0:T(8,128)} %get-tuple-element.91), channel_id=1, source_target_pairs={{1,4},{2,7},{5,0},{6,3},{9,12},{10,15},{13,8},{14,11},{17,20},{18,... | collective-permute-start | bytes 1572872 | tf_op jit(solution)/shard_map/ppermute | solution.py:506
  212.6 8.1 %collective-permute-start.20 = (f32[768,128]{1,0:T(8,128)}, f32[768,128]{1,0:T(8,128)S(1)}, u32[]{:S(2)}, u32[]{:S(2)}) collective-permute-start(f32[768,128]{1,0:T(8,128)} %shard_map.79), channel_id=1, source_target_pairs={{0,4},{3,7},{4,0},{7,3},{8,12},{11,15},{12,8},{15,11},{16,20},{19,... | collective-permute-start | bytes 1179656 | tf_op jit(solution)/shard_map/ppermute | solution.py:513
  217.1 3.6 %collective-permute-start.24 = (f32[512,128]{1,0:T(8,128)}, f32[512,128]{1,0:T(8,128)S(1)}, u32[]{:S(2)}, u32[]{:S(2)}) collective-permute-start(f32[512,128]{1,0:T(8,128)} %shard_map.80), channel_id=1, source_target_pairs={{0,4},{3,7},{4,0},{7,3},{8,12},{11,15},{12,8},{15,11},{16,20},{19,... | collective-permute-start | bytes 786440 | tf_op jit(solution)/shard_map/ppermute | solution.py:513
  (26 other events, 93.1 us)

commit v10 on v6

--- a/solution.py
+++ b/solution.py
@@ -163,11 +163,10 @@
 
 
 def swap_kernel(s, *refs):
-    out, sems = refs[-2:]
-    copies = [
-        (ref.at[2 * pair + 1 - s[0]], out.at[pair, k]) for pair in range(2) for k, ref in enumerate(refs[:-2])
-    ]
-    copy_all(copies, sems)
+    blocks, outs, sems = refs[:4], refs[4:6], refs[6]
+    copy_all([
+        (ref.at[2 * pair + 1 - s[0]], out.at[k]) for pair, out in enumerate(outs) for k, ref in enumerate(blocks)
+    ], sems)
 
 
 def join_block(a, own, corner, rows_of, top, index, weight):
@@ -279,7 +278,7 @@
     stage, sems, tails, top, grand_in, ab, dg = rest[:7]
     p, d, a, dc, f, w, t, pt, dt = pairs(rest[7:])
     r, c = s[0], s[1]
-    blocks = [x for k, ref in enumerate((x0, x1, x2, x3)) for x in (ref.at[first - 3 + r], ex.at[(first - 3) // 2, k])]
+    blocks = [x for k, ref in enumerate((x0, x1, x2, x3)) for x in (ref.at[first - 3 + r], ex.at[k])]
     order = a[0].shape[0]
     own = d[0].shape[0]
     half = order // 2
@@ -339,9 +338,8 @@
     shares_kernel(s, upper.at[0], upper.at[1], upper.at[2], out, sems)
 
 
-def output_kernel(s, *refs):
+def first_output_kernel(s, *refs):
     upper_self, upper_end, upper_shares, self_34, core_34, end_34, cross_34, shares_34 = refs[:8]
-    self_56, core_56, end_56, cross_56 = refs[8:12]
     ab, dg, sems = refs[-3:]
     r, c = s[0], s[1]
     half = ab.shape[1]
@@ -351,9 +349,8 @@
         @pl.when((r == core) & middle)
         def _():
             pair = [self_34, core_34] if core == 0 else [core_34, self_34]
-            last = [self_56, core_56] if core == 0 else [core_56, self_56]
             copies = []
-            for node, ref in enumerate([upper_self.at[k] for k in range(3)] + pair + last):
+            for node, ref in enumerate([upper_self.at[k] for k in range(3)] + pair):
                 copies.append((ref.at[pl.ds(0, half)], ab.at[node]))
                 copies.append((ref.at[pl.ds(half, half)], dg.at[node]))
             copy_all(copies, sems)
@@ -361,7 +358,6 @@
         @pl.when((r == core) & jnp.logical_not(middle))
         def _():
             same, swapped = (3, 4) if core == 0 else (4, 3)
-            last = [end_56, cross_56] if core == 0 else [cross_56, end_56]
             found = [(k, upper_end.at[k], upper_shares, k) for k in range(3)]
             found += [(same, end_34, shares_34, 1), (swapped, cross_34, shares_34, 0)]
             copies = []
@@ -369,10 +365,26 @@
                 copies.append((ref.at[pl.ds(0, half)], ab.at[node]))
                 copies.append((ref.at[pl.ds(half, share)], dg.at[node, pl.ds(core * share, share)]))
                 copies.append((shares.at[pl.ds(k * share, share)], dg.at[node, pl.ds((1 - core) * share, share)]))
-            for node, ref in ((5, last[0]), (6, last[1])):
-                copies.append((ref.at[pl.ds(0, half)], ab.at[node]))
-                copies.append((ref.at[pl.ds(half, half)], dg.at[node]))
             copy_all(copies, sems)
+
+
+def last_output_kernel(s, ab_in, dg_in, self_56, core_56, end_56, cross_56, ab, dg, stage, sems):
+    r, c = s[0], s[1]
+    half = ab.shape[1]
+    middle = (c == 1) | (c == 2)
+    for core in range(2):
+        for inner in range(2):
+            @pl.when((r == core) & (middle == (inner == 1)))
+            def _():
+                pair = [self_56, core_56] if inner else [end_56, cross_56]
+                if core == 1:
+                    pair = pair[::-1]
+                copy_all([(ref, stage.at[k]) for k, ref in enumerate(pair)], sems)
+    copies = []
+    for k in range(2):
+        copies.append((stage.at[k, pl.ds(0, half)], ab.at[5 + k]))
+        copies.append((stage.at[k, pl.ds(half, half)], dg.at[5 + k]))
+    copy_all(copies, sems)
 
 
 def after(x, earlier):
@@ -455,25 +467,35 @@
         return self_out, core_out, lax.ppermute(end_out, "col", home), lax.ppermute(cross_out, both, home_cross)
 
     chosen = after(blocks_l, (ext, upper_home))
-    others = swapped(move(swap_kernel, here, chosen, [(2, 4, packed, TILE)], 8)[0])
-    self_34, core_34, end_34, cross_34 = leaves(3, others, packed)
-    self_56, core_56, end_56, cross_56 = leaves(5, after(others, self_34), half + own)
+    picked_34, picked_56 = move(swap_kernel, here, chosen, [(4, packed, TILE)] * 2, 8)
+    other_34, other_56 = swapped(picked_34), swapped(picked_56)
+    self_34, core_34, end_34, cross_34 = leaves(3, other_34, packed)
+    self_56, core_56, end_56, cross_56 = leaves(5, after(other_56, self_34), half + own)
 
     def shared(kernel, parts, count):
         out = move(kernel, here, parts, [(count * (own // 2), TILE)], count)[0]
         return lax.ppermute(out, both, swap_ends)
 
-    upper_shares = shared(upper_shares_kernel, [upper_home], 3)
+    upper_shares = shared(upper_shares_kernel, [after(upper_home, (self_56, cross_34))], 3)
     shares_34 = shared(shares_kernel, [end_34, cross_34], 2)
     count = panels.shape[0]
-    ancestor_block, diagonal_block = move(
-        output_kernel, here,
+    shapes = [(count, half, TILE), (count, own, TILE)]
+    first_outputs = move(
+        first_output_kernel, here,
         [
-            upper_self, upper_home, upper_shares, self_34, swapped(core_34), end_34, cross_34, shares_34, self_56,
-            swapped(core_56), end_56, cross_56,
+            upper_self, upper_home, upper_shares, self_34, swapped(core_34), end_34, cross_34, shares_34,
         ],
-        [(count, half, TILE), (count, own, TILE)], 3 * count,
+        shapes, 15,
     )
+    ancestor_block, diagonal_block = pl.pallas_call(
+        last_output_kernel,
+        out_shape=[jax.ShapeDtypeStruct(shape, F32) for shape in shapes],
+        in_specs=[pl.BlockSpec(memory_space=pltpu.SMEM)] + [ANY] * 6,
+        out_specs=[ANY] * 2,
+        scratch_shapes=[pltpu.VMEM((2, half + own, TILE), F32), pltpu.SemaphoreType.DMA((4,))],
+        input_output_aliases={1: 0, 2: 1},
+        compiler_params=pltpu.CompilerParams(vmem_limit_bytes=VMEM_LIMIT),
+    )(here, *first_outputs, self_56, swapped(core_56), end_56, cross_56)
     return (ancestor_block[None], diagonal_block[None])
 
 

time: 227 us -> 222 us (0.978)
  waiting for transfers between devices: 82.6 us -> 73.8 us
  Pallas kernels: 84.2 us -> 86.8 us
    ppermute x2, waiting for transfers between devices: 16.7 us -> 8.14 us  [leaves(): lax.ppermute(cross_out, both, home_cross)]
    pallas_call x0 -> x1, Pallas kernels: none -> 2.86 us  [chip_body(): pl.pallas_call(last_output_kernel, out_shape=[jax.ShapeDtypeStruct(shape,...]
    ppermute x5 -> x6, starting transfers between devices: 5.88 us -> 6.74 us  [swapped(): return lax.ppermute(x, both, swap)]
  transfers between devices with their start and end apart: 24 -> 25, of which waited for: 8 -> 7; matrix products, arithmetic and copies ran while one was open for 1% -> 1% of each run, Pallas kernels for 31% -> 34%
where the time goes in v10:
time: 222 us; the launch traced here: 221 us
  Pallas kernels  86.8 us (39%)
  waiting for transfers between devices  73.8 us (33%)
  starting transfers between devices  48.5 us (22%)
  local copies, waits for them, and re-layouts  9.82 us (4%)
    pallas_call x12, Pallas kernels, call(): pl.pallas_call(kernel, out_shape=[jax.ShapeDtypeStruct(o, F32) for o in o...  83.9 us
    ppermute x9, waiting for transfers between devices, straight(): return [x] + [lax.ppermute(x, 'col', route) for route in routes]  55.6 us
    ppermute x9, starting transfers between devices, straight(): return [x] + [lax.ppermute(x, 'col', route) for route in routes]  28.9 us
    unnamed x46, local copies, waits for them, and re-layouts  8.47 us
    ppermute x2, waiting for transfers between devices, leaves(): lax.ppermute(cross_out, both, home_cross)  8.14 us
    ppermute x6, starting transfers between devices, swapped(): return lax.ppermute(x, both, swap)  6.74 us
    ppermute x2, waiting for transfers between devices, leaves(): lax.ppermute(end_out, 'col', home)  5.02 us
  transfers between devices with their start and end apart: 25, of which 7 were waited for; matrix products, arithmetic and copies ran while one was open for 1% of the time, Pallas kernels for 34%

profile of v10, /device:TPU:0, one launch (start us, length us, event | category | flops | bytes accessed | tf_op | source)
XLA Modules:
  0.0 220.9 jit_solution(12824430309958625995)
XLA Ops:
  0.6 4.9 %collective-permute-start.3 = (f32[128,256]{1,0:T(8,128)}, f32[128,256]{1,0:T(8,128)S(1)}, u32[]{:S(2)}, u32[]{:S(2)}) collective-permute-start(f32[128,256]{1,0:T(8,128)} %refs_0_), channel_id=1, source_target_pairs={{0,1},{3,2},{4,5},{7,6},{8,9},{11,10},{12,13},{15,14},{16,17},{19,... | collective-permute-start | bytes 393224 | tf_op jit(solution)/shard_map/ppermute | solution.py:415
  6.3 4.0 %collective-permute-start.5 = (f32[128,256]{1,0:T(8,128)}, f32[128,256]{1,0:T(8,128)S(1)}, u32[]{:S(2)}, u32[]{:S(2)}) collective-permute-start(f32[128,256]{1,0:T(8,128)} %refs_0_), channel_id=1, source_target_pairs={{0,2},{3,1},{4,6},{7,5},{8,10},{11,9},{12,14},{15,13},{16,18},{19,... | collective-permute-start | bytes 393224 | tf_op jit(solution)/shard_map/ppermute | solution.py:415
  12.3 3.1 %shard_map.68.refs_0_ = f32[3,768,128]{2,1,0:T(8,128)} custom-call(s32[56]{0:T(128)} %concatenate.3.s, f32[7,512,128]{2,1,0:T(8,128)} %bitcast.8, f32[7,128,512]{2,1,0:T(8,128)} %bitcast.10), custom_call_target="tpu_custom_call" | custom-call | flops 1000000000 | bytes 1 | tf_op jit(solution)/shard_map/pallas_call | solution.py:100
  15.4 1.5 collective-permute-start
  17.6 3.9 %collective-permute-start.2 = (f32[3,768,128]{2,1,0:T(8,128)}, f32[3,768,128]{2,1,0:T(8,128)S(1)}, u32[]{:S(2)}, u32[]{:S(2)}) collective-permute-start(f32[3,768,128]{2,1,0:T(8,128)} %shard_map.68.refs_0_), channel_id=1, source_target_pairs={{0,2},{3,1},{4,6},{7,5},{8,10},{11,9},{12,14},{15,13},{16,18},{19,... | collective-permute-start | bytes 3538952 | tf_op jit(solution)/shard_map/ppermute | solution.py:415
  22.9 2.6 %shard_map.69.refs_0_.refs_5_ = f32[128,1024]{1,0:T(8,128)} custom-call(s32[56]{0:T(128)} %concatenate.3.s, f32[128,256]{1,0:T(8,128)} %refs_0_, f32[128,256]{1,0:T(8,128)} %copy-done.20, f32[128,256]{1,0:T(8,128)} %copy-done.21, f32[128,256]{1,0:T(8,128)} %copy-done.22), custom_call_target="tpu_custom_call" | custom-call | flops 1000000000 | bytes 1 | tf_op jit(solution)/shard_map/pallas_call | solution.py:100
  27.6 3.3 %shard_map.71.refs_0_.x0 = f32[4,768,128]{2,1,0:T(8,128)} custom-call(s32[56]{0:T(128)} %concatenate.3.s, f32[7,512,128]{2,1,0:T(8,128)} %bitcast.9, f32[7,128,512]{2,1,0:T(8,128)} %bitcast.11), custom_call_target="tpu_custom_call" | custom-call | flops 1000000000 | bytes 1 | tf_op jit(solution)/shard_map/pallas_call | solution.py:100
  32.6 3.5 %shard_map.70 = f32[4,128,1024]{2,1,0:T(8,128)} custom-call(s32[56]{0:T(128)} %concatenate.3.s, f32[128,1024]{1,0:T(8,128)} %shard_map.69.refs_0_.refs_5_, f32[128,1024]{1,0:T(8,128)} %copy-done.6, f32[128,1024]{1,0:T(8,128)} %copy-done.7, f32[128,1024]{1,0:T(8,128)} %copy-done.8), custom_call_target="tpu_custom_call" | custom-call | flops 1000000000 | bytes 1 | tf_op jit(solution)/shard_map/pallas_call | solution.py:100
  36.2 7.3 %collective-permute-done.refs_1_ = f32[3,768,128]{2,1,0:T(8,128)S(1)} collective-permute-done((f32[3,768,128]{2,1,0:T(8,128)}, f32[3,768,128]{2,1,0:T(8,128)S(1)}, u32[]{:S(2)}, u32[]{:S(2)}) %collective-permute-start) | collective-permute-done | bytes 1179680 | tf_op jit(solution)/shard_map/ppermute | solution.py:415
  43.5 23.9 %collective-permute-done.2.refs_3_ = f32[3,768,128]{2,1,0:T(8,128)S(1)} collective-permute-done((f32[3,768,128]{2,1,0:T(8,128)}, f32[3,768,128]{2,1,0:T(8,128)S(1)}, u32[]{:S(2)}, u32[]{:S(2)}) %collective-permute-start.2) | collective-permute-done | bytes 1179680 | tf_op jit(solution)/shard_map/ppermute | solution.py:415
  68.4 5.2 %shard_map.72 = f32[4,3,768,128]{3,2,1,0:T(8,128)} custom-call(s32[56]{0:T(128)} %concatenate.3.s, f32[3,768,128]{2,1,0:T(8,128)} %shard_map.68.refs_0_, f32[3,768,128]{2,1,0:T(8,128)} %copy-done.1, f32[3,768,128]{2,1,0:T(8,128)} %copy-done.2, f32[3,768,128]{2,1,0:T(8,128)} %copy-done.3), custom_call_target="tpu_custom_call" | custom-call | flops 1000000000 | bytes 1 | tf_op jit(solution)/shard_map/pallas_call | solution.py:100
  73.6 2.8 %collective-permute-start.9 = (f32[4,3,768,128]{3,2,1,0:T(8,128)}, f32[4,3,768,128]{3,2,1,0:T(8,128)}, u32[]{:S(2)}, u32[]{:S(2)}) collective-permute-start(f32[4,3,768,128]{3,2,1,0:T(8,128)} %shard_map.72), channel_id=1, source_target_pairs={{1,5},{2,6},{5,1},{6,2},{9,13},{10,14},{13,9},{14,10},{17,21},{18,... | collective-permute-start | bytes 14155784 | tf_op jit(solution)/shard_map/ppermute | solution.py:418
  77.2 8.4 %collective-permute-start.12 = (f32[4,768,128]{2,1,0:T(8,128)S(1)}, f32[4,768,128]{2,1,0:T(8,128)}, u32[]{:S(2)}, u32[]{:S(2)}) collective-permute-start(f32[4,768,128]{2,1,0:T(8,128)S(1)} %copy-done), channel_id=1, source_target_pairs={{0,1},{3,2},{4,5},{7,6},{8,9},{11,10},{12,13},{15,14},{16,17},{19,... | collective-permute-start | bytes 4718600 | tf_op jit(solution)/shard_map/ppermute | solution.py:415
  85.6 1.8 collective-permute-start.13
  87.4 2.9 %collective-permute-start.14 = (f32[4,768,128]{2,1,0:T(8,128)S(1)}, f32[4,768,128]{2,1,0:T(8,128)}, u32[]{:S(2)}, u32[]{:S(2)}) collective-permute-start(f32[4,768,128]{2,1,0:T(8,128)S(1)} %copy-done), channel_id=1, source_target_pairs={{0,2},{3,1},{4,6},{7,5},{8,10},{11,9},{12,14},{15,13},{16,18},{19,... | collective-permute-start | bytes 4718600 | tf_op jit(solution)/shard_map/ppermute | solution.py:415
  90.3 1.3 copy-done.5
  91.6 34.6 %shard_map.73 = (f32[2,1024,512]{2,1,0:T(8,128)}, f32[512,512]{1,0:T(8,128)}, f32[3,1024,128]{2,1,0:T(8,128)}, f32[3,768,128]{2,1,0:T(8,128)}) custom-call(s32[56]{0:T(128)} %concatenate.3.s, f32[3,768,128]{2,1,0:T(8,128)} %shard_map.68.refs_0_, f32[3,768,128]{2,1,0:T(8,128)} %copy-done.1, f32[3,768,128]{2,1,0:T(8,128)} %copy-done.2, ...), custom_call_target="tpu_custom_call" | custom-call | flops 1000000000 | bytes 1 | tf_op jit(solution)/shard_map/pallas_call | solution.py:100
  127.6 24.5 %collective-permute-done.14.refs_3_.x3 = f32[4,768,128]{2,1,0:T(8,128)} collective-permute-done((f32[4,768,128]{2,1,0:T(8,128)S(1)}, f32[4,768,128]{2,1,0:T(8,128)}, u32[]{:S(2)}, u32[]{:S(2)}) %collective-permute-start.14) | collective-permute-done | bytes 1572896 | tf_op jit(solution)/shard_map/ppermute | solution.py:415
  152.0 3.7 %collective-permute-done.11.upper.refs_1_ = f32[3,768,128]{2,1,0:T(8,128)S(1)} collective-permute-done((f32[3,768,128]{2,1,0:T(8,128)}, f32[3,768,128]{2,1,0:T(8,128)S(1)}, u32[]{:S(2)}, u32[]{:S(2)}) %collective-permute-start.11) | collective-permute-done | bytes 1179680 | tf_op jit(solution)/shard_map/ppermute | solution.py:451
  155.7 4.3 %shard_map.74 = (f32[4,768,128]{2,1,0:T(8,128)}, f32[4,768,128]{2,1,0:T(8,128)}) custom-call(s32[56]{0:T(128)} %concatenate.3.s, f32[4,768,128]{2,1,0:T(8,128)} %shard_map.71.refs_0_.x0, f32[4,768,128]{2,1,0:T(8,128)} %collective-permute-done.12.refs_1_.x1, f32[4,768,128]{2,1,0:T(8,128)} %collective-permute-done.13.refs_2_.x2, ...), custom_call_target="tpu_custom_call" | custom-call | flops 1000000000 | bytes 1 | tf_op jit(solution)/shard_map/pallas_call | solution.py:100
  162.9 9.0 %shard_map.75 = (f32[1024,128]{1,0:T(8,128)}, f32[1024,128]{1,0:T(8,128)}, f32[768,128]{1,0:T(8,128)}, f32[768,128]{1,0:T(8,128)}) custom-call(s32[56]{0:T(128)} %concatenate.3.s, f32[4,768,128]{2,1,0:T(8,128)} %shard_map.71.refs_0_.x0, f32[4,768,128]{2,1,0:T(8,128)} %collective-permute-done.12.refs_1_.x1, ...), custom_call_target="tpu_custom_call" | custom-call | flops 10000000000 | bytes 1 | tf_op jit(solution)/shard_map/pallas_call | solution.py:100
  171.9 1.3 collective-permute-start.17
  175.7 9.2 %shard_map.76 = (f32[1024,128]{1,0:T(8,128)}, f32[1024,128]{1,0:T(8,128)}, f32[1024,128]{1,0:T(8,128)}, f32[1024,128]{1,0:T(8,128)}) custom-call(s32[56]{0:T(128)} %concatenate.3.s, f32[4,768,128]{2,1,0:T(8,128)} %shard_map.71.refs_0_.x0, f32[4,768,128]{2,1,0:T(8,128)} %collective-permute-done.12.refs_1_.x1, ...), custom_call_target="tpu_custom_call" | custom-call | flops 10000000000 | bytes 1 | tf_op jit(solution)/shard_map/pallas_call | solution.py:100
  188.2 2.5 %shard_map.77 = f32[768,128]{1,0:T(8,128)} custom-call(s32[56]{0:T(128)} %concatenate.3.s, f32[3,768,128]{2,1,0:T(8,128)} %copy-done.9), custom_call_target="tpu_custom_call" | custom-call | flops 1000000000 | bytes 1 | tf_op jit(solution)/shard_map/pallas_call | solution.py:100
  190.6 5.0 %collective-permute-done.20.refs_0_.refs_5_ = f32[768,128]{1,0:T(8,128)S(1)} collective-permute-done((f32[768,128]{1,0:T(8,128)}, f32[768,128]{1,0:T(8,128)S(1)}, u32[]{:S(2)}, u32[]{:S(2)}) %collective-permute-start.20) | collective-permute-done | bytes 393248 | tf_op jit(solution)/shard_map/ppermute | solution.py:467
  195.7 1.9 collective-permute-start.18
  197.6 2.3 %shard_map.78 = f32[512,128]{1,0:T(8,128)} custom-call(s32[56]{0:T(128)} %concatenate.3.s, f32[768,128]{1,0:T(8,128)} %copy-done.15, f32[768,128]{1,0:T(8,128)} %copy-done.14), custom_call_target="tpu_custom_call" | custom-call | flops 1000000000 | bytes 1 | tf_op jit(solution)/shard_map/pallas_call | solution.py:100
  200.0 2.4 %collective-permute-start.21 = (f32[512,128]{1,0:T(8,128)}, f32[512,128]{1,0:T(8,128)S(1)}, u32[]{:S(2)}, u32[]{:S(2)}) collective-permute-start(f32[512,128]{1,0:T(8,128)} %shard_map.78), channel_id=1, source_target_pairs={{0,4},{3,7},{4,0},{7,3},{8,12},{11,15},{12,8},{15,11},{16,20},{19,... | collective-permute-start | bytes 786440 | tf_op jit(solution)/shard_map/ppermute | solution.py:477
  202.4 1.4 collective-permute-done.21.refs_7_
  204.6 4.3 %shard_map.79 = (f32[7,512,128]{2,1,0:T(8,128)}, f32[7,512,128]{2,1,0:T(8,128)}) custom-call(s32[56]{0:T(128)} %concatenate.3.s, f32[3,1024,128]{2,1,0:T(8,128)} %get-tuple-element.47.refs_0_, f32[3,768,128]{2,1,0:T(8,128)} %copy-done.9, f32[768,128]{1,0:T(8,128)} %copy-done.16, f32[1024,128]{1,0:T(8,128)} %get-tuple-element.58.refs_3_, ...), custom_call_target="tpu_custom_call" | custom-call | flops 1000000000 | bytes 1 | tf_op jit(solution)/shard_map/pallas_call | solution.py:100
  209.0 8.1 %collective-permute-done.24.cross_56 = f32[1024,128]{1,0:T(8,128)S(1)} collective-permute-done((f32[1024,128]{1,0:T(8,128)}, f32[1024,128]{1,0:T(8,128)S(1)}, u32[]{:S(2)}, u32[]{:S(2)}) %collective-permute-start.24) | collective-permute-done | bytes 524320 | tf_op jit(solution)/shard_map/ppermute | solution.py:467
  217.9 2.9 %shard_map.80 = (f32[7,512,128]{2,1,0:T(8,128)}, f32[7,512,128]{2,1,0:T(8,128)}) custom-call(s32[56]{0:T(128)} %concatenate.3.s, f32[7,512,128]{2,1,0:T(8,128)} %get-tuple-element.65.ab_in, f32[7,512,128]{2,1,0:T(8,128)} %get-tuple-element.66.dg_in, f32[1024,128]{1,0:T(8,128)} %get-tuple-element.60.self_56, ...), custom_call_target="tpu_custom_call", output_to_operand_aliasing={{0}: (1, {}), {1}: (2, {})} | custom-call | tf_op jit(solution)/shard_map/pallas_call | solution.py:490
  (80 shorter events, 21.8 us)
Async XLA Ops:
  0.6 17.0 %collective-permute-start.3 = (f32[128,256]{1,0:T(8,128)}, f32[128,256]{1,0:T(8,128)S(1)}, u32[]{:S(2)}, u32[]{:S(2)}) collective-permute-start(f32[128,256]{1,0:T(8,128)} %refs_0_), channel_id=1, source_target_pairs={{0,1},{3,2},{4,5},{7,6},{8,9},{11,10},{12,13},{15,14},{16,17},{19,... | collective-permute-start | bytes 393224 | tf_op jit(solution)/shard_map/ppermute | solution.py:415
  5.6 16.0 %collective-permute-start.4 = (f32[128,256]{1,0:T(8,128)}, f32[128,256]{1,0:T(8,128)S(1)}, u32[]{:S(2)}, u32[]{:S(2)}) collective-permute-start(f32[128,256]{1,0:T(8,128)} %refs_0_), channel_id=1, source_target_pairs={{1,2},{2,1},{5,6},{6,5},{9,10},{10,9},{13,14},{14,13},{17,18},{18,... | collective-permute-start | bytes 393224 | tf_op jit(solution)/shard_map/ppermute | solution.py:415
  6.3 15.3 %collective-permute-start.5 = (f32[128,256]{1,0:T(8,128)}, f32[128,256]{1,0:T(8,128)S(1)}, u32[]{:S(2)}, u32[]{:S(2)}) collective-permute-start(f32[128,256]{1,0:T(8,128)} %refs_0_), channel_id=1, source_target_pairs={{0,2},{3,1},{4,6},{7,5},{8,10},{11,9},{12,14},{15,13},{16,18},{19,... | collective-permute-start | bytes 393224 | tf_op jit(solution)/shard_map/ppermute | solution.py:415
  15.4 28.1 %collective-permute-start = (f32[3,768,128]{2,1,0:T(8,128)}, f32[3,768,128]{2,1,0:T(8,128)S(1)}, u32[]{:S(2)}, u32[]{:S(2)}) collective-permute-start(f32[3,768,128]{2,1,0:T(8,128)} %shard_map.68.refs_0_), channel_id=1, source_target_pairs={{0,1},{3,2},{4,5},{7,6},{8,9},{11,10},{12,13},{15,14},{16,17},{19,... | collective-permute-start | bytes 3538952 | tf_op jit(solution)/shard_map/ppermute | solution.py:415
  16.9 26.6 %collective-permute-start.1 = (f32[3,768,128]{2,1,0:T(8,128)}, f32[3,768,128]{2,1,0:T(8,128)S(1)}, u32[]{:S(2)}, u32[]{:S(2)}) collective-permute-start(f32[3,768,128]{2,1,0:T(8,128)} %shard_map.68.refs_0_), channel_id=1, source_target_pairs={{1,2},{2,1},{5,6},{6,5},{9,10},{10,9},{13,14},{14,13},{17,18},{18,... | collective-permute-start | bytes 3538952 | tf_op jit(solution)/shard_map/ppermute | solution.py:415
  17.6 49.7 %collective-permute-start.2 = (f32[3,768,128]{2,1,0:T(8,128)}, f32[3,768,128]{2,1,0:T(8,128)S(1)}, u32[]{:S(2)}, u32[]{:S(2)}) collective-permute-start(f32[3,768,128]{2,1,0:T(8,128)} %shard_map.68.refs_0_), channel_id=1, source_target_pairs={{0,2},{3,1},{4,6},{7,5},{8,10},{11,9},{12,14},{15,13},{16,18},{19,... | collective-permute-start | bytes 3538952 | tf_op jit(solution)/shard_map/ppermute | solution.py:415
  25.5 1.4 collective-permute-start.6
  26.2 4.8 %collective-permute-start.7 = (f32[128,1024]{1,0:T(8,128)}, f32[128,1024]{1,0:T(8,128)S(1)}, u32[]{:S(2)}, u32[]{:S(2)}) collective-permute-start(f32[128,1024]{1,0:T(8,128)} %shard_map.69.refs_0_.refs_5_), channel_id=1, source_target_pairs={{1,17},{2,18},{5,21},{6,22},{9,25},{10,26},{13,29},{14,30},{17,1},... | collective-permute-start | bytes 1572872 | tf_op jit(solution)/shard_map/ppermute | solution.py:432
  26.9 4.1 %collective-permute-start.8 = (f32[128,1024]{1,0:T(8,128)}, f32[128,1024]{1,0:T(8,128)S(1)}, u32[]{:S(2)}, u32[]{:S(2)}) collective-permute-start(f32[128,1024]{1,0:T(8,128)} %shard_map.69.refs_0_.refs_5_), channel_id=1, source_target_pairs={{1,25},{2,26},{5,29},{6,30},{9,17},{10,18},{13,21},{14,22},{17,9},... | collective-permute-start | bytes 1572872 | tf_op jit(solution)/shard_map/ppermute | solution.py:432
  36.2 40.2 %copy-start.4 = (f32[4,128,1024]{2,1,0:T(8,128)S(1)}, f32[4,128,1024]{2,1,0:T(8,128)}, u32[]{:S(2)}) copy-start(f32[4,128,1024]{2,1,0:T(8,128)} %shard_map.70) | copy-start | bytes 6291460
  36.2 41.0 %copy-start = (f32[4,768,128]{2,1,0:T(8,128)S(1)}, f32[4,768,128]{2,1,0:T(8,128)}, u32[]{:S(2)}) copy-start(f32[4,768,128]{2,1,0:T(8,128)} %shard_map.71.refs_0_.x0) | copy-start | bytes 4718596
  43.5 23.9 %copy-start.1 = (f32[3,768,128]{2,1,0:T(8,128)}, f32[3,768,128]{2,1,0:T(8,128)S(1)}, u32[]{:S(2)}) copy-start(f32[3,768,128]{2,1,0:T(8,128)S(1)} %collective-permute-done.refs_1_) | copy-start | bytes 3538948
  43.5 23.9 %copy-start.2 = (f32[3,768,128]{2,1,0:T(8,128)}, f32[3,768,128]{2,1,0:T(8,128)S(1)}, u32[]{:S(2)}) copy-start(f32[3,768,128]{2,1,0:T(8,128)S(1)} %collective-permute-done.1.refs_2_) | copy-start | bytes 3538948
  73.6 16.8 %collective-permute-start.9 = (f32[4,3,768,128]{3,2,1,0:T(8,128)}, f32[4,3,768,128]{3,2,1,0:T(8,128)}, u32[]{:S(2)}, u32[]{:S(2)}) collective-permute-start(f32[4,3,768,128]{3,2,1,0:T(8,128)} %shard_map.72), channel_id=1, source_target_pairs={{1,5},{2,6},{5,1},{6,2},{9,13},{10,14},{13,9},{14,10},{17,21},{18,... | collective-permute-start | bytes 14155784 | tf_op jit(solution)/shard_map/ppermute | solution.py:418
  76.4 13.9 %collective-permute-start.10 = (f32[4,128,1024]{2,1,0:T(8,128)S(1)}, f32[4,128,1024]{2,1,0:T(8,128)S(1)}, u32[]{:S(2)}, u32[]{:S(2)}) collective-permute-start(f32[4,128,1024]{2,1,0:T(8,128)S(1)} %copy-done.4), channel_id=1, source_target_pairs={{1,5},{2,6},{5,1},{6,2},{9,13},{10,14},{13,9},{14,10},{17,21},{18,... | collective-permute-start | bytes 6291464 | tf_op jit(solution)/shard_map/ppermute | solution.py:418
  77.2 50.4 %collective-permute-start.12 = (f32[4,768,128]{2,1,0:T(8,128)S(1)}, f32[4,768,128]{2,1,0:T(8,128)}, u32[]{:S(2)}, u32[]{:S(2)}) collective-permute-start(f32[4,768,128]{2,1,0:T(8,128)S(1)} %copy-done), channel_id=1, source_target_pairs={{0,1},{3,2},{4,5},{7,6},{8,9},{11,10},{12,13},{15,14},{16,17},{19,... | collective-permute-start | bytes 4718600 | tf_op jit(solution)/shard_map/ppermute | solution.py:415
  85.6 42.0 %collective-permute-start.13 = (f32[4,768,128]{2,1,0:T(8,128)S(1)}, f32[4,768,128]{2,1,0:T(8,128)}, u32[]{:S(2)}, u32[]{:S(2)}) collective-permute-start(f32[4,768,128]{2,1,0:T(8,128)S(1)} %copy-done), channel_id=1, source_target_pairs={{1,2},{2,1},{5,6},{6,5},{9,10},{10,9},{13,14},{14,13},{17,18},{18,... | collective-permute-start | bytes 4718600 | tf_op jit(solution)/shard_map/ppermute | solution.py:415
  87.4 64.6 %collective-permute-start.14 = (f32[4,768,128]{2,1,0:T(8,128)S(1)}, f32[4,768,128]{2,1,0:T(8,128)}, u32[]{:S(2)}, u32[]{:S(2)}) collective-permute-start(f32[4,768,128]{2,1,0:T(8,128)S(1)} %copy-done), channel_id=1, source_target_pairs={{0,2},{3,1},{4,6},{7,5},{8,10},{11,9},{12,14},{15,13},{16,18},{19,... | collective-permute-start | bytes 4718600 | tf_op jit(solution)/shard_map/ppermute | solution.py:415
  126.3 29.4 %collective-permute-start.11 = (f32[3,768,128]{2,1,0:T(8,128)}, f32[3,768,128]{2,1,0:T(8,128)S(1)}, u32[]{:S(2)}, u32[]{:S(2)}) collective-permute-start(f32[3,768,128]{2,1,0:T(8,128)} %get-tuple-element.48), channel_id=1, source_target_pairs={{1,0},{2,3},{5,4},{6,7},{9,8},{10,11},{13,12},{14,15},{17,16},{18,... | collective-permute-start | bytes 3538952 | tf_op jit(solution)/shard_map/ppermute | solution.py:451
  155.7 4.3 %copy-start.9 = (f32[3,768,128]{2,1,0:T(8,128)}, f32[3,768,128]{2,1,0:T(8,128)S(1)}, u32[]{:S(2)}) copy-start(f32[3,768,128]{2,1,0:T(8,128)S(1)} %collective-permute-done.11.upper.refs_1_) | copy-start | bytes 3538948
  160.0 1.8 collective-permute-start.16
  160.8 13.8 %collective-permute-start.15 = (f32[4,768,128]{2,1,0:T(8,128)}, f32[4,768,128]{2,1,0:T(8,128)S(1)}, u32[]{:S(2)}, u32[]{:S(2)}) collective-permute-start(f32[4,768,128]{2,1,0:T(8,128)} %get-tuple-element.55), channel_id=1, source_target_pairs={{1,5},{2,6},{5,1},{6,2},{9,13},{10,14},{13,9},{14,10},{17,21},{18,... | collective-permute-start | bytes 4718600 | tf_op jit(solution)/shard_map/ppermute | solution.py:418
  171.9 14.9 %collective-permute-start.17 = (f32[768,128]{1,0:T(8,128)}, f32[768,128]{1,0:T(8,128)S(1)}, u32[]{:S(2)}, u32[]{:S(2)}) collective-permute-start(f32[768,128]{1,0:T(8,128)} %get-tuple-element.61), channel_id=1, source_target_pairs={{1,4},{2,7},{5,0},{6,3},{9,12},{10,15},{13,8},{14,11},{17,20},{18,... | collective-permute-start | bytes 1179656 | tf_op jit(solution)/shard_map/ppermute | solution.py:467
  173.2 22.4 %collective-permute-start.20 = (f32[768,128]{1,0:T(8,128)}, f32[768,128]{1,0:T(8,128)S(1)}, u32[]{:S(2)}, u32[]{:S(2)}) collective-permute-start(f32[768,128]{1,0:T(8,128)} %get-tuple-element.64), channel_id=1, source_target_pairs={{1,0},{2,3},{5,4},{6,7},{9,8},{10,11},{13,12},{14,15},{17,16},{18,... | collective-permute-start | bytes 1179656 | tf_op jit(solution)/shard_map/ppermute | solution.py:467
  174.5 25.4 %collective-permute-start.19 = (f32[1024,128]{1,0:T(8,128)}, f32[1024,128]{1,0:T(8,128)S(1)}, u32[]{:S(2)}, u32[]{:S(2)}) collective-permute-start(f32[1024,128]{1,0:T(8,128)} %get-tuple-element.63), channel_id=1, source_target_pairs={{1,5},{2,6},{5,1},{6,2},{9,13},{10,14},{13,9},{14,10},{17,21},{18,... | collective-permute-start | bytes 1572872 | tf_op jit(solution)/shard_map/ppermute | solution.py:418
  184.8 24.1 %collective-permute-start.22 = (f32[1024,128]{1,0:T(8,128)}, f32[1024,128]{1,0:T(8,128)S(1)}, u32[]{:S(2)}, u32[]{:S(2)}) collective-permute-start(f32[1024,128]{1,0:T(8,128)} %get-tuple-element.67), channel_id=1, source_target_pairs={{1,5},{2,6},{5,1},{6,2},{9,13},{10,14},{13,9},{14,10},{17,21},{18,... | collective-permute-start | bytes 1572872 | tf_op jit(solution)/shard_map/ppermute | solution.py:418
  185.5 23.4 %collective-permute-start.23 = (f32[1024,128]{1,0:T(8,128)}, f32[1024,128]{1,0:T(8,128)S(1)}, u32[]{:S(2)}, u32[]{:S(2)}) collective-permute-start(f32[1024,128]{1,0:T(8,128)} %get-tuple-element.68), channel_id=1, source_target_pairs={{1,0},{2,3},{5,4},{6,7},{9,8},{10,11},{13,12},{14,15},{17,16},{18,... | collective-permute-start | bytes 1572872 | tf_op jit(solution)/shard_map/ppermute | solution.py:467
  186.9 30.2 %collective-permute-start.24 = (f32[1024,128]{1,0:T(8,128)}, f32[1024,128]{1,0:T(8,128)S(1)}, u32[]{:S(2)}, u32[]{:S(2)}) collective-permute-start(f32[1024,128]{1,0:T(8,128)} %get-tuple-element.69), channel_id=1, source_target_pairs={{1,4},{2,7},{5,0},{6,3},{9,12},{10,15},{13,8},{14,11},{17,20},{18,... | collective-permute-start | bytes 1572872 | tf_op jit(solution)/shard_map/ppermute | solution.py:467
  195.7 8.1 %collective-permute-start.18 = (f32[768,128]{1,0:T(8,128)}, f32[768,128]{1,0:T(8,128)S(1)}, u32[]{:S(2)}, u32[]{:S(2)}) collective-permute-start(f32[768,128]{1,0:T(8,128)} %shard_map.77), channel_id=1, source_target_pairs={{0,4},{3,7},{4,0},{7,3},{8,12},{11,15},{12,8},{15,11},{16,20},{19,... | collective-permute-start | bytes 1179656 | tf_op jit(solution)/shard_map/ppermute | solution.py:477
  200.0 3.8 %collective-permute-start.21 = (f32[512,128]{1,0:T(8,128)}, f32[512,128]{1,0:T(8,128)S(1)}, u32[]{:S(2)}, u32[]{:S(2)}) collective-permute-start(f32[512,128]{1,0:T(8,128)} %shard_map.78), channel_id=1, source_target_pairs={{0,4},{3,7},{4,0},{7,3},{8,12},{11,15},{12,8},{15,11},{16,20},{19,... | collective-permute-start | bytes 786440 | tf_op jit(solution)/shard_map/ppermute | solution.py:477
  208.9 8.2 %copy-start.10 = (f32[1024,128]{1,0:T(8,128)}, f32[1024,128]{1,0:T(8,128)S(1)}, u32[]{:S(2)}) copy-start(f32[1024,128]{1,0:T(8,128)S(1)} %collective-permute-done.22.core_56) | copy-start | bytes 1572868
  209.0 8.2 %copy-start.11 = (f32[1024,128]{1,0:T(8,128)}, f32[1024,128]{1,0:T(8,128)S(1)}, u32[]{:S(2)}) copy-start(f32[1024,128]{1,0:T(8,128)S(1)} %collective-permute-done.23.end_56) | copy-start | bytes 1572868
  (16 other events, 27.4 us)

commit v11 on v10

--- a/solution.py
+++ b/solution.py
@@ -468,9 +468,10 @@
 
     chosen = after(blocks_l, (ext, upper_home))
     picked_34, picked_56 = move(swap_kernel, here, chosen, [(4, packed, TILE)] * 2, 8)
-    other_34, other_56 = swapped(picked_34), swapped(picked_56)
+    other_34 = swapped(picked_34)
     self_34, core_34, end_34, cross_34 = leaves(3, other_34, packed)
-    self_56, core_56, end_56, cross_56 = leaves(5, after(other_56, self_34), half + own)
+    other_56 = swapped(after(picked_56, self_34))
+    self_56, core_56, end_56, cross_56 = leaves(5, other_56, half + own)
 
     def shared(kernel, parts, count):
         out = move(kernel, here, parts, [(count * (own // 2), TILE)], count)[0]

time: 222 us -> 225 us (1.014)
  waiting for transfers between devices: 73.8 us -> 76.2 us
    ppermute x2, waiting for transfers between devices: 8.14 us -> 12.5 us  [leaves(): lax.ppermute(cross_out, both, home_cross)]
    unnamed x46 -> x48, local copies, waits for them, and re-layouts: 8.47 us -> 9.13 us
  transfers between devices with their start and end apart: 25 -> 25, of which waited for: 7 -> 8; matrix products, arithmetic and copies ran while one was open for 1% -> 1% of each run, Pallas kernels for 34% -> 29%
where the time goes in v11:
time: 225 us; the launch traced here: 224 us
  Pallas kernels  86.9 us (39%)
  waiting for transfers between devices  76.2 us (34%)
  starting transfers between devices  48.5 us (22%)
  local copies, waits for them, and re-layouts  10.5 us (5%)
    pallas_call x12, Pallas kernels, call(): pl.pallas_call(kernel, out_shape=[jax.ShapeDtypeStruct(o, F32) for o in o...  84.1 us
    ppermute x9, waiting for transfers between devices, straight(): return [x] + [lax.ppermute(x, 'col', route) for route in routes]  55.7 us
    ppermute x9, starting transfers between devices, straight(): return [x] + [lax.ppermute(x, 'col', route) for route in routes]  28.9 us
    ppermute x2, waiting for transfers between devices, leaves(): lax.ppermute(cross_out, both, home_cross)  12.5 us
    unnamed x48, local copies, waits for them, and re-layouts  9.13 us
    ppermute x6, starting transfers between devices, swapped(): return lax.ppermute(x, both, swap)  6.74 us
  transfers between devices with their start and end apart: 25, of which 8 were waited for; matrix products, arithmetic and copies ran while one was open for 1% of the time, Pallas kernels for 29%

profile of v11, /device:TPU:0, one launch (start us, length us, event | category | flops | bytes accessed | tf_op | source)
XLA Modules:
  0.0 224.1 jit_solution(12502191942723716043)
XLA Ops:
  0.6 4.9 %collective-permute-start.3 = (f32[128,256]{1,0:T(8,128)}, f32[128,256]{1,0:T(8,128)S(1)}, u32[]{:S(2)}, u32[]{:S(2)}) collective-permute-start(f32[128,256]{1,0:T(8,128)} %refs_0_), channel_id=1, source_target_pairs={{0,1},{3,2},{4,5},{7,6},{8,9},{11,10},{12,13},{15,14},{16,17},{19,... | collective-permute-start | bytes 393224 | tf_op jit(solution)/shard_map/ppermute | solution.py:415
  6.3 4.0 %collective-permute-start.5 = (f32[128,256]{1,0:T(8,128)}, f32[128,256]{1,0:T(8,128)S(1)}, u32[]{:S(2)}, u32[]{:S(2)}) collective-permute-start(f32[128,256]{1,0:T(8,128)} %refs_0_), channel_id=1, source_target_pairs={{0,2},{3,1},{4,6},{7,5},{8,10},{11,9},{12,14},{15,13},{16,18},{19,... | collective-permute-start | bytes 393224 | tf_op jit(solution)/shard_map/ppermute | solution.py:415
  11.0 1.3 concatenate.3.s
  12.3 3.1 %shard_map.68.refs_0_ = f32[3,768,128]{2,1,0:T(8,128)} custom-call(s32[56]{0:T(128)} %concatenate.3.s, f32[7,512,128]{2,1,0:T(8,128)} %bitcast.8, f32[7,128,512]{2,1,0:T(8,128)} %bitcast.10), custom_call_target="tpu_custom_call" | custom-call | flops 1000000000 | bytes 1 | tf_op jit(solution)/shard_map/pallas_call | solution.py:100
  15.4 1.5 collective-permute-start
  17.7 3.9 %collective-permute-start.2 = (f32[3,768,128]{2,1,0:T(8,128)}, f32[3,768,128]{2,1,0:T(8,128)S(1)}, u32[]{:S(2)}, u32[]{:S(2)}) collective-permute-start(f32[3,768,128]{2,1,0:T(8,128)} %shard_map.68.refs_0_), channel_id=1, source_target_pairs={{0,2},{3,1},{4,6},{7,5},{8,10},{11,9},{12,14},{15,13},{16,18},{19,... | collective-permute-start | bytes 3538952 | tf_op jit(solution)/shard_map/ppermute | solution.py:415
  22.9 2.6 %shard_map.69.refs_0_.refs_5_ = f32[128,1024]{1,0:T(8,128)} custom-call(s32[56]{0:T(128)} %concatenate.3.s, f32[128,256]{1,0:T(8,128)} %refs_0_, f32[128,256]{1,0:T(8,128)} %copy-done.21, f32[128,256]{1,0:T(8,128)} %copy-done.22, f32[128,256]{1,0:T(8,128)} %copy-done.23), custom_call_target="tpu_custom_call" | custom-call | flops 1000000000 | bytes 1 | tf_op jit(solution)/shard_map/pallas_call | solution.py:100
  27.6 3.3 %shard_map.71.refs_0_.x0 = f32[4,768,128]{2,1,0:T(8,128)} custom-call(s32[56]{0:T(128)} %concatenate.3.s, f32[7,512,128]{2,1,0:T(8,128)} %bitcast.9, f32[7,128,512]{2,1,0:T(8,128)} %bitcast.11), custom_call_target="tpu_custom_call" | custom-call | flops 1000000000 | bytes 1 | tf_op jit(solution)/shard_map/pallas_call | solution.py:100
  32.6 3.5 %shard_map.70 = f32[4,128,1024]{2,1,0:T(8,128)} custom-call(s32[56]{0:T(128)} %concatenate.3.s, f32[128,1024]{1,0:T(8,128)} %shard_map.69.refs_0_.refs_5_, f32[128,1024]{1,0:T(8,128)} %copy-done.6, f32[128,1024]{1,0:T(8,128)} %copy-done.7, f32[128,1024]{1,0:T(8,128)} %copy-done.8), custom_call_target="tpu_custom_call" | custom-call | flops 1000000000 | bytes 1 | tf_op jit(solution)/shard_map/pallas_call | solution.py:100
  36.2 7.3 %collective-permute-done.refs_1_ = f32[3,768,128]{2,1,0:T(8,128)S(1)} collective-permute-done((f32[3,768,128]{2,1,0:T(8,128)}, f32[3,768,128]{2,1,0:T(8,128)S(1)}, u32[]{:S(2)}, u32[]{:S(2)}) %collective-permute-start) | collective-permute-done | bytes 1179680 | tf_op jit(solution)/shard_map/ppermute | solution.py:415
  43.5 23.9 %collective-permute-done.2.refs_3_ = f32[3,768,128]{2,1,0:T(8,128)S(1)} collective-permute-done((f32[3,768,128]{2,1,0:T(8,128)}, f32[3,768,128]{2,1,0:T(8,128)S(1)}, u32[]{:S(2)}, u32[]{:S(2)}) %collective-permute-start.2) | collective-permute-done | bytes 1179680 | tf_op jit(solution)/shard_map/ppermute | solution.py:415
  68.4 5.2 %shard_map.72 = f32[4,3,768,128]{3,2,1,0:T(8,128)} custom-call(s32[56]{0:T(128)} %concatenate.3.s, f32[3,768,128]{2,1,0:T(8,128)} %shard_map.68.refs_0_, f32[3,768,128]{2,1,0:T(8,128)} %copy-done.1, f32[3,768,128]{2,1,0:T(8,128)} %copy-done.2, f32[3,768,128]{2,1,0:T(8,128)} %copy-done.3), custom_call_target="tpu_custom_call" | custom-call | flops 1000000000 | bytes 1 | tf_op jit(solution)/shard_map/pallas_call | solution.py:100
  73.6 2.8 %collective-permute-start.9 = (f32[4,3,768,128]{3,2,1,0:T(8,128)}, f32[4,3,768,128]{3,2,1,0:T(8,128)}, u32[]{:S(2)}, u32[]{:S(2)}) collective-permute-start(f32[4,3,768,128]{3,2,1,0:T(8,128)} %shard_map.72), channel_id=1, source_target_pairs={{1,5},{2,6},{5,1},{6,2},{9,13},{10,14},{13,9},{14,10},{17,21},{18,... | collective-permute-start | bytes 14155784 | tf_op jit(solution)/shard_map/ppermute | solution.py:418
  77.2 8.4 %collective-permute-start.12 = (f32[4,768,128]{2,1,0:T(8,128)S(1)}, f32[4,768,128]{2,1,0:T(8,128)}, u32[]{:S(2)}, u32[]{:S(2)}) collective-permute-start(f32[4,768,128]{2,1,0:T(8,128)S(1)} %copy-done), channel_id=1, source_target_pairs={{0,1},{3,2},{4,5},{7,6},{8,9},{11,10},{12,13},{15,14},{16,17},{19,... | collective-permute-start | bytes 4718600 | tf_op jit(solution)/shard_map/ppermute | solution.py:415
  85.7 1.8 collective-permute-start.13
  87.5 2.9 %collective-permute-start.14 = (f32[4,768,128]{2,1,0:T(8,128)S(1)}, f32[4,768,128]{2,1,0:T(8,128)}, u32[]{:S(2)}, u32[]{:S(2)}) collective-permute-start(f32[4,768,128]{2,1,0:T(8,128)S(1)} %copy-done), channel_id=1, source_target_pairs={{0,2},{3,1},{4,6},{7,5},{8,10},{11,9},{12,14},{15,13},{16,18},{19,... | collective-permute-start | bytes 4718600 | tf_op jit(solution)/shard_map/ppermute | solution.py:415
  91.7 34.6 %shard_map.73 = (f32[2,1024,512]{2,1,0:T(8,128)}, f32[512,512]{1,0:T(8,128)}, f32[3,1024,128]{2,1,0:T(8,128)}, f32[3,768,128]{2,1,0:T(8,128)}) custom-call(s32[56]{0:T(128)} %concatenate.3.s, f32[3,768,128]{2,1,0:T(8,128)} %shard_map.68.refs_0_, f32[3,768,128]{2,1,0:T(8,128)} %copy-done.1, f32[3,768,128]{2,1,0:T(8,128)} %copy-done.2, ...), custom_call_target="tpu_custom_call" | custom-call | flops 1000000000 | bytes 1 | tf_op jit(solution)/shard_map/pallas_call | solution.py:100
  127.6 24.5 %collective-permute-done.14.refs_3_.x3 = f32[4,768,128]{2,1,0:T(8,128)} collective-permute-done((f32[4,768,128]{2,1,0:T(8,128)S(1)}, f32[4,768,128]{2,1,0:T(8,128)}, u32[]{:S(2)}, u32[]{:S(2)}) %collective-permute-start.14) | collective-permute-done | bytes 1572896 | tf_op jit(solution)/shard_map/ppermute | solution.py:415
  152.1 3.7 %collective-permute-done.11.upper.refs_1_ = f32[3,768,128]{2,1,0:T(8,128)S(1)} collective-permute-done((f32[3,768,128]{2,1,0:T(8,128)}, f32[3,768,128]{2,1,0:T(8,128)S(1)}, u32[]{:S(2)}, u32[]{:S(2)}) %collective-permute-start.11) | collective-permute-done | bytes 1179680 | tf_op jit(solution)/shard_map/ppermute | solution.py:451
  155.8 4.2 %shard_map.74 = (f32[4,768,128]{2,1,0:T(8,128)}, f32[4,768,128]{2,1,0:T(8,128)}) custom-call(s32[56]{0:T(128)} %concatenate.3.s, f32[4,768,128]{2,1,0:T(8,128)} %shard_map.71.refs_0_.x0, f32[4,768,128]{2,1,0:T(8,128)} %collective-permute-done.12.refs_1_.x1, f32[4,768,128]{2,1,0:T(8,128)} %collective-permute-done.13.refs_2_.x2, ...), custom_call_target="tpu_custom_call" | custom-call | flops 1000000000 | bytes 1 | tf_op jit(solution)/shard_map/pallas_call | solution.py:100
  162.2 9.1 %shard_map.75 = (f32[1024,128]{1,0:T(8,128)}, f32[1024,128]{1,0:T(8,128)}, f32[768,128]{1,0:T(8,128)}, f32[768,128]{1,0:T(8,128)}) custom-call(s32[56]{0:T(128)} %concatenate.3.s, f32[4,768,128]{2,1,0:T(8,128)} %shard_map.71.refs_0_.x0, f32[4,768,128]{2,1,0:T(8,128)} %collective-permute-done.12.refs_1_.x1, ...), custom_call_target="tpu_custom_call" | custom-call | flops 10000000000 | bytes 1 | tf_op jit(solution)/shard_map/pallas_call | solution.py:100
  176.5 9.2 %shard_map.76 = (f32[1024,128]{1,0:T(8,128)}, f32[1024,128]{1,0:T(8,128)}, f32[1024,128]{1,0:T(8,128)}, f32[1024,128]{1,0:T(8,128)}) custom-call(s32[56]{0:T(128)} %concatenate.3.s, f32[4,768,128]{2,1,0:T(8,128)} %shard_map.71.refs_0_.x0, f32[4,768,128]{2,1,0:T(8,128)} %collective-permute-done.12.refs_1_.x1, ...), custom_call_target="tpu_custom_call" | custom-call | flops 10000000000 | bytes 1 | tf_op jit(solution)/shard_map/pallas_call | solution.py:100
  185.7 3.2 %collective-permute-done.17.refs_1_.refs_6_ = f32[768,128]{1,0:T(8,128)S(1)} collective-permute-done((f32[768,128]{1,0:T(8,128)}, f32[768,128]{1,0:T(8,128)S(1)}, u32[]{:S(2)}, u32[]{:S(2)}) %collective-permute-start.17) | collective-permute-done | bytes 393248 | tf_op jit(solution)/shard_map/ppermute | solution.py:467
  192.2 2.5 %shard_map.77 = f32[768,128]{1,0:T(8,128)} custom-call(s32[56]{0:T(128)} %concatenate.3.s, f32[3,768,128]{2,1,0:T(8,128)} %copy-done.9), custom_call_target="tpu_custom_call" | custom-call | flops 1000000000 | bytes 1 | tf_op jit(solution)/shard_map/pallas_call | solution.py:100
  194.7 3.0 %collective-permute-done.20.refs_0_.refs_5_ = f32[768,128]{1,0:T(8,128)S(1)} collective-permute-done((f32[768,128]{1,0:T(8,128)}, f32[768,128]{1,0:T(8,128)S(1)}, u32[]{:S(2)}, u32[]{:S(2)}) %collective-permute-start.20) | collective-permute-done | bytes 393248 | tf_op jit(solution)/shard_map/ppermute | solution.py:467
  197.6 1.9 collective-permute-start.18
  199.6 2.3 %shard_map.78 = f32[512,128]{1,0:T(8,128)} custom-call(s32[56]{0:T(128)} %concatenate.3.s, f32[768,128]{1,0:T(8,128)} %copy-done.15, f32[768,128]{1,0:T(8,128)} %copy-done.14), custom_call_target="tpu_custom_call" | custom-call | flops 1000000000 | bytes 1 | tf_op jit(solution)/shard_map/pallas_call | solution.py:100
  201.9 2.4 %collective-permute-start.21 = (f32[512,128]{1,0:T(8,128)}, f32[512,128]{1,0:T(8,128)S(1)}, u32[]{:S(2)}, u32[]{:S(2)}) collective-permute-start(f32[512,128]{1,0:T(8,128)} %shard_map.78), channel_id=1, source_target_pairs={{0,4},{3,7},{4,0},{7,3},{8,12},{11,15},{12,8},{15,11},{16,20},{19,... | collective-permute-start | bytes 786440 | tf_op jit(solution)/shard_map/ppermute | solution.py:478
  204.4 1.4 collective-permute-done.21.refs_7_
  206.6 4.3 %shard_map.79 = (f32[7,512,128]{2,1,0:T(8,128)}, f32[7,512,128]{2,1,0:T(8,128)}) custom-call(s32[56]{0:T(128)} %concatenate.3.s, f32[3,1024,128]{2,1,0:T(8,128)} %get-tuple-element.47.refs_0_, f32[3,768,128]{2,1,0:T(8,128)} %copy-done.9, f32[768,128]{1,0:T(8,128)} %copy-done.16, f32[1024,128]{1,0:T(8,128)} %get-tuple-element.58.refs_3_, ...), custom_call_target="tpu_custom_call" | custom-call | flops 1000000000 | bytes 1 | tf_op jit(solution)/shard_map/pallas_call | solution.py:100
  211.0 9.3 %collective-permute-done.24.cross_56 = f32[1024,128]{1,0:T(8,128)S(1)} collective-permute-done((f32[1024,128]{1,0:T(8,128)}, f32[1024,128]{1,0:T(8,128)S(1)}, u32[]{:S(2)}, u32[]{:S(2)}) %collective-permute-start.24) | collective-permute-done | bytes 524320 | tf_op jit(solution)/shard_map/ppermute | solution.py:467
  221.1 2.9 %shard_map.80 = (f32[7,512,128]{2,1,0:T(8,128)}, f32[7,512,128]{2,1,0:T(8,128)}) custom-call(s32[56]{0:T(128)} %concatenate.3.s, f32[7,512,128]{2,1,0:T(8,128)} %get-tuple-element.65.ab_in, f32[7,512,128]{2,1,0:T(8,128)} %get-tuple-element.66.dg_in, f32[1024,128]{1,0:T(8,128)} %get-tuple-element.60.self_56, ...), custom_call_target="tpu_custom_call", output_to_operand_aliasing={{0}: (1, {}), {1}: (2, {})} | custom-call | tf_op jit(solution)/shard_map/pallas_call | solution.py:491
  (82 shorter events, 23.8 us)
Async XLA Ops:
  0.6 17.0 %collective-permute-start.3 = (f32[128,256]{1,0:T(8,128)}, f32[128,256]{1,0:T(8,128)S(1)}, u32[]{:S(2)}, u32[]{:S(2)}) collective-permute-start(f32[128,256]{1,0:T(8,128)} %refs_0_), channel_id=1, source_target_pairs={{0,1},{3,2},{4,5},{7,6},{8,9},{11,10},{12,13},{15,14},{16,17},{19,... | collective-permute-start | bytes 393224 | tf_op jit(solution)/shard_map/ppermute | solution.py:415
  5.6 16.0 %collective-permute-start.4 = (f32[128,256]{1,0:T(8,128)}, f32[128,256]{1,0:T(8,128)S(1)}, u32[]{:S(2)}, u32[]{:S(2)}) collective-permute-start(f32[128,256]{1,0:T(8,128)} %refs_0_), channel_id=1, source_target_pairs={{1,2},{2,1},{5,6},{6,5},{9,10},{10,9},{13,14},{14,13},{17,18},{18,... | collective-permute-start | bytes 393224 | tf_op jit(solution)/shard_map/ppermute | solution.py:415
  6.3 15.4 %collective-permute-start.5 = (f32[128,256]{1,0:T(8,128)}, f32[128,256]{1,0:T(8,128)S(1)}, u32[]{:S(2)}, u32[]{:S(2)}) collective-permute-start(f32[128,256]{1,0:T(8,128)} %refs_0_), channel_id=1, source_target_pairs={{0,2},{3,1},{4,6},{7,5},{8,10},{11,9},{12,14},{15,13},{16,18},{19,... | collective-permute-start | bytes 393224 | tf_op jit(solution)/shard_map/ppermute | solution.py:415
  15.4 28.1 %collective-permute-start = (f32[3,768,128]{2,1,0:T(8,128)}, f32[3,768,128]{2,1,0:T(8,128)S(1)}, u32[]{:S(2)}, u32[]{:S(2)}) collective-permute-start(f32[3,768,128]{2,1,0:T(8,128)} %shard_map.68.refs_0_), channel_id=1, source_target_pairs={{0,1},{3,2},{4,5},{7,6},{8,9},{11,10},{12,13},{15,14},{16,17},{19,... | collective-permute-start | bytes 3538952 | tf_op jit(solution)/shard_map/ppermute | solution.py:415
  16.9 26.6 %collective-permute-start.1 = (f32[3,768,128]{2,1,0:T(8,128)}, f32[3,768,128]{2,1,0:T(8,128)S(1)}, u32[]{:S(2)}, u32[]{:S(2)}) collective-permute-start(f32[3,768,128]{2,1,0:T(8,128)} %shard_map.68.refs_0_), channel_id=1, source_target_pairs={{1,2},{2,1},{5,6},{6,5},{9,10},{10,9},{13,14},{14,13},{17,18},{18,... | collective-permute-start | bytes 3538952 | tf_op jit(solution)/shard_map/ppermute | solution.py:415
  17.7 49.7 %collective-permute-start.2 = (f32[3,768,128]{2,1,0:T(8,128)}, f32[3,768,128]{2,1,0:T(8,128)S(1)}, u32[]{:S(2)}, u32[]{:S(2)}) collective-permute-start(f32[3,768,128]{2,1,0:T(8,128)} %shard_map.68.refs_0_), channel_id=1, source_target_pairs={{0,2},{3,1},{4,6},{7,5},{8,10},{11,9},{12,14},{15,13},{16,18},{19,... | collective-permute-start | bytes 3538952 | tf_op jit(solution)/shard_map/ppermute | solution.py:415
  25.5 1.4 collective-permute-start.6
  26.2 4.8 %collective-permute-start.7 = (f32[128,1024]{1,0:T(8,128)}, f32[128,1024]{1,0:T(8,128)S(1)}, u32[]{:S(2)}, u32[]{:S(2)}) collective-permute-start(f32[128,1024]{1,0:T(8,128)} %shard_map.69.refs_0_.refs_5_), channel_id=1, source_target_pairs={{1,17},{2,18},{5,21},{6,22},{9,25},{10,26},{13,29},{14,30},{17,1},... | collective-permute-start | bytes 1572872 | tf_op jit(solution)/shard_map/ppermute | solution.py:432
  26.9 4.1 %collective-permute-start.8 = (f32[128,1024]{1,0:T(8,128)}, f32[128,1024]{1,0:T(8,128)S(1)}, u32[]{:S(2)}, u32[]{:S(2)}) collective-permute-start(f32[128,1024]{1,0:T(8,128)} %shard_map.69.refs_0_.refs_5_), channel_id=1, source_target_pairs={{1,25},{2,26},{5,29},{6,30},{9,17},{10,18},{13,21},{14,22},{17,9},... | collective-permute-start | bytes 1572872 | tf_op jit(solution)/shard_map/ppermute | solution.py:432
  36.2 40.3 %copy-start.4 = (f32[4,128,1024]{2,1,0:T(8,128)S(1)}, f32[4,128,1024]{2,1,0:T(8,128)}, u32[]{:S(2)}) copy-start(f32[4,128,1024]{2,1,0:T(8,128)} %shard_map.70) | copy-start | bytes 6291460
  36.2 41.1 %copy-start = (f32[4,768,128]{2,1,0:T(8,128)S(1)}, f32[4,768,128]{2,1,0:T(8,128)}, u32[]{:S(2)}) copy-start(f32[4,768,128]{2,1,0:T(8,128)} %shard_map.71.refs_0_.x0) | copy-start | bytes 4718596
  43.5 23.9 %copy-start.1 = (f32[3,768,128]{2,1,0:T(8,128)}, f32[3,768,128]{2,1,0:T(8,128)S(1)}, u32[]{:S(2)}) copy-start(f32[3,768,128]{2,1,0:T(8,128)S(1)} %collective-permute-done.refs_1_) | copy-start | bytes 3538948
  43.5 23.9 %copy-start.2 = (f32[3,768,128]{2,1,0:T(8,128)}, f32[3,768,128]{2,1,0:T(8,128)S(1)}, u32[]{:S(2)}) copy-start(f32[3,768,128]{2,1,0:T(8,128)S(1)} %collective-permute-done.1.refs_2_) | copy-start | bytes 3538948
  73.6 16.8 %collective-permute-start.9 = (f32[4,3,768,128]{3,2,1,0:T(8,128)}, f32[4,3,768,128]{3,2,1,0:T(8,128)}, u32[]{:S(2)}, u32[]{:S(2)}) collective-permute-start(f32[4,3,768,128]{3,2,1,0:T(8,128)} %shard_map.72), channel_id=1, source_target_pairs={{1,5},{2,6},{5,1},{6,2},{9,13},{10,14},{13,9},{14,10},{17,21},{18,... | collective-permute-start | bytes 14155784 | tf_op jit(solution)/shard_map/ppermute | solution.py:418
  76.4 13.9 %collective-permute-start.10 = (f32[4,128,1024]{2,1,0:T(8,128)S(1)}, f32[4,128,1024]{2,1,0:T(8,128)S(1)}, u32[]{:S(2)}, u32[]{:S(2)}) collective-permute-start(f32[4,128,1024]{2,1,0:T(8,128)S(1)} %copy-done.4), channel_id=1, source_target_pairs={{1,5},{2,6},{5,1},{6,2},{9,13},{10,14},{13,9},{14,10},{17,21},{18,... | collective-permute-start | bytes 6291464 | tf_op jit(solution)/shard_map/ppermute | solution.py:418
  77.2 50.4 %collective-permute-start.12 = (f32[4,768,128]{2,1,0:T(8,128)S(1)}, f32[4,768,128]{2,1,0:T(8,128)}, u32[]{:S(2)}, u32[]{:S(2)}) collective-permute-start(f32[4,768,128]{2,1,0:T(8,128)S(1)} %copy-done), channel_id=1, source_target_pairs={{0,1},{3,2},{4,5},{7,6},{8,9},{11,10},{12,13},{15,14},{16,17},{19,... | collective-permute-start | bytes 4718600 | tf_op jit(solution)/shard_map/ppermute | solution.py:415
  85.7 42.0 %collective-permute-start.13 = (f32[4,768,128]{2,1,0:T(8,128)S(1)}, f32[4,768,128]{2,1,0:T(8,128)}, u32[]{:S(2)}, u32[]{:S(2)}) collective-permute-start(f32[4,768,128]{2,1,0:T(8,128)S(1)} %copy-done), channel_id=1, source_target_pairs={{1,2},{2,1},{5,6},{6,5},{9,10},{10,9},{13,14},{14,13},{17,18},{18,... | collective-permute-start | bytes 4718600 | tf_op jit(solution)/shard_map/ppermute | solution.py:415
  87.5 64.6 %collective-permute-start.14 = (f32[4,768,128]{2,1,0:T(8,128)S(1)}, f32[4,768,128]{2,1,0:T(8,128)}, u32[]{:S(2)}, u32[]{:S(2)}) collective-permute-start(f32[4,768,128]{2,1,0:T(8,128)S(1)} %copy-done), channel_id=1, source_target_pairs={{0,2},{3,1},{4,6},{7,5},{8,10},{11,9},{12,14},{15,13},{16,18},{19,... | collective-permute-start | bytes 4718600 | tf_op jit(solution)/shard_map/ppermute | solution.py:415
  126.3 29.4 %collective-permute-start.11 = (f32[3,768,128]{2,1,0:T(8,128)}, f32[3,768,128]{2,1,0:T(8,128)S(1)}, u32[]{:S(2)}, u32[]{:S(2)}) collective-permute-start(f32[3,768,128]{2,1,0:T(8,128)} %get-tuple-element.48), channel_id=1, source_target_pairs={{1,0},{2,3},{5,4},{6,7},{9,8},{10,11},{13,12},{14,15},{17,16},{18,... | collective-permute-start | bytes 3538952 | tf_op jit(solution)/shard_map/ppermute | solution.py:451
  160.0 1.0 collective-permute-start.15
  162.2 9.1 %copy-start.18 = (f32[4,768,128]{2,1,0:T(8,128)S(1)}, f32[4,768,128]{2,1,0:T(8,128)}, u32[]{:S(2)}) copy-start(f32[4,768,128]{2,1,0:T(8,128)} %get-tuple-element.59) | copy-start | bytes 4718596
  171.3 4.1 %collective-permute-start.16 = (f32[4,768,128]{2,1,0:T(8,128)S(1)}, f32[4,768,128]{2,1,0:T(8,128)S(1)}, u32[]{:S(2)}, u32[]{:S(2)}) collective-permute-start(f32[4,768,128]{2,1,0:T(8,128)S(1)} %copy-done.18), channel_id=1, source_target_pairs={{1,5},{2,6},{5,1},{6,2},{9,13},{10,14},{13,9},{14,10},{17,21},{18,... | collective-permute-start | bytes 4718600 | tf_op jit(solution)/shard_map/ppermute | solution.py:418
  172.1 16.8 %collective-permute-start.17 = (f32[768,128]{1,0:T(8,128)}, f32[768,128]{1,0:T(8,128)S(1)}, u32[]{:S(2)}, u32[]{:S(2)}) collective-permute-start(f32[768,128]{1,0:T(8,128)} %get-tuple-element.61), channel_id=1, source_target_pairs={{1,4},{2,7},{5,0},{6,3},{9,12},{10,15},{13,8},{14,11},{17,20},{18,... | collective-permute-start | bytes 1179656 | tf_op jit(solution)/shard_map/ppermute | solution.py:467
  173.4 24.3 %collective-permute-start.20 = (f32[768,128]{1,0:T(8,128)}, f32[768,128]{1,0:T(8,128)S(1)}, u32[]{:S(2)}, u32[]{:S(2)}) collective-permute-start(f32[768,128]{1,0:T(8,128)} %get-tuple-element.64), channel_id=1, source_target_pairs={{1,0},{2,3},{5,4},{6,7},{9,8},{10,11},{13,12},{14,15},{17,16},{18,... | collective-permute-start | bytes 1179656 | tf_op jit(solution)/shard_map/ppermute | solution.py:467
  174.7 27.2 %collective-permute-start.19 = (f32[1024,128]{1,0:T(8,128)}, f32[1024,128]{1,0:T(8,128)S(1)}, u32[]{:S(2)}, u32[]{:S(2)}) collective-permute-start(f32[1024,128]{1,0:T(8,128)} %get-tuple-element.63), channel_id=1, source_target_pairs={{1,5},{2,6},{5,1},{6,2},{9,13},{10,14},{13,9},{14,10},{17,21},{18,... | collective-permute-start | bytes 1572872 | tf_op jit(solution)/shard_map/ppermute | solution.py:418
  188.9 22.0 %collective-permute-start.22 = (f32[1024,128]{1,0:T(8,128)}, f32[1024,128]{1,0:T(8,128)S(1)}, u32[]{:S(2)}, u32[]{:S(2)}) collective-permute-start(f32[1024,128]{1,0:T(8,128)} %get-tuple-element.67), channel_id=1, source_target_pairs={{1,5},{2,6},{5,1},{6,2},{9,13},{10,14},{13,9},{14,10},{17,21},{18,... | collective-permute-start | bytes 1572872 | tf_op jit(solution)/shard_map/ppermute | solution.py:418
  189.6 21.3 %collective-permute-start.23 = (f32[1024,128]{1,0:T(8,128)}, f32[1024,128]{1,0:T(8,128)S(1)}, u32[]{:S(2)}, u32[]{:S(2)}) collective-permute-start(f32[1024,128]{1,0:T(8,128)} %get-tuple-element.68), channel_id=1, source_target_pairs={{1,0},{2,3},{5,4},{6,7},{9,8},{10,11},{13,12},{14,15},{17,16},{18,... | collective-permute-start | bytes 1572872 | tf_op jit(solution)/shard_map/ppermute | solution.py:467
  190.9 29.4 %collective-permute-start.24 = (f32[1024,128]{1,0:T(8,128)}, f32[1024,128]{1,0:T(8,128)S(1)}, u32[]{:S(2)}, u32[]{:S(2)}) collective-permute-start(f32[1024,128]{1,0:T(8,128)} %get-tuple-element.69), channel_id=1, source_target_pairs={{1,4},{2,7},{5,0},{6,3},{9,12},{10,15},{13,8},{14,11},{17,20},{18,... | collective-permute-start | bytes 1572872 | tf_op jit(solution)/shard_map/ppermute | solution.py:467
  197.6 8.1 %collective-permute-start.18 = (f32[768,128]{1,0:T(8,128)}, f32[768,128]{1,0:T(8,128)S(1)}, u32[]{:S(2)}, u32[]{:S(2)}) collective-permute-start(f32[768,128]{1,0:T(8,128)} %shard_map.77), channel_id=1, source_target_pairs={{0,4},{3,7},{4,0},{7,3},{8,12},{11,15},{12,8},{15,11},{16,20},{19,... | collective-permute-start | bytes 1179656 | tf_op jit(solution)/shard_map/ppermute | solution.py:478
  201.9 3.8 %collective-permute-start.21 = (f32[512,128]{1,0:T(8,128)}, f32[512,128]{1,0:T(8,128)S(1)}, u32[]{:S(2)}, u32[]{:S(2)}) collective-permute-start(f32[512,128]{1,0:T(8,128)} %shard_map.78), channel_id=1, source_target_pairs={{0,4},{3,7},{4,0},{7,3},{8,12},{11,15},{12,8},{15,11},{16,20},{19,... | collective-permute-start | bytes 786440 | tf_op jit(solution)/shard_map/ppermute | solution.py:478
  210.9 9.4 %copy-start.10 = (f32[1024,128]{1,0:T(8,128)}, f32[1024,128]{1,0:T(8,128)S(1)}, u32[]{:S(2)}) copy-start(f32[1024,128]{1,0:T(8,128)S(1)} %collective-permute-done.22.core_56) | copy-start | bytes 1572868
  210.9 9.3 %copy-start.11 = (f32[1024,128]{1,0:T(8,128)}, f32[1024,128]{1,0:T(8,128)S(1)}, u32[]{:S(2)}) copy-start(f32[1024,128]{1,0:T(8,128)S(1)} %collective-permute-done.23.end_56) | copy-start | bytes 1572868
  (17 other events, 33.6 us)
